TPU v7x, 32 devices: a whole 2x2x4 slice. The times are simulated.
32 devices in a mesh: groups: 2 (over y), tensor: 4 (over z), width: 4 (over x, core).
Axes of the slice: x: 2, y: 2, z: 4, core: 2. Of those that a mesh axis runs over, the one named last changes fastest.
Arguments:
- tokens: bfloat16 [1024, 8192], P(('groups', 'tensor'), 'width'), parts along dimension 0, may hold values from -60 to 60
- gate_weight: bfloat16 [8192, 14336], P('width', 'tensor'), may hold values from -0.0625 to 0.0625
- up_weight: bfloat16 [8192, 14336], P('width', 'tensor'), may hold values from -0.0625 to 0.0625
- down_weight: bfloat16 [14336, 8192], P('tensor', 'width'), may hold values from -0.046875 to 0.046875
Outputs:
- scaled_output: bfloat16 [1024, 8192], P(('groups', 'tensor'), 'width'), parts along dimension 0
- column_scales: float32 [16384], P(('groups', 'width')), parts along dimension 0
There are 2 independent parts, one for each index of `groups`. A program takes and returns all parts, laid end to end along the dimension named above; an argument that names none is the same for every part. Nothing has to cross between parts.
All inputs are finite; a program needn't handle non-finite values. Where the computation divides by a largest or mean magnitude, that divisor is 1e-20 or more.
Results may differ from a plain program's by a relative error of at most 0.022.
Values may be sent and summed in bfloat16 or wider, within the bound.
No kernel may reach another device: no remote copies, remote signals or barrier semaphores. Data moves between devices by JAX's collectives and lax.ppermute only.
A program may use at most 128 MiB of HBM per device.

v0:
```python
import jax
import jax.numpy as jnp
from jax import lax
from jax.sharding import PartitionSpec as P


def per_device(tokens, gate_weight, up_weight, down_weight):
    units = gate_weight.shape[1]
    piece = lax.all_gather(tokens, "tensor", axis=0, tiled=True)
    gate_part = jnp.dot(piece, gate_weight, preferred_element_type=jnp.float32)
    up_part = jnp.dot(piece, up_weight, preferred_element_type=jnp.float32)
    partial_value = jnp.concatenate([gate_part, up_part], axis=1).astype(jnp.bfloat16)
    sums = lax.psum_scatter(partial_value, "width", scatter_dimension=0, tiled=True).astype(
        jnp.float32
    )
    share = (jax.nn.silu(sums[:, :units]) * sums[:, units:]).astype(jnp.bfloat16)
    hidden = lax.all_gather(share, "width", axis=0, tiled=True)
    output = lax.psum_scatter(
        jnp.dot(hidden, down_weight, preferred_element_type=jnp.float32).astype(jnp.bfloat16),
        "tensor",
        scatter_dimension=0,
        tiled=True,
    ).astype(jnp.float32)
    local_peak = jnp.max(jnp.abs(output), axis=0)
    peak = lax.pmax(local_peak, "tensor")
    scaled_output = (output / (peak + 1e-06)).astype(jnp.bfloat16)
    return (scaled_output, peak / 448.0)


def solution(mesh):
    in_specs = (
        P(("groups", "tensor"), "width"),
        P("width", "tensor"),
        P("width", "tensor"),
        P("tensor", "width"),
    )
    out_specs = (P(("groups", "tensor"), "width"), P(("groups", "width")))
    return jax.shard_map(
        per_device, mesh=mesh, in_specs=in_specs, out_specs=out_specs, check_vma=False
    )
```

profile of v0, /device:TPU:0, one launch (start us, length us, event | category | flops | bytes accessed | tf_op | source)
XLA Modules:
  0.0 267.0 jit_solution(9329863057685077861)
XLA Ops:
  7.2 0.0 all-gather.3.cloned.1.call-start
  7.2 0.7 all-gather.3.cloned.1.call-update
  7.9 0.0 reduce-scatter.3.cloned.1.call-start
  7.9 50.3 %all-gather.3.cloned.1.call-done = bf16[512,2048]{1,0:T(8,128)(2,1)} async-done(((bf16[128,2048]{1,0:T(8,128)(2,1)}), bf16[512,2048]{1,0:T(8,128)(2,1)}) %all-gather.3.cloned.1.call-update) | async-done | bytes 2097168 | tf_op jit(solution)/shard_map/all_gather | solution.py:9
  58.2 0.0 copy-start
  58.2 13.7 %convolution_convert_fusion = bf16[512,3584]{1,0:T(8,128)(2,1)S(1)} fusion(bf16[512,2048]{1,0:T(8,128)(2,1)} %all-gather.3.cloned.1.call-done, bf16[2048,3584]{1,0:T(8,128)(2,1)} %param.6), kind=kOutput, calls=%fused_computation.1 | convolution fusion | flops 7518027776 | bytes 20447232 | tf_op jit(solution)/shard_map/dot_general | solution.py:11
  72.0 0.0 copy-done
  72.0 12.3 %convolution_convert_fusion.1 = bf16[512,3584]{1,0:T(8,128)(2,1)} fusion(bf16[512,2048]{1,0:T(8,128)(2,1)S(1)} %copy-done, bf16[2048,3584]{1,0:T(8,128)(2,1)} %param.5), kind=kOutput, calls=%fused_computation.2 | convolution fusion | flops 7518027776 | bytes 20447232 | tf_op jit(solution)/shard_map/dot_general | solution.py:10
  84.3 6.0 %pad_maximum_fusion = bf16[512,7168]{1,0:T(8,128)(2,1)} fusion(bf16[512,3584]{1,0:T(8,128)(2,1)S(1)} %convolution_convert_fusion, bf16[512,3584]{1,0:T(8,128)(2,1)} %convolution_convert_fusion.1), kind=kLoop, calls=%fused_computation | loop fusion | flops 14680064 | bytes 14680064 | tf_op jit(solution)/shard_map/concatenate | solution.py:12
  90.3 0.0 reduce-scatter.3.cloned.1.call-update
  90.3 0.0 all-gather.5.cloned.1.call-start
  90.4 64.3 %reduce-scatter.3.cloned.1.call-done = bf16[128,7168]{1,0:T(8,128)(2,1)} async-done(((bf16[512,7168]{1,0:T(8,128)(2,1)}), bf16[128,7168]{1,0:T(8,128)(2,1)}) %reduce-scatter.3.cloned.1.call-update) | async-done | bytes 1835024 | tf_op jit(solution)/shard_map/reduce_scatter | solution.py:13
  154.6 1.9 convert_element_type.16
  156.5 1.4 fusion
  157.9 0.0 all-gather.5.cloned.1.call-update
  157.9 0.0 reduce-scatter.5.cloned.1.call-start
  158.0 31.6 %all-gather.5.cloned.1.call-done = bf16[512,3584]{1,0:T(8,128)(2,1)} async-done(((bf16[128,3584]{1,0:T(8,128)(2,1)}), bf16[512,3584]{1,0:T(8,128)(2,1)}) %all-gather.5.cloned.1.call-update) | async-done | bytes 3670032 | tf_op jit(solution)/shard_map/all_gather | solution.py:17
  189.6 13.1 %convolution_convert_fusion.2 = bf16[512,2048]{1,0:T(8,128)(2,1)} fusion(bf16[512,3584]{1,0:T(8,128)(2,1)} %all-gather.5.cloned.1.call-done, bf16[3584,2048]{1,0:T(8,128)(2,1)} %param.7), kind=kOutput, calls=%fused_computation.3 | convolution fusion | flops 7517241344 | bytes 20447232 | tf_op jit(solution)/shard_map/dot_general | solution.py:19
  202.7 0.0 reduce-scatter.5.cloned.1.call-update
  202.7 44.0 %reduce-scatter.5.cloned.1.call-done = bf16[128,2048]{1,0:T(8,128)(2,1)} async-done(((bf16[512,2048]{1,0:T(8,128)(2,1)}), bf16[128,2048]{1,0:T(8,128)(2,1)}) %reduce-scatter.5.cloned.1.call-update) | async-done | bytes 524304 | tf_op jit(solution)/shard_map/reduce_scatter | solution.py:18
  246.7 1.1 fusion.1
  247.9 10.1 %pmax.7 = f32[2048]{0:T(1024)S(1)} all-reduce(f32[2048]{0:T(1024)S(1)} %fusion.1), channel_id=1, replica_groups=mesh['groups'=2,'tensor'=4,'width'=4] {'tensor'}, use_global_device_ids=true, to_apply=%region_3.4 | all-reduce | flops 2048 | bytes 16384 | tf_op jit(solution)/shard_map/pmax | solution.py:25
  257.9 0.6 broadcast_multiply_fusion
  258.5 1.9 fusion.2
Async XLA Ops:
  7.2 51.1 %all-gather.3.cloned.1.call-start = ((), (), s32[]{:S(2)}) async-start(), calls=%async_computation.2 | async-start | bytes 2621440 | tf_op jit(solution)/shard_map/all_gather | solution.py:9
  7.9 146.7 %reduce-scatter.3.cloned.1.call-start = ((), (), s32[]{:S(2)}) async-start(), calls=%async_computation.3 | async-start | bytes 9175040 | tf_op jit(solution)/shard_map/reduce_scatter | solution.py:13
  58.2 13.7 %copy-start = (bf16[512,2048]{1,0:T(8,128)(2,1)S(1)}, bf16[512,2048]{1,0:T(8,128)(2,1)}, u32[]{:S(2)}) copy-start(bf16[512,2048]{1,0:T(8,128)(2,1)} %all-gather.3.cloned.1.call-done) | copy-start | bytes 6291460
  90.3 99.3 %all-gather.5.cloned.1.call-start = ((), (), s32[]{:S(2)}) async-start(), calls=%async_computation.4 | async-start | bytes 4587520 | tf_op jit(solution)/shard_map/all_gather | solution.py:17
  157.9 88.8 %reduce-scatter.5.cloned.1.call-start = ((), (), s32[]{:S(2)}) async-start(), calls=%async_computation.5 | async-start | bytes 2621440 | tf_op jit(solution)/shard_map/reduce_scatter | solution.py:18
Sparse Core Ops, SparseCore 0:
  9.6 48.6 all-gather.2
  90.4 64.1 reduce-scatter.2
  158.0 31.5 all-gather.4
  202.8 43.8 reduce-scatter.4
where the time goes:
time: 267 us
  waiting for transfers between devices  191 us (72%)
  matrix products  39.1 us (15%)
  between operations  13.8 us (5%)
  other arithmetic  12.9 us (5%)
  blocking collectives  10.1 us (4%)
    reduce_scatter x1, waiting for transfers between devices, per_device(): lax.psum_scatter(partial_value, 'width', scatter_dimension=0, tiled=True)  64.3 us
    all_gather x1, waiting for transfers between devices, per_device(): piece = lax.all_gather(tokens, 'tensor', axis=0, tiled=True)  50.3 us
    reduce_scatter x1, waiting for transfers between devices, per_device(): lax.psum_scatter(jnp.dot(hidden, down_weight, preferred_element_type=jnp....  44 us
    all_gather x1, waiting for transfers between devices, per_device(): hidden = lax.all_gather(share, 'width', axis=0, tiled=True)  31.6 us
    dot_general x1, matrix products, per_device(): up_part = jnp.dot(piece, up_weight, preferred_element_type=jnp.float32)  13.7 us
    dot_general x1, matrix products, per_device(): jnp.dot(hidden, down_weight, preferred_element_type=jnp.float32)  13.1 us
    dot_general x1, matrix products, per_device(): gate_part = jnp.dot(piece, gate_weight, preferred_element_type=jnp.float32)  12.3 us
    pmax x1, blocking collectives, per_device(): peak = lax.pmax(local_peak, 'tensor')  10.1 us
  transfers between devices with their start and end apart: 4, of which 4 were waited for; matrix products, arithmetic and copies ran while one was open for 0% of the time, Pallas kernels for 0%

commit v1 on v0

v1 whole, which is shorter than its diff:
```python
import jax
import jax.numpy as jnp
from jax import lax
from jax.experimental import pallas as pl
from jax.experimental.pallas import tpu as pltpu
from jax.sharding import PartitionSpec as P

CORES = 2
CHIPS = 2
WIDTH = CHIPS * CORES
RANKS = 4
AXIS = "tensor"


def swap(value, axis, mask):
    size = RANKS if axis == AXIS else WIDTH
    return lax.ppermute(value, axis, [(i, i ^ mask) for i in range(size)])


def widen(value):
    return value.astype(jnp.float32)


def narrow(value):
    return value.astype(jnp.bfloat16)


def dot(left, right):
    return jnp.dot(left, right, preferred_element_type=jnp.float32)


TILE = 512
GRANT = 4 << 20
COST = (1, 1)
PARTS = 3
VMEM = pl.BlockSpec(memory_space=pltpu.VMEM)


def project_kernel(block_ref, weight_ref, *refs):
    keep_ref, send_ref = refs[-2:]
    cut, units = keep_ref.shape[0], weight_ref.shape[1]
    first = 0 if len(refs) == 2 else units
    for start in range(0, units, TILE):
        value = narrow(dot(block_ref[...], weight_ref[:, start : start + TILE]))
        at = slice(first + start, first + start + TILE)
        keep_ref[:, at] = value[:cut]
        send_ref[:, at] = value[cut:]


def sums_kernel(keep_ref, *refs):
    cores, (mine_ref, send_ref) = refs[:-2], refs[-2:]
    cut = mine_ref.shape[0]
    at = 0
    for core_ref in cores:
        here = slice(at, at + core_ref.shape[1])
        at += core_ref.shape[1]
        chip = narrow(widen(keep_ref[:, here]) + widen(core_ref[...]))
        mine_ref[:, here] = chip[:cut]
        send_ref[:, here] = chip[cut:]


def hidden_kernel(mine_ref, got_ref, send_ref, share_ref, payload_ref, own_ref):
    units = own_ref.shape[1]
    for start in range(0, units, TILE):
        gate = slice(start, start + TILE)
        up = slice(units + start, units + start + TILE)
        both = [widen(mine_ref[:, at]) + widen(got_ref[:, at]) for at in (gate, up)]
        own_ref[:, gate] = narrow(jax.nn.silu(both[0]) * both[1])
    payload_ref[:, : 2 * units] = send_ref[...]
    payload_ref[:, 2 * units :] = own_ref[...]


def hidden_and_join_kernel(
    mine_ref, got_ref, send_ref, share_ref, payload_ref, own_ref, joined_ref
):
    units = own_ref.shape[1]
    cut = own_ref.shape[0]
    hidden_kernel(mine_ref, got_ref, send_ref, share_ref, payload_ref, own_ref)
    joined_ref[:cut] = share_ref[...]
    joined_ref[cut:] = got_ref[:, 2 * units :]


def last_hidden_kernel(mine_ref, got_ref, share_ref, own_ref, joined_ref):
    units = own_ref.shape[1]
    cut = own_ref.shape[0]
    for start in range(0, units, TILE):
        gate = slice(start, start + TILE)
        up = slice(units + start, units + start + TILE)
        both = [widen(mine_ref[:, at]) + widen(got_ref[:, at]) for at in (gate, up)]
        own_ref[:, gate] = narrow(jax.nn.silu(both[0]) * both[1])
    joined_ref[:cut] = share_ref[...]
    joined_ref[cut:] = got_ref[:, 2 * units :]


def output_kernel(mine_ref, core_ref, weight_ref, out_ref):
    hidden = jnp.concatenate([mine_ref[...], core_ref[...]])
    for start in range(0, weight_ref.shape[1], TILE):
        at = slice(start, start + TILE)
        out_ref[:, at] = dot(hidden, weight_ref[:, at]).astype(out_ref.dtype)


def call(kernel, shapes, args, cost, aliases, name):
    flops, size = cost
    return pl.pallas_call(
        kernel,
        out_shape=shapes,
        in_specs=[VMEM] * len(args),
        out_specs=jax.tree.map(lambda _: VMEM, shapes),
        input_output_aliases=aliases,
        compiler_params=pltpu.CompilerParams(vmem_limit_bytes=GRANT),
        cost_estimate=pl.CostEstimate(
            flops=flops, bytes_accessed=size, transcendentals=0
        ),
        name=name,
    )(*args)


def project(block, gate_weight, up_weight):
    rows, units = block.shape[0], gate_weight.shape[1]
    shape = jax.ShapeDtypeStruct((rows // 2, 2 * units), jnp.bfloat16)
    parts = call(
        project_kernel,
        (shape, shape),
        (block, gate_weight),
        COST,
        {},
        "gate",
    )
    return call(
        project_kernel,
        (shape, shape),
        (block, up_weight, *parts),
        COST,
        {2: 0, 3: 1},
        "up",
    )


def combine(mine, core, weight, dtype):
    rows = 2 * mine.shape[0]
    return call(
        output_kernel,
        jax.ShapeDtypeStruct((rows, weight.shape[1]), dtype),
        (mine, core, weight),
        COST,
        {},
        "down",
    )


def plain(tokens, gate_weight, up_weight, down_weight):
    units = gate_weight.shape[1]
    piece = lax.all_gather(tokens, AXIS, axis=0, tiled=True)
    parts = jnp.concatenate([dot(piece, gate_weight), dot(piece, up_weight)], axis=1)
    sums = widen(
        lax.psum_scatter(narrow(parts), "width", scatter_dimension=0, tiled=True)
    )
    share = narrow(jax.nn.silu(sums[:, :units]) * sums[:, units:])
    hidden = lax.all_gather(share, "width", axis=0, tiled=True)
    output = widen(
        lax.psum_scatter(
            narrow(dot(hidden, down_weight)), AXIS, scatter_dimension=0, tiled=True
        )
    )
    peak = lax.pmax(jnp.max(jnp.abs(output), axis=0), AXIS)
    return (narrow(output / (peak + 1e-06)), peak / 448.0)


def pipelined(tokens, gate_weight, up_weight, down_weight):
    units = gate_weight.shape[1]
    me = lax.axis_index("width")
    rows = tokens.shape[0] // WIDTH
    half = rows // 2
    clock = [None]

    def tick(*values):
        if clock[0] is not None:
            values = lax.optimization_barrier((*values, clock[0]))[:-1]
        return values if len(values) > 1 else values[0]

    def done(value):
        clock[0] = value
        return value

    def weave(*blocks):
        return jnp.concatenate(
            [
                block[p * n : (p + 1) * n]
                for p in range(WIDTH)
                for block, n in [(b, b.shape[0] // WIDTH) for b in blocks]
            ]
        )

    def begin(block):
        keep, send = project(tick(block), gate_weight, up_weight)
        done(keep)
        count = send.shape[1] // 128
        cuts = [count * i // PARTS * 128 for i in range(PARTS + 1)]
        return keep, [swap(send[:, a:b], "width", 1) for a, b in zip(cuts, cuts[1:])]

    def add_cores(keep, cores):
        keep, *cores = tick(keep, *cores)
        shape = jax.ShapeDtypeStruct((keep.shape[0] // 2, keep.shape[1]), keep.dtype)
        mine, send = call(
            sums_kernel, (shape, shape), (keep, *cores), COST, {}, "sums"
        )
        done(mine)
        return mine, send

    def hidden(mine, got, send=None, share=None):
        mine, got = tick(mine, got)
        own = jax.ShapeDtypeStruct((mine.shape[0], units), mine.dtype)
        joined = jax.ShapeDtypeStruct((2 * mine.shape[0], units), mine.dtype)
        payload = jax.ShapeDtypeStruct((mine.shape[0], 3 * units), mine.dtype)
        if send is None:
            own, joined = call(
                last_hidden_kernel,
                (own, joined),
                (mine, got, share),
                COST,
                {},
                "hidden",
            )
            payload = own
        elif share is None:
            payload, own = call(
                hidden_kernel, (payload, own), (mine, got, send, send), COST, {}, "hidden"
            )
            joined = None
        else:
            payload, own, joined = call(
                hidden_and_join_kernel,
                (payload, own, joined),
                (mine, got, send, share),
                COST,
                {},
                "hidden",
            )
        done(own)
        return swap(payload, "width", CORES), own, joined

    def finish(mine, core, dtype=jnp.bfloat16):
        mine, core = tick(mine, core)
        return done(combine(mine, core, down_weight, dtype))

    def split(value):
        n = value.shape[0] // (2 * WIDTH)
        parts = [value[i * n : (i + 1) * n] for i in range(2 * WIDTH)]
        return jnp.concatenate(parts[0::2]), jnp.concatenate(parts[1::2])

    order = [x * CORES + c for c in range(CORES) for x in range(CHIPS)]
    own = jnp.concatenate(
        [lax.dynamic_slice_in_dim(tokens, (me ^ j) * rows, rows, 0) for j in order]
    )
    (own,) = lax.optimization_barrier((own,))

    def halves(block):
        first = [block[p * rows : p * rows + half] for p in range(WIDTH)]
        second = [block[p * rows + half : (p + 1) * rows] for p in range(WIDTH)]
        return jnp.concatenate(first), jnp.concatenate(second)

    near = swap(own, AXIS, 1)
    cross = swap(own, AXIS, 2)

    mine0, send0 = add_cores(*begin(own))
    got0 = swap(send0, "width", CORES)
    near, cross = tick(near, cross)
    far = swap(cross, AXIS, 1)
    mine1, send1 = add_cores(*begin(near))

    got1, share0, _ = hidden(mine0, got0, send1)
    cross_first, cross_second = halves(cross)
    far = tick(far)
    far_first, far_second = halves(far)
    mine2, send2 = add_cores(*begin(weave(cross_first, far_first)))

    got2, share1, m0 = hidden(mine1, got1, send2, share0)
    b3 = begin(weave(cross_second, far_second))
    output = finish(m0, swap(m0, "width", 1), jnp.float32)
    mine3, send3 = add_cores(*b3)

    got3, share2, m1 = hidden(mine2, got2, send3, share1)
    p1 = swap(finish(m1, swap(m1, "width", 1)), AXIS, 1)

    got4, share3, m2 = hidden(mine3, got3, None, share2)
    p1 = tick(p1)
    output = done(output + widen(p1))
    cross2, far2 = split(finish(m2, swap(m2, "width", 1), jnp.float32))
    far2 = swap(narrow(far2), AXIS, 1)

    m3 = jnp.concatenate([share3, tick(got4)])
    cross3, far3 = split(finish(m3, swap(m3, "width", 1), jnp.float32))
    far3 = swap(narrow(far3), AXIS, 1)
    far2 = tick(far2)
    z2 = swap(done(narrow(cross2 + widen(far2))), AXIS, 2)
    far3 = tick(far3)
    z3 = swap(done(narrow(cross3 + widen(far3))), AXIS, 2)
    output = output + widen(weave(z2, z3))

    local_peak = jnp.max(jnp.abs(output), axis=0, keepdims=True)
    peak = local_peak
    for k in range(1, RANKS):
        peak = jnp.maximum(peak, swap(local_peak, AXIS, k))
    scaled = narrow(output / (peak + 1e-06))
    result = jnp.zeros_like(scaled)
    for place, j in enumerate(order):
        result = lax.dynamic_update_slice_in_dim(
            result, scaled[place * rows : (place + 1) * rows], (me ^ j) * rows, 0
        )
    return (result, peak[0] / 448.0)


def solution(mesh):
    in_specs = (
        P(("groups", "tensor"), "width"),
        P("width", "tensor"),
        P("width", "tensor"),
        P("tensor", "width"),
    )
    out_specs = (P(("groups", "tensor"), "width"), P(("groups", "width")))
    fits = mesh.shape[AXIS] == RANKS and mesh.shape["width"] == WIDTH
    return jax.shard_map(
        pipelined if fits else plain,
        mesh=mesh,
        in_specs=in_specs,
        out_specs=out_specs,
        check_vma=False,
    )
```

time: 267 us -> 147 us (0.55)
  waiting for transfers between devices: 191 us -> 73.7 us
  matrix products: 39.1 us -> 0 us
  starting transfers between devices: 0.16 us -> 29.2 us
  Pallas kernels: 0 us -> 28.2 us
  local copies, waits for them, and re-layouts: 0.01 us -> 13.4 us
  between operations: 13.8 us -> 1.32 us
  other arithmetic: 12.9 us -> 1.3 us
  blocking collectives: 10.1 us -> 0 us
    reduce_scatter x2 -> x0, waiting for transfers between devices: 108 us -> none  [the longest x1 64.3 us: per_device(): lax.psum_scatter(partial_value, 'width', scatter_dimension=0, tiled=True)]
    all_gather x2 -> x0, waiting for transfers between devices: 81.9 us -> none  [the longest x1 50.3 us: per_device(): piece = lax.all_gather(tokens, 'tensor', axis=0, tiled=True)]
    ppermute x0 -> x32, waiting for transfers between devices: none -> 73.7 us  [swap(): return lax.ppermute(value, axis, [(i, i ^ mask) for i in range(size)])]
    dot_general x3 -> x0, matrix products: 39.1 us -> none  [the longest x1 13.7 us: per_device(): up_part = jnp.dot(piece, up_weight, preferred_element_type=jnp.float32)]
    ppermute x0 -> x32, starting transfers between devices: none -> 29.2 us  [swap(): return lax.ppermute(value, axis, [(i, i ^ mask) for i in range(size)])]
    pallas_call x0 -> x20, Pallas kernels: none -> 28.2 us  [call(): pl.pallas_call(kernel, out_shape=shapes, in_specs=[VMEM] * len(args), out...]
    unnamed x2 -> x45, local copies, waits for them, and re-layouts: 0.01 us -> 11.7 us
    pmax x1 -> x0, blocking collectives: 10.1 us -> none  [per_device(): peak = lax.pmax(local_peak, 'tensor')]
  transfers between devices with their start and end apart: 4 -> 32, of which waited for: 4 -> 19; matrix products, arithmetic and copies ran while one was open for 0% -> 1% of each run, Pallas kernels for 0% -> 17%
where the time goes in v1:
time: 147 us
  waiting for transfers between devices  73.7 us (50%)
  starting transfers between devices  29.2 us (20%)
  Pallas kernels  28.2 us (19%)
  local copies, waits for them, and re-layouts  13.4 us (9%)
    ppermute x32, waiting for transfers between devices, swap(): return lax.ppermute(value, axis, [(i, i ^ mask) for i in range(size)])  73.7 us
    ppermute x32, starting transfers between devices, swap(): return lax.ppermute(value, axis, [(i, i ^ mask) for i in range(size)])  29.2 us
    pallas_call x20, Pallas kernels, call(): pl.pallas_call(kernel, out_shape=shapes, in_specs=[VMEM] * len(args), out...  28.2 us
    unnamed x45, local copies, waits for them, and re-layouts  11.7 us
  transfers between devices with their start and end apart: 32, of which 19 were waited for; matrix products, arithmetic and copies ran while one was open for 1% of the time, Pallas kernels for 17%

profile of v1, /device:TPU:0, one launch (start us, length us, event | category | flops | bytes accessed | tf_op | source)
XLA Modules:
  0.0 147.1 jit_solution(16451138946172182560)
XLA Ops:
  0.7 1.1 constant_dynamic-slice_fusion.3
  1.9 3.1 %collective-permute-start = (bf16[128,2048]{1,0:T(8,128)(2,1)S(1)}, bf16[128,2048]{1,0:T(8,128)(2,1)S(1)}, u32[]{:S(2)}, u32[]{:S(2)}) collective-permute-start(bf16[128,2048]{1,0:T(8,128)(2,1)S(1)} %pad_maximum_fusion.block_ref), channel_id=1, source_target_pairs={{0,4},{4,0},{8,12},{12,8},{1,5},{5,1},{9,13},{13,9},{2,6},{6,2},{1... | collective-permute-start | bytes 1572872 | tf_op jit(solution)/shard_map/ppermute | solution.py:17
  4.9 2.6 %collective-permute-start.1 = (bf16[128,2048]{1,0:T(8,128)(2,1)S(1)}, bf16[128,2048]{1,0:T(8,128)(2,1)S(1)}, u32[]{:S(2)}, u32[]{:S(2)}) collective-permute-start(bf16[128,2048]{1,0:T(8,128)(2,1)S(1)} %pad_maximum_fusion.block_ref), channel_id=1, source_target_pairs={{0,8},{4,12},{8,0},{12,4},{1,9},{5,13},{9,1},{13,5},{2,10},{6,14},... | collective-permute-start | bytes 1572872 | tf_op jit(solution)/shard_map/ppermute | solution.py:17
  7.5 5.2 %copy-done = bf16[2048,3584]{1,0:T(8,128)(2,1)S(1)} copy-done((bf16[2048,3584]{1,0:T(8,128)(2,1)S(1)}, bf16[2048,3584]{1,0:T(8,128)(2,1)}, u32[]{:S(2)}) %copy-start) | copy-done | bytes 14680088
  12.7 2.1 %gate.4 = (bf16[64,7168]{1,0:T(8,128)(2,1)S(1)}, bf16[64,7168]{1,0:T(8,128)(2,1)S(1)}) custom-call(bf16[128,2048]{1,0:T(8,128)(2,1)S(1)} %pad_maximum_fusion.block_ref, bf16[2048,3584]{1,0:T(8,128)(2,1)S(1)} %copy-done), custom_call_target="tpu_custom_call" | custom-call | flops 1 | bytes 1 | tf_op jit(solution)/shard_map/gate/pallas_call | solution.py:104
  14.8 5.5 %copy-done.1 = bf16[2048,3584]{1,0:T(8,128)(2,1)S(1)} copy-done((bf16[2048,3584]{1,0:T(8,128)(2,1)S(1)}, bf16[2048,3584]{1,0:T(8,128)(2,1)}, u32[]{:S(2)}) %copy-start.1) | copy-done | bytes 14680088
  20.3 2.1 %up.4 = (bf16[64,7168]{1,0:T(8,128)(2,1)S(1)}, bf16[64,7168]{1,0:T(8,128)(2,1)S(1)}) custom-call(bf16[128,2048]{1,0:T(8,128)(2,1)S(1)} %pad_maximum_fusion.block_ref, bf16[2048,3584]{1,0:T(8,128)(2,1)S(1)} %copy-done.1, bf16[64,7168]{1,0:T(8,128)(2,1)S(1)} %get-tuple-element.78.refs_0_, ...), custom_call_target="tpu_custom_call", output_to_operand_aliasing={{0}: (2, {}), {1}: (3, {})} | custom-call | flops 1 | bytes 1 | tf_op jit(solution)/shard_map/up/pallas_call | solution.py:104
  23.2 1.8 %collective-permute-done.2.refs_0_ = bf16[64,2304]{1,0:T(8,128)(2,1)S(1)} collective-permute-done((bf16[64,2304]{1,0:T(8,128)(2,1)S(1)}, bf16[64,2304]{1,0:T(8,128)(2,1)S(1)}, u32[]{:S(2)}, u32[]{:S(2)}) %collective-permute-start.2) | collective-permute-done | bytes 294944 | tf_op jit(solution)/shard_map/ppermute | solution.py:17
  25.3 1.6 %collective-permute-start.8 = (bf16[32,7168]{1,0:T(8,128)(2,1)S(1)}, bf16[32,7168]{1,0:T(8,128)(2,1)S(1)}, u32[]{:S(2)}, u32[]{:S(2)}) collective-permute-start(bf16[32,7168]{1,0:T(8,128)(2,1)S(1)} %get-tuple-element.98), channel_id=1, source_target_pairs={{0,2},{1,3},{2,0},{3,1},{4,6},{5,7},{6,4},{7,5},{8,10},{9,11},{10,... | collective-permute-start | bytes 1376264 | tf_op jit(solution)/shard_map/ppermute | solution.py:17
  26.8 1.2 collective-permute-done.block_ref
  28.0 2.5 %collective-permute-done.1 = bf16[128,2048]{1,0:T(8,128)(2,1)S(1)} collective-permute-done((bf16[128,2048]{1,0:T(8,128)(2,1)S(1)}, bf16[128,2048]{1,0:T(8,128)(2,1)S(1)}, u32[]{:S(2)}, u32[]{:S(2)}) %collective-permute-start.1) | collective-permute-done | bytes 524320 | tf_op jit(solution)/shard_map/ppermute | solution.py:17
  30.6 2.1 %gate.5 = (bf16[64,7168]{1,0:T(8,128)(2,1)S(1)}, bf16[64,7168]{1,0:T(8,128)(2,1)S(1)}) custom-call(bf16[128,2048]{1,0:T(8,128)(2,1)S(1)} %collective-permute-done.block_ref, bf16[2048,3584]{1,0:T(8,128)(2,1)S(1)} %bitcast.4), custom_call_target="tpu_custom_call" | custom-call | flops 1 | bytes 1 | tf_op jit(solution)/shard_map/gate/pallas_call | solution.py:104
  32.6 0.5 collective-permute-start.10
  33.2 2.1 %up.5 = (bf16[64,7168]{1,0:T(8,128)(2,1)S(1)}, bf16[64,7168]{1,0:T(8,128)(2,1)S(1)}) custom-call(bf16[128,2048]{1,0:T(8,128)(2,1)S(1)} %collective-permute-done.block_ref, bf16[2048,3584]{1,0:T(8,128)(2,1)S(1)} %bitcast.6, bf16[64,7168]{1,0:T(8,128)(2,1)S(1)} %get-tuple-element.89.refs_0_, ...), custom_call_target="tpu_custom_call", output_to_operand_aliasing={{0}: (2, {}), {1}: (3, {})} | custom-call | flops 1 | bytes 1 | tf_op jit(solution)/shard_map/up/pallas_call | solution.py:104
  36.0 1.9 %collective-permute-done.5.refs_0_ = bf16[64,2304]{1,0:T(8,128)(2,1)S(1)} collective-permute-done((bf16[64,2304]{1,0:T(8,128)(2,1)S(1)}, bf16[64,2304]{1,0:T(8,128)(2,1)S(1)}, u32[]{:S(2)}, u32[]{:S(2)}) %collective-permute-start.5) | collective-permute-done | bytes 294944 | tf_op jit(solution)/shard_map/ppermute | solution.py:17
  38.3 1.6 %collective-permute-start.9 = (bf16[32,10752]{1,0:T(8,128)(2,1)S(1)}, bf16[32,10752]{1,0:T(8,128)(2,1)S(1)}, u32[]{:S(2)}, u32[]{:S(2)}) collective-permute-start(bf16[32,10752]{1,0:T(8,128)(2,1)S(1)} %get-tuple-element.102), channel_id=1, source_target_pairs={{0,2},{1,3},{2,0},{3,1},{4,6},{5,7},{6,4},{7,5},{8,10},{9,11},{10,... | collective-permute-start | bytes 2064392 | tf_op jit(solution)/shard_map/ppermute | solution.py:17
  39.9 4.3 %collective-permute-done.10 = bf16[128,2048]{1,0:T(8,128)(2,1)S(1)} collective-permute-done((bf16[128,2048]{1,0:T(8,128)(2,1)S(1)}, bf16[128,2048]{1,0:T(8,128)(2,1)S(1)}, u32[]{:S(2)}, u32[]{:S(2)}) %collective-permute-start.10) | collective-permute-done | bytes 524320 | tf_op jit(solution)/shard_map/ppermute | solution.py:17
  44.3 2.3 %gate.6 = (bf16[64,7168]{1,0:T(8,128)(2,1)S(1)}, bf16[64,7168]{1,0:T(8,128)(2,1)S(1)}) custom-call(bf16[128,2048]{1,0:T(8,128)(2,1)S(1)} %get-tuple-element.106.block_ref, bf16[2048,3584]{1,0:T(8,128)(2,1)S(1)} %bitcast.4), custom_call_target="tpu_custom_call" | custom-call | flops 1 | bytes 1 | tf_op jit(solution)/shard_map/gate/pallas_call | solution.py:104
  46.5 2.5 %up.6 = (bf16[64,7168]{1,0:T(8,128)(2,1)S(1)}, bf16[64,7168]{1,0:T(8,128)(2,1)S(1)}) custom-call(bf16[128,2048]{1,0:T(8,128)(2,1)S(1)} %get-tuple-element.106.block_ref, bf16[2048,3584]{1,0:T(8,128)(2,1)S(1)} %bitcast.6, bf16[64,7168]{1,0:T(8,128)(2,1)S(1)} %get-tuple-element.107.refs_0_, ...), custom_call_target="tpu_custom_call", output_to_operand_aliasing={{0}: (2, {}), {1}: (3, {})} | custom-call | flops 1 | bytes 1 | tf_op jit(solution)/shard_map/up/pallas_call | solution.py:104
  49.8 1.8 %collective-permute-done.11.refs_0_ = bf16[64,2304]{1,0:T(8,128)(2,1)S(1)} collective-permute-done((bf16[64,2304]{1,0:T(8,128)(2,1)S(1)}, bf16[64,2304]{1,0:T(8,128)(2,1)S(1)}, u32[]{:S(2)}, u32[]{:S(2)}) %collective-permute-start.11) | collective-permute-done | bytes 294944 | tf_op jit(solution)/shard_map/ppermute | solution.py:17
  51.8 4.0 %collective-permute-done.9.got_ref = bf16[32,10752]{1,0:T(8,128)(2,1)S(1)} collective-permute-done((bf16[32,10752]{1,0:T(8,128)(2,1)S(1)}, bf16[32,10752]{1,0:T(8,128)(2,1)S(1)}, u32[]{:S(2)}, u32[]{:S(2)}) %collective-permute-start.9) | collective-permute-done | bytes 688160 | tf_op jit(solution)/shard_map/ppermute | solution.py:17
  56.1 2.3 %gate.7 = (bf16[64,7168]{1,0:T(8,128)(2,1)S(1)}, bf16[64,7168]{1,0:T(8,128)(2,1)S(1)}) custom-call(bf16[128,2048]{1,0:T(8,128)(2,1)S(1)} %get-tuple-element.121.block_ref, bf16[2048,3584]{1,0:T(8,128)(2,1)S(1)} %bitcast.4), custom_call_target="tpu_custom_call" | custom-call | flops 1 | bytes 1 | tf_op jit(solution)/shard_map/gate/pallas_call | solution.py:104
  58.4 1.6 %collective-permute-start.15 = (bf16[32,10752]{1,0:T(8,128)(2,1)S(1)}, bf16[32,10752]{1,0:T(8,128)(2,1)S(1)}, u32[]{:S(2)}, u32[]{:S(2)}) collective-permute-start(bf16[32,10752]{1,0:T(8,128)(2,1)S(1)} %get-tuple-element.127), channel_id=1, source_target_pairs={{0,2},{1,3},{2,0},{3,1},{4,6},{5,7},{6,4},{7,5},{8,10},{9,11},{10,... | collective-permute-start | bytes 2064392 | tf_op jit(solution)/shard_map/ppermute | solution.py:17
  60.0 2.3 %up.7 = (bf16[64,7168]{1,0:T(8,128)(2,1)S(1)}, bf16[64,7168]{1,0:T(8,128)(2,1)S(1)}) custom-call(bf16[128,2048]{1,0:T(8,128)(2,1)S(1)} %get-tuple-element.121.block_ref, bf16[2048,3584]{1,0:T(8,128)(2,1)S(1)} %bitcast.6, bf16[64,7168]{1,0:T(8,128)(2,1)S(1)} %get-tuple-element.122.refs_0_, ...), custom_call_target="tpu_custom_call", output_to_operand_aliasing={{0}: (2, {}), {1}: (3, {})} | custom-call | flops 1 | bytes 1 | tf_op jit(solution)/shard_map/up/pallas_call | solution.py:104
  63.2 2.3 %down.4 = f32[128,2048]{1,0:T(8,128)S(1)} custom-call(bf16[64,3584]{1,0:T(8,128)(2,1)S(1)} %get-tuple-element.125.mine_ref, bf16[64,3584]{1,0:T(8,128)(2,1)S(1)} %collective-permute-done.14.core_ref, bf16[3584,2048]{1,0:T(8,128)(2,1)S(1)} %bitcast.8), custom_call_target="tpu_custom_call" | custom-call | flops 1 | bytes 1 | tf_op jit(solution)/shard_map/down/pallas_call | solution.py:104
  65.8 10.5 %collective-permute-done.15.got_ref = bf16[32,10752]{1,0:T(8,128)(2,1)S(1)} collective-permute-done((bf16[32,10752]{1,0:T(8,128)(2,1)S(1)}, bf16[32,10752]{1,0:T(8,128)(2,1)S(1)}, u32[]{:S(2)}, u32[]{:S(2)}) %collective-permute-start.15) | collective-permute-done | bytes 688160 | tf_op jit(solution)/shard_map/ppermute | solution.py:17
  76.5 1.6 %collective-permute-start.21 = (bf16[32,10752]{1,0:T(8,128)(2,1)S(1)}, bf16[32,10752]{1,0:T(8,128)(2,1)S(1)}, u32[]{:S(2)}, u32[]{:S(2)}) collective-permute-start(bf16[32,10752]{1,0:T(8,128)(2,1)S(1)} %get-tuple-element.141), channel_id=1, source_target_pairs={{0,2},{1,3},{2,0},{3,1},{4,6},{5,7},{6,4},{7,5},{8,10},{9,11},{10,... | collective-permute-start | bytes 2064392 | tf_op jit(solution)/shard_map/ppermute | solution.py:17
  78.0 1.8 %collective-permute-done.19.core_ref = bf16[64,3584]{1,0:T(8,128)(2,1)S(1)} collective-permute-done((bf16[64,3584]{1,0:T(8,128)(2,1)S(1)}, bf16[64,3584]{1,0:T(8,128)(2,1)S(1)}, u32[]{:S(2)}, u32[]{:S(2)}) %collective-permute-start.19) | collective-permute-done | bytes 458784 | tf_op jit(solution)/shard_map/ppermute | solution.py:17
  79.8 2.2 %down.5 = bf16[128,2048]{1,0:T(8,128)(2,1)S(1)} custom-call(bf16[64,3584]{1,0:T(8,128)(2,1)S(1)} %get-tuple-element.139.mine_ref, bf16[64,3584]{1,0:T(8,128)(2,1)S(1)} %collective-permute-done.19.core_ref, bf16[3584,2048]{1,0:T(8,128)(2,1)S(1)} %bitcast.8), custom_call_target="tpu_custom_call" | custom-call | flops 1 | bytes 1 | tf_op jit(solution)/shard_map/down/pallas_call | solution.py:104
  82.0 1.6 %collective-permute-start.20 = (bf16[128,2048]{1,0:T(8,128)(2,1)S(1)}, bf16[128,2048]{1,0:T(8,128)(2,1)S(1)}, u32[]{:S(2)}, u32[]{:S(2)}) collective-permute-start(bf16[128,2048]{1,0:T(8,128)(2,1)S(1)} %down.5), channel_id=1, source_target_pairs={{0,4},{4,0},{8,12},{12,8},{1,5},{5,1},{9,13},{13,9},{2,6},{6,2},{1... | collective-permute-start | bytes 1572872 | tf_op jit(solution)/shard_map/ppermute | solution.py:17
  83.7 9.9 %collective-permute-done.21.got_ref = bf16[32,10752]{1,0:T(8,128)(2,1)S(1)} collective-permute-done((bf16[32,10752]{1,0:T(8,128)(2,1)S(1)}, bf16[32,10752]{1,0:T(8,128)(2,1)S(1)}, u32[]{:S(2)}, u32[]{:S(2)}) %collective-permute-start.21) | collective-permute-done | bytes 688160 | tf_op jit(solution)/shard_map/ppermute | solution.py:17
  93.8 1.6 %collective-permute-start.24 = (bf16[32,3584]{1,0:T(8,128)(2,1)S(1)}, bf16[32,3584]{1,0:T(8,128)(2,1)S(1)}, u32[]{:S(2)}, u32[]{:S(2)}) collective-permute-start(bf16[32,3584]{1,0:T(8,128)(2,1)S(1)} %get-tuple-element.144), channel_id=1, source_target_pairs={{0,2},{1,3},{2,0},{3,1},{4,6},{5,7},{6,4},{7,5},{8,10},{9,11},{10,... | collective-permute-start | bytes 688136 | tf_op jit(solution)/shard_map/ppermute | solution.py:17
  95.4 0.7 collective-permute-done.20
  96.2 2.3 %down.6 = f32[128,2048]{1,0:T(8,128)S(1)} custom-call(bf16[64,3584]{1,0:T(8,128)(2,1)S(1)} %get-tuple-element.147.mine_ref, bf16[64,3584]{1,0:T(8,128)(2,1)S(1)} %collective-permute-done.22.core_ref, bf16[3584,2048]{1,0:T(8,128)(2,1)S(1)} %bitcast.8), custom_call_target="tpu_custom_call" | custom-call | flops 1 | bytes 1 | tf_op jit(solution)/shard_map/down/pallas_call | solution.py:104
  98.6 3.2 %collective-permute-done.24 = bf16[32,3584]{1,0:T(8,128)(2,1)S(1)} collective-permute-done((bf16[32,3584]{1,0:T(8,128)(2,1)S(1)}, bf16[32,3584]{1,0:T(8,128)(2,1)S(1)}, u32[]{:S(2)}, u32[]{:S(2)}) %collective-permute-start.24) | collective-permute-done | bytes 229408 | tf_op jit(solution)/shard_map/ppermute | solution.py:17
  101.9 1.6 %collective-permute-start.23 = (bf16[64,2048]{1,0:T(8,128)(2,1)S(1)}, bf16[64,2048]{1,0:T(8,128)(2,1)S(1)}, u32[]{:S(2)}, u32[]{:S(2)}) collective-permute-start(bf16[64,2048]{1,0:T(8,128)(2,1)S(1)} %pad_maximum_fusion.1), channel_id=1, source_target_pairs={{0,4},{4,0},{8,12},{12,8},{1,5},{5,1},{9,13},{13,9},{2,6},{6,2},{1... | collective-permute-start | bytes 786440 | tf_op jit(solution)/shard_map/ppermute | solution.py:17
  103.7 2.2 %down.7 = f32[128,2048]{1,0:T(8,128)S(1)} custom-call(bf16[64,3584]{1,0:T(8,128)(2,1)S(1)} %constant_dynamic-update-slice_fusion.mine_ref, bf16[64,3584]{1,0:T(8,128)(2,1)S(1)} %collective-permute-done.25.core_ref, bf16[3584,2048]{1,0:T(8,128)(2,1)S(1)} %bitcast.8), custom_call_target="tpu_custom_call" | custom-call | flops 1 | bytes 1 | tf_op jit(solution)/shard_map/down/pallas_call | solution.py:104
  106.0 1.6 %collective-permute-start.27 = (bf16[64,2048]{1,0:T(8,128)(2,1)S(1)}, bf16[64,2048]{1,0:T(8,128)(2,1)S(1)}, u32[]{:S(2)}, u32[]{:S(2)}) collective-permute-start(bf16[64,2048]{1,0:T(8,128)(2,1)S(1)} %pad_maximum_fusion.2), channel_id=1, source_target_pairs={{0,4},{4,0},{8,12},{12,8},{1,5},{5,1},{9,13},{13,9},{2,6},{6,2},{1... | collective-permute-start | bytes 786440 | tf_op jit(solution)/shard_map/ppermute | solution.py:17
  107.7 3.5 %collective-permute-done.23 = bf16[64,2048]{1,0:T(8,128)(2,1)S(1)} collective-permute-done((bf16[64,2048]{1,0:T(8,128)(2,1)S(1)}, bf16[64,2048]{1,0:T(8,128)(2,1)S(1)}, u32[]{:S(2)}, u32[]{:S(2)}) %collective-permute-start.23) | collective-permute-done | bytes 262176 | tf_op jit(solution)/shard_map/ppermute | solution.py:17
  111.2 2.7 %collective-permute-start.26 = (bf16[64,2048]{1,0:T(8,128)(2,1)S(1)}, bf16[64,2048]{1,0:T(8,128)(2,1)S(1)}, u32[]{:S(2)}, u32[]{:S(2)}) collective-permute-start(bf16[64,2048]{1,0:T(8,128)(2,1)S(1)} %fusion), channel_id=1, source_target_pairs={{0,8},{4,12},{8,0},{12,4},{1,9},{5,13},{9,1},{13,5},{2,10},{6,14},... | collective-permute-start | bytes 786440 | tf_op jit(solution)/shard_map/ppermute | solution.py:17
  113.9 6.8 %collective-permute-done.27 = bf16[64,2048]{1,0:T(8,128)(2,1)S(1)} collective-permute-done((bf16[64,2048]{1,0:T(8,128)(2,1)S(1)}, bf16[64,2048]{1,0:T(8,128)(2,1)S(1)}, u32[]{:S(2)}, u32[]{:S(2)}) %collective-permute-start.27) | collective-permute-done | bytes 262176 | tf_op jit(solution)/shard_map/ppermute | solution.py:17
  120.8 11.3 %collective-permute-done.26 = bf16[64,2048]{1,0:T(8,128)(2,1)S(1)} collective-permute-done((bf16[64,2048]{1,0:T(8,128)(2,1)S(1)}, bf16[64,2048]{1,0:T(8,128)(2,1)S(1)}, u32[]{:S(2)}, u32[]{:S(2)}) %collective-permute-start.26) | collective-permute-done | bytes 262176 | tf_op jit(solution)/shard_map/ppermute | solution.py:17
  132.1 4.4 %collective-permute-done.28 = bf16[64,2048]{1,0:T(8,128)(2,1)S(1)} collective-permute-done((bf16[64,2048]{1,0:T(8,128)(2,1)S(1)}, bf16[64,2048]{1,0:T(8,128)(2,1)S(1)}, u32[]{:S(2)}, u32[]{:S(2)}) %collective-permute-start.28) | collective-permute-done | bytes 262176 | tf_op jit(solution)/shard_map/ppermute | solution.py:17
  136.8 3.0 %collective-permute-start.30 = (f32[1,2048]{1,0:T(1,128)S(1)}, f32[1,2048]{1,0:T(1,128)S(1)}, u32[]{:S(2)}, u32[]{:S(2)}) collective-permute-start(f32[1,2048]{1,0:T(1,128)S(1)} %bitcast.11), channel_id=1, source_target_pairs={{0,8},{4,12},{8,0},{12,4},{1,9},{5,13},{9,1},{13,5},{2,10},{6,14},... | collective-permute-start | bytes 24584 | tf_op jit(solution)/shard_map/ppermute | solution.py:17
  139.9 1.3 collective-permute-start.31
  141.5 3.8 %collective-permute-done.31 = f32[1,2048]{1,0:T(1,128)S(1)} collective-permute-done((f32[1,2048]{1,0:T(1,128)S(1)}, f32[1,2048]{1,0:T(1,128)S(1)}, u32[]{:S(2)}, u32[]{:S(2)}) %collective-permute-start.31) | collective-permute-done | bytes 8224 | tf_op jit(solution)/shard_map/ppermute | solution.py:17
  145.3 0.6 broadcast_multiply_fusion
  146.3 0.8 copy-done.2
  (117 shorter events, 6.7 us)
Async XLA Ops:
  1.9 26.1 %collective-permute-start = (bf16[128,2048]{1,0:T(8,128)(2,1)S(1)}, bf16[128,2048]{1,0:T(8,128)(2,1)S(1)}, u32[]{:S(2)}, u32[]{:S(2)}) collective-permute-start(bf16[128,2048]{1,0:T(8,128)(2,1)S(1)} %pad_maximum_fusion.block_ref), channel_id=1, source_target_pairs={{0,4},{4,0},{8,12},{12,8},{1,5},{5,1},{9,13},{13,9},{2,6},{6,2},{1... | collective-permute-start | bytes 1572872 | tf_op jit(solution)/shard_map/ppermute | solution.py:17
  4.9 25.6 %collective-permute-start.1 = (bf16[128,2048]{1,0:T(8,128)(2,1)S(1)}, bf16[128,2048]{1,0:T(8,128)(2,1)S(1)}, u32[]{:S(2)}, u32[]{:S(2)}) collective-permute-start(bf16[128,2048]{1,0:T(8,128)(2,1)S(1)} %pad_maximum_fusion.block_ref), channel_id=1, source_target_pairs={{0,8},{4,12},{8,0},{12,4},{1,9},{5,13},{9,1},{13,5},{2,10},{6,14},... | collective-permute-start | bytes 1572872 | tf_op jit(solution)/shard_map/ppermute | solution.py:17
  7.5 5.2 %copy-start = (bf16[2048,3584]{1,0:T(8,128)(2,1)S(1)}, bf16[2048,3584]{1,0:T(8,128)(2,1)}, u32[]{:S(2)}) copy-start(bf16[2048,3584]{1,0:T(8,128)(2,1)} %weight_ref.18) | copy-start | bytes 44040196
  12.7 17.8 %slice-start = ((s8[14680064]{0:T(1024)(128)(4,1)}), s8[4194304]{0:T(1024)(128)(4,1)S(1)}, s32[]{:S(2)}) async-start(s8[14680064]{0:T(1024)(128)(4,1)} %bitcast.3), calls=%async_computation | async-start | bytes 8388608
  12.7 17.8 %slice-start.1 = ((s8[14680064]{0:T(1024)(128)(4,1)}), s8[4194304]{0:T(1024)(128)(4,1)S(1)}, s32[]{:S(2)}) async-start(s8[14680064]{0:T(1024)(128)(4,1)} %bitcast.3), calls=%async_computation.1 | async-start | bytes 8388608
  14.8 5.5 %copy-start.1 = (bf16[2048,3584]{1,0:T(8,128)(2,1)S(1)}, bf16[2048,3584]{1,0:T(8,128)(2,1)}, u32[]{:S(2)}) copy-start(bf16[2048,3584]{1,0:T(8,128)(2,1)} %weight_ref.19) | copy-start | bytes 44040196
  20.3 10.2 %slice-start.2 = ((s8[14680064]{0:T(1024)(128)(4,1)}), s8[4194304]{0:T(1024)(128)(4,1)S(1)}, s32[]{:S(2)}) async-start(s8[14680064]{0:T(1024)(128)(4,1)} %bitcast.3), calls=%async_computation.2 | async-start | bytes 8388608
  20.3 10.2 %slice-start.3 = ((s8[14680064]{0:T(1024)(128)(4,1)}), s8[2097152]{0:T(1024)(128)(4,1)S(1)}, s32[]{:S(2)}) async-start(s8[14680064]{0:T(1024)(128)(4,1)} %bitcast.3), calls=%async_computation.3 | async-start | bytes 4194304
  20.3 12.8 %slice-start.4 = ((s8[14680064]{0:T(1024)(128)(4,1)}), s8[4194304]{0:T(1024)(128)(4,1)S(1)}, s32[]{:S(2)}) async-start(s8[14680064]{0:T(1024)(128)(4,1)} %bitcast.5), calls=%async_computation.4 | async-start | bytes 8388608
  20.3 12.8 %slice-start.5 = ((s8[14680064]{0:T(1024)(128)(4,1)}), s8[4194304]{0:T(1024)(128)(4,1)S(1)}, s32[]{:S(2)}) async-start(s8[14680064]{0:T(1024)(128)(4,1)} %bitcast.5), calls=%async_computation.5 | async-start | bytes 8388608
  22.4 10.7 %slice-start.6 = ((s8[14680064]{0:T(1024)(128)(4,1)}), s8[4194304]{0:T(1024)(128)(4,1)S(1)}, s32[]{:S(2)}) async-start(s8[14680064]{0:T(1024)(128)(4,1)} %bitcast.5), calls=%async_computation.6 | async-start | bytes 8388608
  22.5 2.5 %collective-permute-start.3 = (bf16[64,2432]{1,0:T(8,128)(2,1)S(1)}, bf16[64,2432]{1,0:T(8,128)(2,1)S(1)}, u32[]{:S(2)}, u32[]{:S(2)}) collective-permute-start(bf16[64,2432]{1,0:T(8,128)(2,1)S(1)} %get-tuple-element.171), channel_id=1, source_target_pairs={{0,1},{1,0},{2,3},{3,2},{4,5},{5,4},{6,7},{7,6},{8,9},{9,8},{10,11... | collective-permute-start | bytes 933896 | tf_op jit(solution)/shard_map/ppermute | solution.py:17
  22.6 2.5 %collective-permute-start.4 = (bf16[64,2432]{1,0:T(8,128)(2,1)S(1)}, bf16[64,2432]{1,0:T(8,128)(2,1)S(1)}, u32[]{:S(2)}, u32[]{:S(2)}) collective-permute-start(bf16[64,2432]{1,0:T(8,128)(2,1)S(1)} %get-tuple-element.170), channel_id=1, source_target_pairs={{0,1},{1,0},{2,3},{3,2},{4,5},{5,4},{6,7},{7,6},{8,9},{9,8},{10,11... | collective-permute-start | bytes 933896 | tf_op jit(solution)/shard_map/ppermute | solution.py:17
  23.1 1.9 %collective-permute-start.2 = (bf16[64,2304]{1,0:T(8,128)(2,1)S(1)}, bf16[64,2304]{1,0:T(8,128)(2,1)S(1)}, u32[]{:S(2)}, u32[]{:S(2)}) collective-permute-start(bf16[64,2304]{1,0:T(8,128)(2,1)S(1)} %slice.176), channel_id=1, source_target_pairs={{0,1},{1,0},{2,3},{3,2},{4,5},{5,4},{6,7},{7,6},{8,9},{9,8},{10,11... | collective-permute-start | bytes 884744 | tf_op jit(solution)/shard_map/ppermute | solution.py:17
  25.3 12.8 %collective-permute-start.8 = (bf16[32,7168]{1,0:T(8,128)(2,1)S(1)}, bf16[32,7168]{1,0:T(8,128)(2,1)S(1)}, u32[]{:S(2)}, u32[]{:S(2)}) collective-permute-start(bf16[32,7168]{1,0:T(8,128)(2,1)S(1)} %get-tuple-element.98), channel_id=1, source_target_pairs={{0,2},{1,3},{2,0},{3,1},{4,6},{5,7},{6,4},{7,5},{8,10},{9,11},{10,... | collective-permute-start | bytes 1376264 | tf_op jit(solution)/shard_map/ppermute | solution.py:17
  30.5 2.6 %slice-start.7 = ((s8[14680064]{0:T(1024)(128)(4,1)}), s8[2097152]{0:T(1024)(128)(4,1)S(1)}, s32[]{:S(2)}) async-start(s8[14680064]{0:T(1024)(128)(4,1)} %bitcast.5), calls=%async_computation.7 | async-start | bytes 4194304
  32.6 11.5 %collective-permute-start.10 = (bf16[128,2048]{1,0:T(8,128)(2,1)S(1)}, bf16[128,2048]{1,0:T(8,128)(2,1)S(1)}, u32[]{:S(2)}, u32[]{:S(2)}) collective-permute-start(bf16[128,2048]{1,0:T(8,128)(2,1)S(1)} %collective-permute-done.1), channel_id=1, source_target_pairs={{0,4},{4,0},{8,12},{12,8},{1,5},{5,1},{9,13},{13,9},{2,6},{6,2},{1... | collective-permute-start | bytes 1572872 | tf_op jit(solution)/shard_map/ppermute | solution.py:17
  35.3 2.5 %collective-permute-start.6 = (bf16[64,2432]{1,0:T(8,128)(2,1)S(1)}, bf16[64,2432]{1,0:T(8,128)(2,1)S(1)}, u32[]{:S(2)}, u32[]{:S(2)}) collective-permute-start(bf16[64,2432]{1,0:T(8,128)(2,1)S(1)} %get-tuple-element.169), channel_id=1, source_target_pairs={{0,1},{1,0},{2,3},{3,2},{4,5},{5,4},{6,7},{7,6},{8,9},{9,8},{10,11... | collective-permute-start | bytes 933896 | tf_op jit(solution)/shard_map/ppermute | solution.py:17
  35.4 2.5 %collective-permute-start.7 = (bf16[64,2432]{1,0:T(8,128)(2,1)S(1)}, bf16[64,2432]{1,0:T(8,128)(2,1)S(1)}, u32[]{:S(2)}, u32[]{:S(2)}) collective-permute-start(bf16[64,2432]{1,0:T(8,128)(2,1)S(1)} %get-tuple-element.168), channel_id=1, source_target_pairs={{0,1},{1,0},{2,3},{3,2},{4,5},{5,4},{6,7},{7,6},{8,9},{9,8},{10,11... | collective-permute-start | bytes 933896 | tf_op jit(solution)/shard_map/ppermute | solution.py:17
  35.9 2.0 %collective-permute-start.5 = (bf16[64,2304]{1,0:T(8,128)(2,1)S(1)}, bf16[64,2304]{1,0:T(8,128)(2,1)S(1)}, u32[]{:S(2)}, u32[]{:S(2)}) collective-permute-start(bf16[64,2304]{1,0:T(8,128)(2,1)S(1)} %slice.179), channel_id=1, source_target_pairs={{0,1},{1,0},{2,3},{3,2},{4,5},{5,4},{6,7},{7,6},{8,9},{9,8},{10,11... | collective-permute-start | bytes 884744 | tf_op jit(solution)/shard_map/ppermute | solution.py:17
  38.3 17.5 %collective-permute-start.9 = (bf16[32,10752]{1,0:T(8,128)(2,1)S(1)}, bf16[32,10752]{1,0:T(8,128)(2,1)S(1)}, u32[]{:S(2)}, u32[]{:S(2)}) collective-permute-start(bf16[32,10752]{1,0:T(8,128)(2,1)S(1)} %get-tuple-element.102), channel_id=1, source_target_pairs={{0,2},{1,3},{2,0},{3,1},{4,6},{5,7},{6,4},{7,5},{8,10},{9,11},{10,... | collective-permute-start | bytes 2064392 | tf_op jit(solution)/shard_map/ppermute | solution.py:17
  49.1 2.5 %collective-permute-start.12 = (bf16[64,2432]{1,0:T(8,128)(2,1)S(1)}, bf16[64,2432]{1,0:T(8,128)(2,1)S(1)}, u32[]{:S(2)}, u32[]{:S(2)}) collective-permute-start(bf16[64,2432]{1,0:T(8,128)(2,1)S(1)} %get-tuple-element.167), channel_id=1, source_target_pairs={{0,1},{1,0},{2,3},{3,2},{4,5},{5,4},{6,7},{7,6},{8,9},{9,8},{10,11... | collective-permute-start | bytes 933896 | tf_op jit(solution)/shard_map/ppermute | solution.py:17
  49.1 2.5 %collective-permute-start.13 = (bf16[64,2432]{1,0:T(8,128)(2,1)S(1)}, bf16[64,2432]{1,0:T(8,128)(2,1)S(1)}, u32[]{:S(2)}, u32[]{:S(2)}) collective-permute-start(bf16[64,2432]{1,0:T(8,128)(2,1)S(1)} %get-tuple-element.166), channel_id=1, source_target_pairs={{0,1},{1,0},{2,3},{3,2},{4,5},{5,4},{6,7},{7,6},{8,9},{9,8},{10,11... | collective-permute-start | bytes 933896 | tf_op jit(solution)/shard_map/ppermute | solution.py:17
  49.7 1.9 %collective-permute-start.11 = (bf16[64,2304]{1,0:T(8,128)(2,1)S(1)}, bf16[64,2304]{1,0:T(8,128)(2,1)S(1)}, u32[]{:S(2)}, u32[]{:S(2)}) collective-permute-start(bf16[64,2304]{1,0:T(8,128)(2,1)S(1)} %slice.190), channel_id=1, source_target_pairs={{0,1},{1,0},{2,3},{3,2},{4,5},{5,4},{6,7},{7,6},{8,9},{9,8},{10,11... | collective-permute-start | bytes 884744 | tf_op jit(solution)/shard_map/ppermute | solution.py:17
  56.0 7.1 %slice-start.8 = ((s8[14680064]{0:T(1024)(128)(4,1)}), s8[4194304]{0:T(1024)(128)(4,1)S(1)}, s32[]{:S(2)}) async-start(s8[14680064]{0:T(1024)(128)(4,1)} %bitcast.7), calls=%async_computation.8 | async-start | bytes 8388608
  56.0 7.1 %slice-start.9 = ((s8[14680064]{0:T(1024)(128)(4,1)}), s8[4194304]{0:T(1024)(128)(4,1)S(1)}, s32[]{:S(2)}) async-start(s8[14680064]{0:T(1024)(128)(4,1)} %bitcast.7), calls=%async_computation.9 | async-start | bytes 8388608
  58.3 4.8 %collective-permute-start.14 = (bf16[64,3584]{1,0:T(8,128)(2,1)S(1)}, bf16[64,3584]{1,0:T(8,128)(2,1)S(1)}, u32[]{:S(2)}, u32[]{:S(2)}) collective-permute-start(bf16[64,3584]{1,0:T(8,128)(2,1)S(1)} %get-tuple-element.125.mine_ref), channel_id=1, source_target_pairs={{0,1},{1,0},{2,3},{3,2},{4,5},{5,4},{6,7},{7,6},{8,9},{9,8},{10,11... | collective-permute-start | bytes 1376264 | tf_op jit(solution)/shard_map/ppermute | solution.py:17
  58.4 17.9 %collective-permute-start.15 = (bf16[32,10752]{1,0:T(8,128)(2,1)S(1)}, bf16[32,10752]{1,0:T(8,128)(2,1)S(1)}, u32[]{:S(2)}, u32[]{:S(2)}) collective-permute-start(bf16[32,10752]{1,0:T(8,128)(2,1)S(1)} %get-tuple-element.127), channel_id=1, source_target_pairs={{0,2},{1,3},{2,0},{3,1},{4,6},{5,7},{6,4},{7,5},{8,10},{9,11},{10,... | collective-permute-start | bytes 2064392 | tf_op jit(solution)/shard_map/ppermute | solution.py:17
  60.0 3.2 %slice-start.10 = ((s8[14680064]{0:T(1024)(128)(4,1)}), s8[4194304]{0:T(1024)(128)(4,1)S(1)}, s32[]{:S(2)}) async-start(s8[14680064]{0:T(1024)(128)(4,1)} %bitcast.7), calls=%async_computation.10 | async-start | bytes 8388608
  60.0 3.2 %slice-start.11 = ((s8[14680064]{0:T(1024)(128)(4,1)}), s8[2097152]{0:T(1024)(128)(4,1)S(1)}, s32[]{:S(2)}) async-start(s8[14680064]{0:T(1024)(128)(4,1)} %bitcast.7), calls=%async_computation.11 | async-start | bytes 4194304
  62.3 3.2 %collective-permute-start.17 = (bf16[64,2432]{1,0:T(8,128)(2,1)S(1)}, bf16[64,2432]{1,0:T(8,128)(2,1)S(1)}, u32[]{:S(2)}, u32[]{:S(2)}) collective-permute-start(bf16[64,2432]{1,0:T(8,128)(2,1)S(1)} %get-tuple-element.165), channel_id=1, source_target_pairs={{0,1},{1,0},{2,3},{3,2},{4,5},{5,4},{6,7},{7,6},{8,9},{9,8},{10,11... | collective-permute-start | bytes 933896 | tf_op jit(solution)/shard_map/ppermute | solution.py:17
  62.5 3.0 %collective-permute-start.18 = (bf16[64,2432]{1,0:T(8,128)(2,1)S(1)}, bf16[64,2432]{1,0:T(8,128)(2,1)S(1)}, u32[]{:S(2)}, u32[]{:S(2)}) collective-permute-start(bf16[64,2432]{1,0:T(8,128)(2,1)S(1)} %get-tuple-element.164), channel_id=1, source_target_pairs={{0,1},{1,0},{2,3},{3,2},{4,5},{5,4},{6,7},{7,6},{8,9},{9,8},{10,11... | collective-permute-start | bytes 933896 | tf_op jit(solution)/shard_map/ppermute | solution.py:17
  62.9 2.6 %collective-permute-start.16 = (bf16[64,2304]{1,0:T(8,128)(2,1)S(1)}, bf16[64,2304]{1,0:T(8,128)(2,1)S(1)}, u32[]{:S(2)}, u32[]{:S(2)}) collective-permute-start(bf16[64,2304]{1,0:T(8,128)(2,1)S(1)} %slice.201), channel_id=1, source_target_pairs={{0,1},{1,0},{2,3},{3,2},{4,5},{5,4},{6,7},{7,6},{8,9},{9,8},{10,11... | collective-permute-start | bytes 884744 | tf_op jit(solution)/shard_map/ppermute | solution.py:17
  76.5 17.1 %collective-permute-start.21 = (bf16[32,10752]{1,0:T(8,128)(2,1)S(1)}, bf16[32,10752]{1,0:T(8,128)(2,1)S(1)}, u32[]{:S(2)}, u32[]{:S(2)}) collective-permute-start(bf16[32,10752]{1,0:T(8,128)(2,1)S(1)} %get-tuple-element.141), channel_id=1, source_target_pairs={{0,2},{1,3},{2,0},{3,1},{4,6},{5,7},{6,4},{7,5},{8,10},{9,11},{10,... | collective-permute-start | bytes 2064392 | tf_op jit(solution)/shard_map/ppermute | solution.py:17
  78.0 1.8 %collective-permute-start.19 = (bf16[64,3584]{1,0:T(8,128)(2,1)S(1)}, bf16[64,3584]{1,0:T(8,128)(2,1)S(1)}, u32[]{:S(2)}, u32[]{:S(2)}) collective-permute-start(bf16[64,3584]{1,0:T(8,128)(2,1)S(1)} %get-tuple-element.139.mine_ref), channel_id=1, source_target_pairs={{0,1},{1,0},{2,3},{3,2},{4,5},{5,4},{6,7},{7,6},{8,9},{9,8},{10,11... | collective-permute-start | bytes 1376264 | tf_op jit(solution)/shard_map/ppermute | solution.py:17
  82.0 14.0 %collective-permute-start.20 = (bf16[128,2048]{1,0:T(8,128)(2,1)S(1)}, bf16[128,2048]{1,0:T(8,128)(2,1)S(1)}, u32[]{:S(2)}, u32[]{:S(2)}) collective-permute-start(bf16[128,2048]{1,0:T(8,128)(2,1)S(1)} %down.5), channel_id=1, source_target_pairs={{0,4},{4,0},{8,12},{12,8},{1,5},{5,1},{9,13},{13,9},{2,6},{6,2},{1... | collective-permute-start | bytes 1572872 | tf_op jit(solution)/shard_map/ppermute | solution.py:17
  93.7 2.5 %collective-permute-start.22 = (bf16[64,3584]{1,0:T(8,128)(2,1)S(1)}, bf16[64,3584]{1,0:T(8,128)(2,1)S(1)}, u32[]{:S(2)}, u32[]{:S(2)}) collective-permute-start(bf16[64,3584]{1,0:T(8,128)(2,1)S(1)} %get-tuple-element.147.mine_ref), channel_id=1, source_target_pairs={{0,1},{1,0},{2,3},{3,2},{4,5},{5,4},{6,7},{7,6},{8,9},{9,8},{10,11... | collective-permute-start | bytes 1376264 | tf_op jit(solution)/shard_map/ppermute | solution.py:17
  93.8 8.0 %collective-permute-start.24 = (bf16[32,3584]{1,0:T(8,128)(2,1)S(1)}, bf16[32,3584]{1,0:T(8,128)(2,1)S(1)}, u32[]{:S(2)}, u32[]{:S(2)}) collective-permute-start(bf16[32,3584]{1,0:T(8,128)(2,1)S(1)} %get-tuple-element.144), channel_id=1, source_target_pairs={{0,2},{1,3},{2,0},{3,1},{4,6},{5,7},{6,4},{7,5},{8,10},{9,11},{10,... | collective-permute-start | bytes 688136 | tf_op jit(solution)/shard_map/ppermute | solution.py:17
  101.8 1.9 %collective-permute-start.25 = (bf16[64,3584]{1,0:T(8,128)(2,1)S(1)}, bf16[64,3584]{1,0:T(8,128)(2,1)S(1)}, u32[]{:S(2)}, u32[]{:S(2)}) collective-permute-start(bf16[64,3584]{1,0:T(8,128)(2,1)S(1)} %constant_dynamic-update-slice_fusion.mine_ref), channel_id=1, source_target_pairs={{0,1},{1,0},{2,3},{3,2},{4,5},{5,4},{6,7},{7,6},{8,9},{9,8},{10,11... | collective-permute-start | bytes 1376264 | tf_op jit(solution)/shard_map/ppermute | solution.py:17
  101.9 9.2 %collective-permute-start.23 = (bf16[64,2048]{1,0:T(8,128)(2,1)S(1)}, bf16[64,2048]{1,0:T(8,128)(2,1)S(1)}, u32[]{:S(2)}, u32[]{:S(2)}) collective-permute-start(bf16[64,2048]{1,0:T(8,128)(2,1)S(1)} %pad_maximum_fusion.1), channel_id=1, source_target_pairs={{0,4},{4,0},{8,12},{12,8},{1,5},{5,1},{9,13},{13,9},{2,6},{6,2},{1... | collective-permute-start | bytes 786440 | tf_op jit(solution)/shard_map/ppermute | solution.py:17
  106.0 14.7 %collective-permute-start.27 = (bf16[64,2048]{1,0:T(8,128)(2,1)S(1)}, bf16[64,2048]{1,0:T(8,128)(2,1)S(1)}, u32[]{:S(2)}, u32[]{:S(2)}) collective-permute-start(bf16[64,2048]{1,0:T(8,128)(2,1)S(1)} %pad_maximum_fusion.2), channel_id=1, source_target_pairs={{0,4},{4,0},{8,12},{12,8},{1,5},{5,1},{9,13},{13,9},{2,6},{6,2},{1... | collective-permute-start | bytes 786440 | tf_op jit(solution)/shard_map/ppermute | solution.py:17
  111.2 20.9 %collective-permute-start.26 = (bf16[64,2048]{1,0:T(8,128)(2,1)S(1)}, bf16[64,2048]{1,0:T(8,128)(2,1)S(1)}, u32[]{:S(2)}, u32[]{:S(2)}) collective-permute-start(bf16[64,2048]{1,0:T(8,128)(2,1)S(1)} %fusion), channel_id=1, source_target_pairs={{0,8},{4,12},{8,0},{12,4},{1,9},{5,13},{9,1},{13,5},{2,10},{6,14},... | collective-permute-start | bytes 786440 | tf_op jit(solution)/shard_map/ppermute | solution.py:17
  120.8 15.8 %collective-permute-start.28 = (bf16[64,2048]{1,0:T(8,128)(2,1)S(1)}, bf16[64,2048]{1,0:T(8,128)(2,1)S(1)}, u32[]{:S(2)}, u32[]{:S(2)}) collective-permute-start(bf16[64,2048]{1,0:T(8,128)(2,1)S(1)} %fusion.1), channel_id=1, source_target_pairs={{0,8},{4,12},{8,0},{12,4},{1,9},{5,13},{9,1},{13,5},{2,10},{6,14},... | collective-permute-start | bytes 786440 | tf_op jit(solution)/shard_map/ppermute | solution.py:17
  136.8 4.5 %collective-permute-start.29 = (f32[1,2048]{1,0:T(1,128)S(1)}, f32[1,2048]{1,0:T(1,128)S(1)}, u32[]{:S(2)}, u32[]{:S(2)}) collective-permute-start(f32[1,2048]{1,0:T(1,128)S(1)} %bitcast.10), channel_id=1, source_target_pairs={{0,4},{4,0},{8,12},{12,8},{1,5},{5,1},{9,13},{13,9},{2,6},{6,2},{1... | collective-permute-start | bytes 24584 | tf_op jit(solution)/shard_map/ppermute | solution.py:17
  136.8 4.7 %collective-permute-start.30 = (f32[1,2048]{1,0:T(1,128)S(1)}, f32[1,2048]{1,0:T(1,128)S(1)}, u32[]{:S(2)}, u32[]{:S(2)}) collective-permute-start(f32[1,2048]{1,0:T(1,128)S(1)} %bitcast.11), channel_id=1, source_target_pairs={{0,8},{4,12},{8,0},{12,4},{1,9},{5,13},{9,1},{13,5},{2,10},{6,14},... | collective-permute-start | bytes 24584 | tf_op jit(solution)/shard_map/ppermute | solution.py:17
  139.9 5.4 %collective-permute-start.31 = (f32[1,2048]{1,0:T(1,128)S(1)}, f32[1,2048]{1,0:T(1,128)S(1)}, u32[]{:S(2)}, u32[]{:S(2)}) collective-permute-start(f32[1,2048]{1,0:T(1,128)S(1)} %bitcast.12), channel_id=1, source_target_pairs={{0,12},{4,8},{8,4},{12,0},{1,13},{5,9},{9,5},{13,1},{2,14},{6,10},... | collective-permute-start | bytes 24584 | tf_op jit(solution)/shard_map/ppermute | solution.py:17
  146.3 0.8 copy-start.2

commit v2 on v0

v2 whole, which is shorter than its diff:
```python
import jax
import jax.numpy as jnp
from jax import lax
from jax.experimental import pallas as pl
from jax.experimental.pallas import tpu as pltpu
from jax.sharding import PartitionSpec as P

CORES = 2
CHIPS = 2
WIDTH = CHIPS * CORES
RANKS = 4
AXIS = "tensor"

TILE = 512
LANES = 128
GRANT = 4 << 20
VMEM = pl.BlockSpec(memory_space=pltpu.VMEM)
SMALL = (1, 1)


def swap(value, axis, mask):
    size = RANKS if axis == AXIS else WIDTH
    return lax.ppermute(value, axis, [(i, i ^ mask) for i in range(size)])


def swap_pieces(values):
    return [swap(value, "width", 1) for value in values]


def widen(value):
    return value.astype(jnp.float32)


def narrow(value):
    return value.astype(jnp.bfloat16)


def dot(left, right):
    return jnp.dot(left, right, preferred_element_type=jnp.float32)


def array(rows, columns, dtype=jnp.bfloat16):
    return jax.ShapeDtypeStruct((rows, columns), dtype)


def call(kernel, shapes, args, name, cost=SMALL, aliases=None):
    flops, size = cost
    return pl.pallas_call(
        kernel,
        out_shape=shapes,
        in_specs=[VMEM] * len(args),
        out_specs=jax.tree.map(lambda _: VMEM, shapes),
        input_output_aliases=aliases or {},
        compiler_params=pltpu.CompilerParams(vmem_limit_bytes=GRANT),
        cost_estimate=pl.CostEstimate(
            flops=flops, bytes_accessed=size, transcendentals=0
        ),
        name=name,
    )(*args)


def cuts(columns, count):
    return [columns // LANES * i // count * LANES for i in range(count + 1)]


def rows_of(order, index, rows):
    return [pl.multiple_of((index ^ j) * rows, rows) for j in order]


ORDER = [x * CORES + c for c in range(CORES) for x in range(CHIPS)]


def arrange_kernel(tokens_ref, own_ref):
    rows = tokens_ref.shape[0] // WIDTH
    half = rows // 2
    starts = rows_of(ORDER, lax.axis_index("width"), rows)
    at = 0
    for pair in (starts[:CHIPS], starts[CHIPS:]):
        for offset in (0, half):
            for start in pair:
                own_ref[at : at + half] = tokens_ref[
                    pl.ds(pl.multiple_of(start + offset, half), half)
                ]
                at += half


def halves_kernel(block_ref, first_ref, second_ref):
    n = block_ref.shape[0] // 4
    first_ref[:n] = block_ref[:n]
    second_ref[:n] = block_ref[n : 2 * n]
    first_ref[n:] = block_ref[2 * n : 3 * n]
    second_ref[n:] = block_ref[3 * n :]


def halves(block):
    shape = array(block.shape[0] // 2, block.shape[1])
    return call(halves_kernel, (shape, shape), (block,), "halves")


def project_kernel(plan, blocks, base, *refs):
    block_refs, weight_ref = refs[:blocks], refs[blocks]
    keep_ref, *send_refs = refs[len(refs) - 1 - sum(len(p[2]) - 1 for p in plan) :]
    parts = [ref[...] for ref in block_refs]
    if blocks > 1:
        n = parts[0].shape[0] // 2
        block = jnp.concatenate([p[:n] for p in parts] + [p[n:] for p in parts])
    else:
        block = parts[0]
    cut, units = keep_ref.shape[0], weight_ref.shape[1]
    edges = {0, units}
    edges.update(range(0, units, TILE))
    for _, _, bounds in plan:
        edges.update(b - base for b in bounds if base < b < base + units)
    edges = sorted(edges)
    for low, high in zip(edges, edges[1:]):
        value = narrow(dot(block, weight_ref[:, low:high]))
        keep_ref[:, base + low : base + high] = value[:cut]
        index = 0
        for first, count, bounds in plan:
            for a, b in zip(bounds, bounds[1:]):
                if a <= base + low < b:
                    rows = slice(cut + first, cut + first + count)
                    send_refs[index][:, base + low - a : base + high - a] = value[rows]
                index += 1


def project(blocks, weights, plan, cost=SMALL):
    rows, units = sum(b.shape[0] for b in blocks), weights[0].shape[1]
    shapes = [array(rows // 2, 2 * units)]
    for _, count, bounds in plan:
        shapes += [array(count, b - a) for a, b in zip(bounds, bounds[1:])]
    shapes = tuple(shapes)
    parts = ()
    for base, weight, name in zip((0, units), weights, ("gate", "up")):

        def kernel(*refs, base=base):
            project_kernel(plan, len(blocks), base, *refs)

        args = (*blocks, weight, *parts)
        aliases = {len(blocks) + 1 + i: i for i in range(len(parts))}
        parts = call(kernel, shapes, args, name, SMALL if base else cost, aliases)
    return parts


def sums_kernel(group, first, cores, keep_ref, *refs):
    cores, outs = refs[:cores], refs[cores:]
    rows, units = cores[0].shape[0], outs[0].shape[1]
    count, half = rows // group, group // 2
    each = 2 * count // len(outs)
    at = 0
    for core_ref in cores:
        low, high = at, at + core_ref.shape[1]
        at = high
        for a, b in ((low, min(high, units)), (max(low, units), high)):
            if a >= b:
                continue
            up = a >= units
            columns = slice(a - units, b - units) if up else slice(a, b)
            chip = narrow(
                widen(keep_ref[first : first + rows, a:b])
                + widen(core_ref[:, a - low : b - low])
            )
            base = each * half if up else 0
            for g in range(count):
                mine_ref, send_ref = outs[g // each * 2 : g // each * 2 + 2]
                to = slice(base + g % each * half, base + (g % each + 1) * half)
                mine_ref[to, columns] = chip[g * group : g * group + half]
                send_ref[to, columns] = chip[g * group + half : (g + 1) * group]


def add_cores(keep, cores, group, first=0, split=1):
    units = keep.shape[1] // 2
    shape = array(cores[0].shape[0] // split, units)

    def kernel(*refs):
        sums_kernel(group, first, len(cores), *refs)

    return call(kernel, (shape,) * (2 * split), (keep, *cores), "sums")


def activate(mine_ref, got_ref, own_ref):
    rows, units = own_ref.shape
    for start in range(0, units, TILE):
        at = slice(start, start + TILE)
        gate = widen(mine_ref[:rows, at]) + widen(got_ref[:rows, at])
        up = widen(mine_ref[rows:, at]) + widen(got_ref[rows : 2 * rows, at])
        own_ref[:, at] = narrow(jax.nn.silu(gate) * up)


def hidden(mine, got, send=None, share=None):
    rows, units = mine.shape[0] // 2, mine.shape[1]
    shapes = [array(rows, units)]
    args = [mine, got]
    if send is not None:
        shapes.append(array(send.shape[0] + rows, units))
        args.append(send)
    if share is not None:
        shapes.append(array(2 * share.shape[0], units))
        args.append(share)

    def kernel(*refs):
        refs = list(refs)
        mine_ref, got_ref = refs[:2]
        outs = refs[len(args) :]
        activate(mine_ref, got_ref, outs[0])
        if send is not None:
            outs[1][: send.shape[0]] = refs[2][...]
            outs[1][send.shape[0] :] = outs[0][...]
        if share is not None:
            n = share.shape[0]
            outs[-1][:n] = refs[len(args) - 1][...]
            outs[-1][n:] = got_ref[2 * rows : 2 * rows + n]

    return call(kernel, tuple(shapes), tuple(args), "hidden")


def join_kernel(share_ref, got_ref, out_ref):
    n = share_ref.shape[0]
    out_ref[:n] = share_ref[...]
    out_ref[n:] = got_ref[...]


def join(share, got):
    shape = array(2 * share.shape[0], share.shape[1])
    return call(join_kernel, shape, (share, got), "join")


def stack_kernel(first_ref, second_ref, out_ref):
    n = first_ref.shape[0]
    out_ref[:n] = first_ref[...]
    out_ref[n:] = second_ref[...]


def join_rows(first, second):
    shape = array(first.shape[0] + second.shape[0], first.shape[1])
    return call(stack_kernel, shape, (first, second), "stack")


def combine(mine, cores, weight, dtypes):
    rows, columns = 2 * mine.shape[0], weight.shape[1]
    count = len(dtypes)
    piece = rows // WIDTH // count
    shapes = tuple(array(rows // count, columns, dtype) for dtype in dtypes)

    def kernel(mine_ref, *refs):
        core_refs, weight_ref, outs = refs[: len(cores)], refs[len(cores)], refs[-count:]
        core = [ref[...] for ref in core_refs]
        core = jnp.concatenate(core, axis=1) if len(core) > 1 else core[0]
        value = jnp.concatenate([mine_ref[...], core])
        for start in range(0, columns, TILE):
            at = slice(start, start + TILE)
            result = dot(value, weight_ref[:, at])
            for p in range(WIDTH):
                for i, out_ref in enumerate(outs):
                    n = (p * count + i) * piece
                    out_ref[p * piece : (p + 1) * piece, at] = result[
                        n : n + piece
                    ].astype(out_ref.dtype)

    return call(kernel, shapes, (mine, *cores, weight), "down")


def add_kernel(part_ref, got_ref, out_ref):
    out_ref[...] = narrow(part_ref[...] + widen(got_ref[...]))


def scale_kernel(first_ref, second_ref, peak_ref, out_ref):
    rows = out_ref.shape[0] // WIDTH
    half = rows // 2
    starts = rows_of(ORDER, lax.axis_index("width"), rows)
    peak = peak_ref[...] + 1e-06
    for place, start in enumerate(starts):
        here = slice(place * half, (place + 1) * half)
        for offset, ref in ((0, first_ref), (half, second_ref)):
            to = pl.ds(pl.multiple_of(start + offset, half), half)
            out_ref[to] = narrow(ref[here] / peak)


def pipelined(tokens, gate_weight, up_weight, down_weight):
    units = gate_weight.shape[1]
    weights = (gate_weight, up_weight)
    rows = tokens.shape[0]
    stay = rows // 2
    group = stay // 2
    three, two = cuts(2 * units, 3), cuts(2 * units, 2)
    uneven = [0, three[2], 2 * units]
    clock = []

    def ticks(values):
        if clock:
            values = lax.optimization_barrier((*values, *clock))[: len(values)]
            clock[:] = [values[0]]
        return list(values)

    def tick(value):
        return ticks([value])[0]

    def done(values):
        clock.append(values[0] if isinstance(values, (tuple, list)) else values)
        return values

    def parts_of(mine, count):
        bounds = cuts(units, count)
        shapes = [array(mine.shape[0], b - a) for a, b in zip(bounds, bounds[1:])]

        def kernel(mine_ref, *outs):
            for a, b, out_ref in zip(bounds, bounds[1:], outs):
                out_ref[...] = mine_ref[:, a:b]

        return swap_pieces(call(kernel, tuple(shapes), (mine,), "pieces"))

    def arrange(block, cost=SMALL):
        return call(arrange_kernel, array(*block.shape), (block,), "arrange", cost)

    big, wide = rows * tokens.shape[1] * units, gate_weight.size
    near = swap(tokens, AXIS, 1)
    own = arrange(tokens, (8 * big, 4 * wide))
    own_first, own_second = halves(own)
    cross_first = swap(own_first, AXIS, 2)

    keep, *sends = project((own,), weights, [(0, stay, three)], (4 * big, 2 * wide))
    done(keep)
    cores = ticks(swap_pieces(sends))
    mine0, send0 = done(add_cores(keep, cores, group))
    got0 = swap(send0, "width", CORES)

    near = done(arrange(tick(near)))
    keep1, *sends = done(
        project((near,), weights, [(0, group, uneven), (group, group, two)])
    )
    cross_first, *sends = ticks([cross_first, *sends])
    sends5 = sends[2:]
    far_first = swap(cross_first, AXIS, 1)
    cross_second = swap(own_second, AXIS, 2)
    cores = ticks(swap_pieces(sends[:2]))
    mine1, send1 = done(add_cores(keep1, cores, group))

    got0 = tick(got0)
    share0, payload = done(hidden(mine0, got0, send1))
    got1 = swap(payload, "width", CORES)

    cores = ticks(swap_pieces(ticks(sends5)))
    mine5, send5 = done(add_cores(keep1, cores, group, group))

    got1 = tick(got1)
    share1, payload, joined0 = done(hidden(mine1, got1, send5, share0))
    got5 = swap(payload, "width", CORES)
    far_first = done(tick(far_first))
    keep, *sends = done(project((cross_first, far_first), weights, [(0, stay, three)]))
    cross_second, *sends = ticks([cross_second, *sends])
    far_second = swap(cross_second, AXIS, 1)
    cores = ticks(swap_pieces(sends))
    mine2, send2 = done(add_cores(keep, cores, group))

    got5 = tick(got5)
    share5, joined1 = done(hidden(mine5, got5, None, share1))
    got2 = swap(send2, "width", CORES)
    far_second = done(tick(far_second))
    keep, *sends = done(
        project((cross_second, far_second), weights, [(0, stay, three)])
    )
    got2, core1, *cores = ticks(
        [got2, swap(joined1, "width", 1), *swap_pieces(sends)]
    )

    (share2,) = done(hidden(mine2, got2))
    over2 = swap(share2, "width", CORES)
    mine3, send3, mine4, send4 = done(add_cores(keep, cores, group, split=2))
    payload = done(join_rows(send4, share5))
    (part1,) = done(combine(joined1, [core1], down_weight, (jnp.bfloat16,)))
    add1 = swap(part1, AXIS, 1)
    core0 = tick(swap(joined0, "width", 1))
    first, second = done(
        combine(joined0, [core0], down_weight, (jnp.float32, jnp.float32))
    )
    over2, payload = ticks([over2, payload])
    got4 = swap(payload, "width", CORES)
    joined2 = done(join(share2, over2))
    core2 = ticks(parts_of(joined2, 2))
    cross2, far2 = done(
        combine(joined2, core2, down_weight, (jnp.float32, jnp.bfloat16))
    )
    far2 = swap(far2, AXIS, 1)
    got3 = swap(tick(send3), "width", CORES)

    got4, add1 = ticks([got4, add1])
    share4, joined5 = done(hidden(mine4, got4, None, share5))
    over4 = swap(share4, "width", CORES)
    far2 = tick(far2)
    add2 = done(call(add_kernel, array(stay, tokens.shape[1]), (cross2, far2), "add"))
    add2 = swap(add2, AXIS, 2)
    over4 = tick(over4)
    joined4 = done(join(share4, over4))
    core4 = ticks(parts_of(joined4, 2))
    (far3,) = done(combine(joined4, core4, down_weight, (jnp.bfloat16,)))
    far3 = swap(far3, AXIS, 1)
    got3 = tick(got3)
    (share3,) = done(hidden(mine3, got3))
    over3 = swap(share3, "width", CORES)
    core5 = ticks(parts_of(joined5, 2))
    (part5,) = done(combine(joined5, core5, down_weight, (jnp.bfloat16,)))
    add5 = swap(part5, AXIS, 1)
    over3, add2 = ticks([over3, add2])
    joined3 = done(join(share3, over3))
    core3 = ticks(parts_of(joined3, 2))
    (cross3,) = done(combine(joined3, core3, down_weight, (jnp.float32,)))
    far3 = tick(far3)
    add3 = done(call(add_kernel, array(stay, tokens.shape[1]), (cross3, far3), "add"))
    add3 = swap(add3, AXIS, 2)

    first = first + widen(add1) + widen(add2)
    second = second + widen(add5) + widen(add3)
    local_peak = jnp.maximum(
        jnp.max(jnp.abs(first), axis=0, keepdims=True),
        jnp.max(jnp.abs(second), axis=0, keepdims=True),
    )
    peak = local_peak
    for k in range(1, RANKS):
        peak = jnp.maximum(peak, swap(local_peak, AXIS, k))
    scaled = call(scale_kernel, array(*tokens.shape), (first, second, peak), "scale")
    return (scaled, peak[0] / 448.0)


def plain(tokens, gate_weight, up_weight, down_weight):
    units = gate_weight.shape[1]
    piece = lax.all_gather(tokens, AXIS, axis=0, tiled=True)
    parts = jnp.concatenate([dot(piece, gate_weight), dot(piece, up_weight)], axis=1)
    sums = widen(
        lax.psum_scatter(narrow(parts), "width", scatter_dimension=0, tiled=True)
    )
    share = narrow(jax.nn.silu(sums[:, :units]) * sums[:, units:])
    hidden_units = lax.all_gather(share, "width", axis=0, tiled=True)
    output = widen(
        lax.psum_scatter(
            narrow(dot(hidden_units, down_weight)),
            AXIS,
            scatter_dimension=0,
            tiled=True,
        )
    )
    peak = lax.pmax(jnp.max(jnp.abs(output), axis=0), AXIS)
    return (narrow(output / (peak + 1e-06)), peak / 448.0)


def solution(mesh):
    in_specs = (
        P(("groups", "tensor"), "width"),
        P("width", "tensor"),
        P("width", "tensor"),
        P("tensor", "width"),
    )
    out_specs = (P(("groups", "tensor"), "width"), P(("groups", "width")))
    fits = mesh.shape[AXIS] == RANKS and mesh.shape["width"] == WIDTH
    return jax.shard_map(
        pipelined if fits else plain,
        mesh=mesh,
        in_specs=in_specs,
        out_specs=out_specs,
        check_vma=False,
    )
```

time: 267 us -> 135 us (0.51)
  waiting for transfers between devices: 191 us -> 53.1 us
  starting transfers between devices: 0.16 us -> 40.2 us
  matrix products: 39.1 us -> 0 us
  Pallas kernels: 0 us -> 35.1 us
  between operations: 13.8 us -> 1.1 us
  other arithmetic: 12.9 us -> 0.83 us
  blocking collectives: 10.1 us -> 0 us
  local copies, waits for them, and re-layouts: 0.01 us -> 4.53 us
    reduce_scatter x2 -> x0, waiting for transfers between devices: 108 us -> none  [the longest x1 64.3 us: per_device(): lax.psum_scatter(partial_value, 'width', scatter_dimension=0, tiled=True)]
    all_gather x2 -> x0, waiting for transfers between devices: 81.9 us -> none  [the longest x1 50.3 us: per_device(): piece = lax.all_gather(tokens, 'tensor', axis=0, tiled=True)]
    ppermute x0 -> x46, waiting for transfers between devices: none -> 53.1 us  [swap(): return lax.ppermute(value, axis, [(i, i ^ mask) for i in range(size)])]
    ppermute x0 -> x46, starting transfers between devices: none -> 40.2 us  [swap(): return lax.ppermute(value, axis, [(i, i ^ mask) for i in range(size)])]
    dot_general x3 -> x0, matrix products: 39.1 us -> none  [the longest x1 13.7 us: per_device(): up_part = jnp.dot(piece, up_weight, preferred_element_type=jnp.float32)]
    pallas_call x0 -> x39, Pallas kernels: none -> 35.1 us  [call(): pl.pallas_call(kernel, out_shape=shapes, in_specs=[VMEM] * len(args), out...]
    pmax x1 -> x0, blocking collectives: 10.1 us -> none  [per_device(): peak = lax.pmax(local_peak, 'tensor')]
    concatenate x1 -> x0, other arithmetic: 5.97 us -> none  [per_device(): jnp.concatenate([gate_part, up_part], axis=1).astype(jnp.bfloat16)]
  transfers between devices with their start and end apart: 4 -> 46, of which waited for: 4 -> 24; matrix products, arithmetic and copies ran while one was open for 0% -> 0% of each run, Pallas kernels for 0% -> 25%
where the time goes in v2:
time: 135 us
  waiting for transfers between devices  53.1 us (39%)
  starting transfers between devices  40.2 us (30%)
  Pallas kernels  35.1 us (26%)
  local copies, waits for them, and re-layouts  4.53 us (3%)
    ppermute x46, waiting for transfers between devices, swap(): return lax.ppermute(value, axis, [(i, i ^ mask) for i in range(size)])  53.1 us
    ppermute x46, starting transfers between devices, swap(): return lax.ppermute(value, axis, [(i, i ^ mask) for i in range(size)])  40.2 us
    pallas_call x39, Pallas kernels, call(): pl.pallas_call(kernel, out_shape=shapes, in_specs=[VMEM] * len(args), out...  35.1 us
    unnamed x20, local copies, waits for them, and re-layouts  4.53 us
  transfers between devices with their start and end apart: 46, of which 24 were waited for; matrix products, arithmetic and copies ran while one was open for 0% of the time, Pallas kernels for 25%

profile of v2, /device:TPU:0, one launch (start us, length us, event | category | flops | bytes accessed | tf_op | source)
XLA Modules:
  0.0 134.9 jit_solution(3932356881548786822)
XLA Ops:
  0.7 3.1 %collective-permute-start = (bf16[128,2048]{1,0:T(8,128)(2,1)}, bf16[128,2048]{1,0:T(8,128)(2,1)S(1)}, u32[]{:S(2)}, u32[]{:S(2)}) collective-permute-start(bf16[128,2048]{1,0:T(8,128)(2,1)} %tokens_ref.1), channel_id=1, source_target_pairs={{0,4},{4,0},{8,12},{12,8},{1,5},{5,1},{9,13},{13,9},{2,6},{6,2},{1... | collective-permute-start | bytes 1572872 | tf_op jit(solution)/shard_map/ppermute | solution.py:23
  3.8 1.8 %copy-done.1 = bf16[128,2048]{1,0:T(8,128)(2,1)S(1)} copy-done((bf16[128,2048]{1,0:T(8,128)(2,1)S(1)}, bf16[128,2048]{1,0:T(8,128)(2,1)}, u32[]{:S(2)}) %copy-start.1) | copy-done | bytes 524312
  6.0 2.1 %gate.4 = (bf16[64,7168]{1,0:T(8,128)(2,1)S(1)}, bf16[64,2304]{1,0:T(8,128)(2,1)S(1)}, bf16[64,2432]{1,0:T(8,128)(2,1)S(1)}, bf16[64,2432]{1,0:T(8,128)(2,1)S(1)}) custom-call(bf16[128,2048]{1,0:T(8,128)(2,1)S(1)} %arrange.2.refs_0_.block_ref, bf16[2048,3584]{1,0:T(8,128)(2,1)S(1)} %copy-done), custom_call_target="tpu_custom_call" | custom-call | flops 3758096384 | bytes 14680064 | tf_op jit(solution)/shard_map/gate/pallas_call | solution.py:48
  8.4 1.2 slice-done.6
  10.4 2.2 %up.4 = (bf16[64,7168]{1,0:T(8,128)(2,1)S(1)}, bf16[64,2304]{1,0:T(8,128)(2,1)S(1)}, bf16[64,2432]{1,0:T(8,128)(2,1)S(1)}, bf16[64,2432]{1,0:T(8,128)(2,1)S(1)}) custom-call(bf16[128,2048]{1,0:T(8,128)(2,1)S(1)} %arrange.2.refs_0_.block_ref, bf16[2048,3584]{1,0:T(8,128)(2,1)S(1)} %bitcast.5, ...), custom_call_target="tpu_custom_call", output_to_operand_aliasing={{0}: (2, {}), {1}: (3, {}), {2}: (4, {}), {3}: (5, {})} | custom-call | flops 1 | bytes 1 | tf_op jit(solution)/shard_map/up/pallas_call | solution.py:48
  13.7 3.7 %collective-permute-start.4 = (bf16[64,2048]{1,0:T(8,128)(2,1)S(1)}, bf16[64,2048]{1,0:T(8,128)(2,1)S(1)}, u32[]{:S(2)}, u32[]{:S(2)}) collective-permute-start(bf16[64,2048]{1,0:T(8,128)(2,1)S(1)} %get-tuple-element.142), channel_id=1, source_target_pairs={{0,8},{4,12},{8,0},{12,4},{1,9},{5,13},{9,1},{13,5},{2,10},{6,14},... | collective-permute-start | bytes 786440 | tf_op jit(solution)/shard_map/ppermute | solution.py:23
  17.6 1.5 %collective-permute-start.7 = (bf16[64,3584]{1,0:T(8,128)(2,1)S(1)}, bf16[64,3584]{1,0:T(8,128)(2,1)S(1)}, u32[]{:S(2)}, u32[]{:S(2)}) collective-permute-start(bf16[64,3584]{1,0:T(8,128)(2,1)S(1)} %get-tuple-element.153), channel_id=1, source_target_pairs={{0,2},{1,3},{2,0},{3,1},{4,6},{5,7},{6,4},{7,5},{8,10},{9,11},{10,... | collective-permute-start | bytes 1376264 | tf_op jit(solution)/shard_map/ppermute | solution.py:23
  19.2 2.1 %gate.5 = (bf16[64,7168]{1,0:T(8,128)(2,1)S(1)}, bf16[32,4736]{1,0:T(8,128)(2,1)S(1)}, bf16[32,2432]{1,0:T(8,128)(2,1)S(1)}, bf16[32,3584]{1,0:T(8,128)(2,1)S(1)}, bf16[32,3584]{1,0:T(8,128)(2,1)S(1)}) custom-call(bf16[128,2048]{1,0:T(8,128)(2,1)S(1)} %arrange.3.refs_0_, bf16[2048,3584]{1,0:T(8,128)(2,1)S(1)} %copy-done), custom_call_target="tpu_custom_call" | custom-call | flops 1 | bytes 1 | tf_op jit(solution)/shard_map/gate/pallas_call | solution.py:48
  21.3 2.2 %up.5 = (bf16[64,7168]{1,0:T(8,128)(2,1)S(1)}, bf16[32,4736]{1,0:T(8,128)(2,1)S(1)}, bf16[32,2432]{1,0:T(8,128)(2,1)S(1)}, bf16[32,3584]{1,0:T(8,128)(2,1)S(1)}, bf16[32,3584]{1,0:T(8,128)(2,1)S(1)}) custom-call(bf16[128,2048]{1,0:T(8,128)(2,1)S(1)} %arrange.3.refs_0_, ...), custom_call_target="tpu_custom_call", output_to_operand_aliasing={{0}: (2, {}), {1}: (3, {}), {2}: (4, {}), {3}: (5, {}), {4}... | custom-call | flops 1 | bytes 1 | tf_op jit(solution)/shard_map/up/pallas_call | solution.py:48
  23.5 6.4 %collective-permute-done.4.refs_0_ = bf16[64,2048]{1,0:T(8,128)(2,1)S(1)} collective-permute-done((bf16[64,2048]{1,0:T(8,128)(2,1)S(1)}, bf16[64,2048]{1,0:T(8,128)(2,1)S(1)}, u32[]{:S(2)}, u32[]{:S(2)}) %collective-permute-start.4) | collective-permute-done | bytes 262176 | tf_op jit(solution)/shard_map/ppermute | solution.py:23
  30.4 1.3 collective-permute-done.6.refs_2_
  32.0 1.6 %collective-permute-start.8 = (bf16[64,3584]{1,0:T(8,128)(2,1)S(1)}, bf16[64,3584]{1,0:T(8,128)(2,1)S(1)}, u32[]{:S(2)}, u32[]{:S(2)}) collective-permute-start(bf16[64,3584]{1,0:T(8,128)(2,1)S(1)} %get-tuple-element.156), channel_id=1, source_target_pairs={{0,2},{1,3},{2,0},{3,1},{4,6},{5,7},{6,4},{7,5},{8,10},{9,11},{10,... | collective-permute-start | bytes 1376264 | tf_op jit(solution)/shard_map/ppermute | solution.py:23
  34.4 3.4 %collective-permute-start.13 = (bf16[64,2048]{1,0:T(8,128)(2,1)S(1)}, bf16[64,2048]{1,0:T(8,128)(2,1)S(1)}, u32[]{:S(2)}, u32[]{:S(2)}) collective-permute-start(bf16[64,2048]{1,0:T(8,128)(2,1)S(1)} %get-tuple-element.175), channel_id=1, source_target_pairs={{0,8},{4,12},{8,0},{12,4},{1,9},{5,13},{9,1},{13,5},{2,10},{6,14},... | collective-permute-start | bytes 786440 | tf_op jit(solution)/shard_map/ppermute | solution.py:23
  38.2 1.0 collective-permute-done.10.refs_2_
  39.6 5.0 %collective-permute-done.8.refs_1_ = bf16[64,3584]{1,0:T(8,128)(2,1)S(1)} collective-permute-done((bf16[64,3584]{1,0:T(8,128)(2,1)S(1)}, bf16[64,3584]{1,0:T(8,128)(2,1)S(1)}, u32[]{:S(2)}, u32[]{:S(2)}) %collective-permute-start.8) | collective-permute-done | bytes 458784 | tf_op jit(solution)/shard_map/ppermute | solution.py:23
  44.8 1.6 %collective-permute-start.18 = (bf16[48,3584]{1,0:T(8,128)(2,1)S(1)}, bf16[48,3584]{1,0:T(8,128)(2,1)S(1)}, u32[]{:S(2)}, u32[]{:S(2)}) collective-permute-start(bf16[48,3584]{1,0:T(8,128)(2,1)S(1)} %get-tuple-element.187), channel_id=1, source_target_pairs={{0,2},{1,3},{2,0},{3,1},{4,6},{5,7},{6,4},{7,5},{8,10},{9,11},{10,... | collective-permute-start | bytes 1032200 | tf_op jit(solution)/shard_map/ppermute | solution.py:23
  47.1 2.1 %gate.6 = (bf16[64,7168]{1,0:T(8,128)(2,1)S(1)}, bf16[64,2304]{1,0:T(8,128)(2,1)S(1)}, bf16[64,2432]{1,0:T(8,128)(2,1)S(1)}, bf16[64,2432]{1,0:T(8,128)(2,1)S(1)}) custom-call(bf16[64,2048]{1,0:T(8,128)(2,1)S(1)} %collective-permute-done.4.refs_0_, bf16[64,2048]{1,0:T(8,128)(2,1)S(1)} %collective-permute-done.12.refs_1_, bf16[2048,3584]{1,0:T(8,128)(2,1)S(1)} %copy-done), custom_call_target="tpu_custom_call" | custom-call | flops 1 | bytes 1 | tf_op jit(solution)/shard_map/gate/pallas_call | solution.py:48
  49.2 2.4 %up.6 = (bf16[64,7168]{1,0:T(8,128)(2,1)S(1)}, bf16[64,2304]{1,0:T(8,128)(2,1)S(1)}, bf16[64,2432]{1,0:T(8,128)(2,1)S(1)}, bf16[64,2432]{1,0:T(8,128)(2,1)S(1)}) custom-call(bf16[64,2048]{1,0:T(8,128)(2,1)S(1)} %collective-permute-done.4.refs_0_, ...), custom_call_target="tpu_custom_call", output_to_operand_aliasing={{0}: (3, {}), {1}: (4, {}), {2}: (5, {}), {3}: (6, {})} | custom-call | flops 1 | bytes 1 | tf_op jit(solution)/shard_map/up/pallas_call | solution.py:48
  52.3 1.9 %collective-permute-done.14.refs_1_ = bf16[64,2304]{1,0:T(8,128)(2,1)S(1)} collective-permute-done((bf16[64,2304]{1,0:T(8,128)(2,1)S(1)}, bf16[64,2304]{1,0:T(8,128)(2,1)S(1)}, u32[]{:S(2)}, u32[]{:S(2)}) %collective-permute-start.14) | collective-permute-done | bytes 294944 | tf_op jit(solution)/shard_map/ppermute | solution.py:23
  54.7 1.2 collective-permute-start.17
  55.9 5.0 %collective-permute-done.20.refs_1_ = bf16[64,2048]{1,0:T(8,128)(2,1)S(1)} collective-permute-done((bf16[64,2048]{1,0:T(8,128)(2,1)S(1)}, bf16[64,2048]{1,0:T(8,128)(2,1)S(1)}, u32[]{:S(2)}, u32[]{:S(2)}) %collective-permute-start.20) | collective-permute-done | bytes 262176 | tf_op jit(solution)/shard_map/ppermute | solution.py:23
  60.9 2.1 %gate.7 = (bf16[64,7168]{1,0:T(8,128)(2,1)S(1)}, bf16[64,2304]{1,0:T(8,128)(2,1)S(1)}, bf16[64,2432]{1,0:T(8,128)(2,1)S(1)}, bf16[64,2432]{1,0:T(8,128)(2,1)S(1)}) custom-call(bf16[64,2048]{1,0:T(8,128)(2,1)S(1)} %collective-permute-done.13.refs_0_, bf16[64,2048]{1,0:T(8,128)(2,1)S(1)} %collective-permute-done.20.refs_1_, bf16[2048,3584]{1,0:T(8,128)(2,1)S(1)} %copy-done), custom_call_target="tpu_custom_call" | custom-call | flops 1 | bytes 1 | tf_op jit(solution)/shard_map/gate/pallas_call | solution.py:48
  63.1 2.2 %up.7 = (bf16[64,7168]{1,0:T(8,128)(2,1)S(1)}, bf16[64,2304]{1,0:T(8,128)(2,1)S(1)}, bf16[64,2432]{1,0:T(8,128)(2,1)S(1)}, bf16[64,2432]{1,0:T(8,128)(2,1)S(1)}) custom-call(bf16[64,2048]{1,0:T(8,128)(2,1)S(1)} %collective-permute-done.13.refs_0_, ...), custom_call_target="tpu_custom_call", output_to_operand_aliasing={{0}: (3, {}), {1}: (4, {}), {2}: (5, {}), {3}: (6, {})} | custom-call | flops 1 | bytes 1 | tf_op jit(solution)/shard_map/up/pallas_call | solution.py:48
  66.4 1.4 %collective-permute-done.21.refs_1_ = bf16[64,2304]{1,0:T(8,128)(2,1)S(1)} collective-permute-done((bf16[64,2304]{1,0:T(8,128)(2,1)S(1)}, bf16[64,2304]{1,0:T(8,128)(2,1)S(1)}, u32[]{:S(2)}, u32[]{:S(2)}) %collective-permute-start.21) | collective-permute-done | bytes 294944 | tf_op jit(solution)/shard_map/ppermute | solution.py:23
  68.0 1.0 collective-permute-start.24
  69.3 2.6 %down.6 = bf16[64,2048]{1,0:T(8,128)(2,1)S(1)} custom-call(bf16[32,3584]{1,0:T(8,128)(2,1)S(1)} %get-tuple-element.190.mine_ref, bf16[32,3584]{1,0:T(8,128)(2,1)S(1)} %collective-permute-done.19.refs_0_, bf16[3584,2048]{1,0:T(8,128)(2,1)S(1)} %bitcast.3), custom_call_target="tpu_custom_call" | custom-call | flops 1 | bytes 1 | tf_op jit(solution)/shard_map/down/pallas_call | solution.py:48
  72.0 2.1 %down.7 = (f32[64,2048]{1,0:T(8,128)S(1)}, f32[64,2048]{1,0:T(8,128)S(1)}) custom-call(bf16[64,3584]{1,0:T(8,128)(2,1)S(1)} %get-tuple-element.167.mine_ref, bf16[64,3584]{1,0:T(8,128)(2,1)S(1)} %collective-permute-done.11.refs_0_, bf16[3584,2048]{1,0:T(8,128)(2,1)S(1)} %bitcast.3), custom_call_target="tpu_custom_call" | custom-call | flops 1 | bytes 1 | tf_op jit(solution)/shard_map/down/pallas_call | solution.py:48
  74.0 1.7 %collective-permute-done.24.got_ref = bf16[32,3584]{1,0:T(8,128)(2,1)S(1)} collective-permute-done((bf16[32,3584]{1,0:T(8,128)(2,1)S(1)}, bf16[32,3584]{1,0:T(8,128)(2,1)S(1)}, u32[]{:S(2)}, u32[]{:S(2)}) %collective-permute-start.24) | collective-permute-done | bytes 229408 | tf_op jit(solution)/shard_map/ppermute | solution.py:23
  77.7 2.3 %down.8 = (f32[64,2048]{1,0:T(8,128)S(1)}, bf16[64,2048]{1,0:T(8,128)(2,1)S(1)}) custom-call(bf16[64,3584]{1,0:T(8,128)(2,1)S(1)} %join.3.mine_ref, bf16[64,1792]{1,0:T(8,128)(2,1)S(1)} %collective-permute-done.27.refs_0_, bf16[64,1792]{1,0:T(8,128)(2,1)S(1)} %collective-permute-done.28.refs_1_, bf16[3584,2048]{1,0:T(8,128)(2,1)S(1)} %bitcast.3), custom_call_target="tpu_custom_call" | custom-call | flops 1 | bytes 1 | tf_op jit(solution)/shard_map/down/pallas_call | solution.py:48
  80.0 1.3 collective-permute-start.31
  81.3 4.8 %collective-permute-done.26 = bf16[64,2048]{1,0:T(8,128)(2,1)S(1)} collective-permute-done((bf16[64,2048]{1,0:T(8,128)(2,1)S(1)}, bf16[64,2048]{1,0:T(8,128)(2,1)S(1)}, u32[]{:S(2)}, u32[]{:S(2)}) %collective-permute-start.26) | collective-permute-done | bytes 262176 | tf_op jit(solution)/shard_map/ppermute | solution.py:23
  86.5 1.3 collective-permute-start.30
  88.6 1.9 %collective-permute-done.31.got_ref = bf16[64,2048]{1,0:T(8,128)(2,1)S(1)} collective-permute-done((bf16[64,2048]{1,0:T(8,128)(2,1)S(1)}, bf16[64,2048]{1,0:T(8,128)(2,1)S(1)}, u32[]{:S(2)}, u32[]{:S(2)}) %collective-permute-start.31) | collective-permute-done | bytes 262176 | tf_op jit(solution)/shard_map/ppermute | solution.py:23
  90.5 2.4 %collective-permute-start.35 = (bf16[64,2048]{1,0:T(8,128)(2,1)S(1)}, bf16[64,2048]{1,0:T(8,128)(2,1)S(1)}, u32[]{:S(2)}, u32[]{:S(2)}) collective-permute-start(bf16[64,2048]{1,0:T(8,128)(2,1)S(1)} %add.26), channel_id=1, source_target_pairs={{0,8},{4,12},{8,0},{12,4},{1,9},{5,13},{9,1},{13,5},{2,10},{6,14},... | collective-permute-start | bytes 786440 | tf_op jit(solution)/shard_map/ppermute | solution.py:23
  94.5 2.6 %down.9 = bf16[64,2048]{1,0:T(8,128)(2,1)S(1)} custom-call(bf16[32,3584]{1,0:T(8,128)(2,1)S(1)} %join.4.mine_ref, bf16[32,1792]{1,0:T(8,128)(2,1)S(1)} %collective-permute-done.32.refs_0_, bf16[32,1792]{1,0:T(8,128)(2,1)S(1)} %collective-permute-done.33.refs_1_, bf16[3584,2048]{1,0:T(8,128)(2,1)S(1)} %bitcast.3), custom_call_target="tpu_custom_call" | custom-call | flops 1 | bytes 1 | tf_op jit(solution)/shard_map/down/pallas_call | solution.py:48
  97.1 1.8 %collective-permute-start.41 = (bf16[64,2048]{1,0:T(8,128)(2,1)S(1)}, bf16[64,2048]{1,0:T(8,128)(2,1)S(1)}, u32[]{:S(2)}, u32[]{:S(2)}) collective-permute-start(bf16[64,2048]{1,0:T(8,128)(2,1)S(1)} %down.9), channel_id=1, source_target_pairs={{0,4},{4,0},{8,12},{12,8},{1,5},{5,1},{9,13},{13,9},{2,6},{6,2},{1... | collective-permute-start | bytes 786440 | tf_op jit(solution)/shard_map/ppermute | solution.py:23
  99.6 0.9 collective-permute-start.34
  100.5 2.6 %down.10 = bf16[64,2048]{1,0:T(8,128)(2,1)S(1)} custom-call(bf16[32,3584]{1,0:T(8,128)(2,1)S(1)} %get-tuple-element.231.mine_ref, bf16[32,1792]{1,0:T(8,128)(2,1)S(1)} %collective-permute-done.36.refs_0_, bf16[32,1792]{1,0:T(8,128)(2,1)S(1)} %collective-permute-done.37.refs_1_, bf16[3584,2048]{1,0:T(8,128)(2,1)S(1)} %bitcast.3), custom_call_target="tpu_custom_call" | custom-call | flops 1 | bytes 1 | tf_op jit(solution)/shard_map/down/pallas_call | solution.py:48
  103.2 1.6 %collective-permute-done.34.got_ref = bf16[16,3584]{1,0:T(8,128)(2,1)S(1)} collective-permute-done((bf16[16,3584]{1,0:T(8,128)(2,1)S(1)}, bf16[16,3584]{1,0:T(8,128)(2,1)S(1)}, u32[]{:S(2)}, u32[]{:S(2)}) %collective-permute-start.34) | collective-permute-done | bytes 114720 | tf_op jit(solution)/shard_map/ppermute | solution.py:23
  106.4 2.6 %down.11.part_ref = f32[64,2048]{1,0:T(8,128)S(1)} custom-call(bf16[32,3584]{1,0:T(8,128)(2,1)S(1)} %join.5.mine_ref, bf16[32,1792]{1,0:T(8,128)(2,1)S(1)} %collective-permute-done.39.refs_0_, bf16[32,1792]{1,0:T(8,128)(2,1)S(1)} %collective-permute-done.40.refs_1_, bf16[3584,2048]{1,0:T(8,128)(2,1)S(1)} %bitcast.3), custom_call_target="tpu_custom_call" | custom-call | flops 1 | bytes 1 | tf_op jit(solution)/shard_map/down/pallas_call | solution.py:48
  109.1 0.8 collective-permute-done.41.got_ref
  110.0 1.8 %collective-permute-start.42 = (bf16[64,2048]{1,0:T(8,128)(2,1)S(1)}, bf16[64,2048]{1,0:T(8,128)(2,1)S(1)}, u32[]{:S(2)}, u32[]{:S(2)}) collective-permute-start(bf16[64,2048]{1,0:T(8,128)(2,1)S(1)} %add.27), channel_id=1, source_target_pairs={{0,8},{4,12},{8,0},{12,4},{1,9},{5,13},{9,1},{13,5},{2,10},{6,14},... | collective-permute-start | bytes 786440 | tf_op jit(solution)/shard_map/ppermute | solution.py:23
  111.9 5.2 %collective-permute-done.38 = bf16[64,2048]{1,0:T(8,128)(2,1)S(1)} collective-permute-done((bf16[64,2048]{1,0:T(8,128)(2,1)S(1)}, bf16[64,2048]{1,0:T(8,128)(2,1)S(1)}, u32[]{:S(2)}, u32[]{:S(2)}) %collective-permute-start.38) | collective-permute-done | bytes 262176 | tf_op jit(solution)/shard_map/ppermute | solution.py:23
  117.0 7.7 %collective-permute-done.42 = bf16[64,2048]{1,0:T(8,128)(2,1)S(1)} collective-permute-done((bf16[64,2048]{1,0:T(8,128)(2,1)S(1)}, bf16[64,2048]{1,0:T(8,128)(2,1)S(1)}, u32[]{:S(2)}, u32[]{:S(2)}) %collective-permute-start.42) | collective-permute-done | bytes 262176 | tf_op jit(solution)/shard_map/ppermute | solution.py:23
  124.9 3.0 %collective-permute-start.44 = (f32[1,2048]{1,0:T(1,128)S(1)}, f32[1,2048]{1,0:T(1,128)S(1)}, u32[]{:S(2)}, u32[]{:S(2)}) collective-permute-start(f32[1,2048]{1,0:T(1,128)S(1)} %bitcast.7), channel_id=1, source_target_pairs={{0,8},{4,12},{8,0},{12,4},{1,9},{5,13},{9,1},{13,5},{2,10},{6,14},... | collective-permute-start | bytes 24584 | tf_op jit(solution)/shard_map/ppermute | solution.py:23
  127.9 1.4 %collective-permute-start.45 = (f32[1,2048]{1,0:T(1,128)S(1)}, f32[1,2048]{1,0:T(1,128)S(1)}, u32[]{:S(2)}, u32[]{:S(2)}) collective-permute-start(f32[1,2048]{1,0:T(1,128)S(1)} %bitcast.8), channel_id=1, source_target_pairs={{0,12},{4,8},{8,4},{12,0},{1,13},{5,9},{9,5},{13,1},{2,14},{6,10},... | collective-permute-start | bytes 24584 | tf_op jit(solution)/shard_map/ppermute | solution.py:23
  129.6 3.8 %collective-permute-done.45 = f32[1,2048]{1,0:T(1,128)S(1)} collective-permute-done((f32[1,2048]{1,0:T(1,128)S(1)}, f32[1,2048]{1,0:T(1,128)S(1)}, u32[]{:S(2)}, u32[]{:S(2)}) %collective-permute-start.45) | collective-permute-done | bytes 8224 | tf_op jit(solution)/shard_map/ppermute | solution.py:23
  134.0 0.9 scale.1
  (109 shorter events, 17.1 us)
Async XLA Ops:
  0.7 8.9 %slice-start.6 = ((s8[14680064]{0:T(1024)(128)(4,1)}), s8[4194304]{0:T(1024)(128)(4,1)S(1)}, s32[]{:S(2)}) async-start(s8[14680064]{0:T(1024)(128)(4,1)} %bitcast.4), calls=%async_computation.6 | async-start | bytes 8388608
  0.7 18.5 %collective-permute-start = (bf16[128,2048]{1,0:T(8,128)(2,1)}, bf16[128,2048]{1,0:T(8,128)(2,1)S(1)}, u32[]{:S(2)}, u32[]{:S(2)}) collective-permute-start(bf16[128,2048]{1,0:T(8,128)(2,1)} %tokens_ref.1), channel_id=1, source_target_pairs={{0,4},{4,0},{8,12},{12,8},{1,5},{5,1},{9,13},{13,9},{2,6},{6,2},{1... | collective-permute-start | bytes 1572872 | tf_op jit(solution)/shard_map/ppermute | solution.py:23
  12.6 4.8 %collective-permute-start.2 = (bf16[64,2432]{1,0:T(8,128)(2,1)S(1)}, bf16[64,2432]{1,0:T(8,128)(2,1)S(1)}, u32[]{:S(2)}, u32[]{:S(2)}) collective-permute-start(bf16[64,2432]{1,0:T(8,128)(2,1)S(1)} %get-tuple-element.128), channel_id=1, source_target_pairs={{0,1},{1,0},{2,3},{3,2},{4,5},{5,4},{6,7},{7,6},{8,9},{9,8},{10,11... | collective-permute-start | bytes 933896 | tf_op jit(solution)/shard_map/ppermute | solution.py:23
  13.1 4.3 %collective-permute-start.3 = (bf16[64,2432]{1,0:T(8,128)(2,1)S(1)}, bf16[64,2432]{1,0:T(8,128)(2,1)S(1)}, u32[]{:S(2)}, u32[]{:S(2)}) collective-permute-start(bf16[64,2432]{1,0:T(8,128)(2,1)S(1)} %get-tuple-element.129), channel_id=1, source_target_pairs={{0,1},{1,0},{2,3},{3,2},{4,5},{5,4},{6,7},{7,6},{8,9},{9,8},{10,11... | collective-permute-start | bytes 933896 | tf_op jit(solution)/shard_map/ppermute | solution.py:23
  13.2 4.2 %collective-permute-start.1 = (bf16[64,2304]{1,0:T(8,128)(2,1)S(1)}, bf16[64,2304]{1,0:T(8,128)(2,1)S(1)}, u32[]{:S(2)}, u32[]{:S(2)}) collective-permute-start(bf16[64,2304]{1,0:T(8,128)(2,1)S(1)} %get-tuple-element.127), channel_id=1, source_target_pairs={{0,1},{1,0},{2,3},{3,2},{4,5},{5,4},{6,7},{7,6},{8,9},{9,8},{10,11... | collective-permute-start | bytes 884744 | tf_op jit(solution)/shard_map/ppermute | solution.py:23
  13.7 16.3 %collective-permute-start.4 = (bf16[64,2048]{1,0:T(8,128)(2,1)S(1)}, bf16[64,2048]{1,0:T(8,128)(2,1)S(1)}, u32[]{:S(2)}, u32[]{:S(2)}) collective-permute-start(bf16[64,2048]{1,0:T(8,128)(2,1)S(1)} %get-tuple-element.142), channel_id=1, source_target_pairs={{0,8},{4,12},{8,0},{12,4},{1,9},{5,13},{9,1},{13,5},{2,10},{6,14},... | collective-permute-start | bytes 786440 | tf_op jit(solution)/shard_map/ppermute | solution.py:23
  17.6 14.2 %collective-permute-start.7 = (bf16[64,3584]{1,0:T(8,128)(2,1)S(1)}, bf16[64,3584]{1,0:T(8,128)(2,1)S(1)}, u32[]{:S(2)}, u32[]{:S(2)}) collective-permute-start(bf16[64,3584]{1,0:T(8,128)(2,1)S(1)} %get-tuple-element.153), channel_id=1, source_target_pairs={{0,2},{1,3},{2,0},{3,1},{4,6},{5,7},{6,4},{7,5},{8,10},{9,11},{10,... | collective-permute-start | bytes 1376264 | tf_op jit(solution)/shard_map/ppermute | solution.py:23
  29.9 1.8 %collective-permute-start.5 = (bf16[32,4736]{1,0:T(8,128)(2,1)S(1)}, bf16[32,4736]{1,0:T(8,128)(2,1)S(1)}, u32[]{:S(2)}, u32[]{:S(2)}) collective-permute-start(bf16[32,4736]{1,0:T(8,128)(2,1)S(1)} %get-tuple-element.147), channel_id=1, source_target_pairs={{0,1},{1,0},{2,3},{3,2},{4,5},{5,4},{6,7},{7,6},{8,9},{9,8},{10,11... | collective-permute-start | bytes 909320 | tf_op jit(solution)/shard_map/ppermute | solution.py:23
  29.9 1.8 %collective-permute-start.6 = (bf16[32,2432]{1,0:T(8,128)(2,1)S(1)}, bf16[32,2432]{1,0:T(8,128)(2,1)S(1)}, u32[]{:S(2)}, u32[]{:S(2)}) collective-permute-start(bf16[32,2432]{1,0:T(8,128)(2,1)S(1)} %get-tuple-element.148), channel_id=1, source_target_pairs={{0,1},{1,0},{2,3},{3,2},{4,5},{5,4},{6,7},{7,6},{8,9},{9,8},{10,11... | collective-permute-start | bytes 466952 | tf_op jit(solution)/shard_map/ppermute | solution.py:23
  32.0 12.6 %collective-permute-start.8 = (bf16[64,3584]{1,0:T(8,128)(2,1)S(1)}, bf16[64,3584]{1,0:T(8,128)(2,1)S(1)}, u32[]{:S(2)}, u32[]{:S(2)}) collective-permute-start(bf16[64,3584]{1,0:T(8,128)(2,1)S(1)} %get-tuple-element.156), channel_id=1, source_target_pairs={{0,2},{1,3},{2,0},{3,1},{4,6},{5,7},{6,4},{7,5},{8,10},{9,11},{10,... | collective-permute-start | bytes 1376264 | tf_op jit(solution)/shard_map/ppermute | solution.py:23
  33.7 13.5 %collective-permute-start.12 = (bf16[64,2048]{1,0:T(8,128)(2,1)S(1)}, bf16[64,2048]{1,0:T(8,128)(2,1)S(1)}, u32[]{:S(2)}, u32[]{:S(2)}) collective-permute-start(bf16[64,2048]{1,0:T(8,128)(2,1)S(1)} %collective-permute-done.4.refs_0_), channel_id=1, source_target_pairs={{0,4},{4,0},{8,12},{12,8},{1,5},{5,1},{9,13},{13,9},{2,6},{6,2},{1... | collective-permute-start | bytes 786440 | tf_op jit(solution)/shard_map/ppermute | solution.py:23
  34.4 17.3 %collective-permute-start.13 = (bf16[64,2048]{1,0:T(8,128)(2,1)S(1)}, bf16[64,2048]{1,0:T(8,128)(2,1)S(1)}, u32[]{:S(2)}, u32[]{:S(2)}) collective-permute-start(bf16[64,2048]{1,0:T(8,128)(2,1)S(1)} %get-tuple-element.175), channel_id=1, source_target_pairs={{0,8},{4,12},{8,0},{12,4},{1,9},{5,13},{9,1},{13,5},{2,10},{6,14},... | collective-permute-start | bytes 786440 | tf_op jit(solution)/shard_map/ppermute | solution.py:23
  37.7 1.5 %collective-permute-start.10 = (bf16[32,3584]{1,0:T(8,128)(2,1)S(1)}, bf16[32,3584]{1,0:T(8,128)(2,1)S(1)}, u32[]{:S(2)}, u32[]{:S(2)}) collective-permute-start(bf16[32,3584]{1,0:T(8,128)(2,1)S(1)} %get-tuple-element.161), channel_id=1, source_target_pairs={{0,1},{1,0},{2,3},{3,2},{4,5},{5,4},{6,7},{7,6},{8,9},{9,8},{10,11... | collective-permute-start | bytes 688136 | tf_op jit(solution)/shard_map/ppermute | solution.py:23
  37.7 1.8 %collective-permute-start.9 = (bf16[32,3584]{1,0:T(8,128)(2,1)S(1)}, bf16[32,3584]{1,0:T(8,128)(2,1)S(1)}, u32[]{:S(2)}, u32[]{:S(2)}) collective-permute-start(bf16[32,3584]{1,0:T(8,128)(2,1)S(1)} %get-tuple-element.160), channel_id=1, source_target_pairs={{0,1},{1,0},{2,3},{3,2},{4,5},{5,4},{6,7},{7,6},{8,9},{9,8},{10,11... | collective-permute-start | bytes 688136 | tf_op jit(solution)/shard_map/ppermute | solution.py:23
  44.8 9.6 %collective-permute-start.18 = (bf16[48,3584]{1,0:T(8,128)(2,1)S(1)}, bf16[48,3584]{1,0:T(8,128)(2,1)S(1)}, u32[]{:S(2)}, u32[]{:S(2)}) collective-permute-start(bf16[48,3584]{1,0:T(8,128)(2,1)S(1)} %get-tuple-element.187), channel_id=1, source_target_pairs={{0,2},{1,3},{2,0},{3,1},{4,6},{5,7},{6,4},{7,5},{8,10},{9,11},{10,... | collective-permute-start | bytes 1032200 | tf_op jit(solution)/shard_map/ppermute | solution.py:23
  51.6 2.5 %collective-permute-start.15 = (bf16[64,2432]{1,0:T(8,128)(2,1)S(1)}, bf16[64,2432]{1,0:T(8,128)(2,1)S(1)}, u32[]{:S(2)}, u32[]{:S(2)}) collective-permute-start(bf16[64,2432]{1,0:T(8,128)(2,1)S(1)} %get-tuple-element.180), channel_id=1, source_target_pairs={{0,1},{1,0},{2,3},{3,2},{4,5},{5,4},{6,7},{7,6},{8,9},{9,8},{10,11... | collective-permute-start | bytes 933896 | tf_op jit(solution)/shard_map/ppermute | solution.py:23
  51.7 2.5 %collective-permute-start.16 = (bf16[64,2432]{1,0:T(8,128)(2,1)S(1)}, bf16[64,2432]{1,0:T(8,128)(2,1)S(1)}, u32[]{:S(2)}, u32[]{:S(2)}) collective-permute-start(bf16[64,2432]{1,0:T(8,128)(2,1)S(1)} %get-tuple-element.181), channel_id=1, source_target_pairs={{0,1},{1,0},{2,3},{3,2},{4,5},{5,4},{6,7},{7,6},{8,9},{9,8},{10,11... | collective-permute-start | bytes 933896 | tf_op jit(solution)/shard_map/ppermute | solution.py:23
  52.2 2.0 %collective-permute-start.14 = (bf16[64,2304]{1,0:T(8,128)(2,1)S(1)}, bf16[64,2304]{1,0:T(8,128)(2,1)S(1)}, u32[]{:S(2)}, u32[]{:S(2)}) collective-permute-start(bf16[64,2304]{1,0:T(8,128)(2,1)S(1)} %get-tuple-element.179), channel_id=1, source_target_pairs={{0,1},{1,0},{2,3},{3,2},{4,5},{5,4},{6,7},{7,6},{8,9},{9,8},{10,11... | collective-permute-start | bytes 884744 | tf_op jit(solution)/shard_map/ppermute | solution.py:23
  52.3 8.7 %collective-permute-start.20 = (bf16[64,2048]{1,0:T(8,128)(2,1)S(1)}, bf16[64,2048]{1,0:T(8,128)(2,1)S(1)}, u32[]{:S(2)}, u32[]{:S(2)}) collective-permute-start(bf16[64,2048]{1,0:T(8,128)(2,1)S(1)} %collective-permute-done.13.refs_0_), channel_id=1, source_target_pairs={{0,4},{4,0},{8,12},{12,8},{1,5},{5,1},{9,13},{13,9},{2,6},{6,2},{1... | collective-permute-start | bytes 786440 | tf_op jit(solution)/shard_map/ppermute | solution.py:23
  54.5 11.4 %collective-permute-start.19 = (bf16[32,3584]{1,0:T(8,128)(2,1)S(1)}, bf16[32,3584]{1,0:T(8,128)(2,1)S(1)}, u32[]{:S(2)}, u32[]{:S(2)}) collective-permute-start(bf16[32,3584]{1,0:T(8,128)(2,1)S(1)} %get-tuple-element.190.mine_ref), channel_id=1, source_target_pairs={{0,1},{1,0},{2,3},{3,2},{4,5},{5,4},{6,7},{7,6},{8,9},{9,8},{10,11... | collective-permute-start | bytes 688136 | tf_op jit(solution)/shard_map/ppermute | solution.py:23
  54.7 13.1 %collective-permute-start.17 = (bf16[64,3584]{1,0:T(8,128)(2,1)S(1)}, bf16[64,3584]{1,0:T(8,128)(2,1)S(1)}, u32[]{:S(2)}, u32[]{:S(2)}) collective-permute-start(bf16[64,3584]{1,0:T(8,128)(2,1)S(1)} %get-tuple-element.186), channel_id=1, source_target_pairs={{0,2},{1,3},{2,0},{3,1},{4,6},{5,7},{6,4},{7,5},{8,10},{9,11},{10,... | collective-permute-start | bytes 1376264 | tf_op jit(solution)/shard_map/ppermute | solution.py:23
  60.9 8.3 %slice-start.1 = ((s8[14680064]{0:T(1024)(128)(4,1)}), s8[4194304]{0:T(1024)(128)(4,1)S(1)}, s32[]{:S(2)}) async-start(s8[14680064]{0:T(1024)(128)(4,1)} %bitcast.2), calls=%async_computation.1 | async-start | bytes 8388608
  65.3 2.5 %collective-permute-start.22 = (bf16[64,2432]{1,0:T(8,128)(2,1)S(1)}, bf16[64,2432]{1,0:T(8,128)(2,1)S(1)}, u32[]{:S(2)}, u32[]{:S(2)}) collective-permute-start(bf16[64,2432]{1,0:T(8,128)(2,1)S(1)} %get-tuple-element.198), channel_id=1, source_target_pairs={{0,1},{1,0},{2,3},{3,2},{4,5},{5,4},{6,7},{7,6},{8,9},{9,8},{10,11... | collective-permute-start | bytes 933896 | tf_op jit(solution)/shard_map/ppermute | solution.py:23
  65.4 2.5 %collective-permute-start.23 = (bf16[64,2432]{1,0:T(8,128)(2,1)S(1)}, bf16[64,2432]{1,0:T(8,128)(2,1)S(1)}, u32[]{:S(2)}, u32[]{:S(2)}) collective-permute-start(bf16[64,2432]{1,0:T(8,128)(2,1)S(1)} %get-tuple-element.199), channel_id=1, source_target_pairs={{0,1},{1,0},{2,3},{3,2},{4,5},{5,4},{6,7},{7,6},{8,9},{9,8},{10,11... | collective-permute-start | bytes 933896 | tf_op jit(solution)/shard_map/ppermute | solution.py:23
  65.9 2.0 %collective-permute-start.21 = (bf16[64,2304]{1,0:T(8,128)(2,1)S(1)}, bf16[64,2304]{1,0:T(8,128)(2,1)S(1)}, u32[]{:S(2)}, u32[]{:S(2)}) collective-permute-start(bf16[64,2304]{1,0:T(8,128)(2,1)S(1)} %get-tuple-element.197), channel_id=1, source_target_pairs={{0,1},{1,0},{2,3},{3,2},{4,5},{5,4},{6,7},{7,6},{8,9},{9,8},{10,11... | collective-permute-start | bytes 884744 | tf_op jit(solution)/shard_map/ppermute | solution.py:23
  65.9 6.0 %collective-permute-start.11 = (bf16[64,3584]{1,0:T(8,128)(2,1)S(1)}, bf16[64,3584]{1,0:T(8,128)(2,1)S(1)}, u32[]{:S(2)}, u32[]{:S(2)}) collective-permute-start(bf16[64,3584]{1,0:T(8,128)(2,1)S(1)} %get-tuple-element.167.mine_ref), channel_id=1, source_target_pairs={{0,1},{1,0},{2,3},{3,2},{4,5},{5,4},{6,7},{7,6},{8,9},{9,8},{10,11... | collective-permute-start | bytes 1376264 | tf_op jit(solution)/shard_map/ppermute | solution.py:23
  68.0 7.7 %collective-permute-start.24 = (bf16[32,3584]{1,0:T(8,128)(2,1)S(1)}, bf16[32,3584]{1,0:T(8,128)(2,1)S(1)}, u32[]{:S(2)}, u32[]{:S(2)}) collective-permute-start(bf16[32,3584]{1,0:T(8,128)(2,1)S(1)} %hidden.9.share_ref), channel_id=1, source_target_pairs={{0,2},{1,3},{2,0},{3,1},{4,6},{5,7},{6,4},{7,5},{8,10},{9,11},{10,... | collective-permute-start | bytes 688136 | tf_op jit(solution)/shard_map/ppermute | solution.py:23
  75.8 1.7 %collective-permute-start.27 = (bf16[64,1792]{1,0:T(8,128)(2,1)S(1)}, bf16[64,1792]{1,0:T(8,128)(2,1)S(1)}, u32[]{:S(2)}, u32[]{:S(2)}) collective-permute-start(bf16[64,1792]{1,0:T(8,128)(2,1)S(1)} %get-tuple-element.213), channel_id=1, source_target_pairs={{0,1},{1,0},{2,3},{3,2},{4,5},{5,4},{6,7},{7,6},{8,9},{9,8},{10,11... | collective-permute-start | bytes 688136 | tf_op jit(solution)/shard_map/ppermute | solution.py:23
  75.9 1.8 %collective-permute-start.28 = (bf16[64,1792]{1,0:T(8,128)(2,1)S(1)}, bf16[64,1792]{1,0:T(8,128)(2,1)S(1)}, u32[]{:S(2)}, u32[]{:S(2)}) collective-permute-start(bf16[64,1792]{1,0:T(8,128)(2,1)S(1)} %get-tuple-element.214), channel_id=1, source_target_pairs={{0,1},{1,0},{2,3},{3,2},{4,5},{5,4},{6,7},{7,6},{8,9},{9,8},{10,11... | collective-permute-start | bytes 688136 | tf_op jit(solution)/shard_map/ppermute | solution.py:23
  76.4 10.0 %collective-permute-start.25 = (bf16[48,3584]{1,0:T(8,128)(2,1)S(1)}, bf16[48,3584]{1,0:T(8,128)(2,1)S(1)}, u32[]{:S(2)}, u32[]{:S(2)}) collective-permute-start(bf16[48,3584]{1,0:T(8,128)(2,1)S(1)} %stack.1), channel_id=1, source_target_pairs={{0,2},{1,3},{2,0},{3,1},{4,6},{5,7},{6,4},{7,5},{8,10},{9,11},{10,... | collective-permute-start | bytes 1032200 | tf_op jit(solution)/shard_map/ppermute | solution.py:23
  76.8 9.2 %collective-permute-start.26 = (bf16[64,2048]{1,0:T(8,128)(2,1)S(1)}, bf16[64,2048]{1,0:T(8,128)(2,1)S(1)}, u32[]{:S(2)}, u32[]{:S(2)}) collective-permute-start(bf16[64,2048]{1,0:T(8,128)(2,1)S(1)} %down.6), channel_id=1, source_target_pairs={{0,4},{4,0},{8,12},{12,8},{1,5},{5,1},{9,13},{13,9},{2,6},{6,2},{1... | collective-permute-start | bytes 786440 | tf_op jit(solution)/shard_map/ppermute | solution.py:23
  80.0 10.5 %collective-permute-start.31 = (bf16[64,2048]{1,0:T(8,128)(2,1)S(1)}, bf16[64,2048]{1,0:T(8,128)(2,1)S(1)}, u32[]{:S(2)}, u32[]{:S(2)}) collective-permute-start(bf16[64,2048]{1,0:T(8,128)(2,1)S(1)} %get-tuple-element.223), channel_id=1, source_target_pairs={{0,4},{4,0},{8,12},{12,8},{1,5},{5,1},{9,13},{13,9},{2,6},{6,2},{1... | collective-permute-start | bytes 786440 | tf_op jit(solution)/shard_map/ppermute | solution.py:23
  86.5 6.4 %collective-permute-start.30 = (bf16[16,3584]{1,0:T(8,128)(2,1)S(1)}, bf16[16,3584]{1,0:T(8,128)(2,1)S(1)}, u32[]{:S(2)}, u32[]{:S(2)}) collective-permute-start(bf16[16,3584]{1,0:T(8,128)(2,1)S(1)} %get-tuple-element.222.share_ref), channel_id=1, source_target_pairs={{0,2},{1,3},{2,0},{3,1},{4,6},{5,7},{6,4},{7,5},{8,10},{9,11},{10,... | collective-permute-start | bytes 344072 | tf_op jit(solution)/shard_map/ppermute | solution.py:23
  87.8 11.8 %collective-permute-start.29 = (bf16[32,3584]{1,0:T(8,128)(2,1)S(1)}, bf16[32,3584]{1,0:T(8,128)(2,1)S(1)}, u32[]{:S(2)}, u32[]{:S(2)}) collective-permute-start(bf16[32,3584]{1,0:T(8,128)(2,1)S(1)} %get-tuple-element.218), channel_id=1, source_target_pairs={{0,2},{1,3},{2,0},{3,1},{4,6},{5,7},{6,4},{7,5},{8,10},{9,11},{10,... | collective-permute-start | bytes 688136 | tf_op jit(solution)/shard_map/ppermute | solution.py:23
  90.5 14.3 %collective-permute-start.35 = (bf16[64,2048]{1,0:T(8,128)(2,1)S(1)}, bf16[64,2048]{1,0:T(8,128)(2,1)S(1)}, u32[]{:S(2)}, u32[]{:S(2)}) collective-permute-start(bf16[64,2048]{1,0:T(8,128)(2,1)S(1)} %add.26), channel_id=1, source_target_pairs={{0,8},{4,12},{8,0},{12,4},{1,9},{5,13},{9,1},{13,5},{2,10},{6,14},... | collective-permute-start | bytes 786440 | tf_op jit(solution)/shard_map/ppermute | solution.py:23
  92.9 1.4 %collective-permute-start.32 = (bf16[32,1792]{1,0:T(8,128)(2,1)S(1)}, bf16[32,1792]{1,0:T(8,128)(2,1)S(1)}, u32[]{:S(2)}, u32[]{:S(2)}) collective-permute-start(bf16[32,1792]{1,0:T(8,128)(2,1)S(1)} %get-tuple-element.226), channel_id=1, source_target_pairs={{0,1},{1,0},{2,3},{3,2},{4,5},{5,4},{6,7},{7,6},{8,9},{9,8},{10,11... | collective-permute-start | bytes 344072 | tf_op jit(solution)/shard_map/ppermute | solution.py:23
  93.0 1.5 %collective-permute-start.33 = (bf16[32,1792]{1,0:T(8,128)(2,1)S(1)}, bf16[32,1792]{1,0:T(8,128)(2,1)S(1)}, u32[]{:S(2)}, u32[]{:S(2)}) collective-permute-start(bf16[32,1792]{1,0:T(8,128)(2,1)S(1)} %get-tuple-element.227), channel_id=1, source_target_pairs={{0,1},{1,0},{2,3},{3,2},{4,5},{5,4},{6,7},{7,6},{8,9},{9,8},{10,11... | collective-permute-start | bytes 344072 | tf_op jit(solution)/shard_map/ppermute | solution.py:23
  97.1 12.8 %collective-permute-start.41 = (bf16[64,2048]{1,0:T(8,128)(2,1)S(1)}, bf16[64,2048]{1,0:T(8,128)(2,1)S(1)}, u32[]{:S(2)}, u32[]{:S(2)}) collective-permute-start(bf16[64,2048]{1,0:T(8,128)(2,1)S(1)} %down.9), channel_id=1, source_target_pairs={{0,4},{4,0},{8,12},{12,8},{1,5},{5,1},{9,13},{13,9},{2,6},{6,2},{1... | collective-permute-start | bytes 786440 | tf_op jit(solution)/shard_map/ppermute | solution.py:23
  98.9 1.6 %collective-permute-start.36 = (bf16[32,1792]{1,0:T(8,128)(2,1)S(1)}, bf16[32,1792]{1,0:T(8,128)(2,1)S(1)}, u32[]{:S(2)}, u32[]{:S(2)}) collective-permute-start(bf16[32,1792]{1,0:T(8,128)(2,1)S(1)} %get-tuple-element.232), channel_id=1, source_target_pairs={{0,1},{1,0},{2,3},{3,2},{4,5},{5,4},{6,7},{7,6},{8,9},{9,8},{10,11... | collective-permute-start | bytes 344072 | tf_op jit(solution)/shard_map/ppermute | solution.py:23
  99.1 1.5 %collective-permute-start.37 = (bf16[32,1792]{1,0:T(8,128)(2,1)S(1)}, bf16[32,1792]{1,0:T(8,128)(2,1)S(1)}, u32[]{:S(2)}, u32[]{:S(2)}) collective-permute-start(bf16[32,1792]{1,0:T(8,128)(2,1)S(1)} %get-tuple-element.233), channel_id=1, source_target_pairs={{0,1},{1,0},{2,3},{3,2},{4,5},{5,4},{6,7},{7,6},{8,9},{9,8},{10,11... | collective-permute-start | bytes 344072 | tf_op jit(solution)/shard_map/ppermute | solution.py:23
  99.6 5.2 %collective-permute-start.34 = (bf16[16,3584]{1,0:T(8,128)(2,1)S(1)}, bf16[16,3584]{1,0:T(8,128)(2,1)S(1)}, u32[]{:S(2)}, u32[]{:S(2)}) collective-permute-start(bf16[16,3584]{1,0:T(8,128)(2,1)S(1)} %hidden.11.share_ref), channel_id=1, source_target_pairs={{0,2},{1,3},{2,0},{3,1},{4,6},{5,7},{6,4},{7,5},{8,10},{9,11},{10,... | collective-permute-start | bytes 344072 | tf_op jit(solution)/shard_map/ppermute | solution.py:23
  104.9 1.4 %collective-permute-start.39 = (bf16[32,1792]{1,0:T(8,128)(2,1)S(1)}, bf16[32,1792]{1,0:T(8,128)(2,1)S(1)}, u32[]{:S(2)}, u32[]{:S(2)}) collective-permute-start(bf16[32,1792]{1,0:T(8,128)(2,1)S(1)} %get-tuple-element.239), channel_id=1, source_target_pairs={{0,1},{1,0},{2,3},{3,2},{4,5},{5,4},{6,7},{7,6},{8,9},{9,8},{10,11... | collective-permute-start | bytes 344072 | tf_op jit(solution)/shard_map/ppermute | solution.py:23
  104.9 1.5 %collective-permute-start.40 = (bf16[32,1792]{1,0:T(8,128)(2,1)S(1)}, bf16[32,1792]{1,0:T(8,128)(2,1)S(1)}, u32[]{:S(2)}, u32[]{:S(2)}) collective-permute-start(bf16[32,1792]{1,0:T(8,128)(2,1)S(1)} %get-tuple-element.240), channel_id=1, source_target_pairs={{0,1},{1,0},{2,3},{3,2},{4,5},{5,4},{6,7},{7,6},{8,9},{9,8},{10,11... | collective-permute-start | bytes 344072 | tf_op jit(solution)/shard_map/ppermute | solution.py:23
  105.4 11.6 %collective-permute-start.38 = (bf16[64,2048]{1,0:T(8,128)(2,1)S(1)}, bf16[64,2048]{1,0:T(8,128)(2,1)S(1)}, u32[]{:S(2)}, u32[]{:S(2)}) collective-permute-start(bf16[64,2048]{1,0:T(8,128)(2,1)S(1)} %down.10), channel_id=1, source_target_pairs={{0,4},{4,0},{8,12},{12,8},{1,5},{5,1},{9,13},{13,9},{2,6},{6,2},{1... | collective-permute-start | bytes 786440 | tf_op jit(solution)/shard_map/ppermute | solution.py:23
  110.0 14.8 %collective-permute-start.42 = (bf16[64,2048]{1,0:T(8,128)(2,1)S(1)}, bf16[64,2048]{1,0:T(8,128)(2,1)S(1)}, u32[]{:S(2)}, u32[]{:S(2)}) collective-permute-start(bf16[64,2048]{1,0:T(8,128)(2,1)S(1)} %add.27), channel_id=1, source_target_pairs={{0,8},{4,12},{8,0},{12,4},{1,9},{5,13},{9,1},{13,5},{2,10},{6,14},... | collective-permute-start | bytes 786440 | tf_op jit(solution)/shard_map/ppermute | solution.py:23
  124.9 4.5 %collective-permute-start.43 = (f32[1,2048]{1,0:T(1,128)S(1)}, f32[1,2048]{1,0:T(1,128)S(1)}, u32[]{:S(2)}, u32[]{:S(2)}) collective-permute-start(f32[1,2048]{1,0:T(1,128)S(1)} %bitcast.6), channel_id=1, source_target_pairs={{0,4},{4,0},{8,12},{12,8},{1,5},{5,1},{9,13},{13,9},{2,6},{6,2},{1... | collective-permute-start | bytes 24584 | tf_op jit(solution)/shard_map/ppermute | solution.py:23
  124.9 4.6 %collective-permute-start.44 = (f32[1,2048]{1,0:T(1,128)S(1)}, f32[1,2048]{1,0:T(1,128)S(1)}, u32[]{:S(2)}, u32[]{:S(2)}) collective-permute-start(f32[1,2048]{1,0:T(1,128)S(1)} %bitcast.7), channel_id=1, source_target_pairs={{0,8},{4,12},{8,0},{12,4},{1,9},{5,13},{9,1},{13,5},{2,10},{6,14},... | collective-permute-start | bytes 24584 | tf_op jit(solution)/shard_map/ppermute | solution.py:23
  127.9 5.4 %collective-permute-start.45 = (f32[1,2048]{1,0:T(1,128)S(1)}, f32[1,2048]{1,0:T(1,128)S(1)}, u32[]{:S(2)}, u32[]{:S(2)}) collective-permute-start(f32[1,2048]{1,0:T(1,128)S(1)} %bitcast.8), channel_id=1, source_target_pairs={{0,12},{4,8},{8,4},{12,0},{1,13},{5,9},{9,5},{13,1},{2,14},{6,10},... | collective-permute-start | bytes 24584 | tf_op jit(solution)/shard_map/ppermute | solution.py:23
  (8 other events, 47.5 us)

commit v3 on v2

--- a/solution.py
+++ b/solution.py
@@ -247,6 +247,8 @@
         core = [ref[...] for ref in core_refs]
         core = jnp.concatenate(core, axis=1) if len(core) > 1 else core[0]
         value = jnp.concatenate([mine_ref[...], core])
+        if rows < 128:
+            value = jnp.concatenate([value] * (128 // rows))
         for start in range(0, columns, TILE):
             at = slice(start, start + TILE)
             result = dot(value, weight_ref[:, at])
@@ -264,11 +266,16 @@
     out_ref[...] = narrow(part_ref[...] + widen(got_ref[...]))
 
 
-def scale_kernel(first_ref, second_ref, peak_ref, out_ref):
+def scale_kernel(first_ref, second_ref, *refs):
+    *peak_refs, out_ref, scales_ref = refs
     rows = out_ref.shape[0] // WIDTH
     half = rows // 2
     starts = rows_of(ORDER, lax.axis_index("width"), rows)
-    peak = peak_ref[...] + 1e-06
+    peak = peak_refs[0][...]
+    for peak_ref in peak_refs[1:]:
+        peak = jnp.maximum(peak, peak_ref[...])
+    scales_ref[...] = peak / 448.0
+    peak = peak + 1e-06
     for place, start in enumerate(starts):
         here = slice(place * half, (place + 1) * half)
         for offset, ref in ((0, first_ref), (half, second_ref)):
@@ -355,26 +362,25 @@
     got5 = tick(got5)
     share5, joined1 = done(hidden(mine5, got5, None, share1))
     got2 = swap(send2, "width", CORES)
+    core1 = ticks(parts_of(joined1, 2))
+    (part1,) = done(combine(joined1, core1, down_weight, (jnp.bfloat16,)))
+    add1 = swap(part1, AXIS, 1)
     far_second = done(tick(far_second))
     keep, *sends = done(
         project((cross_second, far_second), weights, [(0, stay, three)])
     )
-    got2, core1, *cores = ticks(
-        [got2, swap(joined1, "width", 1), *swap_pieces(sends)]
-    )
+    got2, *cores = ticks([got2, *swap_pieces(sends)])
 
     (share2,) = done(hidden(mine2, got2))
     over2 = swap(share2, "width", CORES)
     mine3, send3, mine4, send4 = done(add_cores(keep, cores, group, split=2))
     payload = done(join_rows(send4, share5))
-    (part1,) = done(combine(joined1, [core1], down_weight, (jnp.bfloat16,)))
-    add1 = swap(part1, AXIS, 1)
     core0 = tick(swap(joined0, "width", 1))
     first, second = done(
         combine(joined0, [core0], down_weight, (jnp.float32, jnp.float32))
     )
-    over2, payload = ticks([over2, payload])
     got4 = swap(payload, "width", CORES)
+    over2, add1 = ticks([over2, add1])
     joined2 = done(join(share2, over2))
     core2 = ticks(parts_of(joined2, 2))
     cross2, far2 = done(
@@ -383,7 +389,7 @@
     far2 = swap(far2, AXIS, 1)
     got3 = swap(tick(send3), "width", CORES)
 
-    got4, add1 = ticks([got4, add1])
+    got4 = tick(got4)
     share4, joined5 = done(hidden(mine4, got4, None, share5))
     over4 = swap(share4, "width", CORES)
     far2 = tick(far2)
@@ -414,11 +420,14 @@
         jnp.max(jnp.abs(first), axis=0, keepdims=True),
         jnp.max(jnp.abs(second), axis=0, keepdims=True),
     )
-    peak = local_peak
-    for k in range(1, RANKS):
-        peak = jnp.maximum(peak, swap(local_peak, AXIS, k))
-    scaled = call(scale_kernel, array(*tokens.shape), (first, second, peak), "scale")
-    return (scaled, peak[0] / 448.0)
+    peaks = [swap(local_peak, AXIS, k) for k in range(1, RANKS)]
+    scaled, scales = call(
+        scale_kernel,
+        (array(*tokens.shape), array(1, tokens.shape[1], jnp.float32)),
+        (first, second, local_peak, *peaks),
+        "scale",
+    )
+    return (scaled, scales[0])
 
 
 def plain(tokens, gate_weight, up_weight, down_weight):

time: 135 us -> 133 us (0.985)
  waiting for transfers between devices: 53.1 us -> 56.7 us
  starting transfers between devices: 40.2 us -> 37.4 us
  Pallas kernels: 35.1 us -> 32.9 us
    ppermute x46 -> x47, waiting for transfers between devices: 53.1 us -> 56.7 us  [swap(): return lax.ppermute(value, axis, [(i, i ^ mask) for i in range(size)])]
    ppermute x46 -> x47, starting transfers between devices: 40.2 us -> 37.4 us  [swap(): return lax.ppermute(value, axis, [(i, i ^ mask) for i in range(size)])]
    pallas_call x39 -> x40, Pallas kernels: 35.1 us -> 32.9 us  [call(): pl.pallas_call(kernel, out_shape=shapes, in_specs=[VMEM] * len(args), out...]
  transfers between devices with their start and end apart: 46 -> 47, of which waited for: 24 -> 29; matrix products, arithmetic and copies ran while one was open for 0% -> 0% of each run, Pallas kernels for 25% -> 24%
where the time goes in v3:
time: 133 us
  waiting for transfers between devices  56.7 us (43%)
  starting transfers between devices  37.4 us (28%)
  Pallas kernels  32.9 us (25%)
  local copies, waits for them, and re-layouts  4.53 us (3%)
    ppermute x47, waiting for transfers between devices, swap(): return lax.ppermute(value, axis, [(i, i ^ mask) for i in range(size)])  56.7 us
    ppermute x47, starting transfers between devices, swap(): return lax.ppermute(value, axis, [(i, i ^ mask) for i in range(size)])  37.4 us
    pallas_call x40, Pallas kernels, call(): pl.pallas_call(kernel, out_shape=shapes, in_specs=[VMEM] * len(args), out...  32.9 us
    unnamed x20, local copies, waits for them, and re-layouts  4.53 us
  transfers between devices with their start and end apart: 47, of which 29 were waited for; matrix products, arithmetic and copies ran while one was open for 0% of the time, Pallas kernels for 24%

profile of v3, /device:TPU:0, one launch (start us, length us, event | category | flops | bytes accessed | tf_op | source)
XLA Modules:
  0.0 132.8 jit_solution(214652588216801682)
XLA Ops:
  0.7 3.1 %collective-permute-start = (bf16[128,2048]{1,0:T(8,128)(2,1)}, bf16[128,2048]{1,0:T(8,128)(2,1)S(1)}, u32[]{:S(2)}, u32[]{:S(2)}) collective-permute-start(bf16[128,2048]{1,0:T(8,128)(2,1)} %tokens_ref.1), channel_id=1, source_target_pairs={{0,4},{4,0},{8,12},{12,8},{1,5},{5,1},{9,13},{13,9},{2,6},{6,2},{1... | collective-permute-start | bytes 1572872 | tf_op jit(solution)/shard_map/ppermute | solution.py:23
  3.8 1.8 %copy-done.1 = bf16[128,2048]{1,0:T(8,128)(2,1)S(1)} copy-done((bf16[128,2048]{1,0:T(8,128)(2,1)S(1)}, bf16[128,2048]{1,0:T(8,128)(2,1)}, u32[]{:S(2)}) %copy-start.1) | copy-done | bytes 524312
  6.0 2.1 %gate.4 = (bf16[64,7168]{1,0:T(8,128)(2,1)S(1)}, bf16[64,2304]{1,0:T(8,128)(2,1)S(1)}, bf16[64,2432]{1,0:T(8,128)(2,1)S(1)}, bf16[64,2432]{1,0:T(8,128)(2,1)S(1)}) custom-call(bf16[128,2048]{1,0:T(8,128)(2,1)S(1)} %arrange.2.refs_0_.block_ref, bf16[2048,3584]{1,0:T(8,128)(2,1)S(1)} %copy-done), custom_call_target="tpu_custom_call" | custom-call | flops 3758096384 | bytes 14680064 | tf_op jit(solution)/shard_map/gate/pallas_call | solution.py:48
  8.4 1.2 slice-done.6
  9.5 0.8 slice-done.7
  10.4 2.2 %up.4 = (bf16[64,7168]{1,0:T(8,128)(2,1)S(1)}, bf16[64,2304]{1,0:T(8,128)(2,1)S(1)}, bf16[64,2432]{1,0:T(8,128)(2,1)S(1)}, bf16[64,2432]{1,0:T(8,128)(2,1)S(1)}) custom-call(bf16[128,2048]{1,0:T(8,128)(2,1)S(1)} %arrange.2.refs_0_.block_ref, bf16[2048,3584]{1,0:T(8,128)(2,1)S(1)} %bitcast.5, ...), custom_call_target="tpu_custom_call", output_to_operand_aliasing={{0}: (2, {}), {1}: (3, {}), {2}: (4, {}), {3}: (5, {})} | custom-call | flops 1 | bytes 1 | tf_op jit(solution)/shard_map/up/pallas_call | solution.py:48
  13.7 3.7 %collective-permute-start.4 = (bf16[64,2048]{1,0:T(8,128)(2,1)S(1)}, bf16[64,2048]{1,0:T(8,128)(2,1)S(1)}, u32[]{:S(2)}, u32[]{:S(2)}) collective-permute-start(bf16[64,2048]{1,0:T(8,128)(2,1)S(1)} %get-tuple-element.146), channel_id=1, source_target_pairs={{0,8},{4,12},{8,0},{12,4},{1,9},{5,13},{9,1},{13,5},{2,10},{6,14},... | collective-permute-start | bytes 786440 | tf_op jit(solution)/shard_map/ppermute | solution.py:23
  17.6 1.5 %collective-permute-start.7 = (bf16[64,3584]{1,0:T(8,128)(2,1)S(1)}, bf16[64,3584]{1,0:T(8,128)(2,1)S(1)}, u32[]{:S(2)}, u32[]{:S(2)}) collective-permute-start(bf16[64,3584]{1,0:T(8,128)(2,1)S(1)} %get-tuple-element.157), channel_id=1, source_target_pairs={{0,2},{1,3},{2,0},{3,1},{4,6},{5,7},{6,4},{7,5},{8,10},{9,11},{10,... | collective-permute-start | bytes 1376264 | tf_op jit(solution)/shard_map/ppermute | solution.py:23
  19.2 2.1 %gate.5 = (bf16[64,7168]{1,0:T(8,128)(2,1)S(1)}, bf16[32,4736]{1,0:T(8,128)(2,1)S(1)}, bf16[32,2432]{1,0:T(8,128)(2,1)S(1)}, bf16[32,3584]{1,0:T(8,128)(2,1)S(1)}, bf16[32,3584]{1,0:T(8,128)(2,1)S(1)}) custom-call(bf16[128,2048]{1,0:T(8,128)(2,1)S(1)} %arrange.3.refs_0_, bf16[2048,3584]{1,0:T(8,128)(2,1)S(1)} %copy-done), custom_call_target="tpu_custom_call" | custom-call | flops 1 | bytes 1 | tf_op jit(solution)/shard_map/gate/pallas_call | solution.py:48
  21.3 2.2 %up.5 = (bf16[64,7168]{1,0:T(8,128)(2,1)S(1)}, bf16[32,4736]{1,0:T(8,128)(2,1)S(1)}, bf16[32,2432]{1,0:T(8,128)(2,1)S(1)}, bf16[32,3584]{1,0:T(8,128)(2,1)S(1)}, bf16[32,3584]{1,0:T(8,128)(2,1)S(1)}) custom-call(bf16[128,2048]{1,0:T(8,128)(2,1)S(1)} %arrange.3.refs_0_, ...), custom_call_target="tpu_custom_call", output_to_operand_aliasing={{0}: (2, {}), {1}: (3, {}), {2}: (4, {}), {3}: (5, {}), {4}... | custom-call | flops 1 | bytes 1 | tf_op jit(solution)/shard_map/up/pallas_call | solution.py:48
  23.5 6.4 %collective-permute-done.4.refs_0_ = bf16[64,2048]{1,0:T(8,128)(2,1)S(1)} collective-permute-done((bf16[64,2048]{1,0:T(8,128)(2,1)S(1)}, bf16[64,2048]{1,0:T(8,128)(2,1)S(1)}, u32[]{:S(2)}, u32[]{:S(2)}) %collective-permute-start.4) | collective-permute-done | bytes 262176 | tf_op jit(solution)/shard_map/ppermute | solution.py:23
  30.4 1.3 collective-permute-done.6.refs_2_
  32.0 1.6 %collective-permute-start.8 = (bf16[64,3584]{1,0:T(8,128)(2,1)S(1)}, bf16[64,3584]{1,0:T(8,128)(2,1)S(1)}, u32[]{:S(2)}, u32[]{:S(2)}) collective-permute-start(bf16[64,3584]{1,0:T(8,128)(2,1)S(1)} %get-tuple-element.160), channel_id=1, source_target_pairs={{0,2},{1,3},{2,0},{3,1},{4,6},{5,7},{6,4},{7,5},{8,10},{9,11},{10,... | collective-permute-start | bytes 1376264 | tf_op jit(solution)/shard_map/ppermute | solution.py:23
  34.4 3.4 %collective-permute-start.13 = (bf16[64,2048]{1,0:T(8,128)(2,1)S(1)}, bf16[64,2048]{1,0:T(8,128)(2,1)S(1)}, u32[]{:S(2)}, u32[]{:S(2)}) collective-permute-start(bf16[64,2048]{1,0:T(8,128)(2,1)S(1)} %get-tuple-element.179), channel_id=1, source_target_pairs={{0,8},{4,12},{8,0},{12,4},{1,9},{5,13},{9,1},{13,5},{2,10},{6,14},... | collective-permute-start | bytes 786440 | tf_op jit(solution)/shard_map/ppermute | solution.py:23
  38.2 1.0 collective-permute-done.10.refs_2_
  39.6 5.0 %collective-permute-done.8.refs_1_ = bf16[64,3584]{1,0:T(8,128)(2,1)S(1)} collective-permute-done((bf16[64,3584]{1,0:T(8,128)(2,1)S(1)}, bf16[64,3584]{1,0:T(8,128)(2,1)S(1)}, u32[]{:S(2)}, u32[]{:S(2)}) %collective-permute-start.8) | collective-permute-done | bytes 458784 | tf_op jit(solution)/shard_map/ppermute | solution.py:23
  44.8 1.6 %collective-permute-start.19 = (bf16[48,3584]{1,0:T(8,128)(2,1)S(1)}, bf16[48,3584]{1,0:T(8,128)(2,1)S(1)}, u32[]{:S(2)}, u32[]{:S(2)}) collective-permute-start(bf16[48,3584]{1,0:T(8,128)(2,1)S(1)} %get-tuple-element.191), channel_id=1, source_target_pairs={{0,2},{1,3},{2,0},{3,1},{4,6},{5,7},{6,4},{7,5},{8,10},{9,11},{10,... | collective-permute-start | bytes 1032200 | tf_op jit(solution)/shard_map/ppermute | solution.py:23
  47.1 2.1 %gate.6 = (bf16[64,7168]{1,0:T(8,128)(2,1)S(1)}, bf16[64,2304]{1,0:T(8,128)(2,1)S(1)}, bf16[64,2432]{1,0:T(8,128)(2,1)S(1)}, bf16[64,2432]{1,0:T(8,128)(2,1)S(1)}) custom-call(bf16[64,2048]{1,0:T(8,128)(2,1)S(1)} %collective-permute-done.4.refs_0_, bf16[64,2048]{1,0:T(8,128)(2,1)S(1)} %collective-permute-done.12.refs_1_, bf16[2048,3584]{1,0:T(8,128)(2,1)S(1)} %copy-done), custom_call_target="tpu_custom_call" | custom-call | flops 1 | bytes 1 | tf_op jit(solution)/shard_map/gate/pallas_call | solution.py:48
  49.2 2.4 %up.6 = (bf16[64,7168]{1,0:T(8,128)(2,1)S(1)}, bf16[64,2304]{1,0:T(8,128)(2,1)S(1)}, bf16[64,2432]{1,0:T(8,128)(2,1)S(1)}, bf16[64,2432]{1,0:T(8,128)(2,1)S(1)}) custom-call(bf16[64,2048]{1,0:T(8,128)(2,1)S(1)} %collective-permute-done.4.refs_0_, ...), custom_call_target="tpu_custom_call", output_to_operand_aliasing={{0}: (3, {}), {1}: (4, {}), {2}: (5, {}), {3}: (6, {})} | custom-call | flops 1 | bytes 1 | tf_op jit(solution)/shard_map/up/pallas_call | solution.py:48
  52.3 1.9 %collective-permute-done.14.refs_1_ = bf16[64,2304]{1,0:T(8,128)(2,1)S(1)} collective-permute-done((bf16[64,2304]{1,0:T(8,128)(2,1)S(1)}, bf16[64,2304]{1,0:T(8,128)(2,1)S(1)}, u32[]{:S(2)}, u32[]{:S(2)}) %collective-permute-start.14) | collective-permute-done | bytes 294944 | tf_op jit(solution)/shard_map/ppermute | solution.py:23
  55.7 0.8 collective-permute-done.20.refs_0_
  56.7 2.1 %down.6 = bf16[64,2048]{1,0:T(8,128)(2,1)S(1)} custom-call(bf16[32,3584]{1,0:T(8,128)(2,1)S(1)} %get-tuple-element.194.mine_ref, bf16[32,1792]{1,0:T(8,128)(2,1)S(1)} %collective-permute-done.20.refs_0_, bf16[32,1792]{1,0:T(8,128)(2,1)S(1)} %collective-permute-done.21.refs_1_, bf16[3584,2048]{1,0:T(8,128)(2,1)S(1)} %bitcast.3), custom_call_target="tpu_custom_call" | custom-call | flops 1 | bytes 1 | tf_op jit(solution)/shard_map/down/pallas_call | solution.py:48
  58.8 2.2 %collective-permute-done.18.refs_1_ = bf16[64,2048]{1,0:T(8,128)(2,1)S(1)} collective-permute-done((bf16[64,2048]{1,0:T(8,128)(2,1)S(1)}, bf16[64,2048]{1,0:T(8,128)(2,1)S(1)}, u32[]{:S(2)}, u32[]{:S(2)}) %collective-permute-start.18) | collective-permute-done | bytes 262176 | tf_op jit(solution)/shard_map/ppermute | solution.py:23
  61.0 2.1 %gate.7 = (bf16[64,7168]{1,0:T(8,128)(2,1)S(1)}, bf16[64,2304]{1,0:T(8,128)(2,1)S(1)}, bf16[64,2432]{1,0:T(8,128)(2,1)S(1)}, bf16[64,2432]{1,0:T(8,128)(2,1)S(1)}) custom-call(bf16[64,2048]{1,0:T(8,128)(2,1)S(1)} %collective-permute-done.13.refs_0_, bf16[64,2048]{1,0:T(8,128)(2,1)S(1)} %collective-permute-done.18.refs_1_, bf16[2048,3584]{1,0:T(8,128)(2,1)S(1)} %copy-done), custom_call_target="tpu_custom_call" | custom-call | flops 1 | bytes 1 | tf_op jit(solution)/shard_map/gate/pallas_call | solution.py:48
  63.0 2.2 %up.7 = (bf16[64,7168]{1,0:T(8,128)(2,1)S(1)}, bf16[64,2304]{1,0:T(8,128)(2,1)S(1)}, bf16[64,2432]{1,0:T(8,128)(2,1)S(1)}, bf16[64,2432]{1,0:T(8,128)(2,1)S(1)}) custom-call(bf16[64,2048]{1,0:T(8,128)(2,1)S(1)} %collective-permute-done.13.refs_0_, ...), custom_call_target="tpu_custom_call", output_to_operand_aliasing={{0}: (3, {}), {1}: (4, {}), {2}: (5, {}), {3}: (6, {})} | custom-call | flops 1 | bytes 1 | tf_op jit(solution)/shard_map/up/pallas_call | solution.py:48
  68.8 2.1 %down.7 = (f32[64,2048]{1,0:T(8,128)S(1)}, f32[64,2048]{1,0:T(8,128)S(1)}) custom-call(bf16[64,3584]{1,0:T(8,128)(2,1)S(1)} %get-tuple-element.171.mine_ref, bf16[64,3584]{1,0:T(8,128)(2,1)S(1)} %collective-permute-done.11.refs_0_, bf16[3584,2048]{1,0:T(8,128)(2,1)S(1)} %bitcast.3), custom_call_target="tpu_custom_call" | custom-call | flops 1 | bytes 1 | tf_op jit(solution)/shard_map/down/pallas_call | solution.py:48
  70.9 4.4 %collective-permute-done.26 = bf16[64,2048]{1,0:T(8,128)(2,1)S(1)} collective-permute-done((bf16[64,2048]{1,0:T(8,128)(2,1)S(1)}, bf16[64,2048]{1,0:T(8,128)(2,1)S(1)}, u32[]{:S(2)}, u32[]{:S(2)}) %collective-permute-start.26) | collective-permute-done | bytes 262176 | tf_op jit(solution)/shard_map/ppermute | solution.py:23
  77.7 2.3 %down.8 = (f32[64,2048]{1,0:T(8,128)S(1)}, bf16[64,2048]{1,0:T(8,128)(2,1)S(1)}) custom-call(bf16[64,3584]{1,0:T(8,128)(2,1)S(1)} %join.3.mine_ref, bf16[64,1792]{1,0:T(8,128)(2,1)S(1)} %collective-permute-done.27.refs_0_, bf16[64,1792]{1,0:T(8,128)(2,1)S(1)} %collective-permute-done.28.refs_1_, bf16[3584,2048]{1,0:T(8,128)(2,1)S(1)} %bitcast.3), custom_call_target="tpu_custom_call" | custom-call | flops 1 | bytes 1 | tf_op jit(solution)/shard_map/down/pallas_call | solution.py:48
  80.0 0.9 collective-permute-start.32
  80.9 5.5 %collective-permute-done.30.refs_1_ = bf16[48,3584]{1,0:T(8,128)(2,1)S(1)} collective-permute-done((bf16[48,3584]{1,0:T(8,128)(2,1)S(1)}, bf16[48,3584]{1,0:T(8,128)(2,1)S(1)}, u32[]{:S(2)}, u32[]{:S(2)}) %collective-permute-start.30) | collective-permute-done | bytes 344096 | tf_op jit(solution)/shard_map/ppermute | solution.py:23
  87.0 1.5 %collective-permute-start.29 = (bf16[32,3584]{1,0:T(8,128)(2,1)S(1)}, bf16[32,3584]{1,0:T(8,128)(2,1)S(1)}, u32[]{:S(2)}, u32[]{:S(2)}) collective-permute-start(bf16[32,3584]{1,0:T(8,128)(2,1)S(1)} %get-tuple-element.225), channel_id=1, source_target_pairs={{0,2},{1,3},{2,0},{3,1},{4,6},{5,7},{6,4},{7,5},{8,10},{9,11},{10,... | collective-permute-start | bytes 688136 | tf_op jit(solution)/shard_map/ppermute | solution.py:23
  88.6 2.2 %collective-permute-start.36 = (bf16[64,2048]{1,0:T(8,128)(2,1)S(1)}, bf16[64,2048]{1,0:T(8,128)(2,1)S(1)}, u32[]{:S(2)}, u32[]{:S(2)}) collective-permute-start(bf16[64,2048]{1,0:T(8,128)(2,1)S(1)} %add.26), channel_id=1, source_target_pairs={{0,8},{4,12},{8,0},{12,4},{1,9},{5,13},{9,1},{13,5},{2,10},{6,14},... | collective-permute-start | bytes 786440 | tf_op jit(solution)/shard_map/ppermute | solution.py:23
  90.9 1.8 %collective-permute-done.31.got_ref = bf16[16,3584]{1,0:T(8,128)(2,1)S(1)} collective-permute-done((bf16[16,3584]{1,0:T(8,128)(2,1)S(1)}, bf16[16,3584]{1,0:T(8,128)(2,1)S(1)}, u32[]{:S(2)}, u32[]{:S(2)}) %collective-permute-start.31) | collective-permute-done | bytes 114720 | tf_op jit(solution)/shard_map/ppermute | solution.py:23
  93.2 0.8 collective-permute-done.33.refs_0_
  94.2 2.1 %down.9 = bf16[64,2048]{1,0:T(8,128)(2,1)S(1)} custom-call(bf16[32,3584]{1,0:T(8,128)(2,1)S(1)} %join.4.mine_ref, bf16[32,1792]{1,0:T(8,128)(2,1)S(1)} %collective-permute-done.33.refs_0_, bf16[32,1792]{1,0:T(8,128)(2,1)S(1)} %collective-permute-done.34.refs_1_, bf16[3584,2048]{1,0:T(8,128)(2,1)S(1)} %bitcast.3), custom_call_target="tpu_custom_call" | custom-call | flops 1 | bytes 1 | tf_op jit(solution)/shard_map/down/pallas_call | solution.py:48
  96.3 0.9 collective-permute-start.42
  98.8 2.1 %down.10 = bf16[64,2048]{1,0:T(8,128)(2,1)S(1)} custom-call(bf16[32,3584]{1,0:T(8,128)(2,1)S(1)} %get-tuple-element.237.mine_ref, bf16[32,1792]{1,0:T(8,128)(2,1)S(1)} %collective-permute-done.37.refs_0_, bf16[32,1792]{1,0:T(8,128)(2,1)S(1)} %collective-permute-done.38.refs_1_, bf16[3584,2048]{1,0:T(8,128)(2,1)S(1)} %bitcast.3), custom_call_target="tpu_custom_call" | custom-call | flops 1 | bytes 1 | tf_op jit(solution)/shard_map/down/pallas_call | solution.py:48
  100.9 2.2 %collective-permute-done.35.got_ref = bf16[16,3584]{1,0:T(8,128)(2,1)S(1)} collective-permute-done((bf16[16,3584]{1,0:T(8,128)(2,1)S(1)}, bf16[16,3584]{1,0:T(8,128)(2,1)S(1)}, u32[]{:S(2)}, u32[]{:S(2)}) %collective-permute-start.35) | collective-permute-done | bytes 114720 | tf_op jit(solution)/shard_map/ppermute | solution.py:23
  103.8 1.2 collective-permute-start.39
  104.9 2.1 %down.11.part_ref = f32[64,2048]{1,0:T(8,128)S(1)} custom-call(bf16[32,3584]{1,0:T(8,128)(2,1)S(1)} %join.5.mine_ref, bf16[32,1792]{1,0:T(8,128)(2,1)S(1)} %collective-permute-done.40.refs_0_, bf16[32,1792]{1,0:T(8,128)(2,1)S(1)} %collective-permute-done.41.refs_1_, bf16[3584,2048]{1,0:T(8,128)(2,1)S(1)} %bitcast.3), custom_call_target="tpu_custom_call" | custom-call | flops 1 | bytes 1 | tf_op jit(solution)/shard_map/down/pallas_call | solution.py:48
  107.0 1.3 collective-permute-done.42.got_ref
  108.3 1.1 collective-permute-start.43
  109.5 6.4 %collective-permute-done.39 = bf16[64,2048]{1,0:T(8,128)(2,1)S(1)} collective-permute-done((bf16[64,2048]{1,0:T(8,128)(2,1)S(1)}, bf16[64,2048]{1,0:T(8,128)(2,1)S(1)}, u32[]{:S(2)}, u32[]{:S(2)}) %collective-permute-start.39) | collective-permute-done | bytes 262176 | tf_op jit(solution)/shard_map/ppermute | solution.py:23
  116.0 7.2 %collective-permute-done.43 = bf16[64,2048]{1,0:T(8,128)(2,1)S(1)} collective-permute-done((bf16[64,2048]{1,0:T(8,128)(2,1)S(1)}, bf16[64,2048]{1,0:T(8,128)(2,1)S(1)}, u32[]{:S(2)}, u32[]{:S(2)}) %collective-permute-start.43) | collective-permute-done | bytes 262176 | tf_op jit(solution)/shard_map/ppermute | solution.py:23
  123.4 3.1 %collective-permute-start.45 = (f32[1,2048]{1,0:T(1,128)S(1)}, f32[1,2048]{1,0:T(1,128)S(1)}, u32[]{:S(2)}, u32[]{:S(2)}) collective-permute-start(f32[1,2048]{1,0:T(1,128)S(1)} %bitcast.7), channel_id=1, source_target_pairs={{0,8},{4,12},{8,0},{12,4},{1,9},{5,13},{9,1},{13,5},{2,10},{6,14},... | collective-permute-start | bytes 24584 | tf_op jit(solution)/shard_map/ppermute | solution.py:23
  126.4 1.3 collective-permute-start.46
  128.1 3.8 %collective-permute-done.46.refs_3_ = f32[1,2048]{1,0:T(1,128)S(1)} collective-permute-done((f32[1,2048]{1,0:T(1,128)S(1)}, f32[1,2048]{1,0:T(1,128)S(1)}, u32[]{:S(2)}, u32[]{:S(2)}) %collective-permute-start.46) | collective-permute-done | bytes 8224 | tf_op jit(solution)/shard_map/ppermute | solution.py:23
  131.9 0.9 scale.1
  (111 shorter events, 17.6 us)
Async XLA Ops:
  0.7 18.5 %collective-permute-start = (bf16[128,2048]{1,0:T(8,128)(2,1)}, bf16[128,2048]{1,0:T(8,128)(2,1)S(1)}, u32[]{:S(2)}, u32[]{:S(2)}) collective-permute-start(bf16[128,2048]{1,0:T(8,128)(2,1)} %tokens_ref.1), channel_id=1, source_target_pairs={{0,4},{4,0},{8,12},{12,8},{1,5},{5,1},{9,13},{13,9},{2,6},{6,2},{1... | collective-permute-start | bytes 1572872 | tf_op jit(solution)/shard_map/ppermute | solution.py:23
  12.6 4.8 %collective-permute-start.2 = (bf16[64,2432]{1,0:T(8,128)(2,1)S(1)}, bf16[64,2432]{1,0:T(8,128)(2,1)S(1)}, u32[]{:S(2)}, u32[]{:S(2)}) collective-permute-start(bf16[64,2432]{1,0:T(8,128)(2,1)S(1)} %get-tuple-element.132), channel_id=1, source_target_pairs={{0,1},{1,0},{2,3},{3,2},{4,5},{5,4},{6,7},{7,6},{8,9},{9,8},{10,11... | collective-permute-start | bytes 933896 | tf_op jit(solution)/shard_map/ppermute | solution.py:23
  13.1 4.3 %collective-permute-start.3 = (bf16[64,2432]{1,0:T(8,128)(2,1)S(1)}, bf16[64,2432]{1,0:T(8,128)(2,1)S(1)}, u32[]{:S(2)}, u32[]{:S(2)}) collective-permute-start(bf16[64,2432]{1,0:T(8,128)(2,1)S(1)} %get-tuple-element.133), channel_id=1, source_target_pairs={{0,1},{1,0},{2,3},{3,2},{4,5},{5,4},{6,7},{7,6},{8,9},{9,8},{10,11... | collective-permute-start | bytes 933896 | tf_op jit(solution)/shard_map/ppermute | solution.py:23
  13.2 4.2 %collective-permute-start.1 = (bf16[64,2304]{1,0:T(8,128)(2,1)S(1)}, bf16[64,2304]{1,0:T(8,128)(2,1)S(1)}, u32[]{:S(2)}, u32[]{:S(2)}) collective-permute-start(bf16[64,2304]{1,0:T(8,128)(2,1)S(1)} %get-tuple-element.131), channel_id=1, source_target_pairs={{0,1},{1,0},{2,3},{3,2},{4,5},{5,4},{6,7},{7,6},{8,9},{9,8},{10,11... | collective-permute-start | bytes 884744 | tf_op jit(solution)/shard_map/ppermute | solution.py:23
  13.7 16.3 %collective-permute-start.4 = (bf16[64,2048]{1,0:T(8,128)(2,1)S(1)}, bf16[64,2048]{1,0:T(8,128)(2,1)S(1)}, u32[]{:S(2)}, u32[]{:S(2)}) collective-permute-start(bf16[64,2048]{1,0:T(8,128)(2,1)S(1)} %get-tuple-element.146), channel_id=1, source_target_pairs={{0,8},{4,12},{8,0},{12,4},{1,9},{5,13},{9,1},{13,5},{2,10},{6,14},... | collective-permute-start | bytes 786440 | tf_op jit(solution)/shard_map/ppermute | solution.py:23
  17.6 14.2 %collective-permute-start.7 = (bf16[64,3584]{1,0:T(8,128)(2,1)S(1)}, bf16[64,3584]{1,0:T(8,128)(2,1)S(1)}, u32[]{:S(2)}, u32[]{:S(2)}) collective-permute-start(bf16[64,3584]{1,0:T(8,128)(2,1)S(1)} %get-tuple-element.157), channel_id=1, source_target_pairs={{0,2},{1,3},{2,0},{3,1},{4,6},{5,7},{6,4},{7,5},{8,10},{9,11},{10,... | collective-permute-start | bytes 1376264 | tf_op jit(solution)/shard_map/ppermute | solution.py:23
  29.9 1.8 %collective-permute-start.5 = (bf16[32,4736]{1,0:T(8,128)(2,1)S(1)}, bf16[32,4736]{1,0:T(8,128)(2,1)S(1)}, u32[]{:S(2)}, u32[]{:S(2)}) collective-permute-start(bf16[32,4736]{1,0:T(8,128)(2,1)S(1)} %get-tuple-element.151), channel_id=1, source_target_pairs={{0,1},{1,0},{2,3},{3,2},{4,5},{5,4},{6,7},{7,6},{8,9},{9,8},{10,11... | collective-permute-start | bytes 909320 | tf_op jit(solution)/shard_map/ppermute | solution.py:23
  29.9 1.8 %collective-permute-start.6 = (bf16[32,2432]{1,0:T(8,128)(2,1)S(1)}, bf16[32,2432]{1,0:T(8,128)(2,1)S(1)}, u32[]{:S(2)}, u32[]{:S(2)}) collective-permute-start(bf16[32,2432]{1,0:T(8,128)(2,1)S(1)} %get-tuple-element.152), channel_id=1, source_target_pairs={{0,1},{1,0},{2,3},{3,2},{4,5},{5,4},{6,7},{7,6},{8,9},{9,8},{10,11... | collective-permute-start | bytes 466952 | tf_op jit(solution)/shard_map/ppermute | solution.py:23
  32.0 12.6 %collective-permute-start.8 = (bf16[64,3584]{1,0:T(8,128)(2,1)S(1)}, bf16[64,3584]{1,0:T(8,128)(2,1)S(1)}, u32[]{:S(2)}, u32[]{:S(2)}) collective-permute-start(bf16[64,3584]{1,0:T(8,128)(2,1)S(1)} %get-tuple-element.160), channel_id=1, source_target_pairs={{0,2},{1,3},{2,0},{3,1},{4,6},{5,7},{6,4},{7,5},{8,10},{9,11},{10,... | collective-permute-start | bytes 1376264 | tf_op jit(solution)/shard_map/ppermute | solution.py:23
  33.7 13.5 %collective-permute-start.12 = (bf16[64,2048]{1,0:T(8,128)(2,1)S(1)}, bf16[64,2048]{1,0:T(8,128)(2,1)S(1)}, u32[]{:S(2)}, u32[]{:S(2)}) collective-permute-start(bf16[64,2048]{1,0:T(8,128)(2,1)S(1)} %collective-permute-done.4.refs_0_), channel_id=1, source_target_pairs={{0,4},{4,0},{8,12},{12,8},{1,5},{5,1},{9,13},{13,9},{2,6},{6,2},{1... | collective-permute-start | bytes 786440 | tf_op jit(solution)/shard_map/ppermute | solution.py:23
  34.4 17.3 %collective-permute-start.13 = (bf16[64,2048]{1,0:T(8,128)(2,1)S(1)}, bf16[64,2048]{1,0:T(8,128)(2,1)S(1)}, u32[]{:S(2)}, u32[]{:S(2)}) collective-permute-start(bf16[64,2048]{1,0:T(8,128)(2,1)S(1)} %get-tuple-element.179), channel_id=1, source_target_pairs={{0,8},{4,12},{8,0},{12,4},{1,9},{5,13},{9,1},{13,5},{2,10},{6,14},... | collective-permute-start | bytes 786440 | tf_op jit(solution)/shard_map/ppermute | solution.py:23
  37.7 1.5 %collective-permute-start.10 = (bf16[32,3584]{1,0:T(8,128)(2,1)S(1)}, bf16[32,3584]{1,0:T(8,128)(2,1)S(1)}, u32[]{:S(2)}, u32[]{:S(2)}) collective-permute-start(bf16[32,3584]{1,0:T(8,128)(2,1)S(1)} %get-tuple-element.165), channel_id=1, source_target_pairs={{0,1},{1,0},{2,3},{3,2},{4,5},{5,4},{6,7},{7,6},{8,9},{9,8},{10,11... | collective-permute-start | bytes 688136 | tf_op jit(solution)/shard_map/ppermute | solution.py:23
  37.7 1.8 %collective-permute-start.9 = (bf16[32,3584]{1,0:T(8,128)(2,1)S(1)}, bf16[32,3584]{1,0:T(8,128)(2,1)S(1)}, u32[]{:S(2)}, u32[]{:S(2)}) collective-permute-start(bf16[32,3584]{1,0:T(8,128)(2,1)S(1)} %get-tuple-element.164), channel_id=1, source_target_pairs={{0,1},{1,0},{2,3},{3,2},{4,5},{5,4},{6,7},{7,6},{8,9},{9,8},{10,11... | collective-permute-start | bytes 688136 | tf_op jit(solution)/shard_map/ppermute | solution.py:23
  44.8 10.2 %collective-permute-start.19 = (bf16[48,3584]{1,0:T(8,128)(2,1)S(1)}, bf16[48,3584]{1,0:T(8,128)(2,1)S(1)}, u32[]{:S(2)}, u32[]{:S(2)}) collective-permute-start(bf16[48,3584]{1,0:T(8,128)(2,1)S(1)} %get-tuple-element.191), channel_id=1, source_target_pairs={{0,2},{1,3},{2,0},{3,1},{4,6},{5,7},{6,4},{7,5},{8,10},{9,11},{10,... | collective-permute-start | bytes 1032200 | tf_op jit(solution)/shard_map/ppermute | solution.py:23
  47.1 9.5 %slice-start.1 = ((s8[14680064]{0:T(1024)(128)(4,1)}), s8[4194304]{0:T(1024)(128)(4,1)S(1)}, s32[]{:S(2)}) async-start(s8[14680064]{0:T(1024)(128)(4,1)} %bitcast.2), calls=%async_computation.1 | async-start | bytes 8388608
  51.7 2.5 %collective-permute-start.15 = (bf16[64,2432]{1,0:T(8,128)(2,1)S(1)}, bf16[64,2432]{1,0:T(8,128)(2,1)S(1)}, u32[]{:S(2)}, u32[]{:S(2)}) collective-permute-start(bf16[64,2432]{1,0:T(8,128)(2,1)S(1)} %get-tuple-element.184), channel_id=1, source_target_pairs={{0,1},{1,0},{2,3},{3,2},{4,5},{5,4},{6,7},{7,6},{8,9},{9,8},{10,11... | collective-permute-start | bytes 933896 | tf_op jit(solution)/shard_map/ppermute | solution.py:23
  51.7 2.5 %collective-permute-start.16 = (bf16[64,2432]{1,0:T(8,128)(2,1)S(1)}, bf16[64,2432]{1,0:T(8,128)(2,1)S(1)}, u32[]{:S(2)}, u32[]{:S(2)}) collective-permute-start(bf16[64,2432]{1,0:T(8,128)(2,1)S(1)} %get-tuple-element.185), channel_id=1, source_target_pairs={{0,1},{1,0},{2,3},{3,2},{4,5},{5,4},{6,7},{7,6},{8,9},{9,8},{10,11... | collective-permute-start | bytes 933896 | tf_op jit(solution)/shard_map/ppermute | solution.py:23
  52.2 2.0 %collective-permute-start.14 = (bf16[64,2304]{1,0:T(8,128)(2,1)S(1)}, bf16[64,2304]{1,0:T(8,128)(2,1)S(1)}, u32[]{:S(2)}, u32[]{:S(2)}) collective-permute-start(bf16[64,2304]{1,0:T(8,128)(2,1)S(1)} %get-tuple-element.183), channel_id=1, source_target_pairs={{0,1},{1,0},{2,3},{3,2},{4,5},{5,4},{6,7},{7,6},{8,9},{9,8},{10,11... | collective-permute-start | bytes 884744 | tf_op jit(solution)/shard_map/ppermute | solution.py:23
  52.3 8.7 %collective-permute-start.18 = (bf16[64,2048]{1,0:T(8,128)(2,1)S(1)}, bf16[64,2048]{1,0:T(8,128)(2,1)S(1)}, u32[]{:S(2)}, u32[]{:S(2)}) collective-permute-start(bf16[64,2048]{1,0:T(8,128)(2,1)S(1)} %collective-permute-done.13.refs_0_), channel_id=1, source_target_pairs={{0,4},{4,0},{8,12},{12,8},{1,5},{5,1},{9,13},{13,9},{2,6},{6,2},{1... | collective-permute-start | bytes 786440 | tf_op jit(solution)/shard_map/ppermute | solution.py:23
  54.4 13.4 %collective-permute-start.17 = (bf16[64,3584]{1,0:T(8,128)(2,1)S(1)}, bf16[64,3584]{1,0:T(8,128)(2,1)S(1)}, u32[]{:S(2)}, u32[]{:S(2)}) collective-permute-start(bf16[64,3584]{1,0:T(8,128)(2,1)S(1)} %get-tuple-element.190), channel_id=1, source_target_pairs={{0,2},{1,3},{2,0},{3,1},{4,6},{5,7},{6,4},{7,5},{8,10},{9,11},{10,... | collective-permute-start | bytes 1376264 | tf_op jit(solution)/shard_map/ppermute | solution.py:23
  55.1 1.4 %collective-permute-start.20 = (bf16[32,1792]{1,0:T(8,128)(2,1)S(1)}, bf16[32,1792]{1,0:T(8,128)(2,1)S(1)}, u32[]{:S(2)}, u32[]{:S(2)}) collective-permute-start(bf16[32,1792]{1,0:T(8,128)(2,1)S(1)} %get-tuple-element.195), channel_id=1, source_target_pairs={{0,1},{1,0},{2,3},{3,2},{4,5},{5,4},{6,7},{7,6},{8,9},{9,8},{10,11... | collective-permute-start | bytes 344072 | tf_op jit(solution)/shard_map/ppermute | solution.py:23
  55.2 1.5 %collective-permute-start.21 = (bf16[32,1792]{1,0:T(8,128)(2,1)S(1)}, bf16[32,1792]{1,0:T(8,128)(2,1)S(1)}, u32[]{:S(2)}, u32[]{:S(2)}) collective-permute-start(bf16[32,1792]{1,0:T(8,128)(2,1)S(1)} %get-tuple-element.196), channel_id=1, source_target_pairs={{0,1},{1,0},{2,3},{3,2},{4,5},{5,4},{6,7},{7,6},{8,9},{9,8},{10,11... | collective-permute-start | bytes 344072 | tf_op jit(solution)/shard_map/ppermute | solution.py:23
  65.3 1.6 %collective-permute-start.22 = (bf16[64,2304]{1,0:T(8,128)(2,1)S(1)}, bf16[64,2304]{1,0:T(8,128)(2,1)S(1)}, u32[]{:S(2)}, u32[]{:S(2)}) collective-permute-start(bf16[64,2304]{1,0:T(8,128)(2,1)S(1)} %get-tuple-element.205), channel_id=1, source_target_pairs={{0,1},{1,0},{2,3},{3,2},{4,5},{5,4},{6,7},{7,6},{8,9},{9,8},{10,11... | collective-permute-start | bytes 884744 | tf_op jit(solution)/shard_map/ppermute | solution.py:23
  65.4 2.0 %collective-permute-start.23 = (bf16[64,2432]{1,0:T(8,128)(2,1)S(1)}, bf16[64,2432]{1,0:T(8,128)(2,1)S(1)}, u32[]{:S(2)}, u32[]{:S(2)}) collective-permute-start(bf16[64,2432]{1,0:T(8,128)(2,1)S(1)} %get-tuple-element.206), channel_id=1, source_target_pairs={{0,1},{1,0},{2,3},{3,2},{4,5},{5,4},{6,7},{7,6},{8,9},{9,8},{10,11... | collective-permute-start | bytes 933896 | tf_op jit(solution)/shard_map/ppermute | solution.py:23
  65.9 2.0 %collective-permute-start.24 = (bf16[64,2432]{1,0:T(8,128)(2,1)S(1)}, bf16[64,2432]{1,0:T(8,128)(2,1)S(1)}, u32[]{:S(2)}, u32[]{:S(2)}) collective-permute-start(bf16[64,2432]{1,0:T(8,128)(2,1)S(1)} %get-tuple-element.207), channel_id=1, source_target_pairs={{0,1},{1,0},{2,3},{3,2},{4,5},{5,4},{6,7},{7,6},{8,9},{9,8},{10,11... | collective-permute-start | bytes 933896 | tf_op jit(solution)/shard_map/ppermute | solution.py:23
  65.9 2.9 %collective-permute-start.11 = (bf16[64,3584]{1,0:T(8,128)(2,1)S(1)}, bf16[64,3584]{1,0:T(8,128)(2,1)S(1)}, u32[]{:S(2)}, u32[]{:S(2)}) collective-permute-start(bf16[64,3584]{1,0:T(8,128)(2,1)S(1)} %get-tuple-element.171.mine_ref), channel_id=1, source_target_pairs={{0,1},{1,0},{2,3},{3,2},{4,5},{5,4},{6,7},{7,6},{8,9},{9,8},{10,11... | collective-permute-start | bytes 1376264 | tf_op jit(solution)/shard_map/ppermute | solution.py:23
  66.9 8.3 %collective-permute-start.26 = (bf16[64,2048]{1,0:T(8,128)(2,1)S(1)}, bf16[64,2048]{1,0:T(8,128)(2,1)S(1)}, u32[]{:S(2)}, u32[]{:S(2)}) collective-permute-start(bf16[64,2048]{1,0:T(8,128)(2,1)S(1)} %down.6), channel_id=1, source_target_pairs={{0,4},{4,0},{8,12},{12,8},{1,5},{5,1},{9,13},{13,9},{2,6},{6,2},{1... | collective-permute-start | bytes 786440 | tf_op jit(solution)/shard_map/ppermute | solution.py:23
  68.0 7.7 %collective-permute-start.25 = (bf16[32,3584]{1,0:T(8,128)(2,1)S(1)}, bf16[32,3584]{1,0:T(8,128)(2,1)S(1)}, u32[]{:S(2)}, u32[]{:S(2)}) collective-permute-start(bf16[32,3584]{1,0:T(8,128)(2,1)S(1)} %hidden.9.share_ref), channel_id=1, source_target_pairs={{0,2},{1,3},{2,0},{3,1},{4,6},{5,7},{6,4},{7,5},{8,10},{9,11},{10,... | collective-permute-start | bytes 688136 | tf_op jit(solution)/shard_map/ppermute | solution.py:23
  75.8 1.6 %collective-permute-start.27 = (bf16[64,1792]{1,0:T(8,128)(2,1)S(1)}, bf16[64,1792]{1,0:T(8,128)(2,1)S(1)}, u32[]{:S(2)}, u32[]{:S(2)}) collective-permute-start(bf16[64,1792]{1,0:T(8,128)(2,1)S(1)} %get-tuple-element.220), channel_id=1, source_target_pairs={{0,1},{1,0},{2,3},{3,2},{4,5},{5,4},{6,7},{7,6},{8,9},{9,8},{10,11... | collective-permute-start | bytes 688136 | tf_op jit(solution)/shard_map/ppermute | solution.py:23
  75.8 1.8 %collective-permute-start.28 = (bf16[64,1792]{1,0:T(8,128)(2,1)S(1)}, bf16[64,1792]{1,0:T(8,128)(2,1)S(1)}, u32[]{:S(2)}, u32[]{:S(2)}) collective-permute-start(bf16[64,1792]{1,0:T(8,128)(2,1)S(1)} %get-tuple-element.221), channel_id=1, source_target_pairs={{0,1},{1,0},{2,3},{3,2},{4,5},{5,4},{6,7},{7,6},{8,9},{9,8},{10,11... | collective-permute-start | bytes 688136 | tf_op jit(solution)/shard_map/ppermute | solution.py:23
  76.3 10.0 %collective-permute-start.30 = (bf16[48,3584]{1,0:T(8,128)(2,1)S(1)}, bf16[48,3584]{1,0:T(8,128)(2,1)S(1)}, u32[]{:S(2)}, u32[]{:S(2)}) collective-permute-start(bf16[48,3584]{1,0:T(8,128)(2,1)S(1)} %stack.1), channel_id=1, source_target_pairs={{0,2},{1,3},{2,0},{3,1},{4,6},{5,7},{6,4},{7,5},{8,10},{9,11},{10,... | collective-permute-start | bytes 1032200 | tf_op jit(solution)/shard_map/ppermute | solution.py:23
  80.0 8.6 %collective-permute-start.32 = (bf16[64,2048]{1,0:T(8,128)(2,1)S(1)}, bf16[64,2048]{1,0:T(8,128)(2,1)S(1)}, u32[]{:S(2)}, u32[]{:S(2)}) collective-permute-start(bf16[64,2048]{1,0:T(8,128)(2,1)S(1)} %get-tuple-element.229), channel_id=1, source_target_pairs={{0,4},{4,0},{8,12},{12,8},{1,5},{5,1},{9,13},{13,9},{2,6},{6,2},{1... | collective-permute-start | bytes 786440 | tf_op jit(solution)/shard_map/ppermute | solution.py:23
  86.5 6.1 %collective-permute-start.31 = (bf16[16,3584]{1,0:T(8,128)(2,1)S(1)}, bf16[16,3584]{1,0:T(8,128)(2,1)S(1)}, u32[]{:S(2)}, u32[]{:S(2)}) collective-permute-start(bf16[16,3584]{1,0:T(8,128)(2,1)S(1)} %get-tuple-element.228.share_ref), channel_id=1, source_target_pairs={{0,2},{1,3},{2,0},{3,1},{4,6},{5,7},{6,4},{7,5},{8,10},{9,11},{10,... | collective-permute-start | bytes 344072 | tf_op jit(solution)/shard_map/ppermute | solution.py:23
  87.0 10.8 %collective-permute-start.29 = (bf16[32,3584]{1,0:T(8,128)(2,1)S(1)}, bf16[32,3584]{1,0:T(8,128)(2,1)S(1)}, u32[]{:S(2)}, u32[]{:S(2)}) collective-permute-start(bf16[32,3584]{1,0:T(8,128)(2,1)S(1)} %get-tuple-element.225), channel_id=1, source_target_pairs={{0,2},{1,3},{2,0},{3,1},{4,6},{5,7},{6,4},{7,5},{8,10},{9,11},{10,... | collective-permute-start | bytes 688136 | tf_op jit(solution)/shard_map/ppermute | solution.py:23
  88.6 14.5 %collective-permute-start.36 = (bf16[64,2048]{1,0:T(8,128)(2,1)S(1)}, bf16[64,2048]{1,0:T(8,128)(2,1)S(1)}, u32[]{:S(2)}, u32[]{:S(2)}) collective-permute-start(bf16[64,2048]{1,0:T(8,128)(2,1)S(1)} %add.26), channel_id=1, source_target_pairs={{0,8},{4,12},{8,0},{12,4},{1,9},{5,13},{9,1},{13,5},{2,10},{6,14},... | collective-permute-start | bytes 786440 | tf_op jit(solution)/shard_map/ppermute | solution.py:23
  92.7 1.4 %collective-permute-start.33 = (bf16[32,1792]{1,0:T(8,128)(2,1)S(1)}, bf16[32,1792]{1,0:T(8,128)(2,1)S(1)}, u32[]{:S(2)}, u32[]{:S(2)}) collective-permute-start(bf16[32,1792]{1,0:T(8,128)(2,1)S(1)} %get-tuple-element.232), channel_id=1, source_target_pairs={{0,1},{1,0},{2,3},{3,2},{4,5},{5,4},{6,7},{7,6},{8,9},{9,8},{10,11... | collective-permute-start | bytes 344072 | tf_op jit(solution)/shard_map/ppermute | solution.py:23
  92.8 1.5 %collective-permute-start.34 = (bf16[32,1792]{1,0:T(8,128)(2,1)S(1)}, bf16[32,1792]{1,0:T(8,128)(2,1)S(1)}, u32[]{:S(2)}, u32[]{:S(2)}) collective-permute-start(bf16[32,1792]{1,0:T(8,128)(2,1)S(1)} %get-tuple-element.233), channel_id=1, source_target_pairs={{0,1},{1,0},{2,3},{3,2},{4,5},{5,4},{6,7},{7,6},{8,9},{9,8},{10,11... | collective-permute-start | bytes 344072 | tf_op jit(solution)/shard_map/ppermute | solution.py:23
  96.3 12.0 %collective-permute-start.42 = (bf16[64,2048]{1,0:T(8,128)(2,1)S(1)}, bf16[64,2048]{1,0:T(8,128)(2,1)S(1)}, u32[]{:S(2)}, u32[]{:S(2)}) collective-permute-start(bf16[64,2048]{1,0:T(8,128)(2,1)S(1)} %down.9), channel_id=1, source_target_pairs={{0,4},{4,0},{8,12},{12,8},{1,5},{5,1},{9,13},{13,9},{2,6},{6,2},{1... | collective-permute-start | bytes 786440 | tf_op jit(solution)/shard_map/ppermute | solution.py:23
  97.3 1.4 %collective-permute-start.37 = (bf16[32,1792]{1,0:T(8,128)(2,1)S(1)}, bf16[32,1792]{1,0:T(8,128)(2,1)S(1)}, u32[]{:S(2)}, u32[]{:S(2)}) collective-permute-start(bf16[32,1792]{1,0:T(8,128)(2,1)S(1)} %get-tuple-element.238), channel_id=1, source_target_pairs={{0,1},{1,0},{2,3},{3,2},{4,5},{5,4},{6,7},{7,6},{8,9},{9,8},{10,11... | collective-permute-start | bytes 344072 | tf_op jit(solution)/shard_map/ppermute | solution.py:23
  97.4 1.4 %collective-permute-start.38 = (bf16[32,1792]{1,0:T(8,128)(2,1)S(1)}, bf16[32,1792]{1,0:T(8,128)(2,1)S(1)}, u32[]{:S(2)}, u32[]{:S(2)}) collective-permute-start(bf16[32,1792]{1,0:T(8,128)(2,1)S(1)} %get-tuple-element.239), channel_id=1, source_target_pairs={{0,1},{1,0},{2,3},{3,2},{4,5},{5,4},{6,7},{7,6},{8,9},{9,8},{10,11... | collective-permute-start | bytes 344072 | tf_op jit(solution)/shard_map/ppermute | solution.py:23
  97.9 5.2 %collective-permute-start.35 = (bf16[16,3584]{1,0:T(8,128)(2,1)S(1)}, bf16[16,3584]{1,0:T(8,128)(2,1)S(1)}, u32[]{:S(2)}, u32[]{:S(2)}) collective-permute-start(bf16[16,3584]{1,0:T(8,128)(2,1)S(1)} %hidden.11.share_ref), channel_id=1, source_target_pairs={{0,2},{1,3},{2,0},{3,1},{4,6},{5,7},{6,4},{7,5},{8,10},{9,11},{10,... | collective-permute-start | bytes 344072 | tf_op jit(solution)/shard_map/ppermute | solution.py:23
  103.2 1.7 %collective-permute-start.40 = (bf16[32,1792]{1,0:T(8,128)(2,1)S(1)}, bf16[32,1792]{1,0:T(8,128)(2,1)S(1)}, u32[]{:S(2)}, u32[]{:S(2)}) collective-permute-start(bf16[32,1792]{1,0:T(8,128)(2,1)S(1)} %get-tuple-element.245), channel_id=1, source_target_pairs={{0,1},{1,0},{2,3},{3,2},{4,5},{5,4},{6,7},{7,6},{8,9},{9,8},{10,11... | collective-permute-start | bytes 344072 | tf_op jit(solution)/shard_map/ppermute | solution.py:23
  103.3 1.7 %collective-permute-start.41 = (bf16[32,1792]{1,0:T(8,128)(2,1)S(1)}, bf16[32,1792]{1,0:T(8,128)(2,1)S(1)}, u32[]{:S(2)}, u32[]{:S(2)}) collective-permute-start(bf16[32,1792]{1,0:T(8,128)(2,1)S(1)} %get-tuple-element.246), channel_id=1, source_target_pairs={{0,1},{1,0},{2,3},{3,2},{4,5},{5,4},{6,7},{7,6},{8,9},{9,8},{10,11... | collective-permute-start | bytes 344072 | tf_op jit(solution)/shard_map/ppermute | solution.py:23
  103.8 12.2 %collective-permute-start.39 = (bf16[64,2048]{1,0:T(8,128)(2,1)S(1)}, bf16[64,2048]{1,0:T(8,128)(2,1)S(1)}, u32[]{:S(2)}, u32[]{:S(2)}) collective-permute-start(bf16[64,2048]{1,0:T(8,128)(2,1)S(1)} %down.10), channel_id=1, source_target_pairs={{0,4},{4,0},{8,12},{12,8},{1,5},{5,1},{9,13},{13,9},{2,6},{6,2},{1... | collective-permute-start | bytes 786440 | tf_op jit(solution)/shard_map/ppermute | solution.py:23
  108.3 14.8 %collective-permute-start.43 = (bf16[64,2048]{1,0:T(8,128)(2,1)S(1)}, bf16[64,2048]{1,0:T(8,128)(2,1)S(1)}, u32[]{:S(2)}, u32[]{:S(2)}) collective-permute-start(bf16[64,2048]{1,0:T(8,128)(2,1)S(1)} %add.27), channel_id=1, source_target_pairs={{0,8},{4,12},{8,0},{12,4},{1,9},{5,13},{9,1},{13,5},{2,10},{6,14},... | collective-permute-start | bytes 786440 | tf_op jit(solution)/shard_map/ppermute | solution.py:23
  123.3 4.5 %collective-permute-start.44 = (f32[1,2048]{1,0:T(1,128)S(1)}, f32[1,2048]{1,0:T(1,128)S(1)}, u32[]{:S(2)}, u32[]{:S(2)}) collective-permute-start(f32[1,2048]{1,0:T(1,128)S(1)} %bitcast.6), channel_id=1, source_target_pairs={{0,4},{4,0},{8,12},{12,8},{1,5},{5,1},{9,13},{13,9},{2,6},{6,2},{1... | collective-permute-start | bytes 24584 | tf_op jit(solution)/shard_map/ppermute | solution.py:23
  123.4 4.7 %collective-permute-start.45 = (f32[1,2048]{1,0:T(1,128)S(1)}, f32[1,2048]{1,0:T(1,128)S(1)}, u32[]{:S(2)}, u32[]{:S(2)}) collective-permute-start(f32[1,2048]{1,0:T(1,128)S(1)} %bitcast.7), channel_id=1, source_target_pairs={{0,8},{4,12},{8,0},{12,4},{1,9},{5,13},{9,1},{13,5},{2,10},{6,14},... | collective-permute-start | bytes 24584 | tf_op jit(solution)/shard_map/ppermute | solution.py:23
  126.4 5.4 %collective-permute-start.46 = (f32[1,2048]{1,0:T(1,128)S(1)}, f32[1,2048]{1,0:T(1,128)S(1)}, u32[]{:S(2)}, u32[]{:S(2)}) collective-permute-start(f32[1,2048]{1,0:T(1,128)S(1)} %bitcast.8), channel_id=1, source_target_pairs={{0,12},{4,8},{8,4},{12,0},{1,13},{5,9},{9,5},{13,1},{2,14},{6,10},... | collective-permute-start | bytes 24584 | tf_op jit(solution)/shard_map/ppermute | solution.py:23
  (9 other events, 60.0 us)

commit v4 on v3

--- a/solution.py
+++ b/solution.py
@@ -420,7 +420,7 @@
         jnp.max(jnp.abs(first), axis=0, keepdims=True),
         jnp.max(jnp.abs(second), axis=0, keepdims=True),
     )
-    peaks = [swap(local_peak, AXIS, k) for k in range(1, RANKS)]
+    peaks = [swap(local_peak, AXIS, k) for k in range(RANKS - 1, 0, -1)]
     scaled, scales = call(
         scale_kernel,
         (array(*tokens.shape), array(1, tokens.shape[1], jnp.float32)),

time: 133 us -> 131 us (0.985)
  waiting for transfers between devices: 56.7 us -> 55.2 us
    ppermute x47, waiting for transfers between devices: 56.7 us -> 55.2 us  [swap(): return lax.ppermute(value, axis, [(i, i ^ mask) for i in range(size)])]
where the time goes in v4:
time: 131 us
  waiting for transfers between devices  55.2 us (42%)
  starting transfers between devices  37.4 us (29%)
  Pallas kernels  32.9 us (25%)
  local copies, waits for them, and re-layouts  4.53 us (3%)
    ppermute x47, waiting for transfers between devices, swap(): return lax.ppermute(value, axis, [(i, i ^ mask) for i in range(size)])  55.2 us
    ppermute x47, starting transfers between devices, swap(): return lax.ppermute(value, axis, [(i, i ^ mask) for i in range(size)])  37.4 us
    pallas_call x40, Pallas kernels, call(): pl.pallas_call(kernel, out_shape=shapes, in_specs=[VMEM] * len(args), out...  32.9 us
    unnamed x20, local copies, waits for them, and re-layouts  4.53 us
  transfers between devices with their start and end apart: 47, of which 29 were waited for; matrix products, arithmetic and copies ran while one was open for 0% of the time, Pallas kernels for 24%

profile of v4, /device:TPU:0, one launch (start us, length us, event | category | flops | bytes accessed | tf_op | source)
XLA Modules:
  0.0 131.3 jit_solution(8047286322134488283)
XLA Ops:
  0.7 3.1 %collective-permute-start = (bf16[128,2048]{1,0:T(8,128)(2,1)}, bf16[128,2048]{1,0:T(8,128)(2,1)S(1)}, u32[]{:S(2)}, u32[]{:S(2)}) collective-permute-start(bf16[128,2048]{1,0:T(8,128)(2,1)} %tokens_ref.1), channel_id=1, source_target_pairs={{0,4},{4,0},{8,12},{12,8},{1,5},{5,1},{9,13},{13,9},{2,6},{6,2},{1... | collective-permute-start | bytes 1572872 | tf_op jit(solution)/shard_map/ppermute | solution.py:23
  3.8 1.8 %copy-done.1 = bf16[128,2048]{1,0:T(8,128)(2,1)S(1)} copy-done((bf16[128,2048]{1,0:T(8,128)(2,1)S(1)}, bf16[128,2048]{1,0:T(8,128)(2,1)}, u32[]{:S(2)}) %copy-start.1) | copy-done | bytes 524312
  6.0 2.1 %gate.4 = (bf16[64,7168]{1,0:T(8,128)(2,1)S(1)}, bf16[64,2304]{1,0:T(8,128)(2,1)S(1)}, bf16[64,2432]{1,0:T(8,128)(2,1)S(1)}, bf16[64,2432]{1,0:T(8,128)(2,1)S(1)}) custom-call(bf16[128,2048]{1,0:T(8,128)(2,1)S(1)} %arrange.2.refs_0_.block_ref, bf16[2048,3584]{1,0:T(8,128)(2,1)S(1)} %copy-done), custom_call_target="tpu_custom_call" | custom-call | flops 3758096384 | bytes 14680064 | tf_op jit(solution)/shard_map/gate/pallas_call | solution.py:48
  8.4 1.2 slice-done.6
  9.5 0.8 slice-done.7
  10.4 2.2 %up.4 = (bf16[64,7168]{1,0:T(8,128)(2,1)S(1)}, bf16[64,2304]{1,0:T(8,128)(2,1)S(1)}, bf16[64,2432]{1,0:T(8,128)(2,1)S(1)}, bf16[64,2432]{1,0:T(8,128)(2,1)S(1)}) custom-call(bf16[128,2048]{1,0:T(8,128)(2,1)S(1)} %arrange.2.refs_0_.block_ref, bf16[2048,3584]{1,0:T(8,128)(2,1)S(1)} %bitcast.5, ...), custom_call_target="tpu_custom_call", output_to_operand_aliasing={{0}: (2, {}), {1}: (3, {}), {2}: (4, {}), {3}: (5, {})} | custom-call | flops 1 | bytes 1 | tf_op jit(solution)/shard_map/up/pallas_call | solution.py:48
  13.7 3.7 %collective-permute-start.4 = (bf16[64,2048]{1,0:T(8,128)(2,1)S(1)}, bf16[64,2048]{1,0:T(8,128)(2,1)S(1)}, u32[]{:S(2)}, u32[]{:S(2)}) collective-permute-start(bf16[64,2048]{1,0:T(8,128)(2,1)S(1)} %get-tuple-element.146), channel_id=1, source_target_pairs={{0,8},{4,12},{8,0},{12,4},{1,9},{5,13},{9,1},{13,5},{2,10},{6,14},... | collective-permute-start | bytes 786440 | tf_op jit(solution)/shard_map/ppermute | solution.py:23
  17.6 1.5 %collective-permute-start.7 = (bf16[64,3584]{1,0:T(8,128)(2,1)S(1)}, bf16[64,3584]{1,0:T(8,128)(2,1)S(1)}, u32[]{:S(2)}, u32[]{:S(2)}) collective-permute-start(bf16[64,3584]{1,0:T(8,128)(2,1)S(1)} %get-tuple-element.157), channel_id=1, source_target_pairs={{0,2},{1,3},{2,0},{3,1},{4,6},{5,7},{6,4},{7,5},{8,10},{9,11},{10,... | collective-permute-start | bytes 1376264 | tf_op jit(solution)/shard_map/ppermute | solution.py:23
  19.2 2.1 %gate.5 = (bf16[64,7168]{1,0:T(8,128)(2,1)S(1)}, bf16[32,4736]{1,0:T(8,128)(2,1)S(1)}, bf16[32,2432]{1,0:T(8,128)(2,1)S(1)}, bf16[32,3584]{1,0:T(8,128)(2,1)S(1)}, bf16[32,3584]{1,0:T(8,128)(2,1)S(1)}) custom-call(bf16[128,2048]{1,0:T(8,128)(2,1)S(1)} %arrange.3.refs_0_, bf16[2048,3584]{1,0:T(8,128)(2,1)S(1)} %copy-done), custom_call_target="tpu_custom_call" | custom-call | flops 1 | bytes 1 | tf_op jit(solution)/shard_map/gate/pallas_call | solution.py:48
  21.3 2.2 %up.5 = (bf16[64,7168]{1,0:T(8,128)(2,1)S(1)}, bf16[32,4736]{1,0:T(8,128)(2,1)S(1)}, bf16[32,2432]{1,0:T(8,128)(2,1)S(1)}, bf16[32,3584]{1,0:T(8,128)(2,1)S(1)}, bf16[32,3584]{1,0:T(8,128)(2,1)S(1)}) custom-call(bf16[128,2048]{1,0:T(8,128)(2,1)S(1)} %arrange.3.refs_0_, ...), custom_call_target="tpu_custom_call", output_to_operand_aliasing={{0}: (2, {}), {1}: (3, {}), {2}: (4, {}), {3}: (5, {}), {4}... | custom-call | flops 1 | bytes 1 | tf_op jit(solution)/shard_map/up/pallas_call | solution.py:48
  23.5 6.4 %collective-permute-done.4.refs_0_ = bf16[64,2048]{1,0:T(8,128)(2,1)S(1)} collective-permute-done((bf16[64,2048]{1,0:T(8,128)(2,1)S(1)}, bf16[64,2048]{1,0:T(8,128)(2,1)S(1)}, u32[]{:S(2)}, u32[]{:S(2)}) %collective-permute-start.4) | collective-permute-done | bytes 262176 | tf_op jit(solution)/shard_map/ppermute | solution.py:23
  30.4 1.3 collective-permute-done.6.refs_2_
  32.0 1.6 %collective-permute-start.8 = (bf16[64,3584]{1,0:T(8,128)(2,1)S(1)}, bf16[64,3584]{1,0:T(8,128)(2,1)S(1)}, u32[]{:S(2)}, u32[]{:S(2)}) collective-permute-start(bf16[64,3584]{1,0:T(8,128)(2,1)S(1)} %get-tuple-element.160), channel_id=1, source_target_pairs={{0,2},{1,3},{2,0},{3,1},{4,6},{5,7},{6,4},{7,5},{8,10},{9,11},{10,... | collective-permute-start | bytes 1376264 | tf_op jit(solution)/shard_map/ppermute | solution.py:23
  34.4 3.4 %collective-permute-start.13 = (bf16[64,2048]{1,0:T(8,128)(2,1)S(1)}, bf16[64,2048]{1,0:T(8,128)(2,1)S(1)}, u32[]{:S(2)}, u32[]{:S(2)}) collective-permute-start(bf16[64,2048]{1,0:T(8,128)(2,1)S(1)} %get-tuple-element.179), channel_id=1, source_target_pairs={{0,8},{4,12},{8,0},{12,4},{1,9},{5,13},{9,1},{13,5},{2,10},{6,14},... | collective-permute-start | bytes 786440 | tf_op jit(solution)/shard_map/ppermute | solution.py:23
  38.2 1.0 collective-permute-done.10.refs_2_
  39.6 5.0 %collective-permute-done.8.refs_1_ = bf16[64,3584]{1,0:T(8,128)(2,1)S(1)} collective-permute-done((bf16[64,3584]{1,0:T(8,128)(2,1)S(1)}, bf16[64,3584]{1,0:T(8,128)(2,1)S(1)}, u32[]{:S(2)}, u32[]{:S(2)}) %collective-permute-start.8) | collective-permute-done | bytes 458784 | tf_op jit(solution)/shard_map/ppermute | solution.py:23
  44.8 1.6 %collective-permute-start.19 = (bf16[48,3584]{1,0:T(8,128)(2,1)S(1)}, bf16[48,3584]{1,0:T(8,128)(2,1)S(1)}, u32[]{:S(2)}, u32[]{:S(2)}) collective-permute-start(bf16[48,3584]{1,0:T(8,128)(2,1)S(1)} %get-tuple-element.191), channel_id=1, source_target_pairs={{0,2},{1,3},{2,0},{3,1},{4,6},{5,7},{6,4},{7,5},{8,10},{9,11},{10,... | collective-permute-start | bytes 1032200 | tf_op jit(solution)/shard_map/ppermute | solution.py:23
  47.1 2.1 %gate.6 = (bf16[64,7168]{1,0:T(8,128)(2,1)S(1)}, bf16[64,2304]{1,0:T(8,128)(2,1)S(1)}, bf16[64,2432]{1,0:T(8,128)(2,1)S(1)}, bf16[64,2432]{1,0:T(8,128)(2,1)S(1)}) custom-call(bf16[64,2048]{1,0:T(8,128)(2,1)S(1)} %collective-permute-done.4.refs_0_, bf16[64,2048]{1,0:T(8,128)(2,1)S(1)} %collective-permute-done.12.refs_1_, bf16[2048,3584]{1,0:T(8,128)(2,1)S(1)} %copy-done), custom_call_target="tpu_custom_call" | custom-call | flops 1 | bytes 1 | tf_op jit(solution)/shard_map/gate/pallas_call | solution.py:48
  49.2 2.4 %up.6 = (bf16[64,7168]{1,0:T(8,128)(2,1)S(1)}, bf16[64,2304]{1,0:T(8,128)(2,1)S(1)}, bf16[64,2432]{1,0:T(8,128)(2,1)S(1)}, bf16[64,2432]{1,0:T(8,128)(2,1)S(1)}) custom-call(bf16[64,2048]{1,0:T(8,128)(2,1)S(1)} %collective-permute-done.4.refs_0_, ...), custom_call_target="tpu_custom_call", output_to_operand_aliasing={{0}: (3, {}), {1}: (4, {}), {2}: (5, {}), {3}: (6, {})} | custom-call | flops 1 | bytes 1 | tf_op jit(solution)/shard_map/up/pallas_call | solution.py:48
  52.3 1.9 %collective-permute-done.14.refs_1_ = bf16[64,2304]{1,0:T(8,128)(2,1)S(1)} collective-permute-done((bf16[64,2304]{1,0:T(8,128)(2,1)S(1)}, bf16[64,2304]{1,0:T(8,128)(2,1)S(1)}, u32[]{:S(2)}, u32[]{:S(2)}) %collective-permute-start.14) | collective-permute-done | bytes 294944 | tf_op jit(solution)/shard_map/ppermute | solution.py:23
  55.7 0.8 collective-permute-done.20.refs_0_
  56.7 2.1 %down.6 = bf16[64,2048]{1,0:T(8,128)(2,1)S(1)} custom-call(bf16[32,3584]{1,0:T(8,128)(2,1)S(1)} %get-tuple-element.194.mine_ref, bf16[32,1792]{1,0:T(8,128)(2,1)S(1)} %collective-permute-done.20.refs_0_, bf16[32,1792]{1,0:T(8,128)(2,1)S(1)} %collective-permute-done.21.refs_1_, bf16[3584,2048]{1,0:T(8,128)(2,1)S(1)} %bitcast.3), custom_call_target="tpu_custom_call" | custom-call | flops 1 | bytes 1 | tf_op jit(solution)/shard_map/down/pallas_call | solution.py:48
  58.8 2.2 %collective-permute-done.18.refs_1_ = bf16[64,2048]{1,0:T(8,128)(2,1)S(1)} collective-permute-done((bf16[64,2048]{1,0:T(8,128)(2,1)S(1)}, bf16[64,2048]{1,0:T(8,128)(2,1)S(1)}, u32[]{:S(2)}, u32[]{:S(2)}) %collective-permute-start.18) | collective-permute-done | bytes 262176 | tf_op jit(solution)/shard_map/ppermute | solution.py:23
  61.0 2.1 %gate.7 = (bf16[64,7168]{1,0:T(8,128)(2,1)S(1)}, bf16[64,2304]{1,0:T(8,128)(2,1)S(1)}, bf16[64,2432]{1,0:T(8,128)(2,1)S(1)}, bf16[64,2432]{1,0:T(8,128)(2,1)S(1)}) custom-call(bf16[64,2048]{1,0:T(8,128)(2,1)S(1)} %collective-permute-done.13.refs_0_, bf16[64,2048]{1,0:T(8,128)(2,1)S(1)} %collective-permute-done.18.refs_1_, bf16[2048,3584]{1,0:T(8,128)(2,1)S(1)} %copy-done), custom_call_target="tpu_custom_call" | custom-call | flops 1 | bytes 1 | tf_op jit(solution)/shard_map/gate/pallas_call | solution.py:48
  63.0 2.2 %up.7 = (bf16[64,7168]{1,0:T(8,128)(2,1)S(1)}, bf16[64,2304]{1,0:T(8,128)(2,1)S(1)}, bf16[64,2432]{1,0:T(8,128)(2,1)S(1)}, bf16[64,2432]{1,0:T(8,128)(2,1)S(1)}) custom-call(bf16[64,2048]{1,0:T(8,128)(2,1)S(1)} %collective-permute-done.13.refs_0_, ...), custom_call_target="tpu_custom_call", output_to_operand_aliasing={{0}: (3, {}), {1}: (4, {}), {2}: (5, {}), {3}: (6, {})} | custom-call | flops 1 | bytes 1 | tf_op jit(solution)/shard_map/up/pallas_call | solution.py:48
  68.8 2.1 %down.7 = (f32[64,2048]{1,0:T(8,128)S(1)}, f32[64,2048]{1,0:T(8,128)S(1)}) custom-call(bf16[64,3584]{1,0:T(8,128)(2,1)S(1)} %get-tuple-element.171.mine_ref, bf16[64,3584]{1,0:T(8,128)(2,1)S(1)} %collective-permute-done.11.refs_0_, bf16[3584,2048]{1,0:T(8,128)(2,1)S(1)} %bitcast.3), custom_call_target="tpu_custom_call" | custom-call | flops 1 | bytes 1 | tf_op jit(solution)/shard_map/down/pallas_call | solution.py:48
  70.9 4.4 %collective-permute-done.26 = bf16[64,2048]{1,0:T(8,128)(2,1)S(1)} collective-permute-done((bf16[64,2048]{1,0:T(8,128)(2,1)S(1)}, bf16[64,2048]{1,0:T(8,128)(2,1)S(1)}, u32[]{:S(2)}, u32[]{:S(2)}) %collective-permute-start.26) | collective-permute-done | bytes 262176 | tf_op jit(solution)/shard_map/ppermute | solution.py:23
  77.7 2.3 %down.8 = (f32[64,2048]{1,0:T(8,128)S(1)}, bf16[64,2048]{1,0:T(8,128)(2,1)S(1)}) custom-call(bf16[64,3584]{1,0:T(8,128)(2,1)S(1)} %join.3.mine_ref, bf16[64,1792]{1,0:T(8,128)(2,1)S(1)} %collective-permute-done.27.refs_0_, bf16[64,1792]{1,0:T(8,128)(2,1)S(1)} %collective-permute-done.28.refs_1_, bf16[3584,2048]{1,0:T(8,128)(2,1)S(1)} %bitcast.3), custom_call_target="tpu_custom_call" | custom-call | flops 1 | bytes 1 | tf_op jit(solution)/shard_map/down/pallas_call | solution.py:48
  80.0 0.9 collective-permute-start.32
  80.9 5.5 %collective-permute-done.30.refs_1_ = bf16[48,3584]{1,0:T(8,128)(2,1)S(1)} collective-permute-done((bf16[48,3584]{1,0:T(8,128)(2,1)S(1)}, bf16[48,3584]{1,0:T(8,128)(2,1)S(1)}, u32[]{:S(2)}, u32[]{:S(2)}) %collective-permute-start.30) | collective-permute-done | bytes 344096 | tf_op jit(solution)/shard_map/ppermute | solution.py:23
  87.0 1.5 %collective-permute-start.29 = (bf16[32,3584]{1,0:T(8,128)(2,1)S(1)}, bf16[32,3584]{1,0:T(8,128)(2,1)S(1)}, u32[]{:S(2)}, u32[]{:S(2)}) collective-permute-start(bf16[32,3584]{1,0:T(8,128)(2,1)S(1)} %get-tuple-element.225), channel_id=1, source_target_pairs={{0,2},{1,3},{2,0},{3,1},{4,6},{5,7},{6,4},{7,5},{8,10},{9,11},{10,... | collective-permute-start | bytes 688136 | tf_op jit(solution)/shard_map/ppermute | solution.py:23
  88.6 2.2 %collective-permute-start.36 = (bf16[64,2048]{1,0:T(8,128)(2,1)S(1)}, bf16[64,2048]{1,0:T(8,128)(2,1)S(1)}, u32[]{:S(2)}, u32[]{:S(2)}) collective-permute-start(bf16[64,2048]{1,0:T(8,128)(2,1)S(1)} %add.26), channel_id=1, source_target_pairs={{0,8},{4,12},{8,0},{12,4},{1,9},{5,13},{9,1},{13,5},{2,10},{6,14},... | collective-permute-start | bytes 786440 | tf_op jit(solution)/shard_map/ppermute | solution.py:23
  90.9 1.8 %collective-permute-done.31.got_ref = bf16[16,3584]{1,0:T(8,128)(2,1)S(1)} collective-permute-done((bf16[16,3584]{1,0:T(8,128)(2,1)S(1)}, bf16[16,3584]{1,0:T(8,128)(2,1)S(1)}, u32[]{:S(2)}, u32[]{:S(2)}) %collective-permute-start.31) | collective-permute-done | bytes 114720 | tf_op jit(solution)/shard_map/ppermute | solution.py:23
  94.2 2.1 %down.9 = bf16[64,2048]{1,0:T(8,128)(2,1)S(1)} custom-call(bf16[32,3584]{1,0:T(8,128)(2,1)S(1)} %join.4.mine_ref, bf16[32,1792]{1,0:T(8,128)(2,1)S(1)} %collective-permute-done.33.refs_0_, bf16[32,1792]{1,0:T(8,128)(2,1)S(1)} %collective-permute-done.34.refs_1_, bf16[3584,2048]{1,0:T(8,128)(2,1)S(1)} %bitcast.3), custom_call_target="tpu_custom_call" | custom-call | flops 1 | bytes 1 | tf_op jit(solution)/shard_map/down/pallas_call | solution.py:48
  96.3 0.9 collective-permute-start.42
  98.8 2.1 %down.10 = bf16[64,2048]{1,0:T(8,128)(2,1)S(1)} custom-call(bf16[32,3584]{1,0:T(8,128)(2,1)S(1)} %get-tuple-element.237.mine_ref, bf16[32,1792]{1,0:T(8,128)(2,1)S(1)} %collective-permute-done.37.refs_0_, bf16[32,1792]{1,0:T(8,128)(2,1)S(1)} %collective-permute-done.38.refs_1_, bf16[3584,2048]{1,0:T(8,128)(2,1)S(1)} %bitcast.3), custom_call_target="tpu_custom_call" | custom-call | flops 1 | bytes 1 | tf_op jit(solution)/shard_map/down/pallas_call | solution.py:48
  100.9 2.2 %collective-permute-done.35.got_ref = bf16[16,3584]{1,0:T(8,128)(2,1)S(1)} collective-permute-done((bf16[16,3584]{1,0:T(8,128)(2,1)S(1)}, bf16[16,3584]{1,0:T(8,128)(2,1)S(1)}, u32[]{:S(2)}, u32[]{:S(2)}) %collective-permute-start.35) | collective-permute-done | bytes 114720 | tf_op jit(solution)/shard_map/ppermute | solution.py:23
  103.8 1.2 collective-permute-start.39
  104.9 2.1 %down.11.part_ref = f32[64,2048]{1,0:T(8,128)S(1)} custom-call(bf16[32,3584]{1,0:T(8,128)(2,1)S(1)} %join.5.mine_ref, bf16[32,1792]{1,0:T(8,128)(2,1)S(1)} %collective-permute-done.40.refs_0_, bf16[32,1792]{1,0:T(8,128)(2,1)S(1)} %collective-permute-done.41.refs_1_, bf16[3584,2048]{1,0:T(8,128)(2,1)S(1)} %bitcast.3), custom_call_target="tpu_custom_call" | custom-call | flops 1 | bytes 1 | tf_op jit(solution)/shard_map/down/pallas_call | solution.py:48
  107.0 1.3 collective-permute-done.42.got_ref
  108.3 1.1 collective-permute-start.43
  109.5 6.4 %collective-permute-done.39 = bf16[64,2048]{1,0:T(8,128)(2,1)S(1)} collective-permute-done((bf16[64,2048]{1,0:T(8,128)(2,1)S(1)}, bf16[64,2048]{1,0:T(8,128)(2,1)S(1)}, u32[]{:S(2)}, u32[]{:S(2)}) %collective-permute-start.39) | collective-permute-done | bytes 262176 | tf_op jit(solution)/shard_map/ppermute | solution.py:23
  116.0 7.2 %collective-permute-done.43 = bf16[64,2048]{1,0:T(8,128)(2,1)S(1)} collective-permute-done((bf16[64,2048]{1,0:T(8,128)(2,1)S(1)}, bf16[64,2048]{1,0:T(8,128)(2,1)S(1)}, u32[]{:S(2)}, u32[]{:S(2)}) %collective-permute-start.43) | collective-permute-done | bytes 262176 | tf_op jit(solution)/shard_map/ppermute | solution.py:23
  123.3 2.6 %collective-permute-start.44 = (f32[1,2048]{1,0:T(1,128)S(1)}, f32[1,2048]{1,0:T(1,128)S(1)}, u32[]{:S(2)}, u32[]{:S(2)}) collective-permute-start(f32[1,2048]{1,0:T(1,128)S(1)} %bitcast.6), channel_id=1, source_target_pairs={{0,12},{4,8},{8,4},{12,0},{1,13},{5,9},{9,5},{13,1},{2,14},{6,10},... | collective-permute-start | bytes 24584 | tf_op jit(solution)/shard_map/ppermute | solution.py:23
  125.9 1.9 %collective-permute-start.46 = (f32[1,2048]{1,0:T(1,128)S(1)}, f32[1,2048]{1,0:T(1,128)S(1)}, u32[]{:S(2)}, u32[]{:S(2)}) collective-permute-start(f32[1,2048]{1,0:T(1,128)S(1)} %bitcast.8), channel_id=1, source_target_pairs={{0,4},{4,0},{8,12},{12,8},{1,5},{5,1},{9,13},{13,9},{2,6},{6,2},{1... | collective-permute-start | bytes 24584 | tf_op jit(solution)/shard_map/ppermute | solution.py:23
  127.8 1.1 collective-permute-done.44.refs_1_
  128.9 1.5 %collective-permute-done.45.refs_2_ = f32[1,2048]{1,0:T(1,128)S(1)} collective-permute-done((f32[1,2048]{1,0:T(1,128)S(1)}, f32[1,2048]{1,0:T(1,128)S(1)}, u32[]{:S(2)}, u32[]{:S(2)}) %collective-permute-start.45) | collective-permute-done | bytes 8224 | tf_op jit(solution)/shard_map/ppermute | solution.py:23
  130.4 0.9 scale.1
  (111 shorter events, 18.1 us)
Async XLA Ops:
  0.7 18.5 %collective-permute-start = (bf16[128,2048]{1,0:T(8,128)(2,1)}, bf16[128,2048]{1,0:T(8,128)(2,1)S(1)}, u32[]{:S(2)}, u32[]{:S(2)}) collective-permute-start(bf16[128,2048]{1,0:T(8,128)(2,1)} %tokens_ref.1), channel_id=1, source_target_pairs={{0,4},{4,0},{8,12},{12,8},{1,5},{5,1},{9,13},{13,9},{2,6},{6,2},{1... | collective-permute-start | bytes 1572872 | tf_op jit(solution)/shard_map/ppermute | solution.py:23
  12.6 4.8 %collective-permute-start.2 = (bf16[64,2432]{1,0:T(8,128)(2,1)S(1)}, bf16[64,2432]{1,0:T(8,128)(2,1)S(1)}, u32[]{:S(2)}, u32[]{:S(2)}) collective-permute-start(bf16[64,2432]{1,0:T(8,128)(2,1)S(1)} %get-tuple-element.132), channel_id=1, source_target_pairs={{0,1},{1,0},{2,3},{3,2},{4,5},{5,4},{6,7},{7,6},{8,9},{9,8},{10,11... | collective-permute-start | bytes 933896 | tf_op jit(solution)/shard_map/ppermute | solution.py:23
  13.1 4.3 %collective-permute-start.3 = (bf16[64,2432]{1,0:T(8,128)(2,1)S(1)}, bf16[64,2432]{1,0:T(8,128)(2,1)S(1)}, u32[]{:S(2)}, u32[]{:S(2)}) collective-permute-start(bf16[64,2432]{1,0:T(8,128)(2,1)S(1)} %get-tuple-element.133), channel_id=1, source_target_pairs={{0,1},{1,0},{2,3},{3,2},{4,5},{5,4},{6,7},{7,6},{8,9},{9,8},{10,11... | collective-permute-start | bytes 933896 | tf_op jit(solution)/shard_map/ppermute | solution.py:23
  13.2 4.2 %collective-permute-start.1 = (bf16[64,2304]{1,0:T(8,128)(2,1)S(1)}, bf16[64,2304]{1,0:T(8,128)(2,1)S(1)}, u32[]{:S(2)}, u32[]{:S(2)}) collective-permute-start(bf16[64,2304]{1,0:T(8,128)(2,1)S(1)} %get-tuple-element.131), channel_id=1, source_target_pairs={{0,1},{1,0},{2,3},{3,2},{4,5},{5,4},{6,7},{7,6},{8,9},{9,8},{10,11... | collective-permute-start | bytes 884744 | tf_op jit(solution)/shard_map/ppermute | solution.py:23
  13.7 16.3 %collective-permute-start.4 = (bf16[64,2048]{1,0:T(8,128)(2,1)S(1)}, bf16[64,2048]{1,0:T(8,128)(2,1)S(1)}, u32[]{:S(2)}, u32[]{:S(2)}) collective-permute-start(bf16[64,2048]{1,0:T(8,128)(2,1)S(1)} %get-tuple-element.146), channel_id=1, source_target_pairs={{0,8},{4,12},{8,0},{12,4},{1,9},{5,13},{9,1},{13,5},{2,10},{6,14},... | collective-permute-start | bytes 786440 | tf_op jit(solution)/shard_map/ppermute | solution.py:23
  17.6 14.2 %collective-permute-start.7 = (bf16[64,3584]{1,0:T(8,128)(2,1)S(1)}, bf16[64,3584]{1,0:T(8,128)(2,1)S(1)}, u32[]{:S(2)}, u32[]{:S(2)}) collective-permute-start(bf16[64,3584]{1,0:T(8,128)(2,1)S(1)} %get-tuple-element.157), channel_id=1, source_target_pairs={{0,2},{1,3},{2,0},{3,1},{4,6},{5,7},{6,4},{7,5},{8,10},{9,11},{10,... | collective-permute-start | bytes 1376264 | tf_op jit(solution)/shard_map/ppermute | solution.py:23
  29.9 1.8 %collective-permute-start.5 = (bf16[32,4736]{1,0:T(8,128)(2,1)S(1)}, bf16[32,4736]{1,0:T(8,128)(2,1)S(1)}, u32[]{:S(2)}, u32[]{:S(2)}) collective-permute-start(bf16[32,4736]{1,0:T(8,128)(2,1)S(1)} %get-tuple-element.151), channel_id=1, source_target_pairs={{0,1},{1,0},{2,3},{3,2},{4,5},{5,4},{6,7},{7,6},{8,9},{9,8},{10,11... | collective-permute-start | bytes 909320 | tf_op jit(solution)/shard_map/ppermute | solution.py:23
  29.9 1.8 %collective-permute-start.6 = (bf16[32,2432]{1,0:T(8,128)(2,1)S(1)}, bf16[32,2432]{1,0:T(8,128)(2,1)S(1)}, u32[]{:S(2)}, u32[]{:S(2)}) collective-permute-start(bf16[32,2432]{1,0:T(8,128)(2,1)S(1)} %get-tuple-element.152), channel_id=1, source_target_pairs={{0,1},{1,0},{2,3},{3,2},{4,5},{5,4},{6,7},{7,6},{8,9},{9,8},{10,11... | collective-permute-start | bytes 466952 | tf_op jit(solution)/shard_map/ppermute | solution.py:23
  32.0 12.6 %collective-permute-start.8 = (bf16[64,3584]{1,0:T(8,128)(2,1)S(1)}, bf16[64,3584]{1,0:T(8,128)(2,1)S(1)}, u32[]{:S(2)}, u32[]{:S(2)}) collective-permute-start(bf16[64,3584]{1,0:T(8,128)(2,1)S(1)} %get-tuple-element.160), channel_id=1, source_target_pairs={{0,2},{1,3},{2,0},{3,1},{4,6},{5,7},{6,4},{7,5},{8,10},{9,11},{10,... | collective-permute-start | bytes 1376264 | tf_op jit(solution)/shard_map/ppermute | solution.py:23
  33.7 13.5 %collective-permute-start.12 = (bf16[64,2048]{1,0:T(8,128)(2,1)S(1)}, bf16[64,2048]{1,0:T(8,128)(2,1)S(1)}, u32[]{:S(2)}, u32[]{:S(2)}) collective-permute-start(bf16[64,2048]{1,0:T(8,128)(2,1)S(1)} %collective-permute-done.4.refs_0_), channel_id=1, source_target_pairs={{0,4},{4,0},{8,12},{12,8},{1,5},{5,1},{9,13},{13,9},{2,6},{6,2},{1... | collective-permute-start | bytes 786440 | tf_op jit(solution)/shard_map/ppermute | solution.py:23
  34.4 17.3 %collective-permute-start.13 = (bf16[64,2048]{1,0:T(8,128)(2,1)S(1)}, bf16[64,2048]{1,0:T(8,128)(2,1)S(1)}, u32[]{:S(2)}, u32[]{:S(2)}) collective-permute-start(bf16[64,2048]{1,0:T(8,128)(2,1)S(1)} %get-tuple-element.179), channel_id=1, source_target_pairs={{0,8},{4,12},{8,0},{12,4},{1,9},{5,13},{9,1},{13,5},{2,10},{6,14},... | collective-permute-start | bytes 786440 | tf_op jit(solution)/shard_map/ppermute | solution.py:23
  37.7 1.5 %collective-permute-start.10 = (bf16[32,3584]{1,0:T(8,128)(2,1)S(1)}, bf16[32,3584]{1,0:T(8,128)(2,1)S(1)}, u32[]{:S(2)}, u32[]{:S(2)}) collective-permute-start(bf16[32,3584]{1,0:T(8,128)(2,1)S(1)} %get-tuple-element.165), channel_id=1, source_target_pairs={{0,1},{1,0},{2,3},{3,2},{4,5},{5,4},{6,7},{7,6},{8,9},{9,8},{10,11... | collective-permute-start | bytes 688136 | tf_op jit(solution)/shard_map/ppermute | solution.py:23
  37.7 1.8 %collective-permute-start.9 = (bf16[32,3584]{1,0:T(8,128)(2,1)S(1)}, bf16[32,3584]{1,0:T(8,128)(2,1)S(1)}, u32[]{:S(2)}, u32[]{:S(2)}) collective-permute-start(bf16[32,3584]{1,0:T(8,128)(2,1)S(1)} %get-tuple-element.164), channel_id=1, source_target_pairs={{0,1},{1,0},{2,3},{3,2},{4,5},{5,4},{6,7},{7,6},{8,9},{9,8},{10,11... | collective-permute-start | bytes 688136 | tf_op jit(solution)/shard_map/ppermute | solution.py:23
  44.8 10.2 %collective-permute-start.19 = (bf16[48,3584]{1,0:T(8,128)(2,1)S(1)}, bf16[48,3584]{1,0:T(8,128)(2,1)S(1)}, u32[]{:S(2)}, u32[]{:S(2)}) collective-permute-start(bf16[48,3584]{1,0:T(8,128)(2,1)S(1)} %get-tuple-element.191), channel_id=1, source_target_pairs={{0,2},{1,3},{2,0},{3,1},{4,6},{5,7},{6,4},{7,5},{8,10},{9,11},{10,... | collective-permute-start | bytes 1032200 | tf_op jit(solution)/shard_map/ppermute | solution.py:23
  47.1 9.5 %slice-start.1 = ((s8[14680064]{0:T(1024)(128)(4,1)}), s8[4194304]{0:T(1024)(128)(4,1)S(1)}, s32[]{:S(2)}) async-start(s8[14680064]{0:T(1024)(128)(4,1)} %bitcast.2), calls=%async_computation.1 | async-start | bytes 8388608
  51.7 2.5 %collective-permute-start.15 = (bf16[64,2432]{1,0:T(8,128)(2,1)S(1)}, bf16[64,2432]{1,0:T(8,128)(2,1)S(1)}, u32[]{:S(2)}, u32[]{:S(2)}) collective-permute-start(bf16[64,2432]{1,0:T(8,128)(2,1)S(1)} %get-tuple-element.184), channel_id=1, source_target_pairs={{0,1},{1,0},{2,3},{3,2},{4,5},{5,4},{6,7},{7,6},{8,9},{9,8},{10,11... | collective-permute-start | bytes 933896 | tf_op jit(solution)/shard_map/ppermute | solution.py:23
  51.7 2.5 %collective-permute-start.16 = (bf16[64,2432]{1,0:T(8,128)(2,1)S(1)}, bf16[64,2432]{1,0:T(8,128)(2,1)S(1)}, u32[]{:S(2)}, u32[]{:S(2)}) collective-permute-start(bf16[64,2432]{1,0:T(8,128)(2,1)S(1)} %get-tuple-element.185), channel_id=1, source_target_pairs={{0,1},{1,0},{2,3},{3,2},{4,5},{5,4},{6,7},{7,6},{8,9},{9,8},{10,11... | collective-permute-start | bytes 933896 | tf_op jit(solution)/shard_map/ppermute | solution.py:23
  52.2 2.0 %collective-permute-start.14 = (bf16[64,2304]{1,0:T(8,128)(2,1)S(1)}, bf16[64,2304]{1,0:T(8,128)(2,1)S(1)}, u32[]{:S(2)}, u32[]{:S(2)}) collective-permute-start(bf16[64,2304]{1,0:T(8,128)(2,1)S(1)} %get-tuple-element.183), channel_id=1, source_target_pairs={{0,1},{1,0},{2,3},{3,2},{4,5},{5,4},{6,7},{7,6},{8,9},{9,8},{10,11... | collective-permute-start | bytes 884744 | tf_op jit(solution)/shard_map/ppermute | solution.py:23
  52.3 8.7 %collective-permute-start.18 = (bf16[64,2048]{1,0:T(8,128)(2,1)S(1)}, bf16[64,2048]{1,0:T(8,128)(2,1)S(1)}, u32[]{:S(2)}, u32[]{:S(2)}) collective-permute-start(bf16[64,2048]{1,0:T(8,128)(2,1)S(1)} %collective-permute-done.13.refs_0_), channel_id=1, source_target_pairs={{0,4},{4,0},{8,12},{12,8},{1,5},{5,1},{9,13},{13,9},{2,6},{6,2},{1... | collective-permute-start | bytes 786440 | tf_op jit(solution)/shard_map/ppermute | solution.py:23
  54.4 13.4 %collective-permute-start.17 = (bf16[64,3584]{1,0:T(8,128)(2,1)S(1)}, bf16[64,3584]{1,0:T(8,128)(2,1)S(1)}, u32[]{:S(2)}, u32[]{:S(2)}) collective-permute-start(bf16[64,3584]{1,0:T(8,128)(2,1)S(1)} %get-tuple-element.190), channel_id=1, source_target_pairs={{0,2},{1,3},{2,0},{3,1},{4,6},{5,7},{6,4},{7,5},{8,10},{9,11},{10,... | collective-permute-start | bytes 1376264 | tf_op jit(solution)/shard_map/ppermute | solution.py:23
  55.1 1.4 %collective-permute-start.20 = (bf16[32,1792]{1,0:T(8,128)(2,1)S(1)}, bf16[32,1792]{1,0:T(8,128)(2,1)S(1)}, u32[]{:S(2)}, u32[]{:S(2)}) collective-permute-start(bf16[32,1792]{1,0:T(8,128)(2,1)S(1)} %get-tuple-element.195), channel_id=1, source_target_pairs={{0,1},{1,0},{2,3},{3,2},{4,5},{5,4},{6,7},{7,6},{8,9},{9,8},{10,11... | collective-permute-start | bytes 344072 | tf_op jit(solution)/shard_map/ppermute | solution.py:23
  55.2 1.5 %collective-permute-start.21 = (bf16[32,1792]{1,0:T(8,128)(2,1)S(1)}, bf16[32,1792]{1,0:T(8,128)(2,1)S(1)}, u32[]{:S(2)}, u32[]{:S(2)}) collective-permute-start(bf16[32,1792]{1,0:T(8,128)(2,1)S(1)} %get-tuple-element.196), channel_id=1, source_target_pairs={{0,1},{1,0},{2,3},{3,2},{4,5},{5,4},{6,7},{7,6},{8,9},{9,8},{10,11... | collective-permute-start | bytes 344072 | tf_op jit(solution)/shard_map/ppermute | solution.py:23
  65.3 1.6 %collective-permute-start.22 = (bf16[64,2304]{1,0:T(8,128)(2,1)S(1)}, bf16[64,2304]{1,0:T(8,128)(2,1)S(1)}, u32[]{:S(2)}, u32[]{:S(2)}) collective-permute-start(bf16[64,2304]{1,0:T(8,128)(2,1)S(1)} %get-tuple-element.205), channel_id=1, source_target_pairs={{0,1},{1,0},{2,3},{3,2},{4,5},{5,4},{6,7},{7,6},{8,9},{9,8},{10,11... | collective-permute-start | bytes 884744 | tf_op jit(solution)/shard_map/ppermute | solution.py:23
  65.4 2.0 %collective-permute-start.23 = (bf16[64,2432]{1,0:T(8,128)(2,1)S(1)}, bf16[64,2432]{1,0:T(8,128)(2,1)S(1)}, u32[]{:S(2)}, u32[]{:S(2)}) collective-permute-start(bf16[64,2432]{1,0:T(8,128)(2,1)S(1)} %get-tuple-element.206), channel_id=1, source_target_pairs={{0,1},{1,0},{2,3},{3,2},{4,5},{5,4},{6,7},{7,6},{8,9},{9,8},{10,11... | collective-permute-start | bytes 933896 | tf_op jit(solution)/shard_map/ppermute | solution.py:23
  65.9 2.0 %collective-permute-start.24 = (bf16[64,2432]{1,0:T(8,128)(2,1)S(1)}, bf16[64,2432]{1,0:T(8,128)(2,1)S(1)}, u32[]{:S(2)}, u32[]{:S(2)}) collective-permute-start(bf16[64,2432]{1,0:T(8,128)(2,1)S(1)} %get-tuple-element.207), channel_id=1, source_target_pairs={{0,1},{1,0},{2,3},{3,2},{4,5},{5,4},{6,7},{7,6},{8,9},{9,8},{10,11... | collective-permute-start | bytes 933896 | tf_op jit(solution)/shard_map/ppermute | solution.py:23
  65.9 2.9 %collective-permute-start.11 = (bf16[64,3584]{1,0:T(8,128)(2,1)S(1)}, bf16[64,3584]{1,0:T(8,128)(2,1)S(1)}, u32[]{:S(2)}, u32[]{:S(2)}) collective-permute-start(bf16[64,3584]{1,0:T(8,128)(2,1)S(1)} %get-tuple-element.171.mine_ref), channel_id=1, source_target_pairs={{0,1},{1,0},{2,3},{3,2},{4,5},{5,4},{6,7},{7,6},{8,9},{9,8},{10,11... | collective-permute-start | bytes 1376264 | tf_op jit(solution)/shard_map/ppermute | solution.py:23
  66.9 8.3 %collective-permute-start.26 = (bf16[64,2048]{1,0:T(8,128)(2,1)S(1)}, bf16[64,2048]{1,0:T(8,128)(2,1)S(1)}, u32[]{:S(2)}, u32[]{:S(2)}) collective-permute-start(bf16[64,2048]{1,0:T(8,128)(2,1)S(1)} %down.6), channel_id=1, source_target_pairs={{0,4},{4,0},{8,12},{12,8},{1,5},{5,1},{9,13},{13,9},{2,6},{6,2},{1... | collective-permute-start | bytes 786440 | tf_op jit(solution)/shard_map/ppermute | solution.py:23
  68.0 7.7 %collective-permute-start.25 = (bf16[32,3584]{1,0:T(8,128)(2,1)S(1)}, bf16[32,3584]{1,0:T(8,128)(2,1)S(1)}, u32[]{:S(2)}, u32[]{:S(2)}) collective-permute-start(bf16[32,3584]{1,0:T(8,128)(2,1)S(1)} %hidden.9.share_ref), channel_id=1, source_target_pairs={{0,2},{1,3},{2,0},{3,1},{4,6},{5,7},{6,4},{7,5},{8,10},{9,11},{10,... | collective-permute-start | bytes 688136 | tf_op jit(solution)/shard_map/ppermute | solution.py:23
  75.8 1.6 %collective-permute-start.27 = (bf16[64,1792]{1,0:T(8,128)(2,1)S(1)}, bf16[64,1792]{1,0:T(8,128)(2,1)S(1)}, u32[]{:S(2)}, u32[]{:S(2)}) collective-permute-start(bf16[64,1792]{1,0:T(8,128)(2,1)S(1)} %get-tuple-element.220), channel_id=1, source_target_pairs={{0,1},{1,0},{2,3},{3,2},{4,5},{5,4},{6,7},{7,6},{8,9},{9,8},{10,11... | collective-permute-start | bytes 688136 | tf_op jit(solution)/shard_map/ppermute | solution.py:23
  75.8 1.8 %collective-permute-start.28 = (bf16[64,1792]{1,0:T(8,128)(2,1)S(1)}, bf16[64,1792]{1,0:T(8,128)(2,1)S(1)}, u32[]{:S(2)}, u32[]{:S(2)}) collective-permute-start(bf16[64,1792]{1,0:T(8,128)(2,1)S(1)} %get-tuple-element.221), channel_id=1, source_target_pairs={{0,1},{1,0},{2,3},{3,2},{4,5},{5,4},{6,7},{7,6},{8,9},{9,8},{10,11... | collective-permute-start | bytes 688136 | tf_op jit(solution)/shard_map/ppermute | solution.py:23
  76.3 10.0 %collective-permute-start.30 = (bf16[48,3584]{1,0:T(8,128)(2,1)S(1)}, bf16[48,3584]{1,0:T(8,128)(2,1)S(1)}, u32[]{:S(2)}, u32[]{:S(2)}) collective-permute-start(bf16[48,3584]{1,0:T(8,128)(2,1)S(1)} %stack.1), channel_id=1, source_target_pairs={{0,2},{1,3},{2,0},{3,1},{4,6},{5,7},{6,4},{7,5},{8,10},{9,11},{10,... | collective-permute-start | bytes 1032200 | tf_op jit(solution)/shard_map/ppermute | solution.py:23
  80.0 8.6 %collective-permute-start.32 = (bf16[64,2048]{1,0:T(8,128)(2,1)S(1)}, bf16[64,2048]{1,0:T(8,128)(2,1)S(1)}, u32[]{:S(2)}, u32[]{:S(2)}) collective-permute-start(bf16[64,2048]{1,0:T(8,128)(2,1)S(1)} %get-tuple-element.229), channel_id=1, source_target_pairs={{0,4},{4,0},{8,12},{12,8},{1,5},{5,1},{9,13},{13,9},{2,6},{6,2},{1... | collective-permute-start | bytes 786440 | tf_op jit(solution)/shard_map/ppermute | solution.py:23
  86.5 6.1 %collective-permute-start.31 = (bf16[16,3584]{1,0:T(8,128)(2,1)S(1)}, bf16[16,3584]{1,0:T(8,128)(2,1)S(1)}, u32[]{:S(2)}, u32[]{:S(2)}) collective-permute-start(bf16[16,3584]{1,0:T(8,128)(2,1)S(1)} %get-tuple-element.228.share_ref), channel_id=1, source_target_pairs={{0,2},{1,3},{2,0},{3,1},{4,6},{5,7},{6,4},{7,5},{8,10},{9,11},{10,... | collective-permute-start | bytes 344072 | tf_op jit(solution)/shard_map/ppermute | solution.py:23
  87.0 10.8 %collective-permute-start.29 = (bf16[32,3584]{1,0:T(8,128)(2,1)S(1)}, bf16[32,3584]{1,0:T(8,128)(2,1)S(1)}, u32[]{:S(2)}, u32[]{:S(2)}) collective-permute-start(bf16[32,3584]{1,0:T(8,128)(2,1)S(1)} %get-tuple-element.225), channel_id=1, source_target_pairs={{0,2},{1,3},{2,0},{3,1},{4,6},{5,7},{6,4},{7,5},{8,10},{9,11},{10,... | collective-permute-start | bytes 688136 | tf_op jit(solution)/shard_map/ppermute | solution.py:23
  88.6 14.5 %collective-permute-start.36 = (bf16[64,2048]{1,0:T(8,128)(2,1)S(1)}, bf16[64,2048]{1,0:T(8,128)(2,1)S(1)}, u32[]{:S(2)}, u32[]{:S(2)}) collective-permute-start(bf16[64,2048]{1,0:T(8,128)(2,1)S(1)} %add.26), channel_id=1, source_target_pairs={{0,8},{4,12},{8,0},{12,4},{1,9},{5,13},{9,1},{13,5},{2,10},{6,14},... | collective-permute-start | bytes 786440 | tf_op jit(solution)/shard_map/ppermute | solution.py:23
  92.7 1.4 %collective-permute-start.33 = (bf16[32,1792]{1,0:T(8,128)(2,1)S(1)}, bf16[32,1792]{1,0:T(8,128)(2,1)S(1)}, u32[]{:S(2)}, u32[]{:S(2)}) collective-permute-start(bf16[32,1792]{1,0:T(8,128)(2,1)S(1)} %get-tuple-element.232), channel_id=1, source_target_pairs={{0,1},{1,0},{2,3},{3,2},{4,5},{5,4},{6,7},{7,6},{8,9},{9,8},{10,11... | collective-permute-start | bytes 344072 | tf_op jit(solution)/shard_map/ppermute | solution.py:23
  92.8 1.5 %collective-permute-start.34 = (bf16[32,1792]{1,0:T(8,128)(2,1)S(1)}, bf16[32,1792]{1,0:T(8,128)(2,1)S(1)}, u32[]{:S(2)}, u32[]{:S(2)}) collective-permute-start(bf16[32,1792]{1,0:T(8,128)(2,1)S(1)} %get-tuple-element.233), channel_id=1, source_target_pairs={{0,1},{1,0},{2,3},{3,2},{4,5},{5,4},{6,7},{7,6},{8,9},{9,8},{10,11... | collective-permute-start | bytes 344072 | tf_op jit(solution)/shard_map/ppermute | solution.py:23
  96.3 12.0 %collective-permute-start.42 = (bf16[64,2048]{1,0:T(8,128)(2,1)S(1)}, bf16[64,2048]{1,0:T(8,128)(2,1)S(1)}, u32[]{:S(2)}, u32[]{:S(2)}) collective-permute-start(bf16[64,2048]{1,0:T(8,128)(2,1)S(1)} %down.9), channel_id=1, source_target_pairs={{0,4},{4,0},{8,12},{12,8},{1,5},{5,1},{9,13},{13,9},{2,6},{6,2},{1... | collective-permute-start | bytes 786440 | tf_op jit(solution)/shard_map/ppermute | solution.py:23
  97.3 1.4 %collective-permute-start.37 = (bf16[32,1792]{1,0:T(8,128)(2,1)S(1)}, bf16[32,1792]{1,0:T(8,128)(2,1)S(1)}, u32[]{:S(2)}, u32[]{:S(2)}) collective-permute-start(bf16[32,1792]{1,0:T(8,128)(2,1)S(1)} %get-tuple-element.238), channel_id=1, source_target_pairs={{0,1},{1,0},{2,3},{3,2},{4,5},{5,4},{6,7},{7,6},{8,9},{9,8},{10,11... | collective-permute-start | bytes 344072 | tf_op jit(solution)/shard_map/ppermute | solution.py:23
  97.4 1.4 %collective-permute-start.38 = (bf16[32,1792]{1,0:T(8,128)(2,1)S(1)}, bf16[32,1792]{1,0:T(8,128)(2,1)S(1)}, u32[]{:S(2)}, u32[]{:S(2)}) collective-permute-start(bf16[32,1792]{1,0:T(8,128)(2,1)S(1)} %get-tuple-element.239), channel_id=1, source_target_pairs={{0,1},{1,0},{2,3},{3,2},{4,5},{5,4},{6,7},{7,6},{8,9},{9,8},{10,11... | collective-permute-start | bytes 344072 | tf_op jit(solution)/shard_map/ppermute | solution.py:23
  97.9 5.2 %collective-permute-start.35 = (bf16[16,3584]{1,0:T(8,128)(2,1)S(1)}, bf16[16,3584]{1,0:T(8,128)(2,1)S(1)}, u32[]{:S(2)}, u32[]{:S(2)}) collective-permute-start(bf16[16,3584]{1,0:T(8,128)(2,1)S(1)} %hidden.11.share_ref), channel_id=1, source_target_pairs={{0,2},{1,3},{2,0},{3,1},{4,6},{5,7},{6,4},{7,5},{8,10},{9,11},{10,... | collective-permute-start | bytes 344072 | tf_op jit(solution)/shard_map/ppermute | solution.py:23
  103.2 1.7 %collective-permute-start.40 = (bf16[32,1792]{1,0:T(8,128)(2,1)S(1)}, bf16[32,1792]{1,0:T(8,128)(2,1)S(1)}, u32[]{:S(2)}, u32[]{:S(2)}) collective-permute-start(bf16[32,1792]{1,0:T(8,128)(2,1)S(1)} %get-tuple-element.245), channel_id=1, source_target_pairs={{0,1},{1,0},{2,3},{3,2},{4,5},{5,4},{6,7},{7,6},{8,9},{9,8},{10,11... | collective-permute-start | bytes 344072 | tf_op jit(solution)/shard_map/ppermute | solution.py:23
  103.3 1.7 %collective-permute-start.41 = (bf16[32,1792]{1,0:T(8,128)(2,1)S(1)}, bf16[32,1792]{1,0:T(8,128)(2,1)S(1)}, u32[]{:S(2)}, u32[]{:S(2)}) collective-permute-start(bf16[32,1792]{1,0:T(8,128)(2,1)S(1)} %get-tuple-element.246), channel_id=1, source_target_pairs={{0,1},{1,0},{2,3},{3,2},{4,5},{5,4},{6,7},{7,6},{8,9},{9,8},{10,11... | collective-permute-start | bytes 344072 | tf_op jit(solution)/shard_map/ppermute | solution.py:23
  103.8 12.2 %collective-permute-start.39 = (bf16[64,2048]{1,0:T(8,128)(2,1)S(1)}, bf16[64,2048]{1,0:T(8,128)(2,1)S(1)}, u32[]{:S(2)}, u32[]{:S(2)}) collective-permute-start(bf16[64,2048]{1,0:T(8,128)(2,1)S(1)} %down.10), channel_id=1, source_target_pairs={{0,4},{4,0},{8,12},{12,8},{1,5},{5,1},{9,13},{13,9},{2,6},{6,2},{1... | collective-permute-start | bytes 786440 | tf_op jit(solution)/shard_map/ppermute | solution.py:23
  108.3 14.8 %collective-permute-start.43 = (bf16[64,2048]{1,0:T(8,128)(2,1)S(1)}, bf16[64,2048]{1,0:T(8,128)(2,1)S(1)}, u32[]{:S(2)}, u32[]{:S(2)}) collective-permute-start(bf16[64,2048]{1,0:T(8,128)(2,1)S(1)} %add.27), channel_id=1, source_target_pairs={{0,8},{4,12},{8,0},{12,4},{1,9},{5,13},{9,1},{13,5},{2,10},{6,14},... | collective-permute-start | bytes 786440 | tf_op jit(solution)/shard_map/ppermute | solution.py:23
  123.3 5.6 %collective-permute-start.44 = (f32[1,2048]{1,0:T(1,128)S(1)}, f32[1,2048]{1,0:T(1,128)S(1)}, u32[]{:S(2)}, u32[]{:S(2)}) collective-permute-start(f32[1,2048]{1,0:T(1,128)S(1)} %bitcast.6), channel_id=1, source_target_pairs={{0,12},{4,8},{8,4},{12,0},{1,13},{5,9},{9,5},{13,1},{2,14},{6,10},... | collective-permute-start | bytes 24584 | tf_op jit(solution)/shard_map/ppermute | solution.py:23
  125.9 4.5 %collective-permute-start.45 = (f32[1,2048]{1,0:T(1,128)S(1)}, f32[1,2048]{1,0:T(1,128)S(1)}, u32[]{:S(2)}, u32[]{:S(2)}) collective-permute-start(f32[1,2048]{1,0:T(1,128)S(1)} %bitcast.7), channel_id=1, source_target_pairs={{0,8},{4,12},{8,0},{12,4},{1,9},{5,13},{9,1},{13,5},{2,10},{6,14},... | collective-permute-start | bytes 24584 | tf_op jit(solution)/shard_map/ppermute | solution.py:23
  125.9 4.5 %collective-permute-start.46 = (f32[1,2048]{1,0:T(1,128)S(1)}, f32[1,2048]{1,0:T(1,128)S(1)}, u32[]{:S(2)}, u32[]{:S(2)}) collective-permute-start(f32[1,2048]{1,0:T(1,128)S(1)} %bitcast.8), channel_id=1, source_target_pairs={{0,4},{4,0},{8,12},{12,8},{1,5},{5,1},{9,13},{13,9},{2,6},{6,2},{1... | collective-permute-start | bytes 24584 | tf_op jit(solution)/shard_map/ppermute | solution.py:23
  (9 other events, 60.0 us)

commit v5 on v4

--- a/solution.py
+++ b/solution.py
@@ -266,6 +266,10 @@
     out_ref[...] = narrow(part_ref[...] + widen(got_ref[...]))
 
 
+def peak_kernel(one_ref, other_ref, out_ref):
+    out_ref[...] = jnp.maximum(one_ref[...], other_ref[...])
+
+
 def scale_kernel(first_ref, second_ref, *refs):
     *peak_refs, out_ref, scales_ref = refs
     rows = out_ref.shape[0] // WIDTH
@@ -379,38 +383,38 @@
     first, second = done(
         combine(joined0, [core0], down_weight, (jnp.float32, jnp.float32))
     )
-    got4 = swap(payload, "width", CORES)
+    got4 = swap(tick(payload), "width", CORES)
     over2, add1 = ticks([over2, add1])
     joined2 = done(join(share2, over2))
-    core2 = ticks(parts_of(joined2, 2))
+    core2 = ticks(parts_of(joined2, 3))
     cross2, far2 = done(
         combine(joined2, core2, down_weight, (jnp.float32, jnp.bfloat16))
     )
     far2 = swap(far2, AXIS, 1)
-    got3 = swap(tick(send3), "width", CORES)
 
     got4 = tick(got4)
     share4, joined5 = done(hidden(mine4, got4, None, share5))
     over4 = swap(share4, "width", CORES)
+    over4 = tick(over4)
+    joined4 = done(join(share4, over4))
+    got3 = swap(tick(send3), "width", CORES)
+    core4 = ticks(parts_of(joined4, 2))
+    (far3,) = done(combine(joined4, core4, down_weight, (jnp.bfloat16,)))
+    far3 = swap(far3, AXIS, 1)
     far2 = tick(far2)
     add2 = done(call(add_kernel, array(stay, tokens.shape[1]), (cross2, far2), "add"))
     add2 = swap(add2, AXIS, 2)
-    over4 = tick(over4)
-    joined4 = done(join(share4, over4))
-    core4 = ticks(parts_of(joined4, 2))
-    (far3,) = done(combine(joined4, core4, down_weight, (jnp.bfloat16,)))
-    far3 = swap(far3, AXIS, 1)
     got3 = tick(got3)
     (share3,) = done(hidden(mine3, got3))
     over3 = swap(share3, "width", CORES)
     core5 = ticks(parts_of(joined5, 2))
     (part5,) = done(combine(joined5, core5, down_weight, (jnp.bfloat16,)))
     add5 = swap(part5, AXIS, 1)
-    over3, add2 = ticks([over3, add2])
+    over3 = tick(over3)
     joined3 = done(join(share3, over3))
     core3 = ticks(parts_of(joined3, 2))
     (cross3,) = done(combine(joined3, core3, down_weight, (jnp.float32,)))
-    far3 = tick(far3)
+    far3, add2 = ticks([far3, add2])
     add3 = done(call(add_kernel, array(stay, tokens.shape[1]), (cross3, far3), "add"))
     add3 = swap(add3, AXIS, 2)
 
@@ -420,11 +424,14 @@
         jnp.max(jnp.abs(first), axis=0, keepdims=True),
         jnp.max(jnp.abs(second), axis=0, keepdims=True),
     )
-    peaks = [swap(local_peak, AXIS, k) for k in range(RANKS - 1, 0, -1)]
+    pair_peak = call(
+        peak_kernel, array(*local_peak.shape, jnp.float32), (local_peak, swap(local_peak, AXIS, 2)), "peak"
+    )
+    peaks = [swap(pair_peak, AXIS, 1)]
     scaled, scales = call(
         scale_kernel,
         (array(*tokens.shape), array(1, tokens.shape[1], jnp.float32)),
-        (first, second, local_peak, *peaks),
+        (first, second, pair_peak, *peaks),
         "scale",
     )
     return (scaled, scales[0])

time: 131 us -> 130 us (level)
    pallas_call x40 -> x41, Pallas kernels: 32.9 us -> 32.9 us  [call(): pl.pallas_call(kernel, out_shape=shapes, in_specs=[VMEM] * len(args), out...]
  transfers between devices with their start and end apart: 47 -> 47, of which waited for: 29 -> 28; matrix products, arithmetic and copies ran while one was open for 0% -> 0% of each run, Pallas kernels for 24% -> 24%
where the time goes in v5:
time: 130 us
  waiting for transfers between devices  55 us (42%)
  starting transfers between devices  36.6 us (28%)
  Pallas kernels  32.9 us (25%)
  local copies, waits for them, and re-layouts  4.53 us (3%)
    ppermute x47, waiting for transfers between devices, swap(): return lax.ppermute(value, axis, [(i, i ^ mask) for i in range(size)])  55 us
    ppermute x47, starting transfers between devices, swap(): return lax.ppermute(value, axis, [(i, i ^ mask) for i in range(size)])  36.6 us
    pallas_call x41, Pallas kernels, call(): pl.pallas_call(kernel, out_shape=shapes, in_specs=[VMEM] * len(args), out...  32.9 us
    unnamed x20, local copies, waits for them, and re-layouts  4.53 us
  transfers between devices with their start and end apart: 47, of which 28 were waited for; matrix products, arithmetic and copies ran while one was open for 0% of the time, Pallas kernels for 24%

profile of v5, /device:TPU:0, one launch (start us, length us, event | category | flops | bytes accessed | tf_op | source)
XLA Modules:
  0.0 130.3 jit_solution(4439066016256759885)
XLA Ops:
  0.7 3.1 %collective-permute-start = (bf16[128,2048]{1,0:T(8,128)(2,1)}, bf16[128,2048]{1,0:T(8,128)(2,1)S(1)}, u32[]{:S(2)}, u32[]{:S(2)}) collective-permute-start(bf16[128,2048]{1,0:T(8,128)(2,1)} %tokens_ref.1), channel_id=1, source_target_pairs={{0,4},{4,0},{8,12},{12,8},{1,5},{5,1},{9,13},{13,9},{2,6},{6,2},{1... | collective-permute-start | bytes 1572872 | tf_op jit(solution)/shard_map/ppermute | solution.py:23
  3.8 1.8 %copy-done.1 = bf16[128,2048]{1,0:T(8,128)(2,1)S(1)} copy-done((bf16[128,2048]{1,0:T(8,128)(2,1)S(1)}, bf16[128,2048]{1,0:T(8,128)(2,1)}, u32[]{:S(2)}) %copy-start.1) | copy-done | bytes 524312
  6.0 2.1 %gate.4 = (bf16[64,7168]{1,0:T(8,128)(2,1)S(1)}, bf16[64,2304]{1,0:T(8,128)(2,1)S(1)}, bf16[64,2432]{1,0:T(8,128)(2,1)S(1)}, bf16[64,2432]{1,0:T(8,128)(2,1)S(1)}) custom-call(bf16[128,2048]{1,0:T(8,128)(2,1)S(1)} %arrange.2.refs_0_.block_ref, bf16[2048,3584]{1,0:T(8,128)(2,1)S(1)} %copy-done), custom_call_target="tpu_custom_call" | custom-call | flops 3758096384 | bytes 14680064 | tf_op jit(solution)/shard_map/gate/pallas_call | solution.py:48
  8.4 1.2 slice-done.6
  10.4 2.2 %up.4 = (bf16[64,7168]{1,0:T(8,128)(2,1)S(1)}, bf16[64,2304]{1,0:T(8,128)(2,1)S(1)}, bf16[64,2432]{1,0:T(8,128)(2,1)S(1)}, bf16[64,2432]{1,0:T(8,128)(2,1)S(1)}) custom-call(bf16[128,2048]{1,0:T(8,128)(2,1)S(1)} %arrange.2.refs_0_.block_ref, bf16[2048,3584]{1,0:T(8,128)(2,1)S(1)} %bitcast.5, ...), custom_call_target="tpu_custom_call", output_to_operand_aliasing={{0}: (2, {}), {1}: (3, {}), {2}: (4, {}), {3}: (5, {})} | custom-call | flops 1 | bytes 1 | tf_op jit(solution)/shard_map/up/pallas_call | solution.py:48
  13.7 3.7 %collective-permute-start.4 = (bf16[64,2048]{1,0:T(8,128)(2,1)S(1)}, bf16[64,2048]{1,0:T(8,128)(2,1)S(1)}, u32[]{:S(2)}, u32[]{:S(2)}) collective-permute-start(bf16[64,2048]{1,0:T(8,128)(2,1)S(1)} %get-tuple-element.149), channel_id=1, source_target_pairs={{0,8},{4,12},{8,0},{12,4},{1,9},{5,13},{9,1},{13,5},{2,10},{6,14},... | collective-permute-start | bytes 786440 | tf_op jit(solution)/shard_map/ppermute | solution.py:23
  17.6 1.5 %collective-permute-start.7 = (bf16[64,3584]{1,0:T(8,128)(2,1)S(1)}, bf16[64,3584]{1,0:T(8,128)(2,1)S(1)}, u32[]{:S(2)}, u32[]{:S(2)}) collective-permute-start(bf16[64,3584]{1,0:T(8,128)(2,1)S(1)} %get-tuple-element.160), channel_id=1, source_target_pairs={{0,2},{1,3},{2,0},{3,1},{4,6},{5,7},{6,4},{7,5},{8,10},{9,11},{10,... | collective-permute-start | bytes 1376264 | tf_op jit(solution)/shard_map/ppermute | solution.py:23
  19.2 2.1 %gate.5 = (bf16[64,7168]{1,0:T(8,128)(2,1)S(1)}, bf16[32,4736]{1,0:T(8,128)(2,1)S(1)}, bf16[32,2432]{1,0:T(8,128)(2,1)S(1)}, bf16[32,3584]{1,0:T(8,128)(2,1)S(1)}, bf16[32,3584]{1,0:T(8,128)(2,1)S(1)}) custom-call(bf16[128,2048]{1,0:T(8,128)(2,1)S(1)} %arrange.3.refs_0_, bf16[2048,3584]{1,0:T(8,128)(2,1)S(1)} %copy-done), custom_call_target="tpu_custom_call" | custom-call | flops 1 | bytes 1 | tf_op jit(solution)/shard_map/gate/pallas_call | solution.py:48
  21.3 2.2 %up.5 = (bf16[64,7168]{1,0:T(8,128)(2,1)S(1)}, bf16[32,4736]{1,0:T(8,128)(2,1)S(1)}, bf16[32,2432]{1,0:T(8,128)(2,1)S(1)}, bf16[32,3584]{1,0:T(8,128)(2,1)S(1)}, bf16[32,3584]{1,0:T(8,128)(2,1)S(1)}) custom-call(bf16[128,2048]{1,0:T(8,128)(2,1)S(1)} %arrange.3.refs_0_, ...), custom_call_target="tpu_custom_call", output_to_operand_aliasing={{0}: (2, {}), {1}: (3, {}), {2}: (4, {}), {3}: (5, {}), {4}... | custom-call | flops 1 | bytes 1 | tf_op jit(solution)/shard_map/up/pallas_call | solution.py:48
  23.5 6.4 %collective-permute-done.4.refs_0_ = bf16[64,2048]{1,0:T(8,128)(2,1)S(1)} collective-permute-done((bf16[64,2048]{1,0:T(8,128)(2,1)S(1)}, bf16[64,2048]{1,0:T(8,128)(2,1)S(1)}, u32[]{:S(2)}, u32[]{:S(2)}) %collective-permute-start.4) | collective-permute-done | bytes 262176 | tf_op jit(solution)/shard_map/ppermute | solution.py:23
  30.4 1.3 %collective-permute-done.6.refs_2_ = bf16[32,2432]{1,0:T(8,128)(2,1)S(1)} collective-permute-done((bf16[32,2432]{1,0:T(8,128)(2,1)S(1)}, bf16[32,2432]{1,0:T(8,128)(2,1)S(1)}, u32[]{:S(2)}, u32[]{:S(2)}) %collective-permute-start.6) | collective-permute-done | bytes 155680 | tf_op jit(solution)/shard_map/ppermute | solution.py:23
  32.0 1.6 %collective-permute-start.8 = (bf16[64,3584]{1,0:T(8,128)(2,1)S(1)}, bf16[64,3584]{1,0:T(8,128)(2,1)S(1)}, u32[]{:S(2)}, u32[]{:S(2)}) collective-permute-start(bf16[64,3584]{1,0:T(8,128)(2,1)S(1)} %get-tuple-element.163), channel_id=1, source_target_pairs={{0,2},{1,3},{2,0},{3,1},{4,6},{5,7},{6,4},{7,5},{8,10},{9,11},{10,... | collective-permute-start | bytes 1376264 | tf_op jit(solution)/shard_map/ppermute | solution.py:23
  34.4 3.4 %collective-permute-start.13 = (bf16[64,2048]{1,0:T(8,128)(2,1)S(1)}, bf16[64,2048]{1,0:T(8,128)(2,1)S(1)}, u32[]{:S(2)}, u32[]{:S(2)}) collective-permute-start(bf16[64,2048]{1,0:T(8,128)(2,1)S(1)} %get-tuple-element.182), channel_id=1, source_target_pairs={{0,8},{4,12},{8,0},{12,4},{1,9},{5,13},{9,1},{13,5},{2,10},{6,14},... | collective-permute-start | bytes 786440 | tf_op jit(solution)/shard_map/ppermute | solution.py:23
  38.2 1.0 collective-permute-done.10.refs_2_
  39.6 5.0 %collective-permute-done.8.refs_1_ = bf16[64,3584]{1,0:T(8,128)(2,1)S(1)} collective-permute-done((bf16[64,3584]{1,0:T(8,128)(2,1)S(1)}, bf16[64,3584]{1,0:T(8,128)(2,1)S(1)}, u32[]{:S(2)}, u32[]{:S(2)}) %collective-permute-start.8) | collective-permute-done | bytes 458784 | tf_op jit(solution)/shard_map/ppermute | solution.py:23
  44.8 1.6 %collective-permute-start.19 = (bf16[48,3584]{1,0:T(8,128)(2,1)S(1)}, bf16[48,3584]{1,0:T(8,128)(2,1)S(1)}, u32[]{:S(2)}, u32[]{:S(2)}) collective-permute-start(bf16[48,3584]{1,0:T(8,128)(2,1)S(1)} %get-tuple-element.194), channel_id=1, source_target_pairs={{0,2},{1,3},{2,0},{3,1},{4,6},{5,7},{6,4},{7,5},{8,10},{9,11},{10,... | collective-permute-start | bytes 1032200 | tf_op jit(solution)/shard_map/ppermute | solution.py:23
  47.1 2.1 %gate.6 = (bf16[64,7168]{1,0:T(8,128)(2,1)S(1)}, bf16[64,2304]{1,0:T(8,128)(2,1)S(1)}, bf16[64,2432]{1,0:T(8,128)(2,1)S(1)}, bf16[64,2432]{1,0:T(8,128)(2,1)S(1)}) custom-call(bf16[64,2048]{1,0:T(8,128)(2,1)S(1)} %collective-permute-done.4.refs_0_, bf16[64,2048]{1,0:T(8,128)(2,1)S(1)} %collective-permute-done.12.refs_1_, bf16[2048,3584]{1,0:T(8,128)(2,1)S(1)} %copy-done), custom_call_target="tpu_custom_call" | custom-call | flops 1 | bytes 1 | tf_op jit(solution)/shard_map/gate/pallas_call | solution.py:48
  49.2 2.4 %up.6 = (bf16[64,7168]{1,0:T(8,128)(2,1)S(1)}, bf16[64,2304]{1,0:T(8,128)(2,1)S(1)}, bf16[64,2432]{1,0:T(8,128)(2,1)S(1)}, bf16[64,2432]{1,0:T(8,128)(2,1)S(1)}) custom-call(bf16[64,2048]{1,0:T(8,128)(2,1)S(1)} %collective-permute-done.4.refs_0_, ...), custom_call_target="tpu_custom_call", output_to_operand_aliasing={{0}: (3, {}), {1}: (4, {}), {2}: (5, {}), {3}: (6, {})} | custom-call | flops 1 | bytes 1 | tf_op jit(solution)/shard_map/up/pallas_call | solution.py:48
  52.3 1.9 %collective-permute-done.14.refs_1_ = bf16[64,2304]{1,0:T(8,128)(2,1)S(1)} collective-permute-done((bf16[64,2304]{1,0:T(8,128)(2,1)S(1)}, bf16[64,2304]{1,0:T(8,128)(2,1)S(1)}, u32[]{:S(2)}, u32[]{:S(2)}) %collective-permute-start.14) | collective-permute-done | bytes 294944 | tf_op jit(solution)/shard_map/ppermute | solution.py:23
  56.7 2.1 %down.6 = bf16[64,2048]{1,0:T(8,128)(2,1)S(1)} custom-call(bf16[32,3584]{1,0:T(8,128)(2,1)S(1)} %get-tuple-element.197.mine_ref, bf16[32,1792]{1,0:T(8,128)(2,1)S(1)} %collective-permute-done.20.refs_0_, bf16[32,1792]{1,0:T(8,128)(2,1)S(1)} %collective-permute-done.21.refs_1_, bf16[3584,2048]{1,0:T(8,128)(2,1)S(1)} %bitcast.3), custom_call_target="tpu_custom_call" | custom-call | flops 1 | bytes 1 | tf_op jit(solution)/shard_map/down/pallas_call | solution.py:48
  58.8 2.2 %collective-permute-done.18.refs_1_ = bf16[64,2048]{1,0:T(8,128)(2,1)S(1)} collective-permute-done((bf16[64,2048]{1,0:T(8,128)(2,1)S(1)}, bf16[64,2048]{1,0:T(8,128)(2,1)S(1)}, u32[]{:S(2)}, u32[]{:S(2)}) %collective-permute-start.18) | collective-permute-done | bytes 262176 | tf_op jit(solution)/shard_map/ppermute | solution.py:23
  61.0 2.1 %gate.7 = (bf16[64,7168]{1,0:T(8,128)(2,1)S(1)}, bf16[64,2304]{1,0:T(8,128)(2,1)S(1)}, bf16[64,2432]{1,0:T(8,128)(2,1)S(1)}, bf16[64,2432]{1,0:T(8,128)(2,1)S(1)}) custom-call(bf16[64,2048]{1,0:T(8,128)(2,1)S(1)} %collective-permute-done.13.refs_0_, bf16[64,2048]{1,0:T(8,128)(2,1)S(1)} %collective-permute-done.18.refs_1_, bf16[2048,3584]{1,0:T(8,128)(2,1)S(1)} %copy-done), custom_call_target="tpu_custom_call" | custom-call | flops 1 | bytes 1 | tf_op jit(solution)/shard_map/gate/pallas_call | solution.py:48
  63.0 2.2 %up.7 = (bf16[64,7168]{1,0:T(8,128)(2,1)S(1)}, bf16[64,2304]{1,0:T(8,128)(2,1)S(1)}, bf16[64,2432]{1,0:T(8,128)(2,1)S(1)}, bf16[64,2432]{1,0:T(8,128)(2,1)S(1)}) custom-call(bf16[64,2048]{1,0:T(8,128)(2,1)S(1)} %collective-permute-done.13.refs_0_, ...), custom_call_target="tpu_custom_call", output_to_operand_aliasing={{0}: (3, {}), {1}: (4, {}), {2}: (5, {}), {3}: (6, {})} | custom-call | flops 1 | bytes 1 | tf_op jit(solution)/shard_map/up/pallas_call | solution.py:48
  65.9 1.0 collective-permute-done.22.refs_1_
  68.8 2.1 %down.7 = (f32[64,2048]{1,0:T(8,128)S(1)}, f32[64,2048]{1,0:T(8,128)S(1)}) custom-call(bf16[64,3584]{1,0:T(8,128)(2,1)S(1)} %get-tuple-element.174.mine_ref, bf16[64,3584]{1,0:T(8,128)(2,1)S(1)} %collective-permute-done.11.refs_0_, bf16[3584,2048]{1,0:T(8,128)(2,1)S(1)} %bitcast.3), custom_call_target="tpu_custom_call" | custom-call | flops 1 | bytes 1 | tf_op jit(solution)/shard_map/down/pallas_call | solution.py:48
  70.9 1.6 %collective-permute-start.27 = (bf16[48,3584]{1,0:T(8,128)(2,1)S(1)}, bf16[48,3584]{1,0:T(8,128)(2,1)S(1)}, u32[]{:S(2)}, u32[]{:S(2)}) collective-permute-start(bf16[48,3584]{1,0:T(8,128)(2,1)S(1)} %stack.1), channel_id=1, source_target_pairs={{0,2},{1,3},{2,0},{3,1},{4,6},{5,7},{6,4},{7,5},{8,10},{9,11},{10,... | collective-permute-start | bytes 1032200 | tf_op jit(solution)/shard_map/ppermute | solution.py:23
  72.5 2.8 %collective-permute-done.26 = bf16[64,2048]{1,0:T(8,128)(2,1)S(1)} collective-permute-done((bf16[64,2048]{1,0:T(8,128)(2,1)S(1)}, bf16[64,2048]{1,0:T(8,128)(2,1)S(1)}, u32[]{:S(2)}, u32[]{:S(2)}) %collective-permute-start.26) | collective-permute-done | bytes 262176 | tf_op jit(solution)/shard_map/ppermute | solution.py:23
  75.3 1.2 collective-permute-done.25.got_ref
  77.2 1.0 collective-permute-done.28.refs_0_
  78.5 2.3 %down.8 = (f32[64,2048]{1,0:T(8,128)S(1)}, bf16[64,2048]{1,0:T(8,128)(2,1)S(1)}) custom-call(bf16[64,3584]{1,0:T(8,128)(2,1)S(1)} %join.3.mine_ref, bf16[64,1152]{1,0:T(8,128)(2,1)S(1)} %collective-permute-done.28.refs_0_, bf16[64,1152]{1,0:T(8,128)(2,1)S(1)} %collective-permute-done.29.refs_1_, bf16[64,1280]{1,0:T(8,128)(2,1)S(1)} %collective-permute-done.30.refs_2_, ...), custom_call_target="tpu_custom_call" | custom-call | flops 1 | bytes 1 | tf_op jit(solution)/shard_map/down/pallas_call | solution.py:48
  80.9 2.2 %collective-permute-done.27.refs_1_ = bf16[48,3584]{1,0:T(8,128)(2,1)S(1)} collective-permute-done((bf16[48,3584]{1,0:T(8,128)(2,1)S(1)}, bf16[48,3584]{1,0:T(8,128)(2,1)S(1)}, u32[]{:S(2)}, u32[]{:S(2)}) %collective-permute-start.27) | collective-permute-done | bytes 344096 | tf_op jit(solution)/shard_map/ppermute | solution.py:23
  83.7 0.9 collective-permute-start.35
  84.6 3.4 %collective-permute-done.31.got_ref = bf16[16,3584]{1,0:T(8,128)(2,1)S(1)} collective-permute-done((bf16[16,3584]{1,0:T(8,128)(2,1)S(1)}, bf16[16,3584]{1,0:T(8,128)(2,1)S(1)}, u32[]{:S(2)}, u32[]{:S(2)}) %collective-permute-start.31) | collective-permute-done | bytes 114720 | tf_op jit(solution)/shard_map/ppermute | solution.py:23
  90.2 2.1 %down.9 = bf16[64,2048]{1,0:T(8,128)(2,1)S(1)} custom-call(bf16[32,3584]{1,0:T(8,128)(2,1)S(1)} %join.4.mine_ref, bf16[32,1792]{1,0:T(8,128)(2,1)S(1)} %collective-permute-done.32.refs_0_, bf16[32,1792]{1,0:T(8,128)(2,1)S(1)} %collective-permute-done.33.refs_1_, bf16[3584,2048]{1,0:T(8,128)(2,1)S(1)} %bitcast.3), custom_call_target="tpu_custom_call" | custom-call | flops 1 | bytes 1 | tf_op jit(solution)/shard_map/down/pallas_call | solution.py:48
  92.2 0.9 collective-permute-start.34
  93.2 2.6 %collective-permute-start.36 = (bf16[64,2048]{1,0:T(8,128)(2,1)S(1)}, bf16[64,2048]{1,0:T(8,128)(2,1)S(1)}, u32[]{:S(2)}, u32[]{:S(2)}) collective-permute-start(bf16[64,2048]{1,0:T(8,128)(2,1)S(1)} %add.26), channel_id=1, source_target_pairs={{0,8},{4,12},{8,0},{12,4},{1,9},{5,13},{9,1},{13,5},{2,10},{6,14},... | collective-permute-start | bytes 786440 | tf_op jit(solution)/shard_map/ppermute | solution.py:23
  96.5 1.5 %collective-permute-start.38 = (bf16[16,3584]{1,0:T(8,128)(2,1)S(1)}, bf16[16,3584]{1,0:T(8,128)(2,1)S(1)}, u32[]{:S(2)}, u32[]{:S(2)}) collective-permute-start(bf16[16,3584]{1,0:T(8,128)(2,1)S(1)} %hidden.11.share_ref), channel_id=1, source_target_pairs={{0,2},{1,3},{2,0},{3,1},{4,6},{5,7},{6,4},{7,5},{8,10},{9,11},{10,... | collective-permute-start | bytes 344072 | tf_op jit(solution)/shard_map/ppermute | solution.py:23
  98.1 2.1 %down.10 = bf16[64,2048]{1,0:T(8,128)(2,1)S(1)} custom-call(bf16[32,3584]{1,0:T(8,128)(2,1)S(1)} %get-tuple-element.243.mine_ref, bf16[32,1792]{1,0:T(8,128)(2,1)S(1)} %collective-permute-done.39.refs_0_, bf16[32,1792]{1,0:T(8,128)(2,1)S(1)} %collective-permute-done.40.refs_1_, bf16[3584,2048]{1,0:T(8,128)(2,1)S(1)} %bitcast.3), custom_call_target="tpu_custom_call" | custom-call | flops 1 | bytes 1 | tf_op jit(solution)/shard_map/down/pallas_call | solution.py:48
  100.2 1.6 %collective-permute-done.38.got_ref = bf16[16,3584]{1,0:T(8,128)(2,1)S(1)} collective-permute-done((bf16[16,3584]{1,0:T(8,128)(2,1)S(1)}, bf16[16,3584]{1,0:T(8,128)(2,1)S(1)}, u32[]{:S(2)}, u32[]{:S(2)}) %collective-permute-start.38) | collective-permute-done | bytes 114720 | tf_op jit(solution)/shard_map/ppermute | solution.py:23
  103.3 2.1 %down.11.part_ref = f32[64,2048]{1,0:T(8,128)S(1)} custom-call(bf16[32,3584]{1,0:T(8,128)(2,1)S(1)} %join.5.mine_ref, bf16[32,1792]{1,0:T(8,128)(2,1)S(1)} %collective-permute-done.41.refs_0_, bf16[32,1792]{1,0:T(8,128)(2,1)S(1)} %collective-permute-done.42.refs_1_, bf16[3584,2048]{1,0:T(8,128)(2,1)S(1)} %bitcast.3), custom_call_target="tpu_custom_call" | custom-call | flops 1 | bytes 1 | tf_op jit(solution)/shard_map/down/pallas_call | solution.py:48
  105.4 1.7 %collective-permute-done.34.got_ref = bf16[64,2048]{1,0:T(8,128)(2,1)S(1)} collective-permute-done((bf16[64,2048]{1,0:T(8,128)(2,1)S(1)}, bf16[64,2048]{1,0:T(8,128)(2,1)S(1)}, u32[]{:S(2)}, u32[]{:S(2)}) %collective-permute-start.34) | collective-permute-done | bytes 262176 | tf_op jit(solution)/shard_map/ppermute | solution.py:23
  107.1 1.9 %collective-permute-start.44 = (bf16[64,2048]{1,0:T(8,128)(2,1)S(1)}, bf16[64,2048]{1,0:T(8,128)(2,1)S(1)}, u32[]{:S(2)}, u32[]{:S(2)}) collective-permute-start(bf16[64,2048]{1,0:T(8,128)(2,1)S(1)} %add.27), channel_id=1, source_target_pairs={{0,8},{4,12},{8,0},{12,4},{1,9},{5,13},{9,1},{13,5},{2,10},{6,14},... | collective-permute-start | bytes 786440 | tf_op jit(solution)/shard_map/ppermute | solution.py:23
  109.1 7.2 %collective-permute-done.43 = bf16[64,2048]{1,0:T(8,128)(2,1)S(1)} collective-permute-done((bf16[64,2048]{1,0:T(8,128)(2,1)S(1)}, bf16[64,2048]{1,0:T(8,128)(2,1)S(1)}, u32[]{:S(2)}, u32[]{:S(2)}) %collective-permute-start.43) | collective-permute-done | bytes 262176 | tf_op jit(solution)/shard_map/ppermute | solution.py:23
  116.3 4.7 %collective-permute-done.44 = bf16[64,2048]{1,0:T(8,128)(2,1)S(1)} collective-permute-done((bf16[64,2048]{1,0:T(8,128)(2,1)S(1)}, bf16[64,2048]{1,0:T(8,128)(2,1)S(1)}, u32[]{:S(2)}, u32[]{:S(2)}) %collective-permute-start.44) | collective-permute-done | bytes 262176 | tf_op jit(solution)/shard_map/ppermute | solution.py:23
  121.2 4.5 %collective-permute-done.45.other_ref = f32[1,2048]{1,0:T(1,128)S(1)} collective-permute-done((f32[1,2048]{1,0:T(1,128)S(1)}, f32[1,2048]{1,0:T(1,128)S(1)}, u32[]{:S(2)}, u32[]{:S(2)}) %collective-permute-start.45) | collective-permute-done | bytes 8224 | tf_op jit(solution)/shard_map/ppermute | solution.py:23
  125.8 1.8 %collective-permute-start.46 = (f32[1,2048]{1,0:T(1,128)S(1)}, f32[1,2048]{1,0:T(1,128)S(1)}, u32[]{:S(2)}, u32[]{:S(2)}) collective-permute-start(f32[1,2048]{1,0:T(1,128)S(1)} %peak.1.refs_0_), channel_id=1, source_target_pairs={{0,4},{4,0},{8,12},{12,8},{1,5},{5,1},{9,13},{13,9},{2,6},{6,2},{1... | collective-permute-start | bytes 24584 | tf_op jit(solution)/shard_map/ppermute | solution.py:23
  127.5 1.9 %collective-permute-done.46.refs_1_ = f32[1,2048]{1,0:T(1,128)S(1)} collective-permute-done((f32[1,2048]{1,0:T(1,128)S(1)}, f32[1,2048]{1,0:T(1,128)S(1)}, u32[]{:S(2)}, u32[]{:S(2)}) %collective-permute-start.46) | collective-permute-done | bytes 8224 | tf_op jit(solution)/shard_map/ppermute | solution.py:23
  129.4 0.9 scale.1
  (112 shorter events, 18.1 us)
Async XLA Ops:
  0.7 18.5 %collective-permute-start = (bf16[128,2048]{1,0:T(8,128)(2,1)}, bf16[128,2048]{1,0:T(8,128)(2,1)S(1)}, u32[]{:S(2)}, u32[]{:S(2)}) collective-permute-start(bf16[128,2048]{1,0:T(8,128)(2,1)} %tokens_ref.1), channel_id=1, source_target_pairs={{0,4},{4,0},{8,12},{12,8},{1,5},{5,1},{9,13},{13,9},{2,6},{6,2},{1... | collective-permute-start | bytes 1572872 | tf_op jit(solution)/shard_map/ppermute | solution.py:23
  12.6 4.8 %collective-permute-start.2 = (bf16[64,2432]{1,0:T(8,128)(2,1)S(1)}, bf16[64,2432]{1,0:T(8,128)(2,1)S(1)}, u32[]{:S(2)}, u32[]{:S(2)}) collective-permute-start(bf16[64,2432]{1,0:T(8,128)(2,1)S(1)} %get-tuple-element.135), channel_id=1, source_target_pairs={{0,1},{1,0},{2,3},{3,2},{4,5},{5,4},{6,7},{7,6},{8,9},{9,8},{10,11... | collective-permute-start | bytes 933896 | tf_op jit(solution)/shard_map/ppermute | solution.py:23
  13.1 4.3 %collective-permute-start.3 = (bf16[64,2432]{1,0:T(8,128)(2,1)S(1)}, bf16[64,2432]{1,0:T(8,128)(2,1)S(1)}, u32[]{:S(2)}, u32[]{:S(2)}) collective-permute-start(bf16[64,2432]{1,0:T(8,128)(2,1)S(1)} %get-tuple-element.136), channel_id=1, source_target_pairs={{0,1},{1,0},{2,3},{3,2},{4,5},{5,4},{6,7},{7,6},{8,9},{9,8},{10,11... | collective-permute-start | bytes 933896 | tf_op jit(solution)/shard_map/ppermute | solution.py:23
  13.2 4.2 %collective-permute-start.1 = (bf16[64,2304]{1,0:T(8,128)(2,1)S(1)}, bf16[64,2304]{1,0:T(8,128)(2,1)S(1)}, u32[]{:S(2)}, u32[]{:S(2)}) collective-permute-start(bf16[64,2304]{1,0:T(8,128)(2,1)S(1)} %get-tuple-element.134), channel_id=1, source_target_pairs={{0,1},{1,0},{2,3},{3,2},{4,5},{5,4},{6,7},{7,6},{8,9},{9,8},{10,11... | collective-permute-start | bytes 884744 | tf_op jit(solution)/shard_map/ppermute | solution.py:23
  13.7 16.3 %collective-permute-start.4 = (bf16[64,2048]{1,0:T(8,128)(2,1)S(1)}, bf16[64,2048]{1,0:T(8,128)(2,1)S(1)}, u32[]{:S(2)}, u32[]{:S(2)}) collective-permute-start(bf16[64,2048]{1,0:T(8,128)(2,1)S(1)} %get-tuple-element.149), channel_id=1, source_target_pairs={{0,8},{4,12},{8,0},{12,4},{1,9},{5,13},{9,1},{13,5},{2,10},{6,14},... | collective-permute-start | bytes 786440 | tf_op jit(solution)/shard_map/ppermute | solution.py:23
  17.6 14.2 %collective-permute-start.7 = (bf16[64,3584]{1,0:T(8,128)(2,1)S(1)}, bf16[64,3584]{1,0:T(8,128)(2,1)S(1)}, u32[]{:S(2)}, u32[]{:S(2)}) collective-permute-start(bf16[64,3584]{1,0:T(8,128)(2,1)S(1)} %get-tuple-element.160), channel_id=1, source_target_pairs={{0,2},{1,3},{2,0},{3,1},{4,6},{5,7},{6,4},{7,5},{8,10},{9,11},{10,... | collective-permute-start | bytes 1376264 | tf_op jit(solution)/shard_map/ppermute | solution.py:23
  29.9 1.8 %collective-permute-start.5 = (bf16[32,4736]{1,0:T(8,128)(2,1)S(1)}, bf16[32,4736]{1,0:T(8,128)(2,1)S(1)}, u32[]{:S(2)}, u32[]{:S(2)}) collective-permute-start(bf16[32,4736]{1,0:T(8,128)(2,1)S(1)} %get-tuple-element.154), channel_id=1, source_target_pairs={{0,1},{1,0},{2,3},{3,2},{4,5},{5,4},{6,7},{7,6},{8,9},{9,8},{10,11... | collective-permute-start | bytes 909320 | tf_op jit(solution)/shard_map/ppermute | solution.py:23
  29.9 1.8 %collective-permute-start.6 = (bf16[32,2432]{1,0:T(8,128)(2,1)S(1)}, bf16[32,2432]{1,0:T(8,128)(2,1)S(1)}, u32[]{:S(2)}, u32[]{:S(2)}) collective-permute-start(bf16[32,2432]{1,0:T(8,128)(2,1)S(1)} %get-tuple-element.155), channel_id=1, source_target_pairs={{0,1},{1,0},{2,3},{3,2},{4,5},{5,4},{6,7},{7,6},{8,9},{9,8},{10,11... | collective-permute-start | bytes 466952 | tf_op jit(solution)/shard_map/ppermute | solution.py:23
  32.0 12.6 %collective-permute-start.8 = (bf16[64,3584]{1,0:T(8,128)(2,1)S(1)}, bf16[64,3584]{1,0:T(8,128)(2,1)S(1)}, u32[]{:S(2)}, u32[]{:S(2)}) collective-permute-start(bf16[64,3584]{1,0:T(8,128)(2,1)S(1)} %get-tuple-element.163), channel_id=1, source_target_pairs={{0,2},{1,3},{2,0},{3,1},{4,6},{5,7},{6,4},{7,5},{8,10},{9,11},{10,... | collective-permute-start | bytes 1376264 | tf_op jit(solution)/shard_map/ppermute | solution.py:23
  33.7 13.5 %collective-permute-start.12 = (bf16[64,2048]{1,0:T(8,128)(2,1)S(1)}, bf16[64,2048]{1,0:T(8,128)(2,1)S(1)}, u32[]{:S(2)}, u32[]{:S(2)}) collective-permute-start(bf16[64,2048]{1,0:T(8,128)(2,1)S(1)} %collective-permute-done.4.refs_0_), channel_id=1, source_target_pairs={{0,4},{4,0},{8,12},{12,8},{1,5},{5,1},{9,13},{13,9},{2,6},{6,2},{1... | collective-permute-start | bytes 786440 | tf_op jit(solution)/shard_map/ppermute | solution.py:23
  34.4 17.3 %collective-permute-start.13 = (bf16[64,2048]{1,0:T(8,128)(2,1)S(1)}, bf16[64,2048]{1,0:T(8,128)(2,1)S(1)}, u32[]{:S(2)}, u32[]{:S(2)}) collective-permute-start(bf16[64,2048]{1,0:T(8,128)(2,1)S(1)} %get-tuple-element.182), channel_id=1, source_target_pairs={{0,8},{4,12},{8,0},{12,4},{1,9},{5,13},{9,1},{13,5},{2,10},{6,14},... | collective-permute-start | bytes 786440 | tf_op jit(solution)/shard_map/ppermute | solution.py:23
  37.7 1.5 %collective-permute-start.10 = (bf16[32,3584]{1,0:T(8,128)(2,1)S(1)}, bf16[32,3584]{1,0:T(8,128)(2,1)S(1)}, u32[]{:S(2)}, u32[]{:S(2)}) collective-permute-start(bf16[32,3584]{1,0:T(8,128)(2,1)S(1)} %get-tuple-element.168), channel_id=1, source_target_pairs={{0,1},{1,0},{2,3},{3,2},{4,5},{5,4},{6,7},{7,6},{8,9},{9,8},{10,11... | collective-permute-start | bytes 688136 | tf_op jit(solution)/shard_map/ppermute | solution.py:23
  37.7 1.8 %collective-permute-start.9 = (bf16[32,3584]{1,0:T(8,128)(2,1)S(1)}, bf16[32,3584]{1,0:T(8,128)(2,1)S(1)}, u32[]{:S(2)}, u32[]{:S(2)}) collective-permute-start(bf16[32,3584]{1,0:T(8,128)(2,1)S(1)} %get-tuple-element.167), channel_id=1, source_target_pairs={{0,1},{1,0},{2,3},{3,2},{4,5},{5,4},{6,7},{7,6},{8,9},{9,8},{10,11... | collective-permute-start | bytes 688136 | tf_op jit(solution)/shard_map/ppermute | solution.py:23
  44.8 10.2 %collective-permute-start.19 = (bf16[48,3584]{1,0:T(8,128)(2,1)S(1)}, bf16[48,3584]{1,0:T(8,128)(2,1)S(1)}, u32[]{:S(2)}, u32[]{:S(2)}) collective-permute-start(bf16[48,3584]{1,0:T(8,128)(2,1)S(1)} %get-tuple-element.194), channel_id=1, source_target_pairs={{0,2},{1,3},{2,0},{3,1},{4,6},{5,7},{6,4},{7,5},{8,10},{9,11},{10,... | collective-permute-start | bytes 1032200 | tf_op jit(solution)/shard_map/ppermute | solution.py:23
  47.1 9.5 %slice-start.1 = ((s8[14680064]{0:T(1024)(128)(4,1)}), s8[4194304]{0:T(1024)(128)(4,1)S(1)}, s32[]{:S(2)}) async-start(s8[14680064]{0:T(1024)(128)(4,1)} %bitcast.2), calls=%async_computation.1 | async-start | bytes 8388608
  51.7 2.5 %collective-permute-start.15 = (bf16[64,2432]{1,0:T(8,128)(2,1)S(1)}, bf16[64,2432]{1,0:T(8,128)(2,1)S(1)}, u32[]{:S(2)}, u32[]{:S(2)}) collective-permute-start(bf16[64,2432]{1,0:T(8,128)(2,1)S(1)} %get-tuple-element.187), channel_id=1, source_target_pairs={{0,1},{1,0},{2,3},{3,2},{4,5},{5,4},{6,7},{7,6},{8,9},{9,8},{10,11... | collective-permute-start | bytes 933896 | tf_op jit(solution)/shard_map/ppermute | solution.py:23
  51.7 2.5 %collective-permute-start.16 = (bf16[64,2432]{1,0:T(8,128)(2,1)S(1)}, bf16[64,2432]{1,0:T(8,128)(2,1)S(1)}, u32[]{:S(2)}, u32[]{:S(2)}) collective-permute-start(bf16[64,2432]{1,0:T(8,128)(2,1)S(1)} %get-tuple-element.188), channel_id=1, source_target_pairs={{0,1},{1,0},{2,3},{3,2},{4,5},{5,4},{6,7},{7,6},{8,9},{9,8},{10,11... | collective-permute-start | bytes 933896 | tf_op jit(solution)/shard_map/ppermute | solution.py:23
  52.2 2.0 %collective-permute-start.14 = (bf16[64,2304]{1,0:T(8,128)(2,1)S(1)}, bf16[64,2304]{1,0:T(8,128)(2,1)S(1)}, u32[]{:S(2)}, u32[]{:S(2)}) collective-permute-start(bf16[64,2304]{1,0:T(8,128)(2,1)S(1)} %get-tuple-element.186), channel_id=1, source_target_pairs={{0,1},{1,0},{2,3},{3,2},{4,5},{5,4},{6,7},{7,6},{8,9},{9,8},{10,11... | collective-permute-start | bytes 884744 | tf_op jit(solution)/shard_map/ppermute | solution.py:23
  52.3 8.7 %collective-permute-start.18 = (bf16[64,2048]{1,0:T(8,128)(2,1)S(1)}, bf16[64,2048]{1,0:T(8,128)(2,1)S(1)}, u32[]{:S(2)}, u32[]{:S(2)}) collective-permute-start(bf16[64,2048]{1,0:T(8,128)(2,1)S(1)} %collective-permute-done.13.refs_0_), channel_id=1, source_target_pairs={{0,4},{4,0},{8,12},{12,8},{1,5},{5,1},{9,13},{13,9},{2,6},{6,2},{1... | collective-permute-start | bytes 786440 | tf_op jit(solution)/shard_map/ppermute | solution.py:23
  54.4 13.4 %collective-permute-start.17 = (bf16[64,3584]{1,0:T(8,128)(2,1)S(1)}, bf16[64,3584]{1,0:T(8,128)(2,1)S(1)}, u32[]{:S(2)}, u32[]{:S(2)}) collective-permute-start(bf16[64,3584]{1,0:T(8,128)(2,1)S(1)} %get-tuple-element.193), channel_id=1, source_target_pairs={{0,2},{1,3},{2,0},{3,1},{4,6},{5,7},{6,4},{7,5},{8,10},{9,11},{10,... | collective-permute-start | bytes 1376264 | tf_op jit(solution)/shard_map/ppermute | solution.py:23
  55.1 1.4 %collective-permute-start.20 = (bf16[32,1792]{1,0:T(8,128)(2,1)S(1)}, bf16[32,1792]{1,0:T(8,128)(2,1)S(1)}, u32[]{:S(2)}, u32[]{:S(2)}) collective-permute-start(bf16[32,1792]{1,0:T(8,128)(2,1)S(1)} %get-tuple-element.198), channel_id=1, source_target_pairs={{0,1},{1,0},{2,3},{3,2},{4,5},{5,4},{6,7},{7,6},{8,9},{9,8},{10,11... | collective-permute-start | bytes 344072 | tf_op jit(solution)/shard_map/ppermute | solution.py:23
  55.2 1.5 %collective-permute-start.21 = (bf16[32,1792]{1,0:T(8,128)(2,1)S(1)}, bf16[32,1792]{1,0:T(8,128)(2,1)S(1)}, u32[]{:S(2)}, u32[]{:S(2)}) collective-permute-start(bf16[32,1792]{1,0:T(8,128)(2,1)S(1)} %get-tuple-element.199), channel_id=1, source_target_pairs={{0,1},{1,0},{2,3},{3,2},{4,5},{5,4},{6,7},{7,6},{8,9},{9,8},{10,11... | collective-permute-start | bytes 344072 | tf_op jit(solution)/shard_map/ppermute | solution.py:23
  55.7 13.1 %collective-permute-start.11 = (bf16[64,3584]{1,0:T(8,128)(2,1)S(1)}, bf16[64,3584]{1,0:T(8,128)(2,1)S(1)}, u32[]{:S(2)}, u32[]{:S(2)}) collective-permute-start(bf16[64,3584]{1,0:T(8,128)(2,1)S(1)} %get-tuple-element.174.mine_ref), channel_id=1, source_target_pairs={{0,1},{1,0},{2,3},{3,2},{4,5},{5,4},{6,7},{7,6},{8,9},{9,8},{10,11... | collective-permute-start | bytes 1376264 | tf_op jit(solution)/shard_map/ppermute | solution.py:23
  65.3 1.6 %collective-permute-start.22 = (bf16[64,2304]{1,0:T(8,128)(2,1)S(1)}, bf16[64,2304]{1,0:T(8,128)(2,1)S(1)}, u32[]{:S(2)}, u32[]{:S(2)}) collective-permute-start(bf16[64,2304]{1,0:T(8,128)(2,1)S(1)} %get-tuple-element.208), channel_id=1, source_target_pairs={{0,1},{1,0},{2,3},{3,2},{4,5},{5,4},{6,7},{7,6},{8,9},{9,8},{10,11... | collective-permute-start | bytes 884744 | tf_op jit(solution)/shard_map/ppermute | solution.py:23
  65.4 2.0 %collective-permute-start.23 = (bf16[64,2432]{1,0:T(8,128)(2,1)S(1)}, bf16[64,2432]{1,0:T(8,128)(2,1)S(1)}, u32[]{:S(2)}, u32[]{:S(2)}) collective-permute-start(bf16[64,2432]{1,0:T(8,128)(2,1)S(1)} %get-tuple-element.209), channel_id=1, source_target_pairs={{0,1},{1,0},{2,3},{3,2},{4,5},{5,4},{6,7},{7,6},{8,9},{9,8},{10,11... | collective-permute-start | bytes 933896 | tf_op jit(solution)/shard_map/ppermute | solution.py:23
  65.9 2.0 %collective-permute-start.24 = (bf16[64,2432]{1,0:T(8,128)(2,1)S(1)}, bf16[64,2432]{1,0:T(8,128)(2,1)S(1)}, u32[]{:S(2)}, u32[]{:S(2)}) collective-permute-start(bf16[64,2432]{1,0:T(8,128)(2,1)S(1)} %get-tuple-element.210), channel_id=1, source_target_pairs={{0,1},{1,0},{2,3},{3,2},{4,5},{5,4},{6,7},{7,6},{8,9},{9,8},{10,11... | collective-permute-start | bytes 933896 | tf_op jit(solution)/shard_map/ppermute | solution.py:23
  66.9 8.3 %collective-permute-start.26 = (bf16[64,2048]{1,0:T(8,128)(2,1)S(1)}, bf16[64,2048]{1,0:T(8,128)(2,1)S(1)}, u32[]{:S(2)}, u32[]{:S(2)}) collective-permute-start(bf16[64,2048]{1,0:T(8,128)(2,1)S(1)} %down.6), channel_id=1, source_target_pairs={{0,4},{4,0},{8,12},{12,8},{1,5},{5,1},{9,13},{13,9},{2,6},{6,2},{1... | collective-permute-start | bytes 786440 | tf_op jit(solution)/shard_map/ppermute | solution.py:23
  68.0 8.5 %collective-permute-start.25 = (bf16[32,3584]{1,0:T(8,128)(2,1)S(1)}, bf16[32,3584]{1,0:T(8,128)(2,1)S(1)}, u32[]{:S(2)}, u32[]{:S(2)}) collective-permute-start(bf16[32,3584]{1,0:T(8,128)(2,1)S(1)} %hidden.9.share_ref), channel_id=1, source_target_pairs={{0,2},{1,3},{2,0},{3,1},{4,6},{5,7},{6,4},{7,5},{8,10},{9,11},{10,... | collective-permute-start | bytes 688136 | tf_op jit(solution)/shard_map/ppermute | solution.py:23
  70.9 12.2 %collective-permute-start.27 = (bf16[48,3584]{1,0:T(8,128)(2,1)S(1)}, bf16[48,3584]{1,0:T(8,128)(2,1)S(1)}, u32[]{:S(2)}, u32[]{:S(2)}) collective-permute-start(bf16[48,3584]{1,0:T(8,128)(2,1)S(1)} %stack.1), channel_id=1, source_target_pairs={{0,2},{1,3},{2,0},{3,1},{4,6},{5,7},{6,4},{7,5},{8,10},{9,11},{10,... | collective-permute-start | bytes 1032200 | tf_op jit(solution)/shard_map/ppermute | solution.py:23
  76.6 2.0 %collective-permute-start.30 = (bf16[64,1280]{1,0:T(8,128)(2,1)S(1)}, bf16[64,1280]{1,0:T(8,128)(2,1)S(1)}, u32[]{:S(2)}, u32[]{:S(2)}) collective-permute-start(bf16[64,1280]{1,0:T(8,128)(2,1)S(1)} %get-tuple-element.226), channel_id=1, source_target_pairs={{0,1},{1,0},{2,3},{3,2},{4,5},{5,4},{6,7},{7,6},{8,9},{9,8},{10,11... | collective-permute-start | bytes 491528 | tf_op jit(solution)/shard_map/ppermute | solution.py:23
  76.7 1.6 %collective-permute-start.28 = (bf16[64,1152]{1,0:T(8,128)(2,1)S(1)}, bf16[64,1152]{1,0:T(8,128)(2,1)S(1)}, u32[]{:S(2)}, u32[]{:S(2)}) collective-permute-start(bf16[64,1152]{1,0:T(8,128)(2,1)S(1)} %get-tuple-element.224), channel_id=1, source_target_pairs={{0,1},{1,0},{2,3},{3,2},{4,5},{5,4},{6,7},{7,6},{8,9},{9,8},{10,11... | collective-permute-start | bytes 442376 | tf_op jit(solution)/shard_map/ppermute | solution.py:23
  77.1 1.4 %collective-permute-start.29 = (bf16[64,1152]{1,0:T(8,128)(2,1)S(1)}, bf16[64,1152]{1,0:T(8,128)(2,1)S(1)}, u32[]{:S(2)}, u32[]{:S(2)}) collective-permute-start(bf16[64,1152]{1,0:T(8,128)(2,1)S(1)} %get-tuple-element.225), channel_id=1, source_target_pairs={{0,1},{1,0},{2,3},{3,2},{4,5},{5,4},{6,7},{7,6},{8,9},{9,8},{10,11... | collective-permute-start | bytes 442376 | tf_op jit(solution)/shard_map/ppermute | solution.py:23
  83.2 4.9 %collective-permute-start.31 = (bf16[16,3584]{1,0:T(8,128)(2,1)S(1)}, bf16[16,3584]{1,0:T(8,128)(2,1)S(1)}, u32[]{:S(2)}, u32[]{:S(2)}) collective-permute-start(bf16[16,3584]{1,0:T(8,128)(2,1)S(1)} %get-tuple-element.232.share_ref), channel_id=1, source_target_pairs={{0,2},{1,3},{2,0},{3,1},{4,6},{5,7},{6,4},{7,5},{8,10},{9,11},{10,... | collective-permute-start | bytes 344072 | tf_op jit(solution)/shard_map/ppermute | solution.py:23
  83.7 9.5 %collective-permute-start.35 = (bf16[64,2048]{1,0:T(8,128)(2,1)S(1)}, bf16[64,2048]{1,0:T(8,128)(2,1)S(1)}, u32[]{:S(2)}, u32[]{:S(2)}) collective-permute-start(bf16[64,2048]{1,0:T(8,128)(2,1)S(1)} %get-tuple-element.240), channel_id=1, source_target_pairs={{0,4},{4,0},{8,12},{12,8},{1,5},{5,1},{9,13},{13,9},{2,6},{6,2},{1... | collective-permute-start | bytes 786440 | tf_op jit(solution)/shard_map/ppermute | solution.py:23
  88.0 8.4 %collective-permute-start.37 = (bf16[32,3584]{1,0:T(8,128)(2,1)S(1)}, bf16[32,3584]{1,0:T(8,128)(2,1)S(1)}, u32[]{:S(2)}, u32[]{:S(2)}) collective-permute-start(bf16[32,3584]{1,0:T(8,128)(2,1)S(1)} %get-tuple-element.237), channel_id=1, source_target_pairs={{0,2},{1,3},{2,0},{3,1},{4,6},{5,7},{6,4},{7,5},{8,10},{9,11},{10,... | collective-permute-start | bytes 688136 | tf_op jit(solution)/shard_map/ppermute | solution.py:23
  88.6 1.4 %collective-permute-start.32 = (bf16[32,1792]{1,0:T(8,128)(2,1)S(1)}, bf16[32,1792]{1,0:T(8,128)(2,1)S(1)}, u32[]{:S(2)}, u32[]{:S(2)}) collective-permute-start(bf16[32,1792]{1,0:T(8,128)(2,1)S(1)} %get-tuple-element.234), channel_id=1, source_target_pairs={{0,1},{1,0},{2,3},{3,2},{4,5},{5,4},{6,7},{7,6},{8,9},{9,8},{10,11... | collective-permute-start | bytes 344072 | tf_op jit(solution)/shard_map/ppermute | solution.py:23
  88.7 1.5 %collective-permute-start.33 = (bf16[32,1792]{1,0:T(8,128)(2,1)S(1)}, bf16[32,1792]{1,0:T(8,128)(2,1)S(1)}, u32[]{:S(2)}, u32[]{:S(2)}) collective-permute-start(bf16[32,1792]{1,0:T(8,128)(2,1)S(1)} %get-tuple-element.235), channel_id=1, source_target_pairs={{0,1},{1,0},{2,3},{3,2},{4,5},{5,4},{6,7},{7,6},{8,9},{9,8},{10,11... | collective-permute-start | bytes 344072 | tf_op jit(solution)/shard_map/ppermute | solution.py:23
  92.2 14.8 %collective-permute-start.34 = (bf16[64,2048]{1,0:T(8,128)(2,1)S(1)}, bf16[64,2048]{1,0:T(8,128)(2,1)S(1)}, u32[]{:S(2)}, u32[]{:S(2)}) collective-permute-start(bf16[64,2048]{1,0:T(8,128)(2,1)S(1)} %down.9), channel_id=1, source_target_pairs={{0,4},{4,0},{8,12},{12,8},{1,5},{5,1},{9,13},{13,9},{2,6},{6,2},{1... | collective-permute-start | bytes 786440 | tf_op jit(solution)/shard_map/ppermute | solution.py:23
  93.2 13.8 %collective-permute-start.36 = (bf16[64,2048]{1,0:T(8,128)(2,1)S(1)}, bf16[64,2048]{1,0:T(8,128)(2,1)S(1)}, u32[]{:S(2)}, u32[]{:S(2)}) collective-permute-start(bf16[64,2048]{1,0:T(8,128)(2,1)S(1)} %add.26), channel_id=1, source_target_pairs={{0,8},{4,12},{8,0},{12,4},{1,9},{5,13},{9,1},{13,5},{2,10},{6,14},... | collective-permute-start | bytes 786440 | tf_op jit(solution)/shard_map/ppermute | solution.py:23
  95.8 2.2 %collective-permute-start.39 = (bf16[32,1792]{1,0:T(8,128)(2,1)S(1)}, bf16[32,1792]{1,0:T(8,128)(2,1)S(1)}, u32[]{:S(2)}, u32[]{:S(2)}) collective-permute-start(bf16[32,1792]{1,0:T(8,128)(2,1)S(1)} %get-tuple-element.244), channel_id=1, source_target_pairs={{0,1},{1,0},{2,3},{3,2},{4,5},{5,4},{6,7},{7,6},{8,9},{9,8},{10,11... | collective-permute-start | bytes 344072 | tf_op jit(solution)/shard_map/ppermute | solution.py:23
  95.9 2.1 %collective-permute-start.40 = (bf16[32,1792]{1,0:T(8,128)(2,1)S(1)}, bf16[32,1792]{1,0:T(8,128)(2,1)S(1)}, u32[]{:S(2)}, u32[]{:S(2)}) collective-permute-start(bf16[32,1792]{1,0:T(8,128)(2,1)S(1)} %get-tuple-element.245), channel_id=1, source_target_pairs={{0,1},{1,0},{2,3},{3,2},{4,5},{5,4},{6,7},{7,6},{8,9},{9,8},{10,11... | collective-permute-start | bytes 344072 | tf_op jit(solution)/shard_map/ppermute | solution.py:23
  96.5 5.2 %collective-permute-start.38 = (bf16[16,3584]{1,0:T(8,128)(2,1)S(1)}, bf16[16,3584]{1,0:T(8,128)(2,1)S(1)}, u32[]{:S(2)}, u32[]{:S(2)}) collective-permute-start(bf16[16,3584]{1,0:T(8,128)(2,1)S(1)} %hidden.11.share_ref), channel_id=1, source_target_pairs={{0,2},{1,3},{2,0},{3,1},{4,6},{5,7},{6,4},{7,5},{8,10},{9,11},{10,... | collective-permute-start | bytes 344072 | tf_op jit(solution)/shard_map/ppermute | solution.py:23
  101.8 1.4 %collective-permute-start.41 = (bf16[32,1792]{1,0:T(8,128)(2,1)S(1)}, bf16[32,1792]{1,0:T(8,128)(2,1)S(1)}, u32[]{:S(2)}, u32[]{:S(2)}) collective-permute-start(bf16[32,1792]{1,0:T(8,128)(2,1)S(1)} %get-tuple-element.249), channel_id=1, source_target_pairs={{0,1},{1,0},{2,3},{3,2},{4,5},{5,4},{6,7},{7,6},{8,9},{9,8},{10,11... | collective-permute-start | bytes 344072 | tf_op jit(solution)/shard_map/ppermute | solution.py:23
  101.8 1.5 %collective-permute-start.42 = (bf16[32,1792]{1,0:T(8,128)(2,1)S(1)}, bf16[32,1792]{1,0:T(8,128)(2,1)S(1)}, u32[]{:S(2)}, u32[]{:S(2)}) collective-permute-start(bf16[32,1792]{1,0:T(8,128)(2,1)S(1)} %get-tuple-element.250), channel_id=1, source_target_pairs={{0,1},{1,0},{2,3},{3,2},{4,5},{5,4},{6,7},{7,6},{8,9},{9,8},{10,11... | collective-permute-start | bytes 344072 | tf_op jit(solution)/shard_map/ppermute | solution.py:23
  102.3 14.0 %collective-permute-start.43 = (bf16[64,2048]{1,0:T(8,128)(2,1)S(1)}, bf16[64,2048]{1,0:T(8,128)(2,1)S(1)}, u32[]{:S(2)}, u32[]{:S(2)}) collective-permute-start(bf16[64,2048]{1,0:T(8,128)(2,1)S(1)} %down.10), channel_id=1, source_target_pairs={{0,4},{4,0},{8,12},{12,8},{1,5},{5,1},{9,13},{13,9},{2,6},{6,2},{1... | collective-permute-start | bytes 786440 | tf_op jit(solution)/shard_map/ppermute | solution.py:23
  107.1 13.9 %collective-permute-start.44 = (bf16[64,2048]{1,0:T(8,128)(2,1)S(1)}, bf16[64,2048]{1,0:T(8,128)(2,1)S(1)}, u32[]{:S(2)}, u32[]{:S(2)}) collective-permute-start(bf16[64,2048]{1,0:T(8,128)(2,1)S(1)} %add.27), channel_id=1, source_target_pairs={{0,8},{4,12},{8,0},{12,4},{1,9},{5,13},{9,1},{13,5},{2,10},{6,14},... | collective-permute-start | bytes 786440 | tf_op jit(solution)/shard_map/ppermute | solution.py:23
  121.1 4.6 %collective-permute-start.45 = (f32[1,2048]{1,0:T(1,128)S(1)}, f32[1,2048]{1,0:T(1,128)S(1)}, u32[]{:S(2)}, u32[]{:S(2)}) collective-permute-start(f32[1,2048]{1,0:T(1,128)S(1)} %bitcast.6), channel_id=1, source_target_pairs={{0,8},{4,12},{8,0},{12,4},{1,9},{5,13},{9,1},{13,5},{2,10},{6,14},... | collective-permute-start | bytes 24584 | tf_op jit(solution)/shard_map/ppermute | solution.py:23
  125.8 3.7 %collective-permute-start.46 = (f32[1,2048]{1,0:T(1,128)S(1)}, f32[1,2048]{1,0:T(1,128)S(1)}, u32[]{:S(2)}, u32[]{:S(2)}) collective-permute-start(f32[1,2048]{1,0:T(1,128)S(1)} %peak.1.refs_0_), channel_id=1, source_target_pairs={{0,4},{4,0},{8,12},{12,8},{1,5},{5,1},{9,13},{13,9},{2,6},{6,2},{1... | collective-permute-start | bytes 24584 | tf_op jit(solution)/shard_map/ppermute | solution.py:23
  (9 other events, 60.0 us)

commit v6 on v5

--- a/solution.py
+++ b/solution.py
@@ -262,6 +262,42 @@
     return call(kernel, shapes, (mine, *cores, weight), "down")
 
 
+def join_columns(first, second):
+    cut = first.shape[1]
+
+    def kernel(first_ref, second_ref, out_ref):
+        out_ref[:, :cut] = first_ref[...]
+        out_ref[:, cut:] = second_ref[...]
+
+    shape = array(first.shape[0], cut + second.shape[1])
+    return call(kernel, shape, (first, second), "columns")
+
+
+def combine_parts(mine, cores, weight, dtypes):
+    args = (*mine, *cores)
+    rows, columns = sum(v.shape[0] for v in args), weight.shape[1]
+    count = len(dtypes)
+    piece = rows // WIDTH // count
+    shapes = tuple(array(rows // count, columns, dtype) for dtype in dtypes)
+
+    def kernel(*refs):
+        outs, weight_ref = refs[-count:], refs[len(args)]
+        value = jnp.concatenate([ref[...] for ref in refs[: len(args)]])
+        if rows < 128:
+            value = jnp.concatenate([value] * (128 // rows))
+        for start in range(0, columns, TILE):
+            at = slice(start, start + TILE)
+            result = dot(value, weight_ref[:, at])
+            for p in range(WIDTH):
+                for i, out_ref in enumerate(outs):
+                    n = (p * count + i) * piece
+                    out_ref[p * piece : (p + 1) * piece, at] = result[
+                        n : n + piece
+                    ].astype(out_ref.dtype)
+
+    return call(kernel, shapes, (*args, weight), "down")
+
+
 def add_kernel(part_ref, got_ref, out_ref):
     out_ref[...] = narrow(part_ref[...] + widen(got_ref[...]))
 
@@ -377,6 +413,7 @@
 
     (share2,) = done(hidden(mine2, got2))
     over2 = swap(share2, "width", CORES)
+    early2 = swap(share2, "width", 1)
     mine3, send3, mine4, send4 = done(add_cores(keep, cores, group, split=2))
     payload = done(join_rows(send4, share5))
     core0 = tick(swap(joined0, "width", 1))
@@ -384,22 +421,30 @@
         combine(joined0, [core0], down_weight, (jnp.float32, jnp.float32))
     )
     got4 = swap(tick(payload), "width", CORES)
-    over2, add1 = ticks([over2, add1])
-    joined2 = done(join(share2, over2))
-    core2 = ticks(parts_of(joined2, 3))
+    over2, add1, early2 = ticks([over2, add1, early2])
+    done(over2)
+    core2 = ticks(parts_of(over2, 2))
     cross2, far2 = done(
-        combine(joined2, core2, down_weight, (jnp.float32, jnp.bfloat16))
+        combine_parts(
+            (share2, over2),
+            (early2, done(join_columns(*core2))),
+            down_weight,
+            (jnp.float32, jnp.bfloat16),
+        )
     )
     far2 = swap(far2, AXIS, 1)
 
     got4 = tick(got4)
     share4, joined5 = done(hidden(mine4, got4, None, share5))
     over4 = swap(share4, "width", CORES)
-    over4 = tick(over4)
-    joined4 = done(join(share4, over4))
+    early4 = swap(share4, "width", 1)
+    over4, early4 = ticks([over4, early4])
+    done(over4)
     got3 = swap(tick(send3), "width", CORES)
-    core4 = ticks(parts_of(joined4, 2))
-    (far3,) = done(combine(joined4, core4, down_weight, (jnp.bfloat16,)))
+    core4 = tick(swap(over4, "width", 1))
+    (far3,) = done(
+        combine_parts((share4, over4), (early4, core4), down_weight, (jnp.bfloat16,))
+    )
     far3 = swap(far3, AXIS, 1)
     far2 = tick(far2)
     add2 = done(call(add_kernel, array(stay, tokens.shape[1]), (cross2, far2), "add"))

time: 130 us -> 130 us (level)
    pallas_call x41 -> x39, Pallas kernels: 32.9 us -> 32.8 us  [call(): pl.pallas_call(kernel, out_shape=shapes, in_specs=[VMEM] * len(args), out...]
  transfers between devices with their start and end apart: 47 -> 47, of which waited for: 28 -> 26; matrix products, arithmetic and copies ran while one was open for 0% -> 0% of each run, Pallas kernels for 24% -> 24%
where the time goes in v6:
time: 130 us
  waiting for transfers between devices  55.2 us (42%)
  starting transfers between devices  35.9 us (28%)
  Pallas kernels  32.8 us (25%)
  local copies, waits for them, and re-layouts  4.53 us (3%)
    ppermute x47, waiting for transfers between devices, swap(): return lax.ppermute(value, axis, [(i, i ^ mask) for i in range(size)])  55.2 us
    ppermute x47, starting transfers between devices, swap(): return lax.ppermute(value, axis, [(i, i ^ mask) for i in range(size)])  35.9 us
    pallas_call x39, Pallas kernels, call(): pl.pallas_call(kernel, out_shape=shapes, in_specs=[VMEM] * len(args), out...  32.8 us
    unnamed x20, local copies, waits for them, and re-layouts  4.53 us
  transfers between devices with their start and end apart: 47, of which 26 were waited for; matrix products, arithmetic and copies ran while one was open for 0% of the time, Pallas kernels for 24%

profile of v6, /device:TPU:0, one launch (start us, length us, event | category | flops | bytes accessed | tf_op | source)
XLA Modules:
  0.0 129.7 jit_solution(4735247149988562097)
XLA Ops:
  0.7 3.1 %collective-permute-start = (bf16[128,2048]{1,0:T(8,128)(2,1)}, bf16[128,2048]{1,0:T(8,128)(2,1)S(1)}, u32[]{:S(2)}, u32[]{:S(2)}) collective-permute-start(bf16[128,2048]{1,0:T(8,128)(2,1)} %tokens_ref.1), channel_id=1, source_target_pairs={{0,4},{4,0},{8,12},{12,8},{1,5},{5,1},{9,13},{13,9},{2,6},{6,2},{1... | collective-permute-start | bytes 1572872 | tf_op jit(solution)/shard_map/ppermute | solution.py:23
  3.8 1.8 %copy-done.1 = bf16[128,2048]{1,0:T(8,128)(2,1)S(1)} copy-done((bf16[128,2048]{1,0:T(8,128)(2,1)S(1)}, bf16[128,2048]{1,0:T(8,128)(2,1)}, u32[]{:S(2)}) %copy-start.1) | copy-done | bytes 524312
  6.0 2.1 %gate.4 = (bf16[64,7168]{1,0:T(8,128)(2,1)S(1)}, bf16[64,2304]{1,0:T(8,128)(2,1)S(1)}, bf16[64,2432]{1,0:T(8,128)(2,1)S(1)}, bf16[64,2432]{1,0:T(8,128)(2,1)S(1)}) custom-call(bf16[128,2048]{1,0:T(8,128)(2,1)S(1)} %arrange.2.refs_0_.block_ref, bf16[2048,3584]{1,0:T(8,128)(2,1)S(1)} %copy-done), custom_call_target="tpu_custom_call" | custom-call | flops 3758096384 | bytes 14680064 | tf_op jit(solution)/shard_map/gate/pallas_call | solution.py:48
  8.4 1.2 slice-done.6
  10.4 2.2 %up.4 = (bf16[64,7168]{1,0:T(8,128)(2,1)S(1)}, bf16[64,2304]{1,0:T(8,128)(2,1)S(1)}, bf16[64,2432]{1,0:T(8,128)(2,1)S(1)}, bf16[64,2432]{1,0:T(8,128)(2,1)S(1)}) custom-call(bf16[128,2048]{1,0:T(8,128)(2,1)S(1)} %arrange.2.refs_0_.block_ref, bf16[2048,3584]{1,0:T(8,128)(2,1)S(1)} %bitcast.5, ...), custom_call_target="tpu_custom_call", output_to_operand_aliasing={{0}: (2, {}), {1}: (3, {}), {2}: (4, {}), {3}: (5, {})} | custom-call | flops 1 | bytes 1 | tf_op jit(solution)/shard_map/up/pallas_call | solution.py:48
  13.7 3.7 %collective-permute-start.4 = (bf16[64,2048]{1,0:T(8,128)(2,1)S(1)}, bf16[64,2048]{1,0:T(8,128)(2,1)S(1)}, u32[]{:S(2)}, u32[]{:S(2)}) collective-permute-start(bf16[64,2048]{1,0:T(8,128)(2,1)S(1)} %get-tuple-element.146), channel_id=1, source_target_pairs={{0,8},{4,12},{8,0},{12,4},{1,9},{5,13},{9,1},{13,5},{2,10},{6,14},... | collective-permute-start | bytes 786440 | tf_op jit(solution)/shard_map/ppermute | solution.py:23
  17.6 1.5 %collective-permute-start.7 = (bf16[64,3584]{1,0:T(8,128)(2,1)S(1)}, bf16[64,3584]{1,0:T(8,128)(2,1)S(1)}, u32[]{:S(2)}, u32[]{:S(2)}) collective-permute-start(bf16[64,3584]{1,0:T(8,128)(2,1)S(1)} %get-tuple-element.157), channel_id=1, source_target_pairs={{0,2},{1,3},{2,0},{3,1},{4,6},{5,7},{6,4},{7,5},{8,10},{9,11},{10,... | collective-permute-start | bytes 1376264 | tf_op jit(solution)/shard_map/ppermute | solution.py:23
  19.2 2.1 %gate.5 = (bf16[64,7168]{1,0:T(8,128)(2,1)S(1)}, bf16[32,4736]{1,0:T(8,128)(2,1)S(1)}, bf16[32,2432]{1,0:T(8,128)(2,1)S(1)}, bf16[32,3584]{1,0:T(8,128)(2,1)S(1)}, bf16[32,3584]{1,0:T(8,128)(2,1)S(1)}) custom-call(bf16[128,2048]{1,0:T(8,128)(2,1)S(1)} %arrange.3.refs_0_, bf16[2048,3584]{1,0:T(8,128)(2,1)S(1)} %copy-done), custom_call_target="tpu_custom_call" | custom-call | flops 1 | bytes 1 | tf_op jit(solution)/shard_map/gate/pallas_call | solution.py:48
  21.3 2.2 %up.5 = (bf16[64,7168]{1,0:T(8,128)(2,1)S(1)}, bf16[32,4736]{1,0:T(8,128)(2,1)S(1)}, bf16[32,2432]{1,0:T(8,128)(2,1)S(1)}, bf16[32,3584]{1,0:T(8,128)(2,1)S(1)}, bf16[32,3584]{1,0:T(8,128)(2,1)S(1)}) custom-call(bf16[128,2048]{1,0:T(8,128)(2,1)S(1)} %arrange.3.refs_0_, ...), custom_call_target="tpu_custom_call", output_to_operand_aliasing={{0}: (2, {}), {1}: (3, {}), {2}: (4, {}), {3}: (5, {}), {4}... | custom-call | flops 1 | bytes 1 | tf_op jit(solution)/shard_map/up/pallas_call | solution.py:48
  23.5 6.4 %collective-permute-done.4.refs_0_ = bf16[64,2048]{1,0:T(8,128)(2,1)S(1)} collective-permute-done((bf16[64,2048]{1,0:T(8,128)(2,1)S(1)}, bf16[64,2048]{1,0:T(8,128)(2,1)S(1)}, u32[]{:S(2)}, u32[]{:S(2)}) %collective-permute-start.4) | collective-permute-done | bytes 262176 | tf_op jit(solution)/shard_map/ppermute | solution.py:23
  30.4 1.3 %collective-permute-done.6.refs_2_ = bf16[32,2432]{1,0:T(8,128)(2,1)S(1)} collective-permute-done((bf16[32,2432]{1,0:T(8,128)(2,1)S(1)}, bf16[32,2432]{1,0:T(8,128)(2,1)S(1)}, u32[]{:S(2)}, u32[]{:S(2)}) %collective-permute-start.6) | collective-permute-done | bytes 155680 | tf_op jit(solution)/shard_map/ppermute | solution.py:23
  32.0 1.6 %collective-permute-start.8 = (bf16[64,3584]{1,0:T(8,128)(2,1)S(1)}, bf16[64,3584]{1,0:T(8,128)(2,1)S(1)}, u32[]{:S(2)}, u32[]{:S(2)}) collective-permute-start(bf16[64,3584]{1,0:T(8,128)(2,1)S(1)} %get-tuple-element.160), channel_id=1, source_target_pairs={{0,2},{1,3},{2,0},{3,1},{4,6},{5,7},{6,4},{7,5},{8,10},{9,11},{10,... | collective-permute-start | bytes 1376264 | tf_op jit(solution)/shard_map/ppermute | solution.py:23
  34.4 3.4 %collective-permute-start.13 = (bf16[64,2048]{1,0:T(8,128)(2,1)S(1)}, bf16[64,2048]{1,0:T(8,128)(2,1)S(1)}, u32[]{:S(2)}, u32[]{:S(2)}) collective-permute-start(bf16[64,2048]{1,0:T(8,128)(2,1)S(1)} %get-tuple-element.179), channel_id=1, source_target_pairs={{0,8},{4,12},{8,0},{12,4},{1,9},{5,13},{9,1},{13,5},{2,10},{6,14},... | collective-permute-start | bytes 786440 | tf_op jit(solution)/shard_map/ppermute | solution.py:23
  38.2 1.0 collective-permute-done.10.refs_2_
  39.6 5.0 %collective-permute-done.8.refs_1_ = bf16[64,3584]{1,0:T(8,128)(2,1)S(1)} collective-permute-done((bf16[64,3584]{1,0:T(8,128)(2,1)S(1)}, bf16[64,3584]{1,0:T(8,128)(2,1)S(1)}, u32[]{:S(2)}, u32[]{:S(2)}) %collective-permute-start.8) | collective-permute-done | bytes 458784 | tf_op jit(solution)/shard_map/ppermute | solution.py:23
  44.8 1.6 %collective-permute-start.19 = (bf16[48,3584]{1,0:T(8,128)(2,1)S(1)}, bf16[48,3584]{1,0:T(8,128)(2,1)S(1)}, u32[]{:S(2)}, u32[]{:S(2)}) collective-permute-start(bf16[48,3584]{1,0:T(8,128)(2,1)S(1)} %get-tuple-element.191), channel_id=1, source_target_pairs={{0,2},{1,3},{2,0},{3,1},{4,6},{5,7},{6,4},{7,5},{8,10},{9,11},{10,... | collective-permute-start | bytes 1032200 | tf_op jit(solution)/shard_map/ppermute | solution.py:23
  47.1 2.1 %gate.6 = (bf16[64,7168]{1,0:T(8,128)(2,1)S(1)}, bf16[64,2304]{1,0:T(8,128)(2,1)S(1)}, bf16[64,2432]{1,0:T(8,128)(2,1)S(1)}, bf16[64,2432]{1,0:T(8,128)(2,1)S(1)}) custom-call(bf16[64,2048]{1,0:T(8,128)(2,1)S(1)} %collective-permute-done.4.refs_0_, bf16[64,2048]{1,0:T(8,128)(2,1)S(1)} %collective-permute-done.12.refs_1_, bf16[2048,3584]{1,0:T(8,128)(2,1)S(1)} %copy-done), custom_call_target="tpu_custom_call" | custom-call | flops 1 | bytes 1 | tf_op jit(solution)/shard_map/gate/pallas_call | solution.py:48
  49.2 2.4 %up.6 = (bf16[64,7168]{1,0:T(8,128)(2,1)S(1)}, bf16[64,2304]{1,0:T(8,128)(2,1)S(1)}, bf16[64,2432]{1,0:T(8,128)(2,1)S(1)}, bf16[64,2432]{1,0:T(8,128)(2,1)S(1)}) custom-call(bf16[64,2048]{1,0:T(8,128)(2,1)S(1)} %collective-permute-done.4.refs_0_, ...), custom_call_target="tpu_custom_call", output_to_operand_aliasing={{0}: (3, {}), {1}: (4, {}), {2}: (5, {}), {3}: (6, {})} | custom-call | flops 1 | bytes 1 | tf_op jit(solution)/shard_map/up/pallas_call | solution.py:48
  52.3 1.9 %collective-permute-done.14.refs_1_ = bf16[64,2304]{1,0:T(8,128)(2,1)S(1)} collective-permute-done((bf16[64,2304]{1,0:T(8,128)(2,1)S(1)}, bf16[64,2304]{1,0:T(8,128)(2,1)S(1)}, u32[]{:S(2)}, u32[]{:S(2)}) %collective-permute-start.14) | collective-permute-done | bytes 294944 | tf_op jit(solution)/shard_map/ppermute | solution.py:23
  55.7 1.2 collective-permute-done.20.refs_0_
  57.1 2.1 %down.6 = bf16[64,2048]{1,0:T(8,128)(2,1)S(1)} custom-call(bf16[32,3584]{1,0:T(8,128)(2,1)S(1)} %get-tuple-element.194.mine_ref, bf16[32,1792]{1,0:T(8,128)(2,1)S(1)} %collective-permute-done.20.refs_0_, bf16[32,1792]{1,0:T(8,128)(2,1)S(1)} %collective-permute-done.21.refs_1_, bf16[3584,2048]{1,0:T(8,128)(2,1)S(1)} %bitcast.3), custom_call_target="tpu_custom_call" | custom-call | flops 1 | bytes 1 | tf_op jit(solution)/shard_map/down/pallas_call | solution.py:48
  59.2 1.7 %collective-permute-done.18.refs_1_ = bf16[64,2048]{1,0:T(8,128)(2,1)S(1)} collective-permute-done((bf16[64,2048]{1,0:T(8,128)(2,1)S(1)}, bf16[64,2048]{1,0:T(8,128)(2,1)S(1)}, u32[]{:S(2)}, u32[]{:S(2)}) %collective-permute-start.18) | collective-permute-done | bytes 262176 | tf_op jit(solution)/shard_map/ppermute | solution.py:23
  61.0 2.1 %gate.7 = (bf16[64,7168]{1,0:T(8,128)(2,1)S(1)}, bf16[64,2304]{1,0:T(8,128)(2,1)S(1)}, bf16[64,2432]{1,0:T(8,128)(2,1)S(1)}, bf16[64,2432]{1,0:T(8,128)(2,1)S(1)}) custom-call(bf16[64,2048]{1,0:T(8,128)(2,1)S(1)} %collective-permute-done.13.refs_0_, bf16[64,2048]{1,0:T(8,128)(2,1)S(1)} %collective-permute-done.18.refs_1_, bf16[2048,3584]{1,0:T(8,128)(2,1)S(1)} %copy-done), custom_call_target="tpu_custom_call" | custom-call | flops 1 | bytes 1 | tf_op jit(solution)/shard_map/gate/pallas_call | solution.py:48
  63.0 2.2 %up.7 = (bf16[64,7168]{1,0:T(8,128)(2,1)S(1)}, bf16[64,2304]{1,0:T(8,128)(2,1)S(1)}, bf16[64,2432]{1,0:T(8,128)(2,1)S(1)}, bf16[64,2432]{1,0:T(8,128)(2,1)S(1)}) custom-call(bf16[64,2048]{1,0:T(8,128)(2,1)S(1)} %collective-permute-done.13.refs_0_, ...), custom_call_target="tpu_custom_call", output_to_operand_aliasing={{0}: (3, {}), {1}: (4, {}), {2}: (5, {}), {3}: (6, {})} | custom-call | flops 1 | bytes 1 | tf_op jit(solution)/shard_map/up/pallas_call | solution.py:48
  65.9 1.0 collective-permute-done.22.refs_1_
  68.8 2.1 %down.7 = (f32[64,2048]{1,0:T(8,128)S(1)}, f32[64,2048]{1,0:T(8,128)S(1)}) custom-call(bf16[64,3584]{1,0:T(8,128)(2,1)S(1)} %get-tuple-element.171.mine_ref, bf16[64,3584]{1,0:T(8,128)(2,1)S(1)} %collective-permute-done.11.refs_0_, bf16[3584,2048]{1,0:T(8,128)(2,1)S(1)} %bitcast.3), custom_call_target="tpu_custom_call" | custom-call | flops 1 | bytes 1 | tf_op jit(solution)/shard_map/down/pallas_call | solution.py:48
  70.9 1.6 %collective-permute-start.28 = (bf16[48,3584]{1,0:T(8,128)(2,1)S(1)}, bf16[48,3584]{1,0:T(8,128)(2,1)S(1)}, u32[]{:S(2)}, u32[]{:S(2)}) collective-permute-start(bf16[48,3584]{1,0:T(8,128)(2,1)S(1)} %stack.1), channel_id=1, source_target_pairs={{0,2},{1,3},{2,0},{3,1},{4,6},{5,7},{6,4},{7,5},{8,10},{9,11},{10,... | collective-permute-start | bytes 1032200 | tf_op jit(solution)/shard_map/ppermute | solution.py:23
  72.5 2.8 %collective-permute-done.26 = bf16[64,2048]{1,0:T(8,128)(2,1)S(1)} collective-permute-done((bf16[64,2048]{1,0:T(8,128)(2,1)S(1)}, bf16[64,2048]{1,0:T(8,128)(2,1)S(1)}, u32[]{:S(2)}, u32[]{:S(2)}) %collective-permute-start.26) | collective-permute-done | bytes 262176 | tf_op jit(solution)/shard_map/ppermute | solution.py:23
  75.3 1.2 collective-permute-done.25.mine_ref.refs_1_
  78.1 2.3 %down.8 = (f32[64,2048]{1,0:T(8,128)S(1)}, bf16[64,2048]{1,0:T(8,128)(2,1)S(1)}) custom-call(bf16[32,3584]{1,0:T(8,128)(2,1)S(1)} %hidden.9.refs_0_, bf16[32,3584]{1,0:T(8,128)(2,1)S(1)} %collective-permute-done.25.mine_ref.refs_1_, bf16[32,3584]{1,0:T(8,128)(2,1)S(1)} %collective-permute-done.27.refs_2_, bf16[32,3584]{1,0:T(8,128)(2,1)S(1)} %columns.1.refs_3_, ...), custom_call_target="tpu_custom_call" | custom-call | flops 1 | bytes 1 | tf_op jit(solution)/shard_map/down/pallas_call | solution.py:48
  80.4 2.6 %collective-permute-done.28.refs_1_ = bf16[48,3584]{1,0:T(8,128)(2,1)S(1)} collective-permute-done((bf16[48,3584]{1,0:T(8,128)(2,1)S(1)}, bf16[48,3584]{1,0:T(8,128)(2,1)S(1)}, u32[]{:S(2)}, u32[]{:S(2)}) %collective-permute-start.28) | collective-permute-done | bytes 344096 | tf_op jit(solution)/shard_map/ppermute | solution.py:23
  84.6 3.4 %collective-permute-done.31.refs_1_ = bf16[16,3584]{1,0:T(8,128)(2,1)S(1)} collective-permute-done((bf16[16,3584]{1,0:T(8,128)(2,1)S(1)}, bf16[16,3584]{1,0:T(8,128)(2,1)S(1)}, u32[]{:S(2)}, u32[]{:S(2)}) %collective-permute-start.31) | collective-permute-done | bytes 114720 | tf_op jit(solution)/shard_map/ppermute | solution.py:23
  88.5 1.3 %collective-permute-done.33.refs_3_ = bf16[16,3584]{1,0:T(8,128)(2,1)S(1)} collective-permute-done((bf16[16,3584]{1,0:T(8,128)(2,1)S(1)}, bf16[16,3584]{1,0:T(8,128)(2,1)S(1)}, u32[]{:S(2)}, u32[]{:S(2)}) %collective-permute-start.33) | collective-permute-done | bytes 114720 | tf_op jit(solution)/shard_map/ppermute | solution.py:23
  89.8 2.1 %down.9 = bf16[64,2048]{1,0:T(8,128)(2,1)S(1)} custom-call(bf16[16,3584]{1,0:T(8,128)(2,1)S(1)} %get-tuple-element.228.refs_0_, bf16[16,3584]{1,0:T(8,128)(2,1)S(1)} %collective-permute-done.31.refs_1_, bf16[16,3584]{1,0:T(8,128)(2,1)S(1)} %collective-permute-done.32.refs_2_, bf16[16,3584]{1,0:T(8,128)(2,1)S(1)} %collective-permute-done.33.refs_3_, ...), custom_call_target="tpu_custom_call" | custom-call | flops 1 | bytes 1 | tf_op jit(solution)/shard_map/down/pallas_call | solution.py:48
  91.9 1.1 collective-permute-start.34
  93.0 2.5 %collective-permute-start.36 = (bf16[64,2048]{1,0:T(8,128)(2,1)S(1)}, bf16[64,2048]{1,0:T(8,128)(2,1)S(1)}, u32[]{:S(2)}, u32[]{:S(2)}) collective-permute-start(bf16[64,2048]{1,0:T(8,128)(2,1)S(1)} %add.26), channel_id=1, source_target_pairs={{0,8},{4,12},{8,0},{12,4},{1,9},{5,13},{9,1},{13,5},{2,10},{6,14},... | collective-permute-start | bytes 786440 | tf_op jit(solution)/shard_map/ppermute | solution.py:23
  96.2 1.5 %collective-permute-start.38 = (bf16[16,3584]{1,0:T(8,128)(2,1)S(1)}, bf16[16,3584]{1,0:T(8,128)(2,1)S(1)}, u32[]{:S(2)}, u32[]{:S(2)}) collective-permute-start(bf16[16,3584]{1,0:T(8,128)(2,1)S(1)} %hidden.11.share_ref), channel_id=1, source_target_pairs={{0,2},{1,3},{2,0},{3,1},{4,6},{5,7},{6,4},{7,5},{8,10},{9,11},{10,... | collective-permute-start | bytes 344072 | tf_op jit(solution)/shard_map/ppermute | solution.py:23
  97.7 2.1 %down.10 = bf16[64,2048]{1,0:T(8,128)(2,1)S(1)} custom-call(bf16[32,3584]{1,0:T(8,128)(2,1)S(1)} %get-tuple-element.237.mine_ref, bf16[32,1792]{1,0:T(8,128)(2,1)S(1)} %collective-permute-done.39.refs_0_, bf16[32,1792]{1,0:T(8,128)(2,1)S(1)} %collective-permute-done.40.refs_1_, bf16[3584,2048]{1,0:T(8,128)(2,1)S(1)} %bitcast.3), custom_call_target="tpu_custom_call" | custom-call | flops 1 | bytes 1 | tf_op jit(solution)/shard_map/down/pallas_call | solution.py:48
  99.8 1.6 %collective-permute-done.38.got_ref = bf16[16,3584]{1,0:T(8,128)(2,1)S(1)} collective-permute-done((bf16[16,3584]{1,0:T(8,128)(2,1)S(1)}, bf16[16,3584]{1,0:T(8,128)(2,1)S(1)}, u32[]{:S(2)}, u32[]{:S(2)}) %collective-permute-start.38) | collective-permute-done | bytes 114720 | tf_op jit(solution)/shard_map/ppermute | solution.py:23
  102.0 0.9 collective-permute-start.43
  103.0 2.1 %down.11.part_ref = f32[64,2048]{1,0:T(8,128)S(1)} custom-call(bf16[32,3584]{1,0:T(8,128)(2,1)S(1)} %join.1.mine_ref, bf16[32,1792]{1,0:T(8,128)(2,1)S(1)} %collective-permute-done.41.refs_0_, bf16[32,1792]{1,0:T(8,128)(2,1)S(1)} %collective-permute-done.42.refs_1_, bf16[3584,2048]{1,0:T(8,128)(2,1)S(1)} %bitcast.3), custom_call_target="tpu_custom_call" | custom-call | flops 1 | bytes 1 | tf_op jit(solution)/shard_map/down/pallas_call | solution.py:48
  105.1 1.7 %collective-permute-done.34.got_ref = bf16[64,2048]{1,0:T(8,128)(2,1)S(1)} collective-permute-done((bf16[64,2048]{1,0:T(8,128)(2,1)S(1)}, bf16[64,2048]{1,0:T(8,128)(2,1)S(1)}, u32[]{:S(2)}, u32[]{:S(2)}) %collective-permute-start.34) | collective-permute-done | bytes 262176 | tf_op jit(solution)/shard_map/ppermute | solution.py:23
  106.8 2.0 %collective-permute-start.44 = (bf16[64,2048]{1,0:T(8,128)(2,1)S(1)}, bf16[64,2048]{1,0:T(8,128)(2,1)S(1)}, u32[]{:S(2)}, u32[]{:S(2)}) collective-permute-start(bf16[64,2048]{1,0:T(8,128)(2,1)S(1)} %add.27), channel_id=1, source_target_pairs={{0,8},{4,12},{8,0},{12,4},{1,9},{5,13},{9,1},{13,5},{2,10},{6,14},... | collective-permute-start | bytes 786440 | tf_op jit(solution)/shard_map/ppermute | solution.py:23
  108.9 7.0 %collective-permute-done.43 = bf16[64,2048]{1,0:T(8,128)(2,1)S(1)} collective-permute-done((bf16[64,2048]{1,0:T(8,128)(2,1)S(1)}, bf16[64,2048]{1,0:T(8,128)(2,1)S(1)}, u32[]{:S(2)}, u32[]{:S(2)}) %collective-permute-start.43) | collective-permute-done | bytes 262176 | tf_op jit(solution)/shard_map/ppermute | solution.py:23
  115.9 4.5 %collective-permute-done.44 = bf16[64,2048]{1,0:T(8,128)(2,1)S(1)} collective-permute-done((bf16[64,2048]{1,0:T(8,128)(2,1)S(1)}, bf16[64,2048]{1,0:T(8,128)(2,1)S(1)}, u32[]{:S(2)}, u32[]{:S(2)}) %collective-permute-start.44) | collective-permute-done | bytes 262176 | tf_op jit(solution)/shard_map/ppermute | solution.py:23
  120.6 4.5 %collective-permute-done.45.other_ref = f32[1,2048]{1,0:T(1,128)S(1)} collective-permute-done((f32[1,2048]{1,0:T(1,128)S(1)}, f32[1,2048]{1,0:T(1,128)S(1)}, u32[]{:S(2)}, u32[]{:S(2)}) %collective-permute-start.45) | collective-permute-done | bytes 8224 | tf_op jit(solution)/shard_map/ppermute | solution.py:23
  125.2 1.6 %collective-permute-start.46 = (f32[1,2048]{1,0:T(1,128)S(1)}, f32[1,2048]{1,0:T(1,128)S(1)}, u32[]{:S(2)}, u32[]{:S(2)}) collective-permute-start(f32[1,2048]{1,0:T(1,128)S(1)} %peak.1.refs_0_), channel_id=1, source_target_pairs={{0,4},{4,0},{8,12},{12,8},{1,5},{5,1},{9,13},{13,9},{2,6},{6,2},{1... | collective-permute-start | bytes 24584 | tf_op jit(solution)/shard_map/ppermute | solution.py:23
  126.7 2.1 %collective-permute-done.46.refs_1_ = f32[1,2048]{1,0:T(1,128)S(1)} collective-permute-done((f32[1,2048]{1,0:T(1,128)S(1)}, f32[1,2048]{1,0:T(1,128)S(1)}, u32[]{:S(2)}, u32[]{:S(2)}) %collective-permute-start.46) | collective-permute-done | bytes 8224 | tf_op jit(solution)/shard_map/ppermute | solution.py:23
  (110 shorter events, 17.1 us)
Async XLA Ops:
  0.7 18.5 %collective-permute-start = (bf16[128,2048]{1,0:T(8,128)(2,1)}, bf16[128,2048]{1,0:T(8,128)(2,1)S(1)}, u32[]{:S(2)}, u32[]{:S(2)}) collective-permute-start(bf16[128,2048]{1,0:T(8,128)(2,1)} %tokens_ref.1), channel_id=1, source_target_pairs={{0,4},{4,0},{8,12},{12,8},{1,5},{5,1},{9,13},{13,9},{2,6},{6,2},{1... | collective-permute-start | bytes 1572872 | tf_op jit(solution)/shard_map/ppermute | solution.py:23
  12.6 4.8 %collective-permute-start.2 = (bf16[64,2432]{1,0:T(8,128)(2,1)S(1)}, bf16[64,2432]{1,0:T(8,128)(2,1)S(1)}, u32[]{:S(2)}, u32[]{:S(2)}) collective-permute-start(bf16[64,2432]{1,0:T(8,128)(2,1)S(1)} %get-tuple-element.132), channel_id=1, source_target_pairs={{0,1},{1,0},{2,3},{3,2},{4,5},{5,4},{6,7},{7,6},{8,9},{9,8},{10,11... | collective-permute-start | bytes 933896 | tf_op jit(solution)/shard_map/ppermute | solution.py:23
  13.1 4.3 %collective-permute-start.3 = (bf16[64,2432]{1,0:T(8,128)(2,1)S(1)}, bf16[64,2432]{1,0:T(8,128)(2,1)S(1)}, u32[]{:S(2)}, u32[]{:S(2)}) collective-permute-start(bf16[64,2432]{1,0:T(8,128)(2,1)S(1)} %get-tuple-element.133), channel_id=1, source_target_pairs={{0,1},{1,0},{2,3},{3,2},{4,5},{5,4},{6,7},{7,6},{8,9},{9,8},{10,11... | collective-permute-start | bytes 933896 | tf_op jit(solution)/shard_map/ppermute | solution.py:23
  13.2 4.2 %collective-permute-start.1 = (bf16[64,2304]{1,0:T(8,128)(2,1)S(1)}, bf16[64,2304]{1,0:T(8,128)(2,1)S(1)}, u32[]{:S(2)}, u32[]{:S(2)}) collective-permute-start(bf16[64,2304]{1,0:T(8,128)(2,1)S(1)} %get-tuple-element.131), channel_id=1, source_target_pairs={{0,1},{1,0},{2,3},{3,2},{4,5},{5,4},{6,7},{7,6},{8,9},{9,8},{10,11... | collective-permute-start | bytes 884744 | tf_op jit(solution)/shard_map/ppermute | solution.py:23
  13.7 16.3 %collective-permute-start.4 = (bf16[64,2048]{1,0:T(8,128)(2,1)S(1)}, bf16[64,2048]{1,0:T(8,128)(2,1)S(1)}, u32[]{:S(2)}, u32[]{:S(2)}) collective-permute-start(bf16[64,2048]{1,0:T(8,128)(2,1)S(1)} %get-tuple-element.146), channel_id=1, source_target_pairs={{0,8},{4,12},{8,0},{12,4},{1,9},{5,13},{9,1},{13,5},{2,10},{6,14},... | collective-permute-start | bytes 786440 | tf_op jit(solution)/shard_map/ppermute | solution.py:23
  17.6 14.2 %collective-permute-start.7 = (bf16[64,3584]{1,0:T(8,128)(2,1)S(1)}, bf16[64,3584]{1,0:T(8,128)(2,1)S(1)}, u32[]{:S(2)}, u32[]{:S(2)}) collective-permute-start(bf16[64,3584]{1,0:T(8,128)(2,1)S(1)} %get-tuple-element.157), channel_id=1, source_target_pairs={{0,2},{1,3},{2,0},{3,1},{4,6},{5,7},{6,4},{7,5},{8,10},{9,11},{10,... | collective-permute-start | bytes 1376264 | tf_op jit(solution)/shard_map/ppermute | solution.py:23
  29.9 1.8 %collective-permute-start.5 = (bf16[32,4736]{1,0:T(8,128)(2,1)S(1)}, bf16[32,4736]{1,0:T(8,128)(2,1)S(1)}, u32[]{:S(2)}, u32[]{:S(2)}) collective-permute-start(bf16[32,4736]{1,0:T(8,128)(2,1)S(1)} %get-tuple-element.151), channel_id=1, source_target_pairs={{0,1},{1,0},{2,3},{3,2},{4,5},{5,4},{6,7},{7,6},{8,9},{9,8},{10,11... | collective-permute-start | bytes 909320 | tf_op jit(solution)/shard_map/ppermute | solution.py:23
  29.9 1.8 %collective-permute-start.6 = (bf16[32,2432]{1,0:T(8,128)(2,1)S(1)}, bf16[32,2432]{1,0:T(8,128)(2,1)S(1)}, u32[]{:S(2)}, u32[]{:S(2)}) collective-permute-start(bf16[32,2432]{1,0:T(8,128)(2,1)S(1)} %get-tuple-element.152), channel_id=1, source_target_pairs={{0,1},{1,0},{2,3},{3,2},{4,5},{5,4},{6,7},{7,6},{8,9},{9,8},{10,11... | collective-permute-start | bytes 466952 | tf_op jit(solution)/shard_map/ppermute | solution.py:23
  32.0 12.6 %collective-permute-start.8 = (bf16[64,3584]{1,0:T(8,128)(2,1)S(1)}, bf16[64,3584]{1,0:T(8,128)(2,1)S(1)}, u32[]{:S(2)}, u32[]{:S(2)}) collective-permute-start(bf16[64,3584]{1,0:T(8,128)(2,1)S(1)} %get-tuple-element.160), channel_id=1, source_target_pairs={{0,2},{1,3},{2,0},{3,1},{4,6},{5,7},{6,4},{7,5},{8,10},{9,11},{10,... | collective-permute-start | bytes 1376264 | tf_op jit(solution)/shard_map/ppermute | solution.py:23
  33.7 13.5 %collective-permute-start.12 = (bf16[64,2048]{1,0:T(8,128)(2,1)S(1)}, bf16[64,2048]{1,0:T(8,128)(2,1)S(1)}, u32[]{:S(2)}, u32[]{:S(2)}) collective-permute-start(bf16[64,2048]{1,0:T(8,128)(2,1)S(1)} %collective-permute-done.4.refs_0_), channel_id=1, source_target_pairs={{0,4},{4,0},{8,12},{12,8},{1,5},{5,1},{9,13},{13,9},{2,6},{6,2},{1... | collective-permute-start | bytes 786440 | tf_op jit(solution)/shard_map/ppermute | solution.py:23
  34.4 17.3 %collective-permute-start.13 = (bf16[64,2048]{1,0:T(8,128)(2,1)S(1)}, bf16[64,2048]{1,0:T(8,128)(2,1)S(1)}, u32[]{:S(2)}, u32[]{:S(2)}) collective-permute-start(bf16[64,2048]{1,0:T(8,128)(2,1)S(1)} %get-tuple-element.179), channel_id=1, source_target_pairs={{0,8},{4,12},{8,0},{12,4},{1,9},{5,13},{9,1},{13,5},{2,10},{6,14},... | collective-permute-start | bytes 786440 | tf_op jit(solution)/shard_map/ppermute | solution.py:23
  37.7 1.5 %collective-permute-start.10 = (bf16[32,3584]{1,0:T(8,128)(2,1)S(1)}, bf16[32,3584]{1,0:T(8,128)(2,1)S(1)}, u32[]{:S(2)}, u32[]{:S(2)}) collective-permute-start(bf16[32,3584]{1,0:T(8,128)(2,1)S(1)} %get-tuple-element.165), channel_id=1, source_target_pairs={{0,1},{1,0},{2,3},{3,2},{4,5},{5,4},{6,7},{7,6},{8,9},{9,8},{10,11... | collective-permute-start | bytes 688136 | tf_op jit(solution)/shard_map/ppermute | solution.py:23
  37.7 1.8 %collective-permute-start.9 = (bf16[32,3584]{1,0:T(8,128)(2,1)S(1)}, bf16[32,3584]{1,0:T(8,128)(2,1)S(1)}, u32[]{:S(2)}, u32[]{:S(2)}) collective-permute-start(bf16[32,3584]{1,0:T(8,128)(2,1)S(1)} %get-tuple-element.164), channel_id=1, source_target_pairs={{0,1},{1,0},{2,3},{3,2},{4,5},{5,4},{6,7},{7,6},{8,9},{9,8},{10,11... | collective-permute-start | bytes 688136 | tf_op jit(solution)/shard_map/ppermute | solution.py:23
  44.8 10.2 %collective-permute-start.19 = (bf16[48,3584]{1,0:T(8,128)(2,1)S(1)}, bf16[48,3584]{1,0:T(8,128)(2,1)S(1)}, u32[]{:S(2)}, u32[]{:S(2)}) collective-permute-start(bf16[48,3584]{1,0:T(8,128)(2,1)S(1)} %get-tuple-element.191), channel_id=1, source_target_pairs={{0,2},{1,3},{2,0},{3,1},{4,6},{5,7},{6,4},{7,5},{8,10},{9,11},{10,... | collective-permute-start | bytes 1032200 | tf_op jit(solution)/shard_map/ppermute | solution.py:23
  47.1 10.0 %slice-start.1 = ((s8[14680064]{0:T(1024)(128)(4,1)}), s8[4194304]{0:T(1024)(128)(4,1)S(1)}, s32[]{:S(2)}) async-start(s8[14680064]{0:T(1024)(128)(4,1)} %bitcast.2), calls=%async_computation.1 | async-start | bytes 8388608
  51.7 2.5 %collective-permute-start.15 = (bf16[64,2432]{1,0:T(8,128)(2,1)S(1)}, bf16[64,2432]{1,0:T(8,128)(2,1)S(1)}, u32[]{:S(2)}, u32[]{:S(2)}) collective-permute-start(bf16[64,2432]{1,0:T(8,128)(2,1)S(1)} %get-tuple-element.184), channel_id=1, source_target_pairs={{0,1},{1,0},{2,3},{3,2},{4,5},{5,4},{6,7},{7,6},{8,9},{9,8},{10,11... | collective-permute-start | bytes 933896 | tf_op jit(solution)/shard_map/ppermute | solution.py:23
  51.7 2.5 %collective-permute-start.16 = (bf16[64,2432]{1,0:T(8,128)(2,1)S(1)}, bf16[64,2432]{1,0:T(8,128)(2,1)S(1)}, u32[]{:S(2)}, u32[]{:S(2)}) collective-permute-start(bf16[64,2432]{1,0:T(8,128)(2,1)S(1)} %get-tuple-element.185), channel_id=1, source_target_pairs={{0,1},{1,0},{2,3},{3,2},{4,5},{5,4},{6,7},{7,6},{8,9},{9,8},{10,11... | collective-permute-start | bytes 933896 | tf_op jit(solution)/shard_map/ppermute | solution.py:23
  52.2 2.0 %collective-permute-start.14 = (bf16[64,2304]{1,0:T(8,128)(2,1)S(1)}, bf16[64,2304]{1,0:T(8,128)(2,1)S(1)}, u32[]{:S(2)}, u32[]{:S(2)}) collective-permute-start(bf16[64,2304]{1,0:T(8,128)(2,1)S(1)} %get-tuple-element.183), channel_id=1, source_target_pairs={{0,1},{1,0},{2,3},{3,2},{4,5},{5,4},{6,7},{7,6},{8,9},{9,8},{10,11... | collective-permute-start | bytes 884744 | tf_op jit(solution)/shard_map/ppermute | solution.py:23
  52.3 8.7 %collective-permute-start.18 = (bf16[64,2048]{1,0:T(8,128)(2,1)S(1)}, bf16[64,2048]{1,0:T(8,128)(2,1)S(1)}, u32[]{:S(2)}, u32[]{:S(2)}) collective-permute-start(bf16[64,2048]{1,0:T(8,128)(2,1)S(1)} %collective-permute-done.13.refs_0_), channel_id=1, source_target_pairs={{0,4},{4,0},{8,12},{12,8},{1,5},{5,1},{9,13},{13,9},{2,6},{6,2},{1... | collective-permute-start | bytes 786440 | tf_op jit(solution)/shard_map/ppermute | solution.py:23
  54.4 13.4 %collective-permute-start.17 = (bf16[64,3584]{1,0:T(8,128)(2,1)S(1)}, bf16[64,3584]{1,0:T(8,128)(2,1)S(1)}, u32[]{:S(2)}, u32[]{:S(2)}) collective-permute-start(bf16[64,3584]{1,0:T(8,128)(2,1)S(1)} %get-tuple-element.190), channel_id=1, source_target_pairs={{0,2},{1,3},{2,0},{3,1},{4,6},{5,7},{6,4},{7,5},{8,10},{9,11},{10,... | collective-permute-start | bytes 1376264 | tf_op jit(solution)/shard_map/ppermute | solution.py:23
  55.0 13.8 %collective-permute-start.11 = (bf16[64,3584]{1,0:T(8,128)(2,1)S(1)}, bf16[64,3584]{1,0:T(8,128)(2,1)S(1)}, u32[]{:S(2)}, u32[]{:S(2)}) collective-permute-start(bf16[64,3584]{1,0:T(8,128)(2,1)S(1)} %get-tuple-element.171.mine_ref), channel_id=1, source_target_pairs={{0,1},{1,0},{2,3},{3,2},{4,5},{5,4},{6,7},{7,6},{8,9},{9,8},{10,11... | collective-permute-start | bytes 1376264 | tf_op jit(solution)/shard_map/ppermute | solution.py:23
  55.1 1.9 %collective-permute-start.20 = (bf16[32,1792]{1,0:T(8,128)(2,1)S(1)}, bf16[32,1792]{1,0:T(8,128)(2,1)S(1)}, u32[]{:S(2)}, u32[]{:S(2)}) collective-permute-start(bf16[32,1792]{1,0:T(8,128)(2,1)S(1)} %get-tuple-element.195), channel_id=1, source_target_pairs={{0,1},{1,0},{2,3},{3,2},{4,5},{5,4},{6,7},{7,6},{8,9},{9,8},{10,11... | collective-permute-start | bytes 344072 | tf_op jit(solution)/shard_map/ppermute | solution.py:23
  55.7 1.4 %collective-permute-start.21 = (bf16[32,1792]{1,0:T(8,128)(2,1)S(1)}, bf16[32,1792]{1,0:T(8,128)(2,1)S(1)}, u32[]{:S(2)}, u32[]{:S(2)}) collective-permute-start(bf16[32,1792]{1,0:T(8,128)(2,1)S(1)} %get-tuple-element.196), channel_id=1, source_target_pairs={{0,1},{1,0},{2,3},{3,2},{4,5},{5,4},{6,7},{7,6},{8,9},{9,8},{10,11... | collective-permute-start | bytes 344072 | tf_op jit(solution)/shard_map/ppermute | solution.py:23
  65.3 1.6 %collective-permute-start.22 = (bf16[64,2304]{1,0:T(8,128)(2,1)S(1)}, bf16[64,2304]{1,0:T(8,128)(2,1)S(1)}, u32[]{:S(2)}, u32[]{:S(2)}) collective-permute-start(bf16[64,2304]{1,0:T(8,128)(2,1)S(1)} %get-tuple-element.205), channel_id=1, source_target_pairs={{0,1},{1,0},{2,3},{3,2},{4,5},{5,4},{6,7},{7,6},{8,9},{9,8},{10,11... | collective-permute-start | bytes 884744 | tf_op jit(solution)/shard_map/ppermute | solution.py:23
  65.4 2.0 %collective-permute-start.23 = (bf16[64,2432]{1,0:T(8,128)(2,1)S(1)}, bf16[64,2432]{1,0:T(8,128)(2,1)S(1)}, u32[]{:S(2)}, u32[]{:S(2)}) collective-permute-start(bf16[64,2432]{1,0:T(8,128)(2,1)S(1)} %get-tuple-element.206), channel_id=1, source_target_pairs={{0,1},{1,0},{2,3},{3,2},{4,5},{5,4},{6,7},{7,6},{8,9},{9,8},{10,11... | collective-permute-start | bytes 933896 | tf_op jit(solution)/shard_map/ppermute | solution.py:23
  65.9 2.0 %collective-permute-start.24 = (bf16[64,2432]{1,0:T(8,128)(2,1)S(1)}, bf16[64,2432]{1,0:T(8,128)(2,1)S(1)}, u32[]{:S(2)}, u32[]{:S(2)}) collective-permute-start(bf16[64,2432]{1,0:T(8,128)(2,1)S(1)} %get-tuple-element.207), channel_id=1, source_target_pairs={{0,1},{1,0},{2,3},{3,2},{4,5},{5,4},{6,7},{7,6},{8,9},{9,8},{10,11... | collective-permute-start | bytes 933896 | tf_op jit(solution)/shard_map/ppermute | solution.py:23
  66.9 8.3 %collective-permute-start.26 = (bf16[64,2048]{1,0:T(8,128)(2,1)S(1)}, bf16[64,2048]{1,0:T(8,128)(2,1)S(1)}, u32[]{:S(2)}, u32[]{:S(2)}) collective-permute-start(bf16[64,2048]{1,0:T(8,128)(2,1)S(1)} %down.6), channel_id=1, source_target_pairs={{0,4},{4,0},{8,12},{12,8},{1,5},{5,1},{9,13},{13,9},{2,6},{6,2},{1... | collective-permute-start | bytes 786440 | tf_op jit(solution)/shard_map/ppermute | solution.py:23
  68.0 8.5 %collective-permute-start.25 = (bf16[32,3584]{1,0:T(8,128)(2,1)S(1)}, bf16[32,3584]{1,0:T(8,128)(2,1)S(1)}, u32[]{:S(2)}, u32[]{:S(2)}) collective-permute-start(bf16[32,3584]{1,0:T(8,128)(2,1)S(1)} %hidden.9.refs_0_), channel_id=1, source_target_pairs={{0,2},{1,3},{2,0},{3,1},{4,6},{5,7},{6,4},{7,5},{8,10},{9,11},{10,... | collective-permute-start | bytes 688136 | tf_op jit(solution)/shard_map/ppermute | solution.py:23
  68.5 8.0 %collective-permute-start.27 = (bf16[32,3584]{1,0:T(8,128)(2,1)S(1)}, bf16[32,3584]{1,0:T(8,128)(2,1)S(1)}, u32[]{:S(2)}, u32[]{:S(2)}) collective-permute-start(bf16[32,3584]{1,0:T(8,128)(2,1)S(1)} %hidden.9.refs_0_), channel_id=1, source_target_pairs={{0,1},{1,0},{2,3},{3,2},{4,5},{5,4},{6,7},{7,6},{8,9},{9,8},{10,11... | collective-permute-start | bytes 688136 | tf_op jit(solution)/shard_map/ppermute | solution.py:23
  70.9 12.2 %collective-permute-start.28 = (bf16[48,3584]{1,0:T(8,128)(2,1)S(1)}, bf16[48,3584]{1,0:T(8,128)(2,1)S(1)}, u32[]{:S(2)}, u32[]{:S(2)}) collective-permute-start(bf16[48,3584]{1,0:T(8,128)(2,1)S(1)} %stack.1), channel_id=1, source_target_pairs={{0,2},{1,3},{2,0},{3,1},{4,6},{5,7},{6,4},{7,5},{8,10},{9,11},{10,... | collective-permute-start | bytes 1032200 | tf_op jit(solution)/shard_map/ppermute | solution.py:23
  76.5 1.4 %collective-permute-start.29 = (bf16[32,1792]{1,0:T(8,128)(2,1)S(1)}, bf16[32,1792]{1,0:T(8,128)(2,1)S(1)}, u32[]{:S(2)}, u32[]{:S(2)}) collective-permute-start(bf16[32,1792]{1,0:T(8,128)(2,1)S(1)} %get-tuple-element.221), channel_id=1, source_target_pairs={{0,1},{1,0},{2,3},{3,2},{4,5},{5,4},{6,7},{7,6},{8,9},{9,8},{10,11... | collective-permute-start | bytes 344072 | tf_op jit(solution)/shard_map/ppermute | solution.py:23
  76.6 1.5 %collective-permute-start.30 = (bf16[32,1792]{1,0:T(8,128)(2,1)S(1)}, bf16[32,1792]{1,0:T(8,128)(2,1)S(1)}, u32[]{:S(2)}, u32[]{:S(2)}) collective-permute-start(bf16[32,1792]{1,0:T(8,128)(2,1)S(1)} %get-tuple-element.222), channel_id=1, source_target_pairs={{0,1},{1,0},{2,3},{3,2},{4,5},{5,4},{6,7},{7,6},{8,9},{9,8},{10,11... | collective-permute-start | bytes 344072 | tf_op jit(solution)/shard_map/ppermute | solution.py:23
  83.2 4.9 %collective-permute-start.31 = (bf16[16,3584]{1,0:T(8,128)(2,1)S(1)}, bf16[16,3584]{1,0:T(8,128)(2,1)S(1)}, u32[]{:S(2)}, u32[]{:S(2)}) collective-permute-start(bf16[16,3584]{1,0:T(8,128)(2,1)S(1)} %get-tuple-element.228.refs_0_), channel_id=1, source_target_pairs={{0,2},{1,3},{2,0},{3,1},{4,6},{5,7},{6,4},{7,5},{8,10},{9,11},{10,... | collective-permute-start | bytes 344072 | tf_op jit(solution)/shard_map/ppermute | solution.py:23
  83.7 4.3 %collective-permute-start.32 = (bf16[16,3584]{1,0:T(8,128)(2,1)S(1)}, bf16[16,3584]{1,0:T(8,128)(2,1)S(1)}, u32[]{:S(2)}, u32[]{:S(2)}) collective-permute-start(bf16[16,3584]{1,0:T(8,128)(2,1)S(1)} %get-tuple-element.228.refs_0_), channel_id=1, source_target_pairs={{0,1},{1,0},{2,3},{3,2},{4,5},{5,4},{6,7},{7,6},{8,9},{9,8},{10,11... | collective-permute-start | bytes 344072 | tf_op jit(solution)/shard_map/ppermute | solution.py:23
  83.7 9.3 %collective-permute-start.35 = (bf16[64,2048]{1,0:T(8,128)(2,1)S(1)}, bf16[64,2048]{1,0:T(8,128)(2,1)S(1)}, u32[]{:S(2)}, u32[]{:S(2)}) collective-permute-start(bf16[64,2048]{1,0:T(8,128)(2,1)S(1)} %get-tuple-element.234), channel_id=1, source_target_pairs={{0,4},{4,0},{8,12},{12,8},{1,5},{5,1},{9,13},{13,9},{2,6},{6,2},{1... | collective-permute-start | bytes 786440 | tf_op jit(solution)/shard_map/ppermute | solution.py:23
  88.0 8.1 %collective-permute-start.37 = (bf16[32,3584]{1,0:T(8,128)(2,1)S(1)}, bf16[32,3584]{1,0:T(8,128)(2,1)S(1)}, u32[]{:S(2)}, u32[]{:S(2)}) collective-permute-start(bf16[32,3584]{1,0:T(8,128)(2,1)S(1)} %get-tuple-element.232), channel_id=1, source_target_pairs={{0,2},{1,3},{2,0},{3,1},{4,6},{5,7},{6,4},{7,5},{8,10},{9,11},{10,... | collective-permute-start | bytes 688136 | tf_op jit(solution)/shard_map/ppermute | solution.py:23
  88.5 1.3 %collective-permute-start.33 = (bf16[16,3584]{1,0:T(8,128)(2,1)S(1)}, bf16[16,3584]{1,0:T(8,128)(2,1)S(1)}, u32[]{:S(2)}, u32[]{:S(2)}) collective-permute-start(bf16[16,3584]{1,0:T(8,128)(2,1)S(1)} %collective-permute-done.31.refs_1_), channel_id=1, source_target_pairs={{0,1},{1,0},{2,3},{3,2},{4,5},{5,4},{6,7},{7,6},{8,9},{9,8},{10,11... | collective-permute-start | bytes 344072 | tf_op jit(solution)/shard_map/ppermute | solution.py:23
  91.9 14.8 %collective-permute-start.34 = (bf16[64,2048]{1,0:T(8,128)(2,1)S(1)}, bf16[64,2048]{1,0:T(8,128)(2,1)S(1)}, u32[]{:S(2)}, u32[]{:S(2)}) collective-permute-start(bf16[64,2048]{1,0:T(8,128)(2,1)S(1)} %down.9), channel_id=1, source_target_pairs={{0,4},{4,0},{8,12},{12,8},{1,5},{5,1},{9,13},{13,9},{2,6},{6,2},{1... | collective-permute-start | bytes 786440 | tf_op jit(solution)/shard_map/ppermute | solution.py:23
  93.0 13.7 %collective-permute-start.36 = (bf16[64,2048]{1,0:T(8,128)(2,1)S(1)}, bf16[64,2048]{1,0:T(8,128)(2,1)S(1)}, u32[]{:S(2)}, u32[]{:S(2)}) collective-permute-start(bf16[64,2048]{1,0:T(8,128)(2,1)S(1)} %add.26), channel_id=1, source_target_pairs={{0,8},{4,12},{8,0},{12,4},{1,9},{5,13},{9,1},{13,5},{2,10},{6,14},... | collective-permute-start | bytes 786440 | tf_op jit(solution)/shard_map/ppermute | solution.py:23
  95.5 2.2 %collective-permute-start.39 = (bf16[32,1792]{1,0:T(8,128)(2,1)S(1)}, bf16[32,1792]{1,0:T(8,128)(2,1)S(1)}, u32[]{:S(2)}, u32[]{:S(2)}) collective-permute-start(bf16[32,1792]{1,0:T(8,128)(2,1)S(1)} %get-tuple-element.238), channel_id=1, source_target_pairs={{0,1},{1,0},{2,3},{3,2},{4,5},{5,4},{6,7},{7,6},{8,9},{9,8},{10,11... | collective-permute-start | bytes 344072 | tf_op jit(solution)/shard_map/ppermute | solution.py:23
  95.6 2.1 %collective-permute-start.40 = (bf16[32,1792]{1,0:T(8,128)(2,1)S(1)}, bf16[32,1792]{1,0:T(8,128)(2,1)S(1)}, u32[]{:S(2)}, u32[]{:S(2)}) collective-permute-start(bf16[32,1792]{1,0:T(8,128)(2,1)S(1)} %get-tuple-element.239), channel_id=1, source_target_pairs={{0,1},{1,0},{2,3},{3,2},{4,5},{5,4},{6,7},{7,6},{8,9},{9,8},{10,11... | collective-permute-start | bytes 344072 | tf_op jit(solution)/shard_map/ppermute | solution.py:23
  96.2 5.2 %collective-permute-start.38 = (bf16[16,3584]{1,0:T(8,128)(2,1)S(1)}, bf16[16,3584]{1,0:T(8,128)(2,1)S(1)}, u32[]{:S(2)}, u32[]{:S(2)}) collective-permute-start(bf16[16,3584]{1,0:T(8,128)(2,1)S(1)} %hidden.11.share_ref), channel_id=1, source_target_pairs={{0,2},{1,3},{2,0},{3,1},{4,6},{5,7},{6,4},{7,5},{8,10},{9,11},{10,... | collective-permute-start | bytes 344072 | tf_op jit(solution)/shard_map/ppermute | solution.py:23
  101.4 1.5 %collective-permute-start.41 = (bf16[32,1792]{1,0:T(8,128)(2,1)S(1)}, bf16[32,1792]{1,0:T(8,128)(2,1)S(1)}, u32[]{:S(2)}, u32[]{:S(2)}) collective-permute-start(bf16[32,1792]{1,0:T(8,128)(2,1)S(1)} %get-tuple-element.243), channel_id=1, source_target_pairs={{0,1},{1,0},{2,3},{3,2},{4,5},{5,4},{6,7},{7,6},{8,9},{9,8},{10,11... | collective-permute-start | bytes 344072 | tf_op jit(solution)/shard_map/ppermute | solution.py:23
  101.5 1.5 %collective-permute-start.42 = (bf16[32,1792]{1,0:T(8,128)(2,1)S(1)}, bf16[32,1792]{1,0:T(8,128)(2,1)S(1)}, u32[]{:S(2)}, u32[]{:S(2)}) collective-permute-start(bf16[32,1792]{1,0:T(8,128)(2,1)S(1)} %get-tuple-element.244), channel_id=1, source_target_pairs={{0,1},{1,0},{2,3},{3,2},{4,5},{5,4},{6,7},{7,6},{8,9},{9,8},{10,11... | collective-permute-start | bytes 344072 | tf_op jit(solution)/shard_map/ppermute | solution.py:23
  102.0 13.9 %collective-permute-start.43 = (bf16[64,2048]{1,0:T(8,128)(2,1)S(1)}, bf16[64,2048]{1,0:T(8,128)(2,1)S(1)}, u32[]{:S(2)}, u32[]{:S(2)}) collective-permute-start(bf16[64,2048]{1,0:T(8,128)(2,1)S(1)} %down.10), channel_id=1, source_target_pairs={{0,4},{4,0},{8,12},{12,8},{1,5},{5,1},{9,13},{13,9},{2,6},{6,2},{1... | collective-permute-start | bytes 786440 | tf_op jit(solution)/shard_map/ppermute | solution.py:23
  106.8 13.6 %collective-permute-start.44 = (bf16[64,2048]{1,0:T(8,128)(2,1)S(1)}, bf16[64,2048]{1,0:T(8,128)(2,1)S(1)}, u32[]{:S(2)}, u32[]{:S(2)}) collective-permute-start(bf16[64,2048]{1,0:T(8,128)(2,1)S(1)} %add.27), channel_id=1, source_target_pairs={{0,8},{4,12},{8,0},{12,4},{1,9},{5,13},{9,1},{13,5},{2,10},{6,14},... | collective-permute-start | bytes 786440 | tf_op jit(solution)/shard_map/ppermute | solution.py:23
  120.5 4.6 %collective-permute-start.45 = (f32[1,2048]{1,0:T(1,128)S(1)}, f32[1,2048]{1,0:T(1,128)S(1)}, u32[]{:S(2)}, u32[]{:S(2)}) collective-permute-start(f32[1,2048]{1,0:T(1,128)S(1)} %bitcast.6), channel_id=1, source_target_pairs={{0,8},{4,12},{8,0},{12,4},{1,9},{5,13},{9,1},{13,5},{2,10},{6,14},... | collective-permute-start | bytes 24584 | tf_op jit(solution)/shard_map/ppermute | solution.py:23
  125.2 3.7 %collective-permute-start.46 = (f32[1,2048]{1,0:T(1,128)S(1)}, f32[1,2048]{1,0:T(1,128)S(1)}, u32[]{:S(2)}, u32[]{:S(2)}) collective-permute-start(f32[1,2048]{1,0:T(1,128)S(1)} %peak.1.refs_0_), channel_id=1, source_target_pairs={{0,4},{4,0},{8,12},{12,8},{1,5},{5,1},{9,13},{13,9},{2,6},{6,2},{1... | collective-permute-start | bytes 24584 | tf_op jit(solution)/shard_map/ppermute | solution.py:23
  (9 other events, 61.4 us)

commit v7 on v6

--- a/solution.py
+++ b/solution.py
@@ -452,13 +452,16 @@
     got3 = tick(got3)
     (share3,) = done(hidden(mine3, got3))
     over3 = swap(share3, "width", CORES)
+    early3 = swap(share3, "width", 1)
     core5 = ticks(parts_of(joined5, 2))
     (part5,) = done(combine(joined5, core5, down_weight, (jnp.bfloat16,)))
     add5 = swap(part5, AXIS, 1)
-    over3 = tick(over3)
-    joined3 = done(join(share3, over3))
-    core3 = ticks(parts_of(joined3, 2))
-    (cross3,) = done(combine(joined3, core3, down_weight, (jnp.float32,)))
+    over3, early3 = ticks([over3, early3])
+    done(over3)
+    core3 = tick(swap(over3, "width", 1))
+    (cross3,) = done(
+        combine_parts((share3, over3), (early3, core3), down_weight, (jnp.float32,))
+    )
     far3, add2 = ticks([far3, add2])
     add3 = done(call(add_kernel, array(stay, tokens.shape[1]), (cross3, far3), "add"))
     add3 = swap(add3, AXIS, 2)

time: 130 us -> 130 us (level)
    pallas_call x39 -> x37, Pallas kernels: 32.8 us -> 32.8 us  [call(): pl.pallas_call(kernel, out_shape=shapes, in_specs=[VMEM] * len(args), out...]
  transfers between devices with their start and end apart: 47 -> 47, of which waited for: 26 -> 27; matrix products, arithmetic and copies ran while one was open for 0% -> 0% of each run, Pallas kernels for 24% -> 24%
where the time goes in v7:
time: 130 us
  waiting for transfers between devices  55.3 us (43%)
  starting transfers between devices  35.7 us (27%)
  Pallas kernels  32.8 us (25%)
  local copies, waits for them, and re-layouts  4.53 us (3%)
    ppermute x47, waiting for transfers between devices, swap(): return lax.ppermute(value, axis, [(i, i ^ mask) for i in range(size)])  55.3 us
    ppermute x47, starting transfers between devices, swap(): return lax.ppermute(value, axis, [(i, i ^ mask) for i in range(size)])  35.7 us
    pallas_call x37, Pallas kernels, call(): pl.pallas_call(kernel, out_shape=shapes, in_specs=[VMEM] * len(args), out...  32.8 us
    unnamed x20, local copies, waits for them, and re-layouts  4.53 us
  transfers between devices with their start and end apart: 47, of which 27 were waited for; matrix products, arithmetic and copies ran while one was open for 0% of the time, Pallas kernels for 24%

profile of v7, /device:TPU:0, one launch (start us, length us, event | category | flops | bytes accessed | tf_op | source)
XLA Modules:
  0.0 129.5 jit_solution(10707089834688414798)
XLA Ops:
  0.7 3.1 %collective-permute-start = (bf16[128,2048]{1,0:T(8,128)(2,1)}, bf16[128,2048]{1,0:T(8,128)(2,1)S(1)}, u32[]{:S(2)}, u32[]{:S(2)}) collective-permute-start(bf16[128,2048]{1,0:T(8,128)(2,1)} %tokens_ref.1), channel_id=1, source_target_pairs={{0,4},{4,0},{8,12},{12,8},{1,5},{5,1},{9,13},{13,9},{2,6},{6,2},{1... | collective-permute-start | bytes 1572872 | tf_op jit(solution)/shard_map/ppermute | solution.py:23
  3.8 1.8 %copy-done.1 = bf16[128,2048]{1,0:T(8,128)(2,1)S(1)} copy-done((bf16[128,2048]{1,0:T(8,128)(2,1)S(1)}, bf16[128,2048]{1,0:T(8,128)(2,1)}, u32[]{:S(2)}) %copy-start.1) | copy-done | bytes 524312
  6.0 2.1 %gate.4 = (bf16[64,7168]{1,0:T(8,128)(2,1)S(1)}, bf16[64,2304]{1,0:T(8,128)(2,1)S(1)}, bf16[64,2432]{1,0:T(8,128)(2,1)S(1)}, bf16[64,2432]{1,0:T(8,128)(2,1)S(1)}) custom-call(bf16[128,2048]{1,0:T(8,128)(2,1)S(1)} %arrange.2.refs_0_.block_ref, bf16[2048,3584]{1,0:T(8,128)(2,1)S(1)} %copy-done), custom_call_target="tpu_custom_call" | custom-call | flops 3758096384 | bytes 14680064 | tf_op jit(solution)/shard_map/gate/pallas_call | solution.py:48
  8.4 1.2 slice-done.6
  10.4 2.2 %up.4 = (bf16[64,7168]{1,0:T(8,128)(2,1)S(1)}, bf16[64,2304]{1,0:T(8,128)(2,1)S(1)}, bf16[64,2432]{1,0:T(8,128)(2,1)S(1)}, bf16[64,2432]{1,0:T(8,128)(2,1)S(1)}) custom-call(bf16[128,2048]{1,0:T(8,128)(2,1)S(1)} %arrange.2.refs_0_.block_ref, bf16[2048,3584]{1,0:T(8,128)(2,1)S(1)} %bitcast.5, ...), custom_call_target="tpu_custom_call", output_to_operand_aliasing={{0}: (2, {}), {1}: (3, {}), {2}: (4, {}), {3}: (5, {})} | custom-call | flops 1 | bytes 1 | tf_op jit(solution)/shard_map/up/pallas_call | solution.py:48
  13.7 3.7 %collective-permute-start.4 = (bf16[64,2048]{1,0:T(8,128)(2,1)S(1)}, bf16[64,2048]{1,0:T(8,128)(2,1)S(1)}, u32[]{:S(2)}, u32[]{:S(2)}) collective-permute-start(bf16[64,2048]{1,0:T(8,128)(2,1)S(1)} %get-tuple-element.144), channel_id=1, source_target_pairs={{0,8},{4,12},{8,0},{12,4},{1,9},{5,13},{9,1},{13,5},{2,10},{6,14},... | collective-permute-start | bytes 786440 | tf_op jit(solution)/shard_map/ppermute | solution.py:23
  17.6 1.5 %collective-permute-start.7 = (bf16[64,3584]{1,0:T(8,128)(2,1)S(1)}, bf16[64,3584]{1,0:T(8,128)(2,1)S(1)}, u32[]{:S(2)}, u32[]{:S(2)}) collective-permute-start(bf16[64,3584]{1,0:T(8,128)(2,1)S(1)} %get-tuple-element.155), channel_id=1, source_target_pairs={{0,2},{1,3},{2,0},{3,1},{4,6},{5,7},{6,4},{7,5},{8,10},{9,11},{10,... | collective-permute-start | bytes 1376264 | tf_op jit(solution)/shard_map/ppermute | solution.py:23
  19.2 2.1 %gate.5 = (bf16[64,7168]{1,0:T(8,128)(2,1)S(1)}, bf16[32,4736]{1,0:T(8,128)(2,1)S(1)}, bf16[32,2432]{1,0:T(8,128)(2,1)S(1)}, bf16[32,3584]{1,0:T(8,128)(2,1)S(1)}, bf16[32,3584]{1,0:T(8,128)(2,1)S(1)}) custom-call(bf16[128,2048]{1,0:T(8,128)(2,1)S(1)} %arrange.3.refs_0_, bf16[2048,3584]{1,0:T(8,128)(2,1)S(1)} %copy-done), custom_call_target="tpu_custom_call" | custom-call | flops 1 | bytes 1 | tf_op jit(solution)/shard_map/gate/pallas_call | solution.py:48
  21.3 2.2 %up.5 = (bf16[64,7168]{1,0:T(8,128)(2,1)S(1)}, bf16[32,4736]{1,0:T(8,128)(2,1)S(1)}, bf16[32,2432]{1,0:T(8,128)(2,1)S(1)}, bf16[32,3584]{1,0:T(8,128)(2,1)S(1)}, bf16[32,3584]{1,0:T(8,128)(2,1)S(1)}) custom-call(bf16[128,2048]{1,0:T(8,128)(2,1)S(1)} %arrange.3.refs_0_, ...), custom_call_target="tpu_custom_call", output_to_operand_aliasing={{0}: (2, {}), {1}: (3, {}), {2}: (4, {}), {3}: (5, {}), {4}... | custom-call | flops 1 | bytes 1 | tf_op jit(solution)/shard_map/up/pallas_call | solution.py:48
  23.5 6.4 %collective-permute-done.4.refs_0_ = bf16[64,2048]{1,0:T(8,128)(2,1)S(1)} collective-permute-done((bf16[64,2048]{1,0:T(8,128)(2,1)S(1)}, bf16[64,2048]{1,0:T(8,128)(2,1)S(1)}, u32[]{:S(2)}, u32[]{:S(2)}) %collective-permute-start.4) | collective-permute-done | bytes 262176 | tf_op jit(solution)/shard_map/ppermute | solution.py:23
  30.4 1.3 %collective-permute-done.6.refs_2_ = bf16[32,2432]{1,0:T(8,128)(2,1)S(1)} collective-permute-done((bf16[32,2432]{1,0:T(8,128)(2,1)S(1)}, bf16[32,2432]{1,0:T(8,128)(2,1)S(1)}, u32[]{:S(2)}, u32[]{:S(2)}) %collective-permute-start.6) | collective-permute-done | bytes 155680 | tf_op jit(solution)/shard_map/ppermute | solution.py:23
  32.0 1.6 %collective-permute-start.8 = (bf16[64,3584]{1,0:T(8,128)(2,1)S(1)}, bf16[64,3584]{1,0:T(8,128)(2,1)S(1)}, u32[]{:S(2)}, u32[]{:S(2)}) collective-permute-start(bf16[64,3584]{1,0:T(8,128)(2,1)S(1)} %get-tuple-element.158), channel_id=1, source_target_pairs={{0,2},{1,3},{2,0},{3,1},{4,6},{5,7},{6,4},{7,5},{8,10},{9,11},{10,... | collective-permute-start | bytes 1376264 | tf_op jit(solution)/shard_map/ppermute | solution.py:23
  34.4 3.4 %collective-permute-start.13 = (bf16[64,2048]{1,0:T(8,128)(2,1)S(1)}, bf16[64,2048]{1,0:T(8,128)(2,1)S(1)}, u32[]{:S(2)}, u32[]{:S(2)}) collective-permute-start(bf16[64,2048]{1,0:T(8,128)(2,1)S(1)} %get-tuple-element.177), channel_id=1, source_target_pairs={{0,8},{4,12},{8,0},{12,4},{1,9},{5,13},{9,1},{13,5},{2,10},{6,14},... | collective-permute-start | bytes 786440 | tf_op jit(solution)/shard_map/ppermute | solution.py:23
  38.2 1.0 collective-permute-done.10.refs_2_
  39.6 5.0 %collective-permute-done.8.refs_1_ = bf16[64,3584]{1,0:T(8,128)(2,1)S(1)} collective-permute-done((bf16[64,3584]{1,0:T(8,128)(2,1)S(1)}, bf16[64,3584]{1,0:T(8,128)(2,1)S(1)}, u32[]{:S(2)}, u32[]{:S(2)}) %collective-permute-start.8) | collective-permute-done | bytes 458784 | tf_op jit(solution)/shard_map/ppermute | solution.py:23
  44.8 1.6 %collective-permute-start.19 = (bf16[48,3584]{1,0:T(8,128)(2,1)S(1)}, bf16[48,3584]{1,0:T(8,128)(2,1)S(1)}, u32[]{:S(2)}, u32[]{:S(2)}) collective-permute-start(bf16[48,3584]{1,0:T(8,128)(2,1)S(1)} %get-tuple-element.189), channel_id=1, source_target_pairs={{0,2},{1,3},{2,0},{3,1},{4,6},{5,7},{6,4},{7,5},{8,10},{9,11},{10,... | collective-permute-start | bytes 1032200 | tf_op jit(solution)/shard_map/ppermute | solution.py:23
  47.1 2.1 %gate.6 = (bf16[64,7168]{1,0:T(8,128)(2,1)S(1)}, bf16[64,2304]{1,0:T(8,128)(2,1)S(1)}, bf16[64,2432]{1,0:T(8,128)(2,1)S(1)}, bf16[64,2432]{1,0:T(8,128)(2,1)S(1)}) custom-call(bf16[64,2048]{1,0:T(8,128)(2,1)S(1)} %collective-permute-done.4.refs_0_, bf16[64,2048]{1,0:T(8,128)(2,1)S(1)} %collective-permute-done.12.refs_1_, bf16[2048,3584]{1,0:T(8,128)(2,1)S(1)} %copy-done), custom_call_target="tpu_custom_call" | custom-call | flops 1 | bytes 1 | tf_op jit(solution)/shard_map/gate/pallas_call | solution.py:48
  49.2 2.4 %up.6 = (bf16[64,7168]{1,0:T(8,128)(2,1)S(1)}, bf16[64,2304]{1,0:T(8,128)(2,1)S(1)}, bf16[64,2432]{1,0:T(8,128)(2,1)S(1)}, bf16[64,2432]{1,0:T(8,128)(2,1)S(1)}) custom-call(bf16[64,2048]{1,0:T(8,128)(2,1)S(1)} %collective-permute-done.4.refs_0_, ...), custom_call_target="tpu_custom_call", output_to_operand_aliasing={{0}: (3, {}), {1}: (4, {}), {2}: (5, {}), {3}: (6, {})} | custom-call | flops 1 | bytes 1 | tf_op jit(solution)/shard_map/up/pallas_call | solution.py:48
  52.3 1.9 %collective-permute-done.14.refs_1_ = bf16[64,2304]{1,0:T(8,128)(2,1)S(1)} collective-permute-done((bf16[64,2304]{1,0:T(8,128)(2,1)S(1)}, bf16[64,2304]{1,0:T(8,128)(2,1)S(1)}, u32[]{:S(2)}, u32[]{:S(2)}) %collective-permute-start.14) | collective-permute-done | bytes 294944 | tf_op jit(solution)/shard_map/ppermute | solution.py:23
  55.7 1.2 collective-permute-done.20.refs_0_
  57.1 2.1 %down.6 = bf16[64,2048]{1,0:T(8,128)(2,1)S(1)} custom-call(bf16[32,3584]{1,0:T(8,128)(2,1)S(1)} %get-tuple-element.192.mine_ref, bf16[32,1792]{1,0:T(8,128)(2,1)S(1)} %collective-permute-done.20.refs_0_, bf16[32,1792]{1,0:T(8,128)(2,1)S(1)} %collective-permute-done.21.refs_1_, bf16[3584,2048]{1,0:T(8,128)(2,1)S(1)} %bitcast.3), custom_call_target="tpu_custom_call" | custom-call | flops 1 | bytes 1 | tf_op jit(solution)/shard_map/down/pallas_call | solution.py:48
  59.2 1.7 %collective-permute-done.18.refs_1_ = bf16[64,2048]{1,0:T(8,128)(2,1)S(1)} collective-permute-done((bf16[64,2048]{1,0:T(8,128)(2,1)S(1)}, bf16[64,2048]{1,0:T(8,128)(2,1)S(1)}, u32[]{:S(2)}, u32[]{:S(2)}) %collective-permute-start.18) | collective-permute-done | bytes 262176 | tf_op jit(solution)/shard_map/ppermute | solution.py:23
  61.0 2.1 %gate.7 = (bf16[64,7168]{1,0:T(8,128)(2,1)S(1)}, bf16[64,2304]{1,0:T(8,128)(2,1)S(1)}, bf16[64,2432]{1,0:T(8,128)(2,1)S(1)}, bf16[64,2432]{1,0:T(8,128)(2,1)S(1)}) custom-call(bf16[64,2048]{1,0:T(8,128)(2,1)S(1)} %collective-permute-done.13.refs_0_, bf16[64,2048]{1,0:T(8,128)(2,1)S(1)} %collective-permute-done.18.refs_1_, bf16[2048,3584]{1,0:T(8,128)(2,1)S(1)} %copy-done), custom_call_target="tpu_custom_call" | custom-call | flops 1 | bytes 1 | tf_op jit(solution)/shard_map/gate/pallas_call | solution.py:48
  63.0 2.2 %up.7 = (bf16[64,7168]{1,0:T(8,128)(2,1)S(1)}, bf16[64,2304]{1,0:T(8,128)(2,1)S(1)}, bf16[64,2432]{1,0:T(8,128)(2,1)S(1)}, bf16[64,2432]{1,0:T(8,128)(2,1)S(1)}) custom-call(bf16[64,2048]{1,0:T(8,128)(2,1)S(1)} %collective-permute-done.13.refs_0_, ...), custom_call_target="tpu_custom_call", output_to_operand_aliasing={{0}: (3, {}), {1}: (4, {}), {2}: (5, {}), {3}: (6, {})} | custom-call | flops 1 | bytes 1 | tf_op jit(solution)/shard_map/up/pallas_call | solution.py:48
  65.9 1.0 collective-permute-done.22.refs_1_
  68.8 2.1 %down.7 = (f32[64,2048]{1,0:T(8,128)S(1)}, f32[64,2048]{1,0:T(8,128)S(1)}) custom-call(bf16[64,3584]{1,0:T(8,128)(2,1)S(1)} %get-tuple-element.169.mine_ref, bf16[64,3584]{1,0:T(8,128)(2,1)S(1)} %collective-permute-done.11.refs_0_, bf16[3584,2048]{1,0:T(8,128)(2,1)S(1)} %bitcast.3), custom_call_target="tpu_custom_call" | custom-call | flops 1 | bytes 1 | tf_op jit(solution)/shard_map/down/pallas_call | solution.py:48
  70.9 1.6 %collective-permute-start.28 = (bf16[48,3584]{1,0:T(8,128)(2,1)S(1)}, bf16[48,3584]{1,0:T(8,128)(2,1)S(1)}, u32[]{:S(2)}, u32[]{:S(2)}) collective-permute-start(bf16[48,3584]{1,0:T(8,128)(2,1)S(1)} %stack.1), channel_id=1, source_target_pairs={{0,2},{1,3},{2,0},{3,1},{4,6},{5,7},{6,4},{7,5},{8,10},{9,11},{10,... | collective-permute-start | bytes 1032200 | tf_op jit(solution)/shard_map/ppermute | solution.py:23
  72.5 2.8 %collective-permute-done.26 = bf16[64,2048]{1,0:T(8,128)(2,1)S(1)} collective-permute-done((bf16[64,2048]{1,0:T(8,128)(2,1)S(1)}, bf16[64,2048]{1,0:T(8,128)(2,1)S(1)}, u32[]{:S(2)}, u32[]{:S(2)}) %collective-permute-start.26) | collective-permute-done | bytes 262176 | tf_op jit(solution)/shard_map/ppermute | solution.py:23
  75.3 1.2 collective-permute-done.25.mine_ref.refs_1_
  78.1 2.3 %down.8 = (f32[64,2048]{1,0:T(8,128)S(1)}, bf16[64,2048]{1,0:T(8,128)(2,1)S(1)}) custom-call(bf16[32,3584]{1,0:T(8,128)(2,1)S(1)} %hidden.9.refs_0_, bf16[32,3584]{1,0:T(8,128)(2,1)S(1)} %collective-permute-done.25.mine_ref.refs_1_, bf16[32,3584]{1,0:T(8,128)(2,1)S(1)} %collective-permute-done.27.refs_2_, bf16[32,3584]{1,0:T(8,128)(2,1)S(1)} %columns.1.refs_3_, ...), custom_call_target="tpu_custom_call" | custom-call | flops 1 | bytes 1 | tf_op jit(solution)/shard_map/down/pallas_call | solution.py:48
  80.4 2.6 %collective-permute-done.28.refs_1_ = bf16[48,3584]{1,0:T(8,128)(2,1)S(1)} collective-permute-done((bf16[48,3584]{1,0:T(8,128)(2,1)S(1)}, bf16[48,3584]{1,0:T(8,128)(2,1)S(1)}, u32[]{:S(2)}, u32[]{:S(2)}) %collective-permute-start.28) | collective-permute-done | bytes 344096 | tf_op jit(solution)/shard_map/ppermute | solution.py:23
  84.6 3.4 %collective-permute-done.31.refs_1_ = bf16[16,3584]{1,0:T(8,128)(2,1)S(1)} collective-permute-done((bf16[16,3584]{1,0:T(8,128)(2,1)S(1)}, bf16[16,3584]{1,0:T(8,128)(2,1)S(1)}, u32[]{:S(2)}, u32[]{:S(2)}) %collective-permute-start.31) | collective-permute-done | bytes 114720 | tf_op jit(solution)/shard_map/ppermute | solution.py:23
  89.8 2.1 %down.9 = bf16[64,2048]{1,0:T(8,128)(2,1)S(1)} custom-call(bf16[16,3584]{1,0:T(8,128)(2,1)S(1)} %get-tuple-element.226.refs_0_, bf16[16,3584]{1,0:T(8,128)(2,1)S(1)} %collective-permute-done.31.refs_1_, bf16[16,3584]{1,0:T(8,128)(2,1)S(1)} %collective-permute-done.32.refs_2_, bf16[16,3584]{1,0:T(8,128)(2,1)S(1)} %collective-permute-done.33.refs_3_, ...), custom_call_target="tpu_custom_call" | custom-call | flops 1 | bytes 1 | tf_op jit(solution)/shard_map/down/pallas_call | solution.py:48
  91.9 1.1 collective-permute-start.34
  93.0 2.5 %collective-permute-start.36 = (bf16[64,2048]{1,0:T(8,128)(2,1)S(1)}, bf16[64,2048]{1,0:T(8,128)(2,1)S(1)}, u32[]{:S(2)}, u32[]{:S(2)}) collective-permute-start(bf16[64,2048]{1,0:T(8,128)(2,1)S(1)} %add.26), channel_id=1, source_target_pairs={{0,8},{4,12},{8,0},{12,4},{1,9},{5,13},{9,1},{13,5},{2,10},{6,14},... | collective-permute-start | bytes 786440 | tf_op jit(solution)/shard_map/ppermute | solution.py:23
  95.6 1.5 %collective-permute-start.38 = (bf16[16,3584]{1,0:T(8,128)(2,1)S(1)}, bf16[16,3584]{1,0:T(8,128)(2,1)S(1)}, u32[]{:S(2)}, u32[]{:S(2)}) collective-permute-start(bf16[16,3584]{1,0:T(8,128)(2,1)S(1)} %hidden.11.refs_0_), channel_id=1, source_target_pairs={{0,2},{1,3},{2,0},{3,1},{4,6},{5,7},{6,4},{7,5},{8,10},{9,11},{10,... | collective-permute-start | bytes 344072 | tf_op jit(solution)/shard_map/ppermute | solution.py:23
  97.4 2.1 %down.10 = bf16[64,2048]{1,0:T(8,128)(2,1)S(1)} custom-call(bf16[32,3584]{1,0:T(8,128)(2,1)S(1)} %get-tuple-element.235.mine_ref, bf16[32,1792]{1,0:T(8,128)(2,1)S(1)} %collective-permute-done.40.refs_0_, bf16[32,1792]{1,0:T(8,128)(2,1)S(1)} %collective-permute-done.41.refs_1_, bf16[3584,2048]{1,0:T(8,128)(2,1)S(1)} %bitcast.3), custom_call_target="tpu_custom_call" | custom-call | flops 1 | bytes 1 | tf_op jit(solution)/shard_map/down/pallas_call | solution.py:48
  99.5 1.8 %collective-permute-done.38.refs_1_ = bf16[16,3584]{1,0:T(8,128)(2,1)S(1)} collective-permute-done((bf16[16,3584]{1,0:T(8,128)(2,1)S(1)}, bf16[16,3584]{1,0:T(8,128)(2,1)S(1)}, u32[]{:S(2)}, u32[]{:S(2)}) %collective-permute-start.38) | collective-permute-done | bytes 114720 | tf_op jit(solution)/shard_map/ppermute | solution.py:23
  101.2 0.9 collective-permute-start.43
  102.5 2.1 %down.11.part_ref = f32[64,2048]{1,0:T(8,128)S(1)} custom-call(bf16[16,3584]{1,0:T(8,128)(2,1)S(1)} %hidden.11.refs_0_, bf16[16,3584]{1,0:T(8,128)(2,1)S(1)} %collective-permute-done.38.refs_1_, bf16[16,3584]{1,0:T(8,128)(2,1)S(1)} %collective-permute-done.39.refs_2_, bf16[16,3584]{1,0:T(8,128)(2,1)S(1)} %collective-permute-done.42.refs_3_, ...), custom_call_target="tpu_custom_call" | custom-call | flops 1 | bytes 1 | tf_op jit(solution)/shard_map/down/pallas_call | solution.py:48
  104.6 2.1 %collective-permute-done.34.got_ref = bf16[64,2048]{1,0:T(8,128)(2,1)S(1)} collective-permute-done((bf16[64,2048]{1,0:T(8,128)(2,1)S(1)}, bf16[64,2048]{1,0:T(8,128)(2,1)S(1)}, u32[]{:S(2)}, u32[]{:S(2)}) %collective-permute-start.34) | collective-permute-done | bytes 262176 | tf_op jit(solution)/shard_map/ppermute | solution.py:23
  106.8 2.0 %collective-permute-start.44 = (bf16[64,2048]{1,0:T(8,128)(2,1)S(1)}, bf16[64,2048]{1,0:T(8,128)(2,1)S(1)}, u32[]{:S(2)}, u32[]{:S(2)}) collective-permute-start(bf16[64,2048]{1,0:T(8,128)(2,1)S(1)} %add.27), channel_id=1, source_target_pairs={{0,8},{4,12},{8,0},{12,4},{1,9},{5,13},{9,1},{13,5},{2,10},{6,14},... | collective-permute-start | bytes 786440 | tf_op jit(solution)/shard_map/ppermute | solution.py:23
  108.9 7.1 %collective-permute-done.43 = bf16[64,2048]{1,0:T(8,128)(2,1)S(1)} collective-permute-done((bf16[64,2048]{1,0:T(8,128)(2,1)S(1)}, bf16[64,2048]{1,0:T(8,128)(2,1)S(1)}, u32[]{:S(2)}, u32[]{:S(2)}) %collective-permute-start.43) | collective-permute-done | bytes 262176 | tf_op jit(solution)/shard_map/ppermute | solution.py:23
  116.0 4.2 %collective-permute-done.44 = bf16[64,2048]{1,0:T(8,128)(2,1)S(1)} collective-permute-done((bf16[64,2048]{1,0:T(8,128)(2,1)S(1)}, bf16[64,2048]{1,0:T(8,128)(2,1)S(1)}, u32[]{:S(2)}, u32[]{:S(2)}) %collective-permute-start.44) | collective-permute-done | bytes 262176 | tf_op jit(solution)/shard_map/ppermute | solution.py:23
  120.5 4.5 %collective-permute-done.45.other_ref = f32[1,2048]{1,0:T(1,128)S(1)} collective-permute-done((f32[1,2048]{1,0:T(1,128)S(1)}, f32[1,2048]{1,0:T(1,128)S(1)}, u32[]{:S(2)}, u32[]{:S(2)}) %collective-permute-start.45) | collective-permute-done | bytes 8224 | tf_op jit(solution)/shard_map/ppermute | solution.py:23
  125.0 1.7 %collective-permute-start.46 = (f32[1,2048]{1,0:T(1,128)S(1)}, f32[1,2048]{1,0:T(1,128)S(1)}, u32[]{:S(2)}, u32[]{:S(2)}) collective-permute-start(f32[1,2048]{1,0:T(1,128)S(1)} %peak.1.refs_0_), channel_id=1, source_target_pairs={{0,4},{4,0},{8,12},{12,8},{1,5},{5,1},{9,13},{13,9},{2,6},{6,2},{1... | collective-permute-start | bytes 24584 | tf_op jit(solution)/shard_map/ppermute | solution.py:23
  126.7 1.9 %collective-permute-done.46.refs_1_ = f32[1,2048]{1,0:T(1,128)S(1)} collective-permute-done((f32[1,2048]{1,0:T(1,128)S(1)}, f32[1,2048]{1,0:T(1,128)S(1)}, u32[]{:S(2)}, u32[]{:S(2)}) %collective-permute-start.46) | collective-permute-done | bytes 8224 | tf_op jit(solution)/shard_map/ppermute | solution.py:23
  128.7 0.9 scale.1
  (108 shorter events, 17.0 us)
Async XLA Ops:
  0.7 18.5 %collective-permute-start = (bf16[128,2048]{1,0:T(8,128)(2,1)}, bf16[128,2048]{1,0:T(8,128)(2,1)S(1)}, u32[]{:S(2)}, u32[]{:S(2)}) collective-permute-start(bf16[128,2048]{1,0:T(8,128)(2,1)} %tokens_ref.1), channel_id=1, source_target_pairs={{0,4},{4,0},{8,12},{12,8},{1,5},{5,1},{9,13},{13,9},{2,6},{6,2},{1... | collective-permute-start | bytes 1572872 | tf_op jit(solution)/shard_map/ppermute | solution.py:23
  12.6 4.8 %collective-permute-start.2 = (bf16[64,2432]{1,0:T(8,128)(2,1)S(1)}, bf16[64,2432]{1,0:T(8,128)(2,1)S(1)}, u32[]{:S(2)}, u32[]{:S(2)}) collective-permute-start(bf16[64,2432]{1,0:T(8,128)(2,1)S(1)} %get-tuple-element.130), channel_id=1, source_target_pairs={{0,1},{1,0},{2,3},{3,2},{4,5},{5,4},{6,7},{7,6},{8,9},{9,8},{10,11... | collective-permute-start | bytes 933896 | tf_op jit(solution)/shard_map/ppermute | solution.py:23
  13.1 4.3 %collective-permute-start.3 = (bf16[64,2432]{1,0:T(8,128)(2,1)S(1)}, bf16[64,2432]{1,0:T(8,128)(2,1)S(1)}, u32[]{:S(2)}, u32[]{:S(2)}) collective-permute-start(bf16[64,2432]{1,0:T(8,128)(2,1)S(1)} %get-tuple-element.131), channel_id=1, source_target_pairs={{0,1},{1,0},{2,3},{3,2},{4,5},{5,4},{6,7},{7,6},{8,9},{9,8},{10,11... | collective-permute-start | bytes 933896 | tf_op jit(solution)/shard_map/ppermute | solution.py:23
  13.2 4.2 %collective-permute-start.1 = (bf16[64,2304]{1,0:T(8,128)(2,1)S(1)}, bf16[64,2304]{1,0:T(8,128)(2,1)S(1)}, u32[]{:S(2)}, u32[]{:S(2)}) collective-permute-start(bf16[64,2304]{1,0:T(8,128)(2,1)S(1)} %get-tuple-element.129), channel_id=1, source_target_pairs={{0,1},{1,0},{2,3},{3,2},{4,5},{5,4},{6,7},{7,6},{8,9},{9,8},{10,11... | collective-permute-start | bytes 884744 | tf_op jit(solution)/shard_map/ppermute | solution.py:23
  13.7 16.3 %collective-permute-start.4 = (bf16[64,2048]{1,0:T(8,128)(2,1)S(1)}, bf16[64,2048]{1,0:T(8,128)(2,1)S(1)}, u32[]{:S(2)}, u32[]{:S(2)}) collective-permute-start(bf16[64,2048]{1,0:T(8,128)(2,1)S(1)} %get-tuple-element.144), channel_id=1, source_target_pairs={{0,8},{4,12},{8,0},{12,4},{1,9},{5,13},{9,1},{13,5},{2,10},{6,14},... | collective-permute-start | bytes 786440 | tf_op jit(solution)/shard_map/ppermute | solution.py:23
  17.6 14.2 %collective-permute-start.7 = (bf16[64,3584]{1,0:T(8,128)(2,1)S(1)}, bf16[64,3584]{1,0:T(8,128)(2,1)S(1)}, u32[]{:S(2)}, u32[]{:S(2)}) collective-permute-start(bf16[64,3584]{1,0:T(8,128)(2,1)S(1)} %get-tuple-element.155), channel_id=1, source_target_pairs={{0,2},{1,3},{2,0},{3,1},{4,6},{5,7},{6,4},{7,5},{8,10},{9,11},{10,... | collective-permute-start | bytes 1376264 | tf_op jit(solution)/shard_map/ppermute | solution.py:23
  29.9 1.8 %collective-permute-start.5 = (bf16[32,4736]{1,0:T(8,128)(2,1)S(1)}, bf16[32,4736]{1,0:T(8,128)(2,1)S(1)}, u32[]{:S(2)}, u32[]{:S(2)}) collective-permute-start(bf16[32,4736]{1,0:T(8,128)(2,1)S(1)} %get-tuple-element.149), channel_id=1, source_target_pairs={{0,1},{1,0},{2,3},{3,2},{4,5},{5,4},{6,7},{7,6},{8,9},{9,8},{10,11... | collective-permute-start | bytes 909320 | tf_op jit(solution)/shard_map/ppermute | solution.py:23
  29.9 1.8 %collective-permute-start.6 = (bf16[32,2432]{1,0:T(8,128)(2,1)S(1)}, bf16[32,2432]{1,0:T(8,128)(2,1)S(1)}, u32[]{:S(2)}, u32[]{:S(2)}) collective-permute-start(bf16[32,2432]{1,0:T(8,128)(2,1)S(1)} %get-tuple-element.150), channel_id=1, source_target_pairs={{0,1},{1,0},{2,3},{3,2},{4,5},{5,4},{6,7},{7,6},{8,9},{9,8},{10,11... | collective-permute-start | bytes 466952 | tf_op jit(solution)/shard_map/ppermute | solution.py:23
  32.0 12.6 %collective-permute-start.8 = (bf16[64,3584]{1,0:T(8,128)(2,1)S(1)}, bf16[64,3584]{1,0:T(8,128)(2,1)S(1)}, u32[]{:S(2)}, u32[]{:S(2)}) collective-permute-start(bf16[64,3584]{1,0:T(8,128)(2,1)S(1)} %get-tuple-element.158), channel_id=1, source_target_pairs={{0,2},{1,3},{2,0},{3,1},{4,6},{5,7},{6,4},{7,5},{8,10},{9,11},{10,... | collective-permute-start | bytes 1376264 | tf_op jit(solution)/shard_map/ppermute | solution.py:23
  33.7 13.5 %collective-permute-start.12 = (bf16[64,2048]{1,0:T(8,128)(2,1)S(1)}, bf16[64,2048]{1,0:T(8,128)(2,1)S(1)}, u32[]{:S(2)}, u32[]{:S(2)}) collective-permute-start(bf16[64,2048]{1,0:T(8,128)(2,1)S(1)} %collective-permute-done.4.refs_0_), channel_id=1, source_target_pairs={{0,4},{4,0},{8,12},{12,8},{1,5},{5,1},{9,13},{13,9},{2,6},{6,2},{1... | collective-permute-start | bytes 786440 | tf_op jit(solution)/shard_map/ppermute | solution.py:23
  34.4 17.3 %collective-permute-start.13 = (bf16[64,2048]{1,0:T(8,128)(2,1)S(1)}, bf16[64,2048]{1,0:T(8,128)(2,1)S(1)}, u32[]{:S(2)}, u32[]{:S(2)}) collective-permute-start(bf16[64,2048]{1,0:T(8,128)(2,1)S(1)} %get-tuple-element.177), channel_id=1, source_target_pairs={{0,8},{4,12},{8,0},{12,4},{1,9},{5,13},{9,1},{13,5},{2,10},{6,14},... | collective-permute-start | bytes 786440 | tf_op jit(solution)/shard_map/ppermute | solution.py:23
  37.7 1.5 %collective-permute-start.10 = (bf16[32,3584]{1,0:T(8,128)(2,1)S(1)}, bf16[32,3584]{1,0:T(8,128)(2,1)S(1)}, u32[]{:S(2)}, u32[]{:S(2)}) collective-permute-start(bf16[32,3584]{1,0:T(8,128)(2,1)S(1)} %get-tuple-element.163), channel_id=1, source_target_pairs={{0,1},{1,0},{2,3},{3,2},{4,5},{5,4},{6,7},{7,6},{8,9},{9,8},{10,11... | collective-permute-start | bytes 688136 | tf_op jit(solution)/shard_map/ppermute | solution.py:23
  37.7 1.8 %collective-permute-start.9 = (bf16[32,3584]{1,0:T(8,128)(2,1)S(1)}, bf16[32,3584]{1,0:T(8,128)(2,1)S(1)}, u32[]{:S(2)}, u32[]{:S(2)}) collective-permute-start(bf16[32,3584]{1,0:T(8,128)(2,1)S(1)} %get-tuple-element.162), channel_id=1, source_target_pairs={{0,1},{1,0},{2,3},{3,2},{4,5},{5,4},{6,7},{7,6},{8,9},{9,8},{10,11... | collective-permute-start | bytes 688136 | tf_op jit(solution)/shard_map/ppermute | solution.py:23
  44.8 10.2 %collective-permute-start.19 = (bf16[48,3584]{1,0:T(8,128)(2,1)S(1)}, bf16[48,3584]{1,0:T(8,128)(2,1)S(1)}, u32[]{:S(2)}, u32[]{:S(2)}) collective-permute-start(bf16[48,3584]{1,0:T(8,128)(2,1)S(1)} %get-tuple-element.189), channel_id=1, source_target_pairs={{0,2},{1,3},{2,0},{3,1},{4,6},{5,7},{6,4},{7,5},{8,10},{9,11},{10,... | collective-permute-start | bytes 1032200 | tf_op jit(solution)/shard_map/ppermute | solution.py:23
  47.1 10.0 %slice-start.1 = ((s8[14680064]{0:T(1024)(128)(4,1)}), s8[4194304]{0:T(1024)(128)(4,1)S(1)}, s32[]{:S(2)}) async-start(s8[14680064]{0:T(1024)(128)(4,1)} %bitcast.2), calls=%async_computation.1 | async-start | bytes 8388608
  51.7 2.5 %collective-permute-start.15 = (bf16[64,2432]{1,0:T(8,128)(2,1)S(1)}, bf16[64,2432]{1,0:T(8,128)(2,1)S(1)}, u32[]{:S(2)}, u32[]{:S(2)}) collective-permute-start(bf16[64,2432]{1,0:T(8,128)(2,1)S(1)} %get-tuple-element.182), channel_id=1, source_target_pairs={{0,1},{1,0},{2,3},{3,2},{4,5},{5,4},{6,7},{7,6},{8,9},{9,8},{10,11... | collective-permute-start | bytes 933896 | tf_op jit(solution)/shard_map/ppermute | solution.py:23
  51.7 2.5 %collective-permute-start.16 = (bf16[64,2432]{1,0:T(8,128)(2,1)S(1)}, bf16[64,2432]{1,0:T(8,128)(2,1)S(1)}, u32[]{:S(2)}, u32[]{:S(2)}) collective-permute-start(bf16[64,2432]{1,0:T(8,128)(2,1)S(1)} %get-tuple-element.183), channel_id=1, source_target_pairs={{0,1},{1,0},{2,3},{3,2},{4,5},{5,4},{6,7},{7,6},{8,9},{9,8},{10,11... | collective-permute-start | bytes 933896 | tf_op jit(solution)/shard_map/ppermute | solution.py:23
  52.2 2.0 %collective-permute-start.14 = (bf16[64,2304]{1,0:T(8,128)(2,1)S(1)}, bf16[64,2304]{1,0:T(8,128)(2,1)S(1)}, u32[]{:S(2)}, u32[]{:S(2)}) collective-permute-start(bf16[64,2304]{1,0:T(8,128)(2,1)S(1)} %get-tuple-element.181), channel_id=1, source_target_pairs={{0,1},{1,0},{2,3},{3,2},{4,5},{5,4},{6,7},{7,6},{8,9},{9,8},{10,11... | collective-permute-start | bytes 884744 | tf_op jit(solution)/shard_map/ppermute | solution.py:23
  52.3 8.7 %collective-permute-start.18 = (bf16[64,2048]{1,0:T(8,128)(2,1)S(1)}, bf16[64,2048]{1,0:T(8,128)(2,1)S(1)}, u32[]{:S(2)}, u32[]{:S(2)}) collective-permute-start(bf16[64,2048]{1,0:T(8,128)(2,1)S(1)} %collective-permute-done.13.refs_0_), channel_id=1, source_target_pairs={{0,4},{4,0},{8,12},{12,8},{1,5},{5,1},{9,13},{13,9},{2,6},{6,2},{1... | collective-permute-start | bytes 786440 | tf_op jit(solution)/shard_map/ppermute | solution.py:23
  54.4 13.4 %collective-permute-start.17 = (bf16[64,3584]{1,0:T(8,128)(2,1)S(1)}, bf16[64,3584]{1,0:T(8,128)(2,1)S(1)}, u32[]{:S(2)}, u32[]{:S(2)}) collective-permute-start(bf16[64,3584]{1,0:T(8,128)(2,1)S(1)} %get-tuple-element.188), channel_id=1, source_target_pairs={{0,2},{1,3},{2,0},{3,1},{4,6},{5,7},{6,4},{7,5},{8,10},{9,11},{10,... | collective-permute-start | bytes 1376264 | tf_op jit(solution)/shard_map/ppermute | solution.py:23
  55.0 13.8 %collective-permute-start.11 = (bf16[64,3584]{1,0:T(8,128)(2,1)S(1)}, bf16[64,3584]{1,0:T(8,128)(2,1)S(1)}, u32[]{:S(2)}, u32[]{:S(2)}) collective-permute-start(bf16[64,3584]{1,0:T(8,128)(2,1)S(1)} %get-tuple-element.169.mine_ref), channel_id=1, source_target_pairs={{0,1},{1,0},{2,3},{3,2},{4,5},{5,4},{6,7},{7,6},{8,9},{9,8},{10,11... | collective-permute-start | bytes 1376264 | tf_op jit(solution)/shard_map/ppermute | solution.py:23
  55.1 1.9 %collective-permute-start.20 = (bf16[32,1792]{1,0:T(8,128)(2,1)S(1)}, bf16[32,1792]{1,0:T(8,128)(2,1)S(1)}, u32[]{:S(2)}, u32[]{:S(2)}) collective-permute-start(bf16[32,1792]{1,0:T(8,128)(2,1)S(1)} %get-tuple-element.193), channel_id=1, source_target_pairs={{0,1},{1,0},{2,3},{3,2},{4,5},{5,4},{6,7},{7,6},{8,9},{9,8},{10,11... | collective-permute-start | bytes 344072 | tf_op jit(solution)/shard_map/ppermute | solution.py:23
  55.7 1.4 %collective-permute-start.21 = (bf16[32,1792]{1,0:T(8,128)(2,1)S(1)}, bf16[32,1792]{1,0:T(8,128)(2,1)S(1)}, u32[]{:S(2)}, u32[]{:S(2)}) collective-permute-start(bf16[32,1792]{1,0:T(8,128)(2,1)S(1)} %get-tuple-element.194), channel_id=1, source_target_pairs={{0,1},{1,0},{2,3},{3,2},{4,5},{5,4},{6,7},{7,6},{8,9},{9,8},{10,11... | collective-permute-start | bytes 344072 | tf_op jit(solution)/shard_map/ppermute | solution.py:23
  65.3 1.6 %collective-permute-start.22 = (bf16[64,2304]{1,0:T(8,128)(2,1)S(1)}, bf16[64,2304]{1,0:T(8,128)(2,1)S(1)}, u32[]{:S(2)}, u32[]{:S(2)}) collective-permute-start(bf16[64,2304]{1,0:T(8,128)(2,1)S(1)} %get-tuple-element.203), channel_id=1, source_target_pairs={{0,1},{1,0},{2,3},{3,2},{4,5},{5,4},{6,7},{7,6},{8,9},{9,8},{10,11... | collective-permute-start | bytes 884744 | tf_op jit(solution)/shard_map/ppermute | solution.py:23
  65.4 2.0 %collective-permute-start.23 = (bf16[64,2432]{1,0:T(8,128)(2,1)S(1)}, bf16[64,2432]{1,0:T(8,128)(2,1)S(1)}, u32[]{:S(2)}, u32[]{:S(2)}) collective-permute-start(bf16[64,2432]{1,0:T(8,128)(2,1)S(1)} %get-tuple-element.204), channel_id=1, source_target_pairs={{0,1},{1,0},{2,3},{3,2},{4,5},{5,4},{6,7},{7,6},{8,9},{9,8},{10,11... | collective-permute-start | bytes 933896 | tf_op jit(solution)/shard_map/ppermute | solution.py:23
  65.9 2.0 %collective-permute-start.24 = (bf16[64,2432]{1,0:T(8,128)(2,1)S(1)}, bf16[64,2432]{1,0:T(8,128)(2,1)S(1)}, u32[]{:S(2)}, u32[]{:S(2)}) collective-permute-start(bf16[64,2432]{1,0:T(8,128)(2,1)S(1)} %get-tuple-element.205), channel_id=1, source_target_pairs={{0,1},{1,0},{2,3},{3,2},{4,5},{5,4},{6,7},{7,6},{8,9},{9,8},{10,11... | collective-permute-start | bytes 933896 | tf_op jit(solution)/shard_map/ppermute | solution.py:23
  66.9 8.3 %collective-permute-start.26 = (bf16[64,2048]{1,0:T(8,128)(2,1)S(1)}, bf16[64,2048]{1,0:T(8,128)(2,1)S(1)}, u32[]{:S(2)}, u32[]{:S(2)}) collective-permute-start(bf16[64,2048]{1,0:T(8,128)(2,1)S(1)} %down.6), channel_id=1, source_target_pairs={{0,4},{4,0},{8,12},{12,8},{1,5},{5,1},{9,13},{13,9},{2,6},{6,2},{1... | collective-permute-start | bytes 786440 | tf_op jit(solution)/shard_map/ppermute | solution.py:23
  68.0 8.5 %collective-permute-start.25 = (bf16[32,3584]{1,0:T(8,128)(2,1)S(1)}, bf16[32,3584]{1,0:T(8,128)(2,1)S(1)}, u32[]{:S(2)}, u32[]{:S(2)}) collective-permute-start(bf16[32,3584]{1,0:T(8,128)(2,1)S(1)} %hidden.9.refs_0_), channel_id=1, source_target_pairs={{0,2},{1,3},{2,0},{3,1},{4,6},{5,7},{6,4},{7,5},{8,10},{9,11},{10,... | collective-permute-start | bytes 688136 | tf_op jit(solution)/shard_map/ppermute | solution.py:23
  68.5 8.0 %collective-permute-start.27 = (bf16[32,3584]{1,0:T(8,128)(2,1)S(1)}, bf16[32,3584]{1,0:T(8,128)(2,1)S(1)}, u32[]{:S(2)}, u32[]{:S(2)}) collective-permute-start(bf16[32,3584]{1,0:T(8,128)(2,1)S(1)} %hidden.9.refs_0_), channel_id=1, source_target_pairs={{0,1},{1,0},{2,3},{3,2},{4,5},{5,4},{6,7},{7,6},{8,9},{9,8},{10,11... | collective-permute-start | bytes 688136 | tf_op jit(solution)/shard_map/ppermute | solution.py:23
  70.9 12.2 %collective-permute-start.28 = (bf16[48,3584]{1,0:T(8,128)(2,1)S(1)}, bf16[48,3584]{1,0:T(8,128)(2,1)S(1)}, u32[]{:S(2)}, u32[]{:S(2)}) collective-permute-start(bf16[48,3584]{1,0:T(8,128)(2,1)S(1)} %stack.1), channel_id=1, source_target_pairs={{0,2},{1,3},{2,0},{3,1},{4,6},{5,7},{6,4},{7,5},{8,10},{9,11},{10,... | collective-permute-start | bytes 1032200 | tf_op jit(solution)/shard_map/ppermute | solution.py:23
  76.5 1.4 %collective-permute-start.29 = (bf16[32,1792]{1,0:T(8,128)(2,1)S(1)}, bf16[32,1792]{1,0:T(8,128)(2,1)S(1)}, u32[]{:S(2)}, u32[]{:S(2)}) collective-permute-start(bf16[32,1792]{1,0:T(8,128)(2,1)S(1)} %get-tuple-element.219), channel_id=1, source_target_pairs={{0,1},{1,0},{2,3},{3,2},{4,5},{5,4},{6,7},{7,6},{8,9},{9,8},{10,11... | collective-permute-start | bytes 344072 | tf_op jit(solution)/shard_map/ppermute | solution.py:23
  76.6 1.5 %collective-permute-start.30 = (bf16[32,1792]{1,0:T(8,128)(2,1)S(1)}, bf16[32,1792]{1,0:T(8,128)(2,1)S(1)}, u32[]{:S(2)}, u32[]{:S(2)}) collective-permute-start(bf16[32,1792]{1,0:T(8,128)(2,1)S(1)} %get-tuple-element.220), channel_id=1, source_target_pairs={{0,1},{1,0},{2,3},{3,2},{4,5},{5,4},{6,7},{7,6},{8,9},{9,8},{10,11... | collective-permute-start | bytes 344072 | tf_op jit(solution)/shard_map/ppermute | solution.py:23
  83.2 4.9 %collective-permute-start.31 = (bf16[16,3584]{1,0:T(8,128)(2,1)S(1)}, bf16[16,3584]{1,0:T(8,128)(2,1)S(1)}, u32[]{:S(2)}, u32[]{:S(2)}) collective-permute-start(bf16[16,3584]{1,0:T(8,128)(2,1)S(1)} %get-tuple-element.226.refs_0_), channel_id=1, source_target_pairs={{0,2},{1,3},{2,0},{3,1},{4,6},{5,7},{6,4},{7,5},{8,10},{9,11},{10,... | collective-permute-start | bytes 344072 | tf_op jit(solution)/shard_map/ppermute | solution.py:23
  83.7 4.3 %collective-permute-start.32 = (bf16[16,3584]{1,0:T(8,128)(2,1)S(1)}, bf16[16,3584]{1,0:T(8,128)(2,1)S(1)}, u32[]{:S(2)}, u32[]{:S(2)}) collective-permute-start(bf16[16,3584]{1,0:T(8,128)(2,1)S(1)} %get-tuple-element.226.refs_0_), channel_id=1, source_target_pairs={{0,1},{1,0},{2,3},{3,2},{4,5},{5,4},{6,7},{7,6},{8,9},{9,8},{10,11... | collective-permute-start | bytes 344072 | tf_op jit(solution)/shard_map/ppermute | solution.py:23
  83.7 9.3 %collective-permute-start.35 = (bf16[64,2048]{1,0:T(8,128)(2,1)S(1)}, bf16[64,2048]{1,0:T(8,128)(2,1)S(1)}, u32[]{:S(2)}, u32[]{:S(2)}) collective-permute-start(bf16[64,2048]{1,0:T(8,128)(2,1)S(1)} %get-tuple-element.232), channel_id=1, source_target_pairs={{0,4},{4,0},{8,12},{12,8},{1,5},{5,1},{9,13},{13,9},{2,6},{6,2},{1... | collective-permute-start | bytes 786440 | tf_op jit(solution)/shard_map/ppermute | solution.py:23
  88.0 7.5 %collective-permute-start.37 = (bf16[32,3584]{1,0:T(8,128)(2,1)S(1)}, bf16[32,3584]{1,0:T(8,128)(2,1)S(1)}, u32[]{:S(2)}, u32[]{:S(2)}) collective-permute-start(bf16[32,3584]{1,0:T(8,128)(2,1)S(1)} %get-tuple-element.230), channel_id=1, source_target_pairs={{0,2},{1,3},{2,0},{3,1},{4,6},{5,7},{6,4},{7,5},{8,10},{9,11},{10,... | collective-permute-start | bytes 688136 | tf_op jit(solution)/shard_map/ppermute | solution.py:23
  88.5 1.3 %collective-permute-start.33 = (bf16[16,3584]{1,0:T(8,128)(2,1)S(1)}, bf16[16,3584]{1,0:T(8,128)(2,1)S(1)}, u32[]{:S(2)}, u32[]{:S(2)}) collective-permute-start(bf16[16,3584]{1,0:T(8,128)(2,1)S(1)} %collective-permute-done.31.refs_1_), channel_id=1, source_target_pairs={{0,1},{1,0},{2,3},{3,2},{4,5},{5,4},{6,7},{7,6},{8,9},{9,8},{10,11... | collective-permute-start | bytes 344072 | tf_op jit(solution)/shard_map/ppermute | solution.py:23
  88.5 8.6 %collective-permute-start.40 = (bf16[32,1792]{1,0:T(8,128)(2,1)S(1)}, bf16[32,1792]{1,0:T(8,128)(2,1)S(1)}, u32[]{:S(2)}, u32[]{:S(2)}) collective-permute-start(bf16[32,1792]{1,0:T(8,128)(2,1)S(1)} %get-tuple-element.236), channel_id=1, source_target_pairs={{0,1},{1,0},{2,3},{3,2},{4,5},{5,4},{6,7},{7,6},{8,9},{9,8},{10,11... | collective-permute-start | bytes 344072 | tf_op jit(solution)/shard_map/ppermute | solution.py:23
  91.9 14.8 %collective-permute-start.34 = (bf16[64,2048]{1,0:T(8,128)(2,1)S(1)}, bf16[64,2048]{1,0:T(8,128)(2,1)S(1)}, u32[]{:S(2)}, u32[]{:S(2)}) collective-permute-start(bf16[64,2048]{1,0:T(8,128)(2,1)S(1)} %down.9), channel_id=1, source_target_pairs={{0,4},{4,0},{8,12},{12,8},{1,5},{5,1},{9,13},{13,9},{2,6},{6,2},{1... | collective-permute-start | bytes 786440 | tf_op jit(solution)/shard_map/ppermute | solution.py:23
  93.0 13.7 %collective-permute-start.36 = (bf16[64,2048]{1,0:T(8,128)(2,1)S(1)}, bf16[64,2048]{1,0:T(8,128)(2,1)S(1)}, u32[]{:S(2)}, u32[]{:S(2)}) collective-permute-start(bf16[64,2048]{1,0:T(8,128)(2,1)S(1)} %add.26), channel_id=1, source_target_pairs={{0,8},{4,12},{8,0},{12,4},{1,9},{5,13},{9,1},{13,5},{2,10},{6,14},... | collective-permute-start | bytes 786440 | tf_op jit(solution)/shard_map/ppermute | solution.py:23
  95.5 1.9 %collective-permute-start.41 = (bf16[32,1792]{1,0:T(8,128)(2,1)S(1)}, bf16[32,1792]{1,0:T(8,128)(2,1)S(1)}, u32[]{:S(2)}, u32[]{:S(2)}) collective-permute-start(bf16[32,1792]{1,0:T(8,128)(2,1)S(1)} %get-tuple-element.237), channel_id=1, source_target_pairs={{0,1},{1,0},{2,3},{3,2},{4,5},{5,4},{6,7},{7,6},{8,9},{9,8},{10,11... | collective-permute-start | bytes 344072 | tf_op jit(solution)/shard_map/ppermute | solution.py:23
  95.6 5.6 %collective-permute-start.38 = (bf16[16,3584]{1,0:T(8,128)(2,1)S(1)}, bf16[16,3584]{1,0:T(8,128)(2,1)S(1)}, u32[]{:S(2)}, u32[]{:S(2)}) collective-permute-start(bf16[16,3584]{1,0:T(8,128)(2,1)S(1)} %hidden.11.refs_0_), channel_id=1, source_target_pairs={{0,2},{1,3},{2,0},{3,1},{4,6},{5,7},{6,4},{7,5},{8,10},{9,11},{10,... | collective-permute-start | bytes 344072 | tf_op jit(solution)/shard_map/ppermute | solution.py:23
  97.1 4.1 %collective-permute-start.39 = (bf16[16,3584]{1,0:T(8,128)(2,1)S(1)}, bf16[16,3584]{1,0:T(8,128)(2,1)S(1)}, u32[]{:S(2)}, u32[]{:S(2)}) collective-permute-start(bf16[16,3584]{1,0:T(8,128)(2,1)S(1)} %hidden.11.refs_0_), channel_id=1, source_target_pairs={{0,1},{1,0},{2,3},{3,2},{4,5},{5,4},{6,7},{7,6},{8,9},{9,8},{10,11... | collective-permute-start | bytes 344072 | tf_op jit(solution)/shard_map/ppermute | solution.py:23
  101.2 1.3 %collective-permute-start.42 = (bf16[16,3584]{1,0:T(8,128)(2,1)S(1)}, bf16[16,3584]{1,0:T(8,128)(2,1)S(1)}, u32[]{:S(2)}, u32[]{:S(2)}) collective-permute-start(bf16[16,3584]{1,0:T(8,128)(2,1)S(1)} %collective-permute-done.38.refs_1_), channel_id=1, source_target_pairs={{0,1},{1,0},{2,3},{3,2},{4,5},{5,4},{6,7},{7,6},{8,9},{9,8},{10,11... | collective-permute-start | bytes 344072 | tf_op jit(solution)/shard_map/ppermute | solution.py:23
  101.2 14.8 %collective-permute-start.43 = (bf16[64,2048]{1,0:T(8,128)(2,1)S(1)}, bf16[64,2048]{1,0:T(8,128)(2,1)S(1)}, u32[]{:S(2)}, u32[]{:S(2)}) collective-permute-start(bf16[64,2048]{1,0:T(8,128)(2,1)S(1)} %down.10), channel_id=1, source_target_pairs={{0,4},{4,0},{8,12},{12,8},{1,5},{5,1},{9,13},{13,9},{2,6},{6,2},{1... | collective-permute-start | bytes 786440 | tf_op jit(solution)/shard_map/ppermute | solution.py:23
  106.8 13.5 %collective-permute-start.44 = (bf16[64,2048]{1,0:T(8,128)(2,1)S(1)}, bf16[64,2048]{1,0:T(8,128)(2,1)S(1)}, u32[]{:S(2)}, u32[]{:S(2)}) collective-permute-start(bf16[64,2048]{1,0:T(8,128)(2,1)S(1)} %add.27), channel_id=1, source_target_pairs={{0,8},{4,12},{8,0},{12,4},{1,9},{5,13},{9,1},{13,5},{2,10},{6,14},... | collective-permute-start | bytes 786440 | tf_op jit(solution)/shard_map/ppermute | solution.py:23
  120.4 4.6 %collective-permute-start.45 = (f32[1,2048]{1,0:T(1,128)S(1)}, f32[1,2048]{1,0:T(1,128)S(1)}, u32[]{:S(2)}, u32[]{:S(2)}) collective-permute-start(f32[1,2048]{1,0:T(1,128)S(1)} %bitcast.6), channel_id=1, source_target_pairs={{0,8},{4,12},{8,0},{12,4},{1,9},{5,13},{9,1},{13,5},{2,10},{6,14},... | collective-permute-start | bytes 24584 | tf_op jit(solution)/shard_map/ppermute | solution.py:23
  125.0 3.7 %collective-permute-start.46 = (f32[1,2048]{1,0:T(1,128)S(1)}, f32[1,2048]{1,0:T(1,128)S(1)}, u32[]{:S(2)}, u32[]{:S(2)}) collective-permute-start(f32[1,2048]{1,0:T(1,128)S(1)} %peak.1.refs_0_), channel_id=1, source_target_pairs={{0,4},{4,0},{8,12},{12,8},{1,5},{5,1},{9,13},{13,9},{2,6},{6,2},{1... | collective-permute-start | bytes 24584 | tf_op jit(solution)/shard_map/ppermute | solution.py:23
  (9 other events, 61.4 us)
